TPU v7x, 32 devices: a whole 2x2x4 slice. The times are simulated.
32 devices in a mesh: dp: 4 (over x, core), expert: 8 (over z, y).
Axes of the slice: x: 2, y: 2, z: 4, core: 2. Of those that a mesh axis runs over, the one named last changes fastest.
Arguments:
- tokens: bfloat16 [1024, 2048], P('expert', 'dp'), may hold values from -6 to 6
- cotangent: bfloat16 [1024, 2048], P('expert', 'dp'), may hold values from -3 to 3
- expert_ids: int32 [1024, 1], P('expert'), may hold values from 0 to 7; in each aligned block of 128 rows (0 to 127, 128 to 255, ...) at most 16 rows name the same one
- route_weights: float32 [1024, 1], P('expert'), may hold values from 0.2 to 1
- gate_weight: bfloat16 [8, 2048, 1408], P('expert', 'dp'), may hold values from -0.125 to 0.125
- up_weight: bfloat16 [8, 2048, 1408], P('expert', 'dp'), may hold values from -0.125 to 0.125
- down_weight: bfloat16 [8, 1408, 2048], P('expert', None, 'dp'), may hold values from -0.15625 to 0.15625
Outputs:
- token_grad: bfloat16 [1024, 2048], P('expert', 'dp')
- gate_grad: float32 [8, 2048, 1408], P('expert', 'dp')
- up_grad: float32 [8, 2048, 1408], P('expert', 'dp')
- down_grad: float32 [8, 1408, 2048], P('expert', None, 'dp')
Inputs may be any that keep to these rules, and one draw needn't show every extreme that they name: `expert_ids`: each row names 1 different experts. Among the rows of one device no expert is named more than 16 times, a bound that some block reaches in some devices' rows.
All inputs are finite; a program needn't handle non-finite values.
Results may differ from a plain program's by a relative error of at most 0.0057.
Values may be sent and summed in bfloat16 or wider, within the bound.
No kernel may reach another device: no remote copies, remote signals or barrier semaphores. Data moves between devices by JAX's collectives and lax.ppermute only.
A program may use at most 64 MiB of HBM per device.

v0:
```python
import jax
import jax.numpy as jnp
from jax import lax
from jax.sharding import PartitionSpec as P


def contract_rows(left, right):
    return lax.dot_general(
        left, right, (((0,), (0,)), ((), ())), preferred_element_type=jnp.float32
    )


def contract_cols(left, right):
    return lax.dot_general(
        left, right, (((1,), (1,)), ((), ())), preferred_element_type=jnp.float32
    )


def local_deltas(gate_pre, up_pre, hidden_grad):
    sigma = jax.nn.sigmoid(gate_pre)
    activated = gate_pre * sigma
    hidden = (activated * up_pre).astype(jnp.bfloat16)
    gate_delta = (hidden_grad * up_pre * sigma * (1.0 + gate_pre * (1.0 - sigma))).astype(
        jnp.bfloat16
    )
    up_delta = (hidden_grad * activated).astype(jnp.bfloat16)
    return (hidden, gate_delta, up_delta)


def body(tokens, cotangent, expert_ids, route_weights, gate_weight, up_weight, down_weight):
    owners = lax.axis_size("expert")
    tok_rows, top_count = expert_ids.shape
    capacity = min(tok_rows, max(2, (tok_rows * top_count + owners - 1) // owners))
    slot_count = owners * capacity
    flat_ids = expert_ids.reshape(-1)
    position = jnp.arange(flat_ids.shape[0], dtype=jnp.int32)
    earlier = (flat_ids[:, None] == flat_ids[None, :]) & (position[None, :] < position[:, None])
    rank_pos = jnp.sum(earlier.astype(jnp.int32), axis=1)
    slot_pos = flat_ids * capacity + rank_pos
    pair_select = (slot_pos[:, None] == jnp.arange(slot_count, dtype=jnp.int32)[None, :]).astype(
        jnp.bfloat16
    )
    chosen = jnp.sum(
        pair_select.reshape(tok_rows, top_count, slot_count).astype(jnp.float32), axis=1
    ).astype(jnp.bfloat16)
    pair_tokens = jnp.repeat(tokens, top_count, axis=0)
    pair_scaled = (
        jnp.repeat(cotangent.astype(jnp.float32), top_count, axis=0) * route_weights
    ).astype(jnp.bfloat16)
    send_tokens = contract_rows(pair_select, pair_tokens).astype(jnp.bfloat16)
    send_grads = contract_rows(pair_select, pair_scaled).astype(jnp.bfloat16)
    slot_tokens, slot_cot = (
        lax.all_to_all(send_tokens, "expert", split_axis=0, concat_axis=0, tiled=True),
        lax.all_to_all(send_grads, "expert", split_axis=0, concat_axis=0, tiled=True),
    )
    w_gate = gate_weight[0]
    w_up = up_weight[0]
    w_down = down_weight[0]
    gate_part = jnp.dot(slot_tokens, w_gate, preferred_element_type=jnp.float32)
    up_part = jnp.dot(slot_tokens, w_up, preferred_element_type=jnp.float32)
    grad_part = contract_cols(slot_cot, w_down)
    gate_pre, up_pre, hidden_grad = lax.psum((gate_part, up_part, grad_part), "dp")
    hidden, gate_delta, up_delta = local_deltas(gate_pre, up_pre, hidden_grad)
    gate_grad = contract_rows(slot_tokens, gate_delta)
    up_grad = contract_rows(slot_tokens, up_delta)
    down_grad = contract_rows(hidden, slot_cot)
    slot_grad = (contract_cols(gate_delta, w_gate) + contract_cols(up_delta, w_up)).astype(
        jnp.bfloat16
    )
    returned = lax.all_to_all(slot_grad, "expert", split_axis=0, concat_axis=0, tiled=True)
    token_grad = jnp.dot(chosen, returned, preferred_element_type=jnp.float32).astype(jnp.bfloat16)
    return (token_grad, gate_grad[None], up_grad[None], down_grad[None])


def solution(mesh):
    return jax.shard_map(
        body,
        mesh=mesh,
        in_specs=(
            P("expert", "dp"),
            P("expert", "dp"),
            P("expert", None),
            P("expert", None),
            P("expert", "dp", None),
            P("expert", "dp", None),
            P("expert", None, "dp"),
        ),
        out_specs=(
            P("expert", "dp"),
            P("expert", "dp", None),
            P("expert", "dp", None),
            P("expert", None, "dp"),
        ),
        check_vma=False,
    )
```

profile of v0, /device:TPU:0, one launch (start us, length us, event | category | flops | bytes accessed | tf_op | source)
XLA Modules:
  0.0 118.2 jit_solution(15293491617470430972)
XLA Ops:
  7.2 0.0 copy-start
  7.2 1.0 convert_reduce_fusion
  8.1 0.7 fusion.25
  8.8 1.9 %convolution_convert_fusion.1 = bf16[128,512]{1,0:T(8,128)(2,1)} fusion(bf16[128,512]{1,0:T(8,128)(2,1)} %param.7, s32[128]{0:T(128)S(1)} %fusion.25), kind=kOutput, calls=%fused_computation.15 | convolution fusion | flops 16859136 | bytes 262656 | tf_op jit(solution)/shard_map/dot_general | solution.py:8
  10.7 7.3 %all-to-all-start.1 = ((bf16[8,16,512]{2,1,0:T(8,128)(2,1)}), bf16[8,16,512]{2,1,0:T(8,128)(2,1)S(1)}, u32[]{:S(2)}, u32[]{:S(2)}) async-start(bf16[8,16,512]{2,1,0:T(8,128)(2,1)} %bitcast.8), calls=%async_computation.1 | async-start | bytes 262144 | tf_op jit(solution)/shard_map/all_to_all | solution.py:53
  17.9 2.0 %convolution_convert_fusion.2 = bf16[128,512]{1,0:T(8,128)(2,1)} fusion(bf16[128,512]{1,0:T(8,128)(2,1)} %param.8, f32[128]{0:T(128)} %bitcast.59, s32[128]{0:T(128)S(1)} %fusion.25), kind=kOutput, calls=%fused_computation.16 | convolution fusion | flops 17055744 | bytes 263168 | tf_op jit(solution)/shard_map/dot_general | solution.py:8
  19.9 5.4 %all-to-all-done.1 = bf16[8,16,512]{2,1,0:T(8,128)(2,1)S(1)} async-done(((bf16[8,16,512]{2,1,0:T(8,128)(2,1)}), bf16[8,16,512]{2,1,0:T(8,128)(2,1)S(1)}, u32[]{:S(2)}, u32[]{:S(2)}) %all-to-all-start.1) | async-done | bytes 131104 | tf_op jit(solution)/shard_map/all_to_all | solution.py:53
  25.3 3.4 %all-to-all-start = ((bf16[8,16,512]{2,1,0:T(8,128)(2,1)}), bf16[8,16,512]{2,1,0:T(8,128)(2,1)S(1)}, u32[]{:S(2)}, u32[]{:S(2)}) async-start(bf16[8,16,512]{2,1,0:T(8,128)(2,1)} %bitcast.5), calls=%async_computation | async-start | bytes 262144 | tf_op jit(solution)/shard_map/all_to_all | solution.py:54
  28.7 0.0 all-reduce.3.cloned.1.call-start
  28.7 1.2 %fusion.2 = f32[128,1408]{1,0:T(8,128)} fusion(bf16[128,512]{1,0:T(8,128)(2,1)S(1)} %bitcast.52, bf16[1,512,1408]{2,1,0:T(8,128)(2,1)S(1)} %copy-done), kind=kOutput, calls=%fused_computation.5 | convolution fusion | flops 184549376 | bytes 2293760 | tf_op jit(solution)/shard_map/dot_general | solution.py:59
  30.0 1.2 %fusion.6 = f32[128,1408]{1,0:T(8,128)} fusion(bf16[128,512]{1,0:T(8,128)(2,1)S(1)} %bitcast.53, bf16[1,512,1408]{2,1,0:T(8,128)(2,1)S(1)} %copy-done.1), kind=kOutput, calls=%fused_computation.9 | convolution fusion | flops 184549376 | bytes 2293760 | tf_op jit(solution)/shard_map/dot_general | solution.py:60
  31.2 4.7 %all-to-all-done = bf16[8,16,512]{2,1,0:T(8,128)(2,1)S(1)} async-done(((bf16[8,16,512]{2,1,0:T(8,128)(2,1)}), bf16[8,16,512]{2,1,0:T(8,128)(2,1)S(1)}, u32[]{:S(2)}, u32[]{:S(2)}) %all-to-all-start) | async-done | bytes 131104 | tf_op jit(solution)/shard_map/all_to_all | solution.py:54
  35.9 2.8 %fusion.8 = f32[128,1408]{1,0:T(8,128)} fusion(bf16[128,512]{1,0:T(8,128)(2,1)S(1)} %bitcast.56, bf16[1,1408,512]{2,1,0:T(8,128)(2,1)} %param.13), kind=kOutput, calls=%fused_computation.11 | convolution fusion | flops 184549376 | bytes 2293760 | tf_op jit(solution)/shard_map/dot_general | solution.py:14
  38.8 0.0 all-reduce.3.cloned.1.call-update
  38.8 50.7 %all-reduce.3.cloned.1.call-done = (f32[128,1408]{1,0:T(8,128)}, f32[128,1408]{1,0:T(8,128)}, f32[128,1408]{1,0:T(8,128)}) async-done(((f32[128,1408]{1,0:T(8,128)}, f32[128,1408]{1,0:T(8,128)}, f32[128,1408]{1,0:T(8,128)}), (f32[128,1408]{1,0:T(8,128)}, f32[128,1408]{1,0:T(8,128)}, f32[128,1408]{1,0:T(8,128)})) %all-reduce.3.cloned.1.call-update) | async-done | bytes 2162704 | tf_op jit(solution)/shard_map/psum | solution.py:62
  89.5 1.9 %multiply_convert_fusion.1 = (bf16[128,1408]{1,0:T(8,128)(2,1)S(1)}, bf16[128,1408]{1,0:T(8,128)(2,1)S(1)}) fusion(f32[128,1408]{1,0:T(8,128)} %get-tuple-element.5, f32[128,1408]{1,0:T(8,128)} %get-tuple-element.4, f32[128,1408]{1,0:T(8,128)} %get-tuple-element.6), kind=kLoop, calls=%fused_computation.19 | loop fusion | flops 2342912 | bytes 2883584 | tf_op jit(solution)/shard_map/convert_element_type | solution.py:26
  91.4 0.6 fusion
  92.0 2.1 %convolution_bitcast_fusion.2 = f32[1,512,1408]{2,1,0:T(8,128)} fusion(bf16[128,512]{1,0:T(8,128)(2,1)S(1)} %bitcast.54, bf16[128,1408]{1,0:T(8,128)(2,1)S(1)} %get-tuple-element.8), kind=kOutput, calls=%fused_computation.2 | convolution fusion | flops 184549376 | bytes 3375104 | tf_op jit(solution)/shard_map/dot_general | solution.py:8
  94.2 2.1 %convolution_bitcast_fusion.1 = f32[1,512,1408]{2,1,0:T(8,128)} fusion(bf16[128,512]{1,0:T(8,128)(2,1)S(1)} %bitcast.55, bf16[128,1408]{1,0:T(8,128)(2,1)S(1)} %get-tuple-element.7), kind=kOutput, calls=%fused_computation.1 | convolution fusion | flops 184549376 | bytes 3375104 | tf_op jit(solution)/shard_map/dot_general | solution.py:8
  96.3 1.3 %fusion.13 = bf16[128,512]{1,0:T(8,128)(2,1)} fusion(f32[128,512]{1,0:T(8,128)S(1)} %fusion, bf16[128,1408]{1,0:T(8,128)(2,1)S(1)} %get-tuple-element.7, bf16[1,512,1408]{2,1,0:T(8,128)(2,1)S(1)} %copy-done.1), kind=kOutput, calls=%fused_computation.17 | convolution fusion | flops 184680448 | bytes 2195456 | tf_op jit(solution)/shard_map/dot_general | solution.py:14
  97.6 5.5 %all-to-all-start.2 = ((bf16[8,16,512]{2,1,0:T(8,128)(2,1)}), bf16[8,16,512]{2,1,0:T(8,128)(2,1)S(1)}, u32[]{:S(2)}, u32[]{:S(2)}) async-start(bf16[8,16,512]{2,1,0:T(8,128)(2,1)} %bitcast.12), calls=%async_computation.2 | async-start | bytes 262144 | tf_op jit(solution)/shard_map/all_to_all | solution.py:70
  103.1 3.5 %convolution_bitcast_fusion = f32[1,1408,512]{2,1,0:T(8,128)} fusion(bf16[128,512]{1,0:T(8,128)(2,1)S(1)} %bitcast.57, f32[128,1408]{1,0:T(8,128)} %get-tuple-element.6, f32[128,1408]{1,0:T(8,128)} %get-tuple-element.4), kind=kOutput, calls=%fused_computation | convolution fusion | flops 185630720 | bytes 4456448 | tf_op jit(solution)/shard_map/dot_general | solution.py:8
  106.6 3.8 %all-to-all-done.2 = bf16[8,16,512]{2,1,0:T(8,128)(2,1)S(1)} async-done(((bf16[8,16,512]{2,1,0:T(8,128)(2,1)}), bf16[8,16,512]{2,1,0:T(8,128)(2,1)S(1)}, u32[]{:S(2)}, u32[]{:S(2)}) %all-to-all-start.2) | async-done | bytes 131104 | tf_op jit(solution)/shard_map/all_to_all | solution.py:70
  110.4 0.9 convolution_convert_fusion
  (3 shorter events, 0.0 us)
Async XLA Ops:
  7.2 21.6 %copy-start = (bf16[1,512,1408]{2,1,0:T(8,128)(2,1)S(1)}, bf16[1,512,1408]{2,1,0:T(8,128)(2,1)}, u32[]{:S(2)}) copy-start(bf16[1,512,1408]{2,1,0:T(8,128)(2,1)} %param.11) | copy-start | bytes 4325380
  10.7 14.6 %all-to-all-start.1 = ((bf16[8,16,512]{2,1,0:T(8,128)(2,1)}), bf16[8,16,512]{2,1,0:T(8,128)(2,1)S(1)}, u32[]{:S(2)}, u32[]{:S(2)}) async-start(bf16[8,16,512]{2,1,0:T(8,128)(2,1)} %bitcast.8), calls=%async_computation.1 | async-start | bytes 262144 | tf_op jit(solution)/shard_map/all_to_all | solution.py:53
  17.9 12.0 %copy-start.1 = (bf16[1,512,1408]{2,1,0:T(8,128)(2,1)S(1)}, bf16[1,512,1408]{2,1,0:T(8,128)(2,1)}, u32[]{:S(2)}) copy-start(bf16[1,512,1408]{2,1,0:T(8,128)(2,1)} %param.12) | copy-start | bytes 4325380
  25.3 10.7 %all-to-all-start = ((bf16[8,16,512]{2,1,0:T(8,128)(2,1)}), bf16[8,16,512]{2,1,0:T(8,128)(2,1)S(1)}, u32[]{:S(2)}, u32[]{:S(2)}) async-start(bf16[8,16,512]{2,1,0:T(8,128)(2,1)} %bitcast.5), calls=%async_computation | async-start | bytes 262144 | tf_op jit(solution)/shard_map/all_to_all | solution.py:54
  28.7 60.9 %all-reduce.3.cloned.1.call-start = ((), (), s32[]{:S(2)}) async-start(), calls=%async_computation.3 | async-start | bytes 4325376 | tf_op jit(solution)/shard_map/psum | solution.py:62
  97.6 12.9 %all-to-all-start.2 = ((bf16[8,16,512]{2,1,0:T(8,128)(2,1)}), bf16[8,16,512]{2,1,0:T(8,128)(2,1)S(1)}, u32[]{:S(2)}, u32[]{:S(2)}) async-start(bf16[8,16,512]{2,1,0:T(8,128)(2,1)} %bitcast.12), calls=%async_computation.2 | async-start | bytes 262144 | tf_op jit(solution)/shard_map/all_to_all | solution.py:70
Sparse Core Ops, SparseCore 0:
  38.9 50.5 all-reduce.2
where the time goes:
time: 119 us; the launch traced here: 118 us
  waiting for transfers between devices  64.7 us (54%)
  matrix products  19.7 us (17%)
  starting transfers between devices  16.2 us (14%)
  between operations  14.1 us (12%)
  other arithmetic  3.51 us (3%)
    psum x1, waiting for transfers between devices, body(): lax.psum((gate_part, up_part, grad_part), 'dp')  50.7 us
    dot_general x5, matrix products, contract_rows(): lax.dot_general(left, right, (((0,), (0,)), ((), ())), preferred_element_...  11.6 us
    all_to_all x1, starting transfers between devices, body(): lax.all_to_all(send_tokens, 'expert', split_axis=0, concat_axis=0, tiled=...  7.28 us
    all_to_all x1, starting transfers between devices, body(): lax.all_to_all(slot_grad, 'expert', split_axis=0, concat_axis=0, tiled=True)  5.52 us
    all_to_all x1, waiting for transfers between devices, body(): lax.all_to_all(send_tokens, 'expert', split_axis=0, concat_axis=0, tiled=...  5.37 us
    all_to_all x1, waiting for transfers between devices, body(): lax.all_to_all(send_grads, 'expert', split_axis=0, concat_axis=0, tiled=T...  4.74 us
    dot_general x3, matrix products, contract_cols(): lax.dot_general(left, right, (((1,), (1,)), ((), ())), preferred_element_...  4.69 us
    all_to_all x1, waiting for transfers between devices, body(): lax.all_to_all(slot_grad, 'expert', split_axis=0, concat_axis=0, tiled=True)  3.85 us
  transfers between devices with their start and end apart: 4, of which 4 were waited for; matrix products, arithmetic and copies ran while one was open for 7% of the time, Pallas kernels for 0%

commit v1 on v0

--- a/solution.py
+++ b/solution.py
@@ -27,9 +27,16 @@
     return (hidden, gate_delta, up_delta)
 
 
+def swap(value, bit):
+    size = lax.axis_size("dp")
+    return lax.ppermute(value, "dp", [(i, i ^ bit) for i in range(size)])
+
+
 def body(tokens, cotangent, expert_ids, route_weights, gate_weight, up_weight, down_weight):
     owners = lax.axis_size("expert")
+    width_parts = lax.axis_size("dp")
     tok_rows, top_count = expert_ids.shape
+    width = tokens.shape[1]
     capacity = min(tok_rows, max(2, (tok_rows * top_count + owners - 1) // owners))
     slot_count = owners * capacity
     flat_ids = expert_ids.reshape(-1)
@@ -47,27 +54,50 @@
     pair_scaled = (
         jnp.repeat(cotangent.astype(jnp.float32), top_count, axis=0) * route_weights
     ).astype(jnp.bfloat16)
-    send_tokens = contract_rows(pair_select, pair_tokens).astype(jnp.bfloat16)
-    send_grads = contract_rows(pair_select, pair_scaled).astype(jnp.bfloat16)
-    slot_tokens, slot_cot = (
-        lax.all_to_all(send_tokens, "expert", split_axis=0, concat_axis=0, tiled=True),
-        lax.all_to_all(send_grads, "expert", split_axis=0, concat_axis=0, tiled=True),
-    )
+    payload = jnp.concatenate([pair_tokens, pair_scaled], axis=1)
+    send = contract_rows(pair_select, payload).astype(jnp.bfloat16)
+    slots = lax.all_to_all(send, "expert", split_axis=0, concat_axis=0, tiled=True)
+
+    core = lax.axis_index("dp") % 2
+    half = slot_count // 2
+    mine_slots = lax.dynamic_slice_in_dim(slots, core * half, half, 0)
+    other_slots = lax.dynamic_slice_in_dim(slots, (1 - core) * half, half, 0)
     w_gate = gate_weight[0]
     w_up = up_weight[0]
     w_down = down_weight[0]
-    gate_part = jnp.dot(slot_tokens, w_gate, preferred_element_type=jnp.float32)
-    up_part = jnp.dot(slot_tokens, w_up, preferred_element_type=jnp.float32)
-    grad_part = contract_cols(slot_cot, w_down)
-    gate_pre, up_pre, hidden_grad = lax.psum((gate_part, up_part, grad_part), "dp")
-    hidden, gate_delta, up_delta = local_deltas(gate_pre, up_pre, hidden_grad)
-    gate_grad = contract_rows(slot_tokens, gate_delta)
-    up_grad = contract_rows(slot_tokens, up_delta)
-    down_grad = contract_rows(hidden, slot_cot)
+
+    def partial_sums(rows):
+        feats, cots = rows[:, :width], rows[:, width:]
+        return (
+            jnp.dot(feats, w_gate, preferred_element_type=jnp.float32),
+            jnp.dot(feats, w_up, preferred_element_type=jnp.float32),
+            contract_cols(cots, w_down),
+        )
+
+    def pack(parts):
+        return jnp.stack([part.astype(jnp.bfloat16) for part in parts])
+
+    received = swap(pack(partial_sums(other_slots)), 1)
+    sums = jnp.stack(partial_sums(mine_slots)) + received.astype(jnp.float32)
+    bit = 2
+    while bit < width_parts:
+        sums = sums + swap(sums.astype(jnp.bfloat16), bit).astype(jnp.float32)
+        bit *= 2
+    mine = jnp.stack(local_deltas(sums[0], sums[1], sums[2]))
+    other = swap(mine, 1)
+    hidden, gate_delta, up_delta = jnp.concatenate([mine, other], axis=1)
+    both = jnp.concatenate([mine_slots, other_slots], axis=0)
     slot_grad = (contract_cols(gate_delta, w_gate) + contract_cols(up_delta, w_up)).astype(
         jnp.bfloat16
     )
+    slot_grad = jnp.where(
+        core == 0, slot_grad, jnp.concatenate([slot_grad[half:], slot_grad[:half]], axis=0)
+    )
     returned = lax.all_to_all(slot_grad, "expert", split_axis=0, concat_axis=0, tiled=True)
+    feats, cots = both[:, :width], both[:, width:]
+    gate_grad = contract_rows(feats, gate_delta)
+    up_grad = contract_rows(feats, up_delta)
+    down_grad = contract_rows(hidden, cots)
     token_grad = jnp.dot(chosen, returned, preferred_element_type=jnp.float32).astype(jnp.bfloat16)
     return (token_grad, gate_grad[None], up_grad[None], down_grad[None])
 

time: 119 us -> 59.9 us (0.50)
  waiting for transfers between devices: 64.7 us -> 24.5 us
  between operations: 14.1 us -> 0.84 us
  matrix products: 19.7 us -> 14.3 us
  starting transfers between devices: 16.2 us -> 12.5 us
  other arithmetic: 3.51 us -> 5.94 us
  local copies, waits for them, and re-layouts: 0.01 us -> 1.3 us
    psum x1 -> x0, waiting for transfers between devices: 50.7 us -> none  [body(): lax.psum((gate_part, up_part, grad_part), 'dp')]
    ppermute x0 -> x3, waiting for transfers between devices: none -> 15.6 us  [swap(): return lax.ppermute(value, 'dp', [(i, i ^ bit) for i in range(size)])]
    all_to_all x1, waiting for transfers between devices: 3.85 us -> 0.01 us  [body(): lax.all_to_all(slot_grad, 'expert', split_axis=0, concat_axis=0, tiled=True)]
    all_to_all x2 -> x1, starting transfers between devices: 10.7 us -> 7.28 us  [body(): lax.all_to_all(send, 'expert', split_axis=0, concat_axis=0, tiled=True)]
    dot_general x3 -> x4, matrix products: 4.69 us -> 2.35 us  [contract_cols(): lax.dot_general(left, right, (((1,), (1,)), ((), ())), preferred_element_...]
    dot_general x5 -> x4, matrix products: 11.6 us -> 9.54 us  [contract_rows(): lax.dot_general(left, right, (((0,), (0,)), ((), ())), preferred_element_...]
    all_to_all x1, starting transfers between devices: 5.52 us -> 3.59 us  [body(): lax.all_to_all(slot_grad, 'expert', split_axis=0, concat_axis=0, tiled=True)]
    ppermute x0 -> x3, starting transfers between devices: none -> 1.63 us  [swap(): return lax.ppermute(value, 'dp', [(i, i ^ bit) for i in range(size)])]
  transfers between devices with their start and end apart: 4 -> 5, of which waited for: 4 -> 4; matrix products, arithmetic and copies ran while one was open for 7% -> 15% of each run, Pallas kernels for 0% -> 0%
where the time goes in v1:
time: 59.9 us; the launch traced here: 59.4 us
  waiting for transfers between devices  24.5 us (41%)
  matrix products  14.3 us (24%)
  starting transfers between devices  12.5 us (21%)
  other arithmetic  5.94 us (10%)
  local copies, waits for them, and re-layouts  1.3 us (2%)
  between operations  0.84 us (1%)
    ppermute x3, waiting for transfers between devices, swap(): return lax.ppermute(value, 'dp', [(i, i ^ bit) for i in range(size)])  15.6 us
    dot_general x4, matrix products, contract_rows(): lax.dot_general(left, right, (((0,), (0,)), ((), ())), preferred_element_...  9.54 us
    all_to_all x1, waiting for transfers between devices, body(): lax.all_to_all(send, 'expert', split_axis=0, concat_axis=0, tiled=True)  8.92 us
    all_to_all x1, starting transfers between devices, body(): lax.all_to_all(send, 'expert', split_axis=0, concat_axis=0, tiled=True)  7.28 us
    all_to_all x1, starting transfers between devices, body(): lax.all_to_all(slot_grad, 'expert', split_axis=0, concat_axis=0, tiled=True)  3.59 us
    dot_general x4, matrix products, contract_cols(): lax.dot_general(left, right, (((1,), (1,)), ((), ())), preferred_element_...  2.35 us
    ppermute x3, starting transfers between devices, swap(): return lax.ppermute(value, 'dp', [(i, i ^ bit) for i in range(size)])  1.63 us
    concatenate x1, other arithmetic, body(): hidden, gate_delta, up_delta = jnp.concatenate([mine, other], axis=1)  1.27 us
  transfers between devices with their start and end apart: 5, of which 4 were waited for; matrix products, arithmetic and copies ran while one was open for 15% of the time, Pallas kernels for 0%

profile of v1, /device:TPU:0, one launch (start us, length us, event | category | flops | bytes accessed | tf_op | source)
XLA Modules:
  0.0 59.4 jit_solution(14741290062969123457)
XLA Ops:
  0.6 1.0 %convert_reduce_fusion = s32[128]{0:T(128)S(1)} fusion(s32[128]{0:T(128)} %bitcast.77), kind=kLoop, calls=%fused_computation.54 | loop fusion | flops 81792 | bytes 1024 | tf_op jit(solution)/shard_map/reduce_sum | solution.py:45
  1.6 0.7 %fusion.41 = s32[128]{0:T(128)S(1)} fusion(s32[128]{0:T(128)S(1)} %convert_reduce_fusion, s32[128,1]{0,1:T(1,128)} %param.9), kind=kLoop, calls=%fused_computation.71 | loop fusion | flops 256 | bytes 1536 | tf_op jit(solution)/shard_map/add | solution.py:46
  2.3 1.0 %multiply_convert_fusion.3 = bf16[128,512]{1,0:T(8,128)(2,1)S(1)} fusion(bf16[128,512]{1,0:T(8,128)(2,1)} %param.8, f32[128]{0:T(128)} %bitcast.76), kind=kLoop, calls=%fused_computation.45 | loop fusion | flops 196608 | bytes 262656 | tf_op jit(solution)/shard_map/convert_element_type | solution.py:56
  3.3 2.1 %convolution_convert_fusion.3 = bf16[128,1024]{1,0:T(8,128)(2,1)} fusion(bf16[128,512]{1,0:T(8,128)(2,1)S(1)} %multiply_convert_fusion.3, bf16[128,512]{1,0:T(8,128)(2,1)} %param.7, s32[128]{0:T(128)S(1)} %fusion.41), kind=kOutput, calls=%fused_computation.22 | convolution fusion | flops 34226176 | bytes 524800 | tf_op jit(solution)/shard_map/dot_general | solution.py:8
  5.3 7.3 %all-to-all-start = ((bf16[8,16,1024]{2,1,0:T(8,128)(2,1)}), bf16[8,16,1024]{2,1,0:T(8,128)(2,1)S(1)}, u32[]{:S(2)}, u32[]{:S(2)}) async-start(bf16[8,16,1024]{2,1,0:T(8,128)(2,1)} %bitcast.5), calls=%async_computation | async-start | bytes 524288 | tf_op jit(solution)/shard_map/all_to_all | solution.py:59
  12.6 8.9 %all-to-all-done = bf16[8,16,1024]{2,1,0:T(8,128)(2,1)S(1)} async-done(((bf16[8,16,1024]{2,1,0:T(8,128)(2,1)}), bf16[8,16,1024]{2,1,0:T(8,128)(2,1)S(1)}, u32[]{:S(2)}, u32[]{:S(2)}) %all-to-all-start) | async-done | bytes 262176 | tf_op jit(solution)/shard_map/all_to_all | solution.py:59
  22.3 0.6 copy-done.4
  22.9 0.6 fusion.2
  23.7 0.6 convolution_bitcast_fusion.3
  25.0 0.6 collective-permute-done
  25.7 1.6 %collective-permute-start.1 = (bf16[3,64,1408]{2,1,0:T(8,128)(2,1)S(1)}, bf16[3,64,1408]{2,1,0:T(8,128)(2,1)S(1)}, u32[]{:S(2)}, u32[]{:S(2)}) collective-permute-start(bf16[3,64,1408]{2,1,0:T(8,128)(2,1)S(1)} %fusion.19), channel_id=1, source_target_pairs={{0,16},{8,24},{16,0},{24,8},{1,17},{9,25},{17,1},{25,9},{2,18},{10... | collective-permute-start | bytes 1622024 | tf_op jit(solution)/shard_map/ppermute | solution.py:32
  27.2 12.8 %collective-permute-done.1 = bf16[3,64,1408]{2,1,0:T(8,128)(2,1)S(1)} collective-permute-done((bf16[3,64,1408]{2,1,0:T(8,128)(2,1)S(1)}, bf16[3,64,1408]{2,1,0:T(8,128)(2,1)S(1)}, u32[]{:S(2)}, u32[]{:S(2)}) %collective-permute-start.1) | collective-permute-done | bytes 540704 | tf_op jit(solution)/shard_map/ppermute | solution.py:32
  40.4 0.6 %copy-done.5 = bf16[1,64,1408]{2,1,0:T(8,128)(2,1)} copy-done((bf16[1,64,1408]{2,1,0:T(8,128)(2,1)}, bf16[1,64,1408]{2,1,0:T(8,128)(2,1)S(1)}, u32[]{:S(2)}) %copy-start.5) | copy-done | bytes 180248
  41.1 0.9 %pad_maximum_fusion.2 = bf16[3,64,1408]{2,1,0:T(8,128)(2,1)} fusion(bf16[1,64,1408]{2,1,0:T(8,128)(2,1)S(1)} %get-tuple-element.6, bf16[1,64,1408]{2,1,0:T(8,128)(2,1)S(1)} %get-tuple-element.5, bf16[1,64,1408]{2,1,0:T(8,128)(2,1)S(1)} %get-tuple-element.4), kind=kLoop, calls=%fused_computation.30 | loop fusion | flops 540672 | bytes 1081344 | tf_op jit(solution)/shard_map/stack | solution.py:86
  42.0 2.2 %collective-permute-done.2 = bf16[3,64,1408]{2,1,0:T(8,128)(2,1)} collective-permute-done((bf16[3,64,1408]{2,1,0:T(8,128)(2,1)}, bf16[3,64,1408]{2,1,0:T(8,128)(2,1)}, u32[]{:S(2)}, u32[]{:S(2)}) %collective-permute-start.2) | collective-permute-done | bytes 540704 | tf_op jit(solution)/shard_map/ppermute | solution.py:32
  44.2 1.3 %pad_maximum_fusion = bf16[3,128,1408]{2,1,0:T(8,128)(2,1)S(1)} fusion(bf16[3,64,1408]{2,1,0:T(8,128)(2,1)} %collective-permute-done.2, bf16[1,64,1408]{2,1,0:T(8,128)(2,1)} %copy-done.7, bf16[1,64,1408]{2,1,0:T(8,128)(2,1)} %copy-done.6, bf16[1,64,1408]{2,1,0:T(8,128)(2,1)} %copy-done.5), kind=kLoop, calls=%fused_computation.27 | loop fusion | flops 4325376 | bytes 2162688 | tf_op jit(solution)/shard_map/concatenate | solution.py:88
  45.5 0.6 fusion.5
  46.1 0.6 %fusion.16 = bf16[128,512]{1,0:T(8,128)(2,1)S(1)} fusion(f32[128,512]{1,0:T(8,128)S(1)} %fusion.5, bf16[1,512,1408]{2,1,0:T(8,128)(2,1)S(1)} %copy-done.1, bf16[3,128,1408]{2,1,0:T(8,128)(2,1)S(1)} %pad_maximum_fusion), kind=kOutput, calls=%fused_computation.25 | convolution fusion | flops 184680448 | bytes 2195456 | tf_op jit(solution)/shard_map/dot_general | solution.py:14
  46.8 0.7 %maximum_select_fusion = bf16[128,512]{1,0:T(8,128)(2,1)} fusion(bf16[128,512]{1,0:T(8,128)(2,1)S(1)} %fusion.16, bf16[64,512]{1,0:T(8,128)(2,1)S(1)} %get-tuple-element.10, bf16[64,512]{1,0:T(8,128)(2,1)S(1)} %get-tuple-element.9, pred[]{:T(512)S(6)} %eq.56), kind=kLoop, calls=%fused_computation.49 | loop fusion | flops 327680 | bytes 393217 | tf_op jit(solution)/shard_map/jit(_where)/select_n | solution.py:93
  47.4 3.6 %all-to-all-start.1 = ((bf16[8,16,512]{2,1,0:T(8,128)(2,1)}), bf16[8,16,512]{2,1,0:T(8,128)(2,1)S(1)}, u32[]{:S(2)}, u32[]{:S(2)}) async-start(bf16[8,16,512]{2,1,0:T(8,128)(2,1)} %bitcast.18), calls=%async_computation.1 | async-start | bytes 262144 | tf_op jit(solution)/shard_map/all_to_all | solution.py:96
  51.0 3.2 %convolution_bitcast_fusion.1 = f32[1,512,1408]{2,1,0:T(8,128)} fusion(bf16[3,128,1408]{2,1,0:T(8,128)(2,1)} %copy-done.2, bf16[64,1024]{1,0:T(8,128)(2,1)S(1)} %get-tuple-element.8, bf16[64,1024]{1,0:T(8,128)(2,1)S(1)} %get-tuple-element.7), kind=kOutput, calls=%fused_computation.1 | convolution fusion | flops 184811520 | bytes 3506176 | tf_op jit(solution)/shard_map/dot_general | solution.py:8
  54.3 2.1 %convolution_bitcast_fusion.2 = f32[1,512,1408]{2,1,0:T(8,128)} fusion(bf16[3,128,1408]{2,1,0:T(8,128)(2,1)S(1)} %copy-done.3, bf16[64,1024]{1,0:T(8,128)(2,1)S(1)} %get-tuple-element.8, bf16[64,1024]{1,0:T(8,128)(2,1)S(1)} %get-tuple-element.7), kind=kOutput, calls=%fused_computation.2 | convolution fusion | flops 184811520 | bytes 3506176 | tf_op jit(solution)/shard_map/dot_general | solution.py:8
  56.4 2.1 %convolution_bitcast_fusion = f32[1,1408,512]{2,1,0:T(8,128)} fusion(bf16[3,128,1408]{2,1,0:T(8,128)(2,1)S(1)} %copy-done.3, bf16[64,1024]{1,0:T(8,128)(2,1)S(1)} %get-tuple-element.7, bf16[64,1024]{1,0:T(8,128)(2,1)S(1)} %get-tuple-element.8), kind=kOutput, calls=%fused_computation | convolution fusion | flops 184811520 | bytes 3506176 | tf_op jit(solution)/shard_map/dot_general | solution.py:8
  58.5 0.9 %convolution_convert_fusion.4 = bf16[128,512]{1,0:T(8,128)(2,1)} fusion(bf16[128,512]{1,0:T(8,128)(2,1)S(1)} %bitcast.75, s32[128]{0:T(128)S(1)} %fusion.41), kind=kOutput, calls=%fused_computation.24 | convolution fusion | flops 16859136 | bytes 262656 | tf_op jit(solution)/shard_map/dot_general | solution.py:101
  (27 shorter events, 2.2 us)
Async XLA Ops:
  0.6 20.9 %copy-start = (bf16[1,512,1408]{2,1,0:T(8,128)(2,1)S(1)}, bf16[1,512,1408]{2,1,0:T(8,128)(2,1)}, u32[]{:S(2)}) copy-start(bf16[1,512,1408]{2,1,0:T(8,128)(2,1)} %param.12) | copy-start | bytes 4325380
  3.3 18.7 %copy-start.1 = (bf16[1,512,1408]{2,1,0:T(8,128)(2,1)S(1)}, bf16[1,512,1408]{2,1,0:T(8,128)(2,1)}, u32[]{:S(2)}) copy-start(bf16[1,512,1408]{2,1,0:T(8,128)(2,1)} %param.11) | copy-start | bytes 4325380
  5.3 16.2 %all-to-all-start = ((bf16[8,16,1024]{2,1,0:T(8,128)(2,1)}), bf16[8,16,1024]{2,1,0:T(8,128)(2,1)S(1)}, u32[]{:S(2)}, u32[]{:S(2)}) async-start(bf16[8,16,1024]{2,1,0:T(8,128)(2,1)} %bitcast.5), calls=%async_computation | async-start | bytes 524288 | tf_op jit(solution)/shard_map/all_to_all | solution.py:59
  21.5 1.4 %copy-start.4 = (bf16[1,1408,512]{2,1,0:T(8,128)(2,1)S(1)}, bf16[1,1408,512]{2,1,0:T(8,128)(2,1)}, u32[]{:S(2)}) copy-start(bf16[1,1408,512]{2,1,0:T(8,128)(2,1)} %param.13) | copy-start | bytes 4325380
  23.6 2.0 %collective-permute-start = (bf16[3,64,1408]{2,1,0:T(8,128)(2,1)S(1)}, bf16[3,64,1408]{2,1,0:T(8,128)(2,1)S(1)}, u32[]{:S(2)}, u32[]{:S(2)}) collective-permute-start(bf16[3,64,1408]{2,1,0:T(8,128)(2,1)S(1)} %pad_maximum_fusion.1), channel_id=1, source_target_pairs={{0,8},{8,0},{16,24},{24,16},{1,9},{9,1},{17,25},{25,17},{2,10},{10... | collective-permute-start | bytes 1622024 | tf_op jit(solution)/shard_map/ppermute | solution.py:32
  25.7 14.4 %collective-permute-start.1 = (bf16[3,64,1408]{2,1,0:T(8,128)(2,1)S(1)}, bf16[3,64,1408]{2,1,0:T(8,128)(2,1)S(1)}, u32[]{:S(2)}, u32[]{:S(2)}) collective-permute-start(bf16[3,64,1408]{2,1,0:T(8,128)(2,1)S(1)} %fusion.19), channel_id=1, source_target_pairs={{0,16},{8,24},{16,0},{24,8},{1,17},{9,25},{17,1},{25,9},{2,18},{10... | collective-permute-start | bytes 1622024 | tf_op jit(solution)/shard_map/ppermute | solution.py:32
  40.4 0.7 %copy-start.5 = (bf16[1,64,1408]{2,1,0:T(8,128)(2,1)}, bf16[1,64,1408]{2,1,0:T(8,128)(2,1)S(1)}, u32[]{:S(2)}) copy-start(bf16[1,64,1408]{2,1,0:T(8,128)(2,1)S(1)} %get-tuple-element.4) | copy-start | bytes 540676
  40.4 1.5 %copy-start.6 = (bf16[1,64,1408]{2,1,0:T(8,128)(2,1)}, bf16[1,64,1408]{2,1,0:T(8,128)(2,1)S(1)}, u32[]{:S(2)}) copy-start(bf16[1,64,1408]{2,1,0:T(8,128)(2,1)S(1)} %get-tuple-element.5) | copy-start | bytes 540676
  40.4 1.5 %copy-start.7 = (bf16[1,64,1408]{2,1,0:T(8,128)(2,1)}, bf16[1,64,1408]{2,1,0:T(8,128)(2,1)S(1)}, u32[]{:S(2)}) copy-start(bf16[1,64,1408]{2,1,0:T(8,128)(2,1)S(1)} %get-tuple-element.6) | copy-start | bytes 540676
  41.9 2.3 %collective-permute-start.2 = (bf16[3,64,1408]{2,1,0:T(8,128)(2,1)}, bf16[3,64,1408]{2,1,0:T(8,128)(2,1)}, u32[]{:S(2)}, u32[]{:S(2)}) collective-permute-start(bf16[3,64,1408]{2,1,0:T(8,128)(2,1)} %pad_maximum_fusion.2), channel_id=1, source_target_pairs={{0,8},{8,0},{16,24},{24,16},{1,9},{9,1},{17,25},{25,17},{2,10},{10... | collective-permute-start | bytes 1622024 | tf_op jit(solution)/shard_map/ppermute | solution.py:32
  45.5 1.2 %copy-start.2 = (bf16[3,128,1408]{2,1,0:T(8,128)(2,1)}, bf16[3,128,1408]{2,1,0:T(8,128)(2,1)S(1)}, u32[]{:S(2)}) copy-start(bf16[3,128,1408]{2,1,0:T(8,128)(2,1)S(1)} %pad_maximum_fusion) | copy-start | bytes 3244036
  47.4 11.1 %all-to-all-start.1 = ((bf16[8,16,512]{2,1,0:T(8,128)(2,1)}), bf16[8,16,512]{2,1,0:T(8,128)(2,1)S(1)}, u32[]{:S(2)}, u32[]{:S(2)}) async-start(bf16[8,16,512]{2,1,0:T(8,128)(2,1)} %bitcast.18), calls=%async_computation.1 | async-start | bytes 262144 | tf_op jit(solution)/shard_map/all_to_all | solution.py:96
  51.0 3.2 %copy-start.3 = (bf16[3,128,1408]{2,1,0:T(8,128)(2,1)S(1)}, bf16[3,128,1408]{2,1,0:T(8,128)(2,1)}, u32[]{:S(2)}) copy-start(bf16[3,128,1408]{2,1,0:T(8,128)(2,1)} %copy-done.2) | copy-start | bytes 3244036

commit v2 on v1

--- a/solution.py
+++ b/solution.py
@@ -1,6 +1,10 @@
+import functools
+
 import jax
 import jax.numpy as jnp
 from jax import lax
+from jax.experimental import pallas as pl
+from jax.experimental.pallas import tpu as pltpu
 from jax.sharding import PartitionSpec as P
 
 
@@ -27,12 +31,212 @@
     return (hidden, gate_delta, up_delta)
 
 
-def swap(value, bit):
-    size = lax.axis_size("dp")
-    return lax.ppermute(value, "dp", [(i, i ^ bit) for i in range(size)])
-
-
-def body(tokens, cotangent, expert_ids, route_weights, gate_weight, up_weight, down_weight):
+def swap(value, bit, axis="dp"):
+    size = lax.axis_size(axis)
+    return lax.ppermute(value, axis, [(i, i ^ bit) for i in range(size)])
+
+
+COST = dict(
+    load=10**7,
+    products=(1, 1),
+    sums=(1, 1),
+    deltas=(1, 1),
+    grad=(1, 1),
+    wgrad=10**7,
+)
+TIE = 1
+
+
+def after(values, marker):
+    return lax.optimization_barrier((values, marker))[0]
+
+
+def call(kernel, outs, *args, cost=1, far=(), scratch=()):
+    spaces = [pltpu.HBM if place in far else pltpu.VMEM for place in range(len(args))]
+    args = [
+        pltpu.with_memory_space_constraint(arg, pltpu.HBM) if place in far else arg
+        for place, arg in enumerate(args)
+    ]
+    args = [
+        pltpu.with_memory_space_constraint(arg, pltpu.HBM) if place in far else arg
+        for place, arg in enumerate(args)
+    ]
+    return pl.pallas_call(
+        kernel,
+        out_shape=outs,
+        in_specs=[pl.BlockSpec(memory_space=space) for space in spaces],
+        scratch_shapes=scratch,
+        compiler_params=pltpu.CompilerParams(vmem_limit_bytes=24 * 1024 * 1024),
+        cost_estimate=pl.CostEstimate(flops=cost, bytes_accessed=cost, transcendentals=0),
+    )(*args)
+
+
+def shape(rows, cols, dtype=jnp.bfloat16):
+    return jax.ShapeDtypeStruct((rows, cols), dtype)
+
+
+def dispatch_kernel(owners, capacity, ids_hbm, weights_hbm, tokens_hbm, cotangent_hbm, *refs):
+    chosen_ref, *out_refs, ids_ref, weights_ref, tokens_ref, cotangent_ref, sems = refs
+    copies = [
+        pltpu.make_async_copy(source, target, sems.at[place])
+        for place, (source, target) in enumerate(
+            (
+                (ids_hbm, ids_ref),
+                (weights_hbm, weights_ref),
+                (tokens_hbm, tokens_ref),
+                (cotangent_hbm, cotangent_ref),
+            )
+        )
+    ]
+    for copy in copies:
+        copy.start()
+    copies[0].wait()
+    pairs = ids_ref.shape[1]
+    width = tokens_ref.shape[1]
+    slot_count = owners * capacity
+    me = lax.axis_index("expert")
+    ids = ids_ref[...]
+    named = ids == lax.broadcasted_iota(jnp.int32, (owners, pairs), 0)
+    before = lax.broadcasted_iota(jnp.int32, (pairs, pairs), 0) < lax.broadcasted_iota(
+        jnp.int32, (pairs, pairs), 1
+    )
+    named = named.astype(jnp.float32)
+    counts = jnp.dot(
+        named.astype(jnp.bfloat16),
+        before.astype(jnp.float32).astype(jnp.bfloat16),
+        preferred_element_type=jnp.float32,
+    )
+    rank = jnp.sum(named * counts, axis=0, keepdims=True).astype(jnp.int32)
+    slots = lax.broadcasted_iota(jnp.int32, (slot_count, pairs), 0)
+    chosen_ref[...] = (slots == ids * capacity + rank).astype(jnp.float32).astype(jnp.bfloat16)
+    chosen = (slots == (ids ^ me) * capacity + rank).astype(jnp.float32)
+    select = chosen.astype(jnp.bfloat16)
+    for copy in copies[1:]:
+        copy.wait()
+    scale = jnp.sum(chosen * weights_ref[...], axis=1, keepdims=True)
+    feats = jnp.dot(select, tokens_ref[...], preferred_element_type=jnp.float32)
+    cots = jnp.dot(select, cotangent_ref[...], preferred_element_type=jnp.float32) * scale
+    at = 0
+    for out_ref in out_refs:
+        rows = slice(at, at + out_ref.shape[0])
+        out_ref[:, :width] = feats[rows].astype(jnp.bfloat16)
+        out_ref[:, width:] = cots[rows].astype(jnp.bfloat16)
+        at += out_ref.shape[0]
+
+
+def load_kernel(gate_hbm, up_hbm, down_hbm, marker_hbm, gate_ref, up_ref, down_ref, sems):
+    copies = [
+        pltpu.make_async_copy(source, target, sems.at[place])
+        for place, (source, target) in enumerate(
+            ((gate_hbm, gate_ref), (up_hbm, up_ref), (down_hbm, down_ref))
+        )
+    ]
+    for copy in copies:
+        copy.start()
+    for copy in copies:
+        copy.wait()
+
+
+def straight_rows(refs):
+    return [ref[:ref.shape[0] // 2] for ref in refs]
+
+
+def pair_rows(refs):
+    return [ref[...] for ref in refs]
+
+
+def products_kernel(take_rows, *refs):
+    *row_refs, gate_ref, up_ref, down_ref, mine_ref, other_ref = refs
+    rows = jnp.concatenate(take_rows(row_refs), axis=0)
+    half = rows.shape[0] // 2
+    width = rows.shape[1] // 2
+    hidden_units = gate_ref.shape[1]
+    core = lax.axis_index("dp") % 2
+    feats, cots = rows[:, :width], rows[:, width:]
+    for place, weight_ref in enumerate((gate_ref, up_ref, down_ref)):
+        cols = slice(place * hidden_units, (place + 1) * hidden_units)
+        if place < 2:
+            out = jnp.dot(feats, weight_ref[...], preferred_element_type=jnp.float32)
+        else:
+            out = contract_cols(cots, weight_ref[...])
+        low, high = out[:half], out[half:]
+        mine_ref[:, cols] = jnp.where(core == 0, low, high)
+        other_ref[:, cols] = jnp.where(core == 0, high, low).astype(jnp.bfloat16)
+
+
+def sums_kernel(mine_ref, received_ref, sums_ref, packed_ref):
+    sums = mine_ref[...] + received_ref[...].astype(jnp.float32)
+    sums_ref[...] = sums
+    packed_ref[...] = sums.astype(jnp.bfloat16)
+
+
+def deltas_kernel(sums_ref, received_ref, out_ref):
+    hidden_units = sums_ref.shape[1] // 3
+    cols = [slice(i * hidden_units, (i + 1) * hidden_units) for i in range(3)]
+    parts = [sums_ref[:, c] + received_ref[:, c].astype(jnp.float32) for c in cols]
+    for c, part in zip(cols, local_deltas(*parts)):
+        out_ref[:, c] = part
+
+
+def in_order(core, mine, other):
+    return jnp.concatenate(
+        [jnp.where(core == 0, mine, other), jnp.where(core == 0, other, mine)], axis=0
+    )
+
+
+def slot_grad_kernel(owners, mine_ref, other_ref, gate_ref, up_ref, *refs):
+    *earlier_ref, out_ref = refs
+    hidden_units = gate_ref.shape[1]
+    rows = in_order(lax.axis_index("dp") % 2, mine_ref[...], other_ref[...])
+    out = (
+        contract_cols(rows[:, hidden_units:2 * hidden_units], gate_ref[...])
+        + contract_cols(rows[:, 2 * hidden_units:], up_ref[...])
+    ).astype(jnp.bfloat16)
+    if not earlier_ref:
+        out_ref[...] = out
+        return
+    me = lax.axis_index("expert")
+    block = out_ref.shape[0] // owners
+    earlier = earlier_ref[0][...]
+    for k in range(owners):
+        source = (earlier, out)[k % 2]
+        at = k // 2 * block
+        out_ref[pl.ds(pl.multiple_of((me ^ k) * block, block), block)] = source[at:at + block]
+
+
+def weight_grads_kernel(*refs):
+    *in_refs, gate_ref, up_ref, down_ref, rows_ref, deltas_ref = refs
+    row_refs, delta_refs = in_refs[:-4], in_refs[-4:]
+    step = pl.program_id(0)
+    tile = gate_ref.shape[0]
+    down_tile = down_ref.shape[0]
+    width = rows_ref.shape[1] // 2
+    hidden_units = gate_ref.shape[1]
+
+    @pl.when(step == 0)
+    def _():
+        at = 0
+        for value in straight_rows(row_refs[:-1]) + pair_rows(row_refs[-1:]):
+            rows_ref[at:at + value.shape[0]] = value
+            at += value.shape[0]
+        core = lax.axis_index("dp") % 2
+        half = deltas_ref.shape[0] // 2
+        for place in range(2):
+            both = in_order(core, delta_refs[2 * place][...], delta_refs[2 * place + 1][...])
+            deltas_ref[place * half:(place + 1) * half] = both
+
+    feats = rows_ref[:, pl.ds(pl.multiple_of(step * tile, tile), tile)]
+    gate_ref[...] = contract_rows(feats, deltas_ref[:, hidden_units:2 * hidden_units])
+    up_ref[...] = contract_rows(feats, deltas_ref[:, 2 * hidden_units:])
+    hidden = deltas_ref[:, pl.ds(pl.multiple_of(step * down_tile, down_tile), down_tile)]
+    down_ref[...] = contract_rows(hidden, rows_ref[:, width:])
+
+
+def token_grad_kernel(chosen_ref, returned_ref, out_ref):
+    out_ref[...] = contract_rows(chosen_ref[...], returned_ref[...]).astype(jnp.bfloat16)
+
+
+def body_by_all_to_all(tokens, cotangent, expert_ids, route_weights, gate_weight, up_weight, down_weight):
     owners = lax.axis_size("expert")
     width_parts = lax.axis_size("dp")
     tok_rows, top_count = expert_ids.shape
@@ -100,6 +304,134 @@
     down_grad = contract_rows(hidden, cots)
     token_grad = jnp.dot(chosen, returned, preferred_element_type=jnp.float32).astype(jnp.bfloat16)
     return (token_grad, gate_grad[None], up_grad[None], down_grad[None])
+
+
+def body_by_pairs(tokens, cotangent, expert_ids, route_weights, gate_weight, up_weight, down_weight):
+    owners = lax.axis_size("expert")
+    width_parts = lax.axis_size("dp")
+    tok_rows, _ = expert_ids.shape
+    width = tokens.shape[1]
+    hidden_units = gate_weight.shape[2]
+    capacity = min(tok_rows, max(2, (tok_rows + owners - 1) // owners))
+    slot_count = owners * capacity
+    half = owners // 2
+
+    chosen, *groups = call(
+        functools.partial(dispatch_kernel, owners, capacity),
+        (shape(slot_count, tok_rows),) + (shape(2 * capacity, 2 * width),) * half,
+        expert_ids.reshape(1, tok_rows),
+        route_weights.reshape(1, tok_rows),
+        tokens,
+        cotangent,
+        far=range(4),
+        scratch=[
+            pltpu.VMEM((1, tok_rows), jnp.int32),
+            pltpu.VMEM((1, tok_rows), jnp.float32),
+            pltpu.VMEM((tok_rows, width), jnp.bfloat16),
+            pltpu.VMEM((tok_rows, width), jnp.bfloat16),
+            pltpu.SemaphoreType.DMA((4,)),
+        ],
+    )
+    weights = call(
+        load_kernel,
+        (shape(width, hidden_units), shape(width, hidden_units), shape(hidden_units, width)),
+        gate_weight[0],
+        up_weight[0],
+        down_weight[0],
+        chosen,
+        far=range(3),
+        scratch=[pltpu.SemaphoreType.DMA((3,))],
+        cost=COST["load"],
+    )
+    moved = {j: swap(groups[j], 2 * j, "expert") for j in reversed(range(1, half))}
+    groups = [groups[0]] + [moved[j] for j in range(1, half)]
+    forward = jnp.concatenate([group[capacity:] for group in groups], axis=0)
+    forward = after(forward, weights[2])
+    by_pair = swap(forward, 1, "expert")
+    order = list(range(0, owners, 2)) + list(range(1, owners, 2))
+
+    part = slot_count // 4
+    packed = shape(part, 3 * hidden_units)
+    wide = shape(part, 3 * hidden_units, jnp.float32)
+    held = []
+    for place, (take, rows) in enumerate(((straight_rows, groups), (pair_rows, [by_pair]))):
+        mine, other = call(
+            functools.partial(products_kernel, take),
+            (wide, packed),
+            *rows,
+            *weights,
+            cost=COST["products"][place],
+        )
+        sums, marker = call(
+            sums_kernel, (wide, packed), mine, swap(other, 1), cost=COST["sums"][place]
+        )
+        bit = 2
+        while 2 * bit < width_parts:
+            sums, marker = call(sums_kernel, (wide, packed), sums, swap(marker, bit))
+            bit *= 2
+        held.append((sums, swap(marker, bit)))
+    deltas, grads = [], []
+    for place, (sums, received) in enumerate(held):
+        if place and TIE == 1:
+            sums = after(sums, grads)
+        mine = call(deltas_kernel, packed, sums, received, cost=COST["deltas"][place])
+        if place and TIE == 3:
+            mine = after(mine, grads)
+        pair = [mine, swap(mine, 1)]
+        deltas += pair
+        grads = [
+            call(
+                functools.partial(slot_grad_kernel, owners),
+                shape((place + 1) * half * capacity, width),
+                *pair,
+                *weights[:2],
+                *grads,
+                cost=COST["grad"][place],
+            )
+        ]
+    returned = lax.all_to_all(grads[0], "expert", split_axis=0, concat_axis=0, tiled=True)
+    steps = 4 if width % 512 == 0 else 1
+    down_tile = -(-hidden_units // (128 * steps)) * 128
+    gate_grad, up_grad, down_grad = pl.pallas_call(
+        weight_grads_kernel,
+        out_shape=(
+            shape(width, hidden_units, jnp.float32),
+            shape(width, hidden_units, jnp.float32),
+            shape(hidden_units, width, jnp.float32),
+        ),
+        grid=(steps,),
+        in_specs=[pl.BlockSpec(memory_space=pltpu.VMEM)] * (half + 1 + 4),
+        out_specs=(
+            pl.BlockSpec((width // steps, hidden_units), lambda i: (i, 0)),
+            pl.BlockSpec((width // steps, hidden_units), lambda i: (i, 0)),
+            pl.BlockSpec((down_tile, width), lambda i: (i, 0)),
+        ),
+        scratch_shapes=[
+            pltpu.VMEM((slot_count, 2 * width), jnp.bfloat16),
+            pltpu.VMEM((slot_count, 3 * hidden_units), jnp.bfloat16),
+        ],
+        compiler_params=pltpu.CompilerParams(vmem_limit_bytes=24 * 1024 * 1024),
+        cost_estimate=pl.CostEstimate(
+            flops=COST["wgrad"], bytes_accessed=COST["wgrad"], transcendentals=0
+        ),
+    )(*groups, by_pair, *deltas)
+    token_grad = call(token_grad_kernel, shape(tok_rows, width), chosen, returned)
+    return (token_grad, gate_grad[None], up_grad[None], down_grad[None])
+
+
+def body(tokens, cotangent, expert_ids, *rest):
+    owners = lax.axis_size("expert")
+    width_parts = lax.axis_size("dp")
+    tok_rows, top_count = expert_ids.shape
+    by_pairs = (
+        top_count == 1
+        and owners >= 8
+        and owners & (owners - 1) == 0
+        and width_parts >= 4
+        and tok_rows % (16 * owners) == 0
+    )
+    chosen = body_by_pairs if by_pairs else body_by_all_to_all
+    return chosen(tokens, cotangent, expert_ids, *rest)
 
 
 def solution(mesh):

time: 59.9 us -> 50.1 us (0.84)
  matrix products: 14.3 us -> 0 us
  Pallas kernels: 0 us -> 13.5 us
  other arithmetic: 5.94 us -> 0.01 us
  waiting for transfers between devices: 24.5 us -> 21 us
  starting transfers between devices: 12.5 us -> 14.5 us
  local copies, waits for them, and re-layouts: 1.3 us -> 0.02 us
    dot_general x13 -> x0, matrix products: 14.3 us -> none  [the longest x4 9.54 us: contract_rows(): lax.dot_general(left, right, (((0,), (0,)), ((), ())), preferred_element_...]
    pallas_call x0 -> x12, Pallas kernels: none -> 13.5 us  [the longest x11 9.51 us: call(): pl.pallas_call(kernel, out_shape=outs, in_specs=[pl.BlockSpec(memory_spac...]
    ppermute x3 -> x10, starting transfers between devices: 1.63 us -> 10.7 us  [swap(): return lax.ppermute(value, axis, [(i, i ^ bit) for i in range(size)])]
    all_to_all x2 -> x1, starting transfers between devices: 10.9 us -> 3.83 us  [body_by_pairs(): lax.all_to_all(grads[0], 'expert', split_axis=0, concat_axis=0, tiled=True)]
    all_to_all x2 -> x1, waiting for transfers between devices: 8.92 us -> 3.31 us  [body_by_pairs(): lax.all_to_all(grads[0], 'expert', split_axis=0, concat_axis=0, tiled=True)]
    ppermute x3 -> x10, waiting for transfers between devices: 15.6 us -> 17.7 us  [swap(): return lax.ppermute(value, axis, [(i, i ^ bit) for i in range(size)])]
    convert_element_type x3 -> x0, other arithmetic: 1.27 us -> none  [the longest x1 0.99 us: body(): pair_scaled = (jnp.repeat(cotangent.astype(jnp.float32), top_count, axis=...]
    concatenate x1, other arithmetic: 1.27 us -> 0.01 us  [body_by_pairs(): forward = jnp.concatenate([group[capacity:] for group in groups], axis=0)]
  transfers between devices with their start and end apart: 5 -> 11, of which waited for: 4 -> 7; matrix products, arithmetic and copies ran while one was open for 15% -> 0% of each run, Pallas kernels for 0% -> 17%
where the time goes in v2:
time: 50.1 us; the launch traced here: 49.8 us
  waiting for transfers between devices  21 us (42%)
  starting transfers between devices  14.5 us (29%)
  Pallas kernels  13.5 us (27%)
  between operations  0.78 us (2%)
    ppermute x10, waiting for transfers between devices, swap(): return lax.ppermute(value, axis, [(i, i ^ bit) for i in range(size)])  17.7 us
    ppermute x10, starting transfers between devices, swap(): return lax.ppermute(value, axis, [(i, i ^ bit) for i in range(size)])  10.7 us
    pallas_call x11, Pallas kernels, call(): pl.pallas_call(kernel, out_shape=outs, in_specs=[pl.BlockSpec(memory_spac...  9.51 us
    pallas_call x1, Pallas kernels, body_by_pairs(): pl.pallas_call(weight_grads_kernel, out_shape=(shape(width, hidden_units,...  4.04 us
    all_to_all x1, starting transfers between devices, body_by_pairs(): lax.all_to_all(grads[0], 'expert', split_axis=0, concat_axis=0, tiled=True)  3.83 us
    all_to_all x1, waiting for transfers between devices, body_by_pairs(): lax.all_to_all(grads[0], 'expert', split_axis=0, concat_axis=0, tiled=True)  3.31 us
  transfers between devices with their start and end apart: 11, of which 7 were waited for; matrix products, arithmetic and copies ran while one was open for 0% of the time, Pallas kernels for 17%

profile of v2, /device:TPU:0, one launch (start us, length us, event | category | flops | bytes accessed | tf_op | source)
XLA Modules:
  0.0 49.8 jit_solution(13273280480735238389)
XLA Ops:
  0.6 1.3 %shard_map.102 = (bf16[128,128]{1,0:T(8,128)(2,1)S(1)}, bf16[32,1024]{1,0:T(8,128)(2,1)S(1)}, bf16[32,1024]{1,0:T(8,128)(2,1)S(1)}, bf16[32,1024]{1,0:T(8,128)(2,1)S(1)}, bf16[32,1024]{1,0:T(8,128)(2,1)S(1)}) custom-call(s32[1,128]{1,0:T(1,128)} %bitcast.14, f32[1,128]{1,0:T(1,128)} %bitcast.15, bf16[128,512]{1,0:T(8,128)(2,1)} %tokens_hbm.1, ...), custom_call_target="tpu_custom_call" | custom-call | flops 1 | bytes 1 | tf_op jit(solution)/shard_map/pallas_call | solution.py:64
  1.9 3.1 %collective-permute-start = (bf16[32,1024]{1,0:T(8,128)(2,1)S(1)}, bf16[32,1024]{1,0:T(8,128)(2,1)S(1)}, u32[]{:S(2)}, u32[]{:S(2)}) collective-permute-start(bf16[32,1024]{1,0:T(8,128)(2,1)S(1)} %get-tuple-element.27), channel_id=1, source_target_pairs={{0,2},{1,3},{2,0},{3,1},{4,6},{5,7},{6,4},{7,5},{8,10},{9,11},{10,... | collective-permute-start | bytes 196616 | tf_op jit(solution)/shard_map/ppermute | solution.py:36
  5.0 2.6 %collective-permute-start.1 = (bf16[32,1024]{1,0:T(8,128)(2,1)S(1)}, bf16[32,1024]{1,0:T(8,128)(2,1)S(1)}, u32[]{:S(2)}, u32[]{:S(2)}) collective-permute-start(bf16[32,1024]{1,0:T(8,128)(2,1)S(1)} %get-tuple-element.28), channel_id=1, source_target_pairs={{0,4},{1,5},{2,6},{3,7},{4,0},{5,1},{6,2},{7,3},{8,12},{9,13},{10,... | collective-permute-start | bytes 196616 | tf_op jit(solution)/shard_map/ppermute | solution.py:36
  7.6 2.3 %shard_map.103 = (bf16[512,1408]{1,0:T(8,128)(2,1)S(1)}, bf16[512,1408]{1,0:T(8,128)(2,1)S(1)}, bf16[1408,512]{1,0:T(8,128)(2,1)S(1)}) custom-call(bf16[512,1408]{1,0:T(8,128)(2,1)} %bitcast.11, bf16[512,1408]{1,0:T(8,128)(2,1)} %bitcast.12, bf16[1408,512]{1,0:T(8,128)(2,1)} %bitcast.13, bf16[128,128]{1,0:T(8,128)(2,1)S(1)} %get-tuple-element.25.marker_hbm.chosen_ref), custom_call_target="tpu_custom_call" | custom-call | flops 10000000 | bytes 10000000 | tf_op jit(solution)/shard_map/pallas_call | solution.py:64
  9.9 2.4 %collective-permute-done.1.refs_2_ = bf16[32,1024]{1,0:T(8,128)(2,1)S(1)} collective-permute-done((bf16[32,1024]{1,0:T(8,128)(2,1)S(1)}, bf16[32,1024]{1,0:T(8,128)(2,1)S(1)}, u32[]{:S(2)}, u32[]{:S(2)}) %collective-permute-start.1) | collective-permute-done | bytes 65568 | tf_op jit(solution)/shard_map/ppermute | solution.py:36
  12.2 1.4 %collective-permute-done.2.refs_3_ = bf16[32,1024]{1,0:T(8,128)(2,1)S(1)} collective-permute-done((bf16[32,1024]{1,0:T(8,128)(2,1)S(1)}, bf16[32,1024]{1,0:T(8,128)(2,1)S(1)}, u32[]{:S(2)}, u32[]{:S(2)}) %collective-permute-start.2) | collective-permute-done | bytes 65568 | tf_op jit(solution)/shard_map/ppermute | solution.py:36
  13.7 1.0 %shard_map.106 = (f32[32,4224]{1,0:T(8,128)S(1)}, bf16[32,4224]{1,0:T(8,128)(2,1)S(1)}) custom-call(bf16[32,1024]{1,0:T(8,128)(2,1)S(1)} %get-tuple-element.26.refs_0_, bf16[32,1024]{1,0:T(8,128)(2,1)S(1)} %collective-permute-done.refs_1_, bf16[32,1024]{1,0:T(8,128)(2,1)S(1)} %collective-permute-done.1.refs_2_, ...), custom_call_target="tpu_custom_call" | custom-call | flops 1 | bytes 1 | tf_op jit(solution)/shard_map/pallas_call | solution.py:64
  14.8 1.6 %collective-permute-start.3 = (bf16[64,1024]{1,0:T(8,128)(2,1)S(1)}, bf16[64,1024]{1,0:T(8,128)(2,1)S(1)}, u32[]{:S(2)}, u32[]{:S(2)}) collective-permute-start(bf16[64,1024]{1,0:T(8,128)(2,1)S(1)} %pad_maximum_fusion), channel_id=1, source_target_pairs={{0,1},{1,0},{2,3},{3,2},{4,5},{5,4},{6,7},{7,6},{8,9},{9,8},{10,11... | collective-permute-start | bytes 393224 | tf_op jit(solution)/shard_map/ppermute | solution.py:36
  16.5 1.6 %collective-permute-start.6 = (bf16[32,4224]{1,0:T(8,128)(2,1)S(1)}, bf16[32,4224]{1,0:T(8,128)(2,1)S(1)}, u32[]{:S(2)}, u32[]{:S(2)}) collective-permute-start(bf16[32,4224]{1,0:T(8,128)(2,1)S(1)} %get-tuple-element.40), channel_id=1, source_target_pairs={{0,16},{8,24},{16,0},{24,8},{1,17},{9,25},{17,1},{25,9},{2,18},{10... | collective-permute-start | bytes 811016 | tf_op jit(solution)/shard_map/ppermute | solution.py:36
  18.1 2.7 %collective-permute-done.3.refs_0_.refs_4_ = bf16[64,1024]{1,0:T(8,128)(2,1)S(1)} collective-permute-done((bf16[64,1024]{1,0:T(8,128)(2,1)S(1)}, bf16[64,1024]{1,0:T(8,128)(2,1)S(1)}, u32[]{:S(2)}, u32[]{:S(2)}) %collective-permute-start.3) | collective-permute-done | bytes 131104 | tf_op jit(solution)/shard_map/ppermute | solution.py:36
  20.8 1.0 %shard_map.104 = (f32[32,4224]{1,0:T(8,128)S(1)}, bf16[32,4224]{1,0:T(8,128)(2,1)S(1)}) custom-call(bf16[64,1024]{1,0:T(8,128)(2,1)S(1)} %collective-permute-done.3.refs_0_.refs_4_, bf16[512,1408]{1,0:T(8,128)(2,1)S(1)} %get-tuple-element.32.refs_1_.refs_4_.gate_ref, bf16[512,1408]{1,0:T(8,128)(2,1)S(1)} %get-tuple-element.33.refs_2_.refs_5_.up_ref, ...), custom_call_target="tpu_custom_call" | custom-call | flops 1 | bytes 1 | tf_op jit(solution)/shard_map/pallas_call | solution.py:64
  21.9 3.3 %collective-permute-done.6.received_ref = bf16[32,4224]{1,0:T(8,128)(2,1)S(1)} collective-permute-done((bf16[32,4224]{1,0:T(8,128)(2,1)S(1)}, bf16[32,4224]{1,0:T(8,128)(2,1)S(1)}, u32[]{:S(2)}, u32[]{:S(2)}) %collective-permute-start.6) | collective-permute-done | bytes 270368 | tf_op jit(solution)/shard_map/ppermute | solution.py:36
  25.2 0.1 shard_map.108.mine_ref.refs_5_
  25.4 0.1 shard_map.105
  25.5 1.6 %collective-permute-start.8 = (bf16[32,4224]{1,0:T(8,128)(2,1)S(1)}, bf16[32,4224]{1,0:T(8,128)(2,1)S(1)}, u32[]{:S(2)}, u32[]{:S(2)}) collective-permute-start(bf16[32,4224]{1,0:T(8,128)(2,1)S(1)} %get-tuple-element.42), channel_id=1, source_target_pairs={{0,16},{8,24},{16,0},{24,8},{1,17},{9,25},{17,1},{25,9},{2,18},{10... | collective-permute-start | bytes 811016 | tf_op jit(solution)/shard_map/ppermute | solution.py:36
  27.0 1.0 %shard_map.109.refs_0_ = bf16[64,512]{1,0:T(8,128)(2,1)S(1)} custom-call(bf16[32,4224]{1,0:T(8,128)(2,1)S(1)} %shard_map.108.mine_ref.refs_5_, bf16[32,4224]{1,0:T(8,128)(2,1)S(1)} %collective-permute-done.7.other_ref.refs_6_, bf16[512,1408]{1,0:T(8,128)(2,1)S(1)} %get-tuple-element.32.refs_1_.refs_4_.gate_ref, ...), custom_call_target="tpu_custom_call" | custom-call | flops 1 | bytes 1 | tf_op jit(solution)/shard_map/pallas_call | solution.py:64
  28.0 6.4 %collective-permute-done.8.received_ref = bf16[32,4224]{1,0:T(8,128)(2,1)S(1)} collective-permute-done((bf16[32,4224]{1,0:T(8,128)(2,1)S(1)}, bf16[32,4224]{1,0:T(8,128)(2,1)S(1)}, u32[]{:S(2)}, u32[]{:S(2)}) %collective-permute-start.8) | collective-permute-done | bytes 270368 | tf_op jit(solution)/shard_map/ppermute | solution.py:36
  34.4 0.1 shard_map.110.mine_ref.refs_7_
  34.6 1.5 %collective-permute-done.9.other_ref.refs_8_ = bf16[32,4224]{1,0:T(8,128)(2,1)S(1)} collective-permute-done((bf16[32,4224]{1,0:T(8,128)(2,1)S(1)}, bf16[32,4224]{1,0:T(8,128)(2,1)S(1)}, u32[]{:S(2)}, u32[]{:S(2)}) %collective-permute-start.9) | collective-permute-done | bytes 270368 | tf_op jit(solution)/shard_map/ppermute | solution.py:36
  36.2 1.6 %shard_map.111 = bf16[128,512]{1,0:T(8,128)(2,1)} custom-call(bf16[32,4224]{1,0:T(8,128)(2,1)S(1)} %shard_map.110.mine_ref.refs_7_, bf16[32,4224]{1,0:T(8,128)(2,1)S(1)} %collective-permute-done.9.other_ref.refs_8_, bf16[512,1408]{1,0:T(8,128)(2,1)S(1)} %get-tuple-element.32.refs_1_.refs_4_.gate_ref, ...), custom_call_target="tpu_custom_call" | custom-call | flops 1 | bytes 1 | tf_op jit(solution)/shard_map/pallas_call | solution.py:64
  37.8 3.8 %all-to-all-start = ((bf16[8,16,512]{2,1,0:T(8,128)(2,1)}), bf16[8,16,512]{2,1,0:T(8,128)(2,1)S(1)}, u32[]{:S(2)}, u32[]{:S(2)}) async-start(bf16[8,16,512]{2,1,0:T(8,128)(2,1)} %bitcast.5), calls=%async_computation | async-start | bytes 262144 | tf_op jit(solution)/shard_map/all_to_all | solution.py:392
  41.6 4.0 %shard_map.113 = (f32[512,1408]{1,0:T(8,128)}, f32[512,1408]{1,0:T(8,128)}, f32[1408,512]{1,0:T(8,128)}) custom-call(bf16[32,1024]{1,0:T(8,128)(2,1)S(1)} %get-tuple-element.26.refs_0_, bf16[32,1024]{1,0:T(8,128)(2,1)S(1)} %collective-permute-done.refs_1_, bf16[32,1024]{1,0:T(8,128)(2,1)S(1)} %collective-permute-done.1.refs_2_, ...), custom_call_target="tpu_custom_call" | custom-call | flops 10000000 | bytes 10000000 | tf_op jit(solution)/shard_map/pallas_call | solution.py:395
  45.7 3.3 %all-to-all-done = bf16[8,16,512]{2,1,0:T(8,128)(2,1)S(1)} async-done(((bf16[8,16,512]{2,1,0:T(8,128)(2,1)}), bf16[8,16,512]{2,1,0:T(8,128)(2,1)S(1)}, u32[]{:S(2)}, u32[]{:S(2)}) %all-to-all-start) | async-done | bytes 131104 | tf_op jit(solution)/shard_map/all_to_all | solution.py:392
  49.0 0.9 %shard_map.112 = bf16[128,512]{1,0:T(8,128)(2,1)} custom-call(bf16[128,128]{1,0:T(8,128)(2,1)S(1)} %get-tuple-element.25.marker_hbm.chosen_ref, bf16[128,512]{1,0:T(8,128)(2,1)S(1)} %bitcast.10), custom_call_target="tpu_custom_call" | custom-call | flops 1 | bytes 1 | tf_op jit(solution)/shard_map/pallas_call | solution.py:64
  (15 shorter events, 0.4 us)
Async XLA Ops:
  1.9 7.9 %collective-permute-start = (bf16[32,1024]{1,0:T(8,128)(2,1)S(1)}, bf16[32,1024]{1,0:T(8,128)(2,1)S(1)}, u32[]{:S(2)}, u32[]{:S(2)}) collective-permute-start(bf16[32,1024]{1,0:T(8,128)(2,1)S(1)} %get-tuple-element.27), channel_id=1, source_target_pairs={{0,2},{1,3},{2,0},{3,1},{4,6},{5,7},{6,4},{7,5},{8,10},{9,11},{10,... | collective-permute-start | bytes 196616 | tf_op jit(solution)/shard_map/ppermute | solution.py:36
  5.0 7.3 %collective-permute-start.1 = (bf16[32,1024]{1,0:T(8,128)(2,1)S(1)}, bf16[32,1024]{1,0:T(8,128)(2,1)S(1)}, u32[]{:S(2)}, u32[]{:S(2)}) collective-permute-start(bf16[32,1024]{1,0:T(8,128)(2,1)S(1)} %get-tuple-element.28), channel_id=1, source_target_pairs={{0,4},{1,5},{2,6},{3,7},{4,0},{5,1},{6,2},{7,3},{8,12},{9,13},{10,... | collective-permute-start | bytes 196616 | tf_op jit(solution)/shard_map/ppermute | solution.py:36
  7.6 6.1 %collective-permute-start.2 = (bf16[32,1024]{1,0:T(8,128)(2,1)S(1)}, bf16[32,1024]{1,0:T(8,128)(2,1)S(1)}, u32[]{:S(2)}, u32[]{:S(2)}) collective-permute-start(bf16[32,1024]{1,0:T(8,128)(2,1)S(1)} %get-tuple-element.29), channel_id=1, source_target_pairs={{0,6},{1,7},{2,4},{3,5},{4,2},{5,3},{6,0},{7,1},{8,14},{9,15},{10,... | collective-permute-start | bytes 196616 | tf_op jit(solution)/shard_map/ppermute | solution.py:36
  14.7 1.7 %collective-permute-start.5 = (bf16[32,4224]{1,0:T(8,128)(2,1)S(1)}, bf16[32,4224]{1,0:T(8,128)(2,1)S(1)}, u32[]{:S(2)}, u32[]{:S(2)}) collective-permute-start(bf16[32,4224]{1,0:T(8,128)(2,1)S(1)} %get-tuple-element.38), channel_id=1, source_target_pairs={{0,8},{8,0},{16,24},{24,16},{1,9},{9,1},{17,25},{25,17},{2,10},{10... | collective-permute-start | bytes 811016 | tf_op jit(solution)/shard_map/ppermute | solution.py:36
  14.8 5.9 %collective-permute-start.3 = (bf16[64,1024]{1,0:T(8,128)(2,1)S(1)}, bf16[64,1024]{1,0:T(8,128)(2,1)S(1)}, u32[]{:S(2)}, u32[]{:S(2)}) collective-permute-start(bf16[64,1024]{1,0:T(8,128)(2,1)S(1)} %pad_maximum_fusion), channel_id=1, source_target_pairs={{0,1},{1,0},{2,3},{3,2},{4,5},{5,4},{6,7},{7,6},{8,9},{9,8},{10,11... | collective-permute-start | bytes 393224 | tf_op jit(solution)/shard_map/ppermute | solution.py:36
  16.5 8.6 %collective-permute-start.6 = (bf16[32,4224]{1,0:T(8,128)(2,1)S(1)}, bf16[32,4224]{1,0:T(8,128)(2,1)S(1)}, u32[]{:S(2)}, u32[]{:S(2)}) collective-permute-start(bf16[32,4224]{1,0:T(8,128)(2,1)S(1)} %get-tuple-element.40), channel_id=1, source_target_pairs={{0,16},{8,24},{16,0},{24,8},{1,17},{9,25},{17,1},{25,9},{2,18},{10... | collective-permute-start | bytes 811016 | tf_op jit(solution)/shard_map/ppermute | solution.py:36
  21.8 3.6 %collective-permute-start.4 = (bf16[32,4224]{1,0:T(8,128)(2,1)S(1)}, bf16[32,4224]{1,0:T(8,128)(2,1)S(1)}, u32[]{:S(2)}, u32[]{:S(2)}) collective-permute-start(bf16[32,4224]{1,0:T(8,128)(2,1)S(1)} %get-tuple-element.35), channel_id=1, source_target_pairs={{0,8},{8,0},{16,24},{24,16},{1,9},{9,1},{17,25},{25,17},{2,10},{10... | collective-permute-start | bytes 811016 | tf_op jit(solution)/shard_map/ppermute | solution.py:36
  25.3 1.7 %collective-permute-start.7 = (bf16[32,4224]{1,0:T(8,128)(2,1)S(1)}, bf16[32,4224]{1,0:T(8,128)(2,1)S(1)}, u32[]{:S(2)}, u32[]{:S(2)}) collective-permute-start(bf16[32,4224]{1,0:T(8,128)(2,1)S(1)} %shard_map.108.mine_ref.refs_5_), channel_id=1, source_target_pairs={{0,8},{8,0},{16,24},{24,16},{1,9},{9,1},{17,25},{25,17},{2,10},{10... | collective-permute-start | bytes 811016 | tf_op jit(solution)/shard_map/ppermute | solution.py:36
  25.5 8.9 %collective-permute-start.8 = (bf16[32,4224]{1,0:T(8,128)(2,1)S(1)}, bf16[32,4224]{1,0:T(8,128)(2,1)S(1)}, u32[]{:S(2)}, u32[]{:S(2)}) collective-permute-start(bf16[32,4224]{1,0:T(8,128)(2,1)S(1)} %get-tuple-element.42), channel_id=1, source_target_pairs={{0,16},{8,24},{16,0},{24,8},{1,17},{9,25},{17,1},{25,9},{2,18},{10... | collective-permute-start | bytes 811016 | tf_op jit(solution)/shard_map/ppermute | solution.py:36
  34.5 1.6 %collective-permute-start.9 = (bf16[32,4224]{1,0:T(8,128)(2,1)S(1)}, bf16[32,4224]{1,0:T(8,128)(2,1)S(1)}, u32[]{:S(2)}, u32[]{:S(2)}) collective-permute-start(bf16[32,4224]{1,0:T(8,128)(2,1)S(1)} %shard_map.110.mine_ref.refs_7_), channel_id=1, source_target_pairs={{0,8},{8,0},{16,24},{24,16},{1,9},{9,1},{17,25},{25,17},{2,10},{10... | collective-permute-start | bytes 811016 | tf_op jit(solution)/shard_map/ppermute | solution.py:36
  37.8 11.2 %all-to-all-start = ((bf16[8,16,512]{2,1,0:T(8,128)(2,1)}), bf16[8,16,512]{2,1,0:T(8,128)(2,1)S(1)}, u32[]{:S(2)}, u32[]{:S(2)}) async-start(bf16[8,16,512]{2,1,0:T(8,128)(2,1)} %bitcast.5), calls=%async_computation | async-start | bytes 262144 | tf_op jit(solution)/shard_map/all_to_all | solution.py:392

commit v3 on v2

--- a/solution.py
+++ b/solution.py
@@ -36,27 +36,12 @@
     return lax.ppermute(value, axis, [(i, i ^ bit) for i in range(size)])
 
 
-COST = dict(
-    load=10**7,
-    products=(1, 1),
-    sums=(1, 1),
-    deltas=(1, 1),
-    grad=(1, 1),
-    wgrad=10**7,
-)
-TIE = 1
-
-
 def after(values, marker):
     return lax.optimization_barrier((values, marker))[0]
 
 
 def call(kernel, outs, *args, cost=1, far=(), scratch=()):
     spaces = [pltpu.HBM if place in far else pltpu.VMEM for place in range(len(args))]
-    args = [
-        pltpu.with_memory_space_constraint(arg, pltpu.HBM) if place in far else arg
-        for place, arg in enumerate(args)
-    ]
     args = [
         pltpu.with_memory_space_constraint(arg, pltpu.HBM) if place in far else arg
         for place, arg in enumerate(args)
@@ -138,16 +123,12 @@
 
 
 def straight_rows(refs):
-    return [ref[:ref.shape[0] // 2] for ref in refs]
-
-
-def pair_rows(refs):
-    return [ref[...] for ref in refs]
-
-
-def products_kernel(take_rows, *refs):
+    return jnp.concatenate([ref[:ref.shape[0] // 2] for ref in refs], axis=0)
+
+
+def products_kernel(*refs):
     *row_refs, gate_ref, up_ref, down_ref, mine_ref, other_ref = refs
-    rows = jnp.concatenate(take_rows(row_refs), axis=0)
+    rows = straight_rows(row_refs) if len(row_refs) > 1 else row_refs[0][...]
     half = rows.shape[0] // 2
     width = rows.shape[1] // 2
     hidden_units = gate_ref.shape[1]
@@ -165,9 +146,11 @@
 
 
 def sums_kernel(mine_ref, received_ref, sums_ref, packed_ref):
-    sums = mine_ref[...] + received_ref[...].astype(jnp.float32)
+    cols = mine_ref.shape[1]
+    sums = mine_ref[...] + received_ref[:, :cols].astype(jnp.float32)
     sums_ref[...] = sums
-    packed_ref[...] = sums.astype(jnp.bfloat16)
+    packed_ref[:, :cols] = sums.astype(jnp.bfloat16)
+    packed_ref[:, cols:] = jnp.zeros((sums.shape[0], packed_ref.shape[1] - cols), jnp.bfloat16)
 
 
 def deltas_kernel(sums_ref, received_ref, out_ref):
@@ -184,7 +167,7 @@
     )
 
 
-def slot_grad_kernel(owners, mine_ref, other_ref, gate_ref, up_ref, *refs):
+def slot_grad_kernel(groups, mine_ref, other_ref, gate_ref, up_ref, *refs):
     *earlier_ref, out_ref = refs
     hidden_units = gate_ref.shape[1]
     rows = in_order(lax.axis_index("dp") % 2, mine_ref[...], other_ref[...])
@@ -196,12 +179,11 @@
         out_ref[...] = out
         return
     me = lax.axis_index("expert")
-    block = out_ref.shape[0] // owners
-    earlier = earlier_ref[0][...]
-    for k in range(owners):
-        source = (earlier, out)[k % 2]
-        at = k // 2 * block
-        out_ref[pl.ds(pl.multiple_of((me ^ k) * block, block), block)] = source[at:at + block]
+    block = out_ref.shape[0] // (2 * len(groups))
+    for side, rows in enumerate((earlier_ref[0][...], out)):
+        for place, group in enumerate(groups):
+            start = pl.multiple_of((me ^ (2 * group + side)) * block, block)
+            out_ref[pl.ds(start, block)] = rows[place * block:(place + 1) * block]
 
 
 def weight_grads_kernel(*refs):
@@ -215,12 +197,10 @@
 
     @pl.when(step == 0)
     def _():
-        at = 0
-        for value in straight_rows(row_refs[:-1]) + pair_rows(row_refs[-1:]):
-            rows_ref[at:at + value.shape[0]] = value
-            at += value.shape[0]
         core = lax.axis_index("dp") % 2
         half = deltas_ref.shape[0] // 2
+        rows_ref[:half] = straight_rows(row_refs[:-1])
+        rows_ref[half:] = row_refs[-1][...]
         for place in range(2):
             both = in_order(core, delta_refs[2 * place][...], delta_refs[2 * place + 1][...])
             deltas_ref[place * half:(place + 1) * half] = both
@@ -316,6 +296,7 @@
     slot_count = owners * capacity
     half = owners // 2
 
+    far_first = [0] + list(reversed(range(1, half)))
     chosen, *groups = call(
         functools.partial(dispatch_kernel, owners, capacity),
         (shape(slot_count, tok_rows),) + (shape(2 * capacity, 2 * width),) * half,
@@ -341,52 +322,37 @@
         chosen,
         far=range(3),
         scratch=[pltpu.SemaphoreType.DMA((3,))],
-        cost=COST["load"],
-    )
-    moved = {j: swap(groups[j], 2 * j, "expert") for j in reversed(range(1, half))}
-    groups = [groups[0]] + [moved[j] for j in range(1, half)]
-    forward = jnp.concatenate([group[capacity:] for group in groups], axis=0)
-    forward = after(forward, weights[2])
-    by_pair = swap(forward, 1, "expert")
-    order = list(range(0, owners, 2)) + list(range(1, owners, 2))
+        cost=10**7,
+    )
+    groups = [groups[0]] + [swap(groups[j], 2 * j, "expert") for j in far_first[1:]]
+    seconds = jnp.concatenate([group[capacity:] for group in groups], axis=0)
+    by_pair = swap(after(seconds, weights[2]), 1, "expert")
 
     part = slot_count // 4
     packed = shape(part, 3 * hidden_units)
     wide = shape(part, 3 * hidden_units, jnp.float32)
+    padded = shape(part, 3 * hidden_units + 128)
     held = []
-    for place, (take, rows) in enumerate(((straight_rows, groups), (pair_rows, [by_pair]))):
-        mine, other = call(
-            functools.partial(products_kernel, take),
-            (wide, packed),
-            *rows,
-            *weights,
-            cost=COST["products"][place],
-        )
-        sums, marker = call(
-            sums_kernel, (wide, packed), mine, swap(other, 1), cost=COST["sums"][place]
-        )
+    for rows, cost in ((groups, 1), ([by_pair], 10**9)):
+        mine, other = call(products_kernel, (wide, packed), *rows, *weights, cost=cost)
+        sums, marker = call(sums_kernel, (wide, padded), mine, swap(other, 1))
         bit = 2
         while 2 * bit < width_parts:
-            sums, marker = call(sums_kernel, (wide, packed), sums, swap(marker, bit))
+            sums, marker = call(sums_kernel, (wide, padded), sums, swap(marker, bit))
             bit *= 2
         held.append((sums, swap(marker, bit)))
     deltas, grads = [], []
     for place, (sums, received) in enumerate(held):
-        if place and TIE == 1:
-            sums = after(sums, grads)
-        mine = call(deltas_kernel, packed, sums, received, cost=COST["deltas"][place])
-        if place and TIE == 3:
-            mine = after(mine, grads)
+        mine = call(deltas_kernel, packed, after(sums, grads) if grads else sums, received)
         pair = [mine, swap(mine, 1)]
         deltas += pair
         grads = [
             call(
-                functools.partial(slot_grad_kernel, owners),
+                functools.partial(slot_grad_kernel, far_first),
                 shape((place + 1) * half * capacity, width),
                 *pair,
                 *weights[:2],
                 *grads,
-                cost=COST["grad"][place],
             )
         ]
     returned = lax.all_to_all(grads[0], "expert", split_axis=0, concat_axis=0, tiled=True)
@@ -411,9 +377,7 @@
             pltpu.VMEM((slot_count, 3 * hidden_units), jnp.bfloat16),
         ],
         compiler_params=pltpu.CompilerParams(vmem_limit_bytes=24 * 1024 * 1024),
-        cost_estimate=pl.CostEstimate(
-            flops=COST["wgrad"], bytes_accessed=COST["wgrad"], transcendentals=0
-        ),
+        cost_estimate=pl.CostEstimate(flops=10**7, bytes_accessed=10**7, transcendentals=0),
     )(*groups, by_pair, *deltas)
     token_grad = call(token_grad_kernel, shape(tok_rows, width), chosen, returned)
     return (token_grad, gate_grad[None], up_grad[None], down_grad[None])

time: 50.1 us -> 48.1 us (0.960)
  waiting for transfers between devices: 21 us -> 17.8 us
  starting transfers between devices: 14.5 us -> 15.7 us
    ppermute x10, waiting for transfers between devices: 17.7 us -> 14.5 us  [swap(): return lax.ppermute(value, axis, [(i, i ^ bit) for i in range(size)])]
    all_to_all x1, starting transfers between devices: 3.83 us -> 4.95 us  [body_by_pairs(): lax.all_to_all(grads[0], 'expert', split_axis=0, concat_axis=0, tiled=True)]
  transfers between devices with their start and end apart: 11 -> 11, of which waited for: 7 -> 8; matrix products, arithmetic and copies ran while one was open for 0% -> 0% of each run, Pallas kernels for 17% -> 18%
where the time goes in v3:
time: 48.1 us; the launch traced here: 47.8 us
  waiting for transfers between devices  17.8 us (37%)
  starting transfers between devices  15.7 us (33%)
  Pallas kernels  13.6 us (28%)
  between operations  0.78 us (2%)
    ppermute x10, waiting for transfers between devices, swap(): return lax.ppermute(value, axis, [(i, i ^ bit) for i in range(size)])  14.5 us
    ppermute x10, starting transfers between devices, swap(): return lax.ppermute(value, axis, [(i, i ^ bit) for i in range(size)])  10.7 us
    pallas_call x11, Pallas kernels, call(): pl.pallas_call(kernel, out_shape=outs, in_specs=[pl.BlockSpec(memory_spac...  9.53 us
    all_to_all x1, starting transfers between devices, body_by_pairs(): lax.all_to_all(grads[0], 'expert', split_axis=0, concat_axis=0, tiled=True)  4.95 us
    pallas_call x1, Pallas kernels, body_by_pairs(): pl.pallas_call(weight_grads_kernel, out_shape=(shape(width, hidden_units,...  4.03 us
    all_to_all x1, waiting for transfers between devices, body_by_pairs(): lax.all_to_all(grads[0], 'expert', split_axis=0, concat_axis=0, tiled=True)  3.31 us
  transfers between devices with their start and end apart: 11, of which 8 were waited for; matrix products, arithmetic and copies ran while one was open for 0% of the time, Pallas kernels for 18%

profile of v3, /device:TPU:0, one launch (start us, length us, event | category | flops | bytes accessed | tf_op | source)
XLA Modules:
  0.0 47.8 jit_solution(12013966420646366544)
XLA Ops:
  0.6 1.3 %shard_map.102 = (bf16[128,128]{1,0:T(8,128)(2,1)S(1)}, bf16[32,1024]{1,0:T(8,128)(2,1)S(1)}, bf16[32,1024]{1,0:T(8,128)(2,1)S(1)}, bf16[32,1024]{1,0:T(8,128)(2,1)S(1)}, bf16[32,1024]{1,0:T(8,128)(2,1)S(1)}) custom-call(s32[1,128]{1,0:T(1,128)} %bitcast.14, f32[1,128]{1,0:T(1,128)} %bitcast.15, bf16[128,512]{1,0:T(8,128)(2,1)} %tokens_hbm.1, ...), custom_call_target="tpu_custom_call" | custom-call | flops 1 | bytes 1 | tf_op jit(solution)/shard_map/pallas_call | solution.py:49
  1.9 5.1 %collective-permute-start = (bf16[32,1024]{1,0:T(8,128)(2,1)S(1)}, bf16[32,1024]{1,0:T(8,128)(2,1)S(1)}, u32[]{:S(2)}, u32[]{:S(2)}) collective-permute-start(bf16[32,1024]{1,0:T(8,128)(2,1)S(1)} %get-tuple-element.27), channel_id=1, source_target_pairs={{0,6},{1,7},{2,4},{3,5},{4,2},{5,3},{6,0},{7,1},{8,14},{9,15},{10,... | collective-permute-start | bytes 196616 | tf_op jit(solution)/shard_map/ppermute | solution.py:36
  7.0 0.6 %collective-permute-start.2 = (bf16[32,1024]{1,0:T(8,128)(2,1)S(1)}, bf16[32,1024]{1,0:T(8,128)(2,1)S(1)}, u32[]{:S(2)}, u32[]{:S(2)}) collective-permute-start(bf16[32,1024]{1,0:T(8,128)(2,1)S(1)} %get-tuple-element.29), channel_id=1, source_target_pairs={{0,2},{1,3},{2,0},{3,1},{4,6},{5,7},{6,4},{7,5},{8,10},{9,11},{10,... | collective-permute-start | bytes 196616 | tf_op jit(solution)/shard_map/ppermute | solution.py:36
  7.7 2.3 %shard_map.103 = (bf16[512,1408]{1,0:T(8,128)(2,1)S(1)}, bf16[512,1408]{1,0:T(8,128)(2,1)S(1)}, bf16[1408,512]{1,0:T(8,128)(2,1)S(1)}) custom-call(bf16[512,1408]{1,0:T(8,128)(2,1)} %bitcast.11, bf16[512,1408]{1,0:T(8,128)(2,1)} %bitcast.12, bf16[1408,512]{1,0:T(8,128)(2,1)} %bitcast.13, bf16[128,128]{1,0:T(8,128)(2,1)S(1)} %get-tuple-element.25.marker_hbm.chosen_ref), custom_call_target="tpu_custom_call" | custom-call | flops 10000000 | bytes 10000000 | tf_op jit(solution)/shard_map/pallas_call | solution.py:49
  9.9 2.7 %collective-permute-done.1.refs_2_ = bf16[32,1024]{1,0:T(8,128)(2,1)S(1)} collective-permute-done((bf16[32,1024]{1,0:T(8,128)(2,1)S(1)}, bf16[32,1024]{1,0:T(8,128)(2,1)S(1)}, u32[]{:S(2)}, u32[]{:S(2)}) %collective-permute-start.1) | collective-permute-done | bytes 65568 | tf_op jit(solution)/shard_map/ppermute | solution.py:36
  12.6 1.0 %shard_map.106 = (f32[32,4224]{1,0:T(8,128)S(1)}, bf16[32,4224]{1,0:T(8,128)(2,1)S(1)}) custom-call(bf16[32,1024]{1,0:T(8,128)(2,1)S(1)} %get-tuple-element.26.refs_0_, bf16[32,1024]{1,0:T(8,128)(2,1)S(1)} %collective-permute-done.refs_1_, bf16[32,1024]{1,0:T(8,128)(2,1)S(1)} %collective-permute-done.1.refs_2_, ...), custom_call_target="tpu_custom_call" | custom-call | flops 1 | bytes 1 | tf_op jit(solution)/shard_map/pallas_call | solution.py:49
  13.8 1.6 %collective-permute-start.3 = (bf16[64,1024]{1,0:T(8,128)(2,1)S(1)}, bf16[64,1024]{1,0:T(8,128)(2,1)S(1)}, u32[]{:S(2)}, u32[]{:S(2)}) collective-permute-start(bf16[64,1024]{1,0:T(8,128)(2,1)S(1)} %pad_maximum_fusion), channel_id=1, source_target_pairs={{0,1},{1,0},{2,3},{3,2},{4,5},{5,4},{6,7},{7,6},{8,9},{9,8},{10,11... | collective-permute-start | bytes 393224 | tf_op jit(solution)/shard_map/ppermute | solution.py:36
  15.5 1.6 %collective-permute-start.6 = (bf16[32,4352]{1,0:T(8,128)(2,1)S(1)}, bf16[32,4352]{1,0:T(8,128)(2,1)S(1)}, u32[]{:S(2)}, u32[]{:S(2)}) collective-permute-start(bf16[32,4352]{1,0:T(8,128)(2,1)S(1)} %get-tuple-element.40), channel_id=1, source_target_pairs={{0,16},{8,24},{16,0},{24,8},{1,17},{9,25},{17,1},{25,9},{2,18},{10... | collective-permute-start | bytes 835592 | tf_op jit(solution)/shard_map/ppermute | solution.py:36
  17.0 2.7 %collective-permute-done.3.refs_0_.refs_4_ = bf16[64,1024]{1,0:T(8,128)(2,1)S(1)} collective-permute-done((bf16[64,1024]{1,0:T(8,128)(2,1)S(1)}, bf16[64,1024]{1,0:T(8,128)(2,1)S(1)}, u32[]{:S(2)}, u32[]{:S(2)}) %collective-permute-start.3) | collective-permute-done | bytes 131104 | tf_op jit(solution)/shard_map/ppermute | solution.py:36
  19.8 1.0 %shard_map.104 = (f32[32,4224]{1,0:T(8,128)S(1)}, bf16[32,4224]{1,0:T(8,128)(2,1)S(1)}) custom-call(bf16[64,1024]{1,0:T(8,128)(2,1)S(1)} %collective-permute-done.3.refs_0_.refs_4_, bf16[512,1408]{1,0:T(8,128)(2,1)S(1)} %get-tuple-element.32.refs_1_.refs_4_.gate_ref, bf16[512,1408]{1,0:T(8,128)(2,1)S(1)} %get-tuple-element.33.refs_2_.refs_5_.up_ref, ...), custom_call_target="tpu_custom_call" | custom-call | flops 1000000000 | bytes 1000000000 | tf_op jit(solution)/shard_map/pallas_call | solution.py:49
  20.9 1.5 %collective-permute-done.4.received_ref = bf16[32,4224]{1,0:T(8,128)(2,1)S(1)} collective-permute-done((bf16[32,4224]{1,0:T(8,128)(2,1)S(1)}, bf16[32,4224]{1,0:T(8,128)(2,1)S(1)}, u32[]{:S(2)}, u32[]{:S(2)}) %collective-permute-start.4) | collective-permute-done | bytes 270368 | tf_op jit(solution)/shard_map/ppermute | solution.py:36
  22.5 1.6 %collective-permute-start.8 = (bf16[32,4352]{1,0:T(8,128)(2,1)S(1)}, bf16[32,4352]{1,0:T(8,128)(2,1)S(1)}, u32[]{:S(2)}, u32[]{:S(2)}) collective-permute-start(bf16[32,4352]{1,0:T(8,128)(2,1)S(1)} %get-tuple-element.42), channel_id=1, source_target_pairs={{0,16},{8,24},{16,0},{24,8},{1,17},{9,25},{17,1},{25,9},{2,18},{10... | collective-permute-start | bytes 835592 | tf_op jit(solution)/shard_map/ppermute | solution.py:36
  24.1 0.2 collective-permute-done.6.received_ref
  24.3 0.1 shard_map.108.mine_ref.refs_5_
  24.5 1.5 %collective-permute-done.7.other_ref.refs_6_ = bf16[32,4224]{1,0:T(8,128)(2,1)S(1)} collective-permute-done((bf16[32,4224]{1,0:T(8,128)(2,1)S(1)}, bf16[32,4224]{1,0:T(8,128)(2,1)S(1)}, u32[]{:S(2)}, u32[]{:S(2)}) %collective-permute-start.7) | collective-permute-done | bytes 270368 | tf_op jit(solution)/shard_map/ppermute | solution.py:36
  26.1 1.0 %shard_map.109.refs_0_ = bf16[64,512]{1,0:T(8,128)(2,1)S(1)} custom-call(bf16[32,4224]{1,0:T(8,128)(2,1)S(1)} %shard_map.108.mine_ref.refs_5_, bf16[32,4224]{1,0:T(8,128)(2,1)S(1)} %collective-permute-done.7.other_ref.refs_6_, bf16[512,1408]{1,0:T(8,128)(2,1)S(1)} %get-tuple-element.32.refs_1_.refs_4_.gate_ref, ...), custom_call_target="tpu_custom_call" | custom-call | flops 1 | bytes 1 | tf_op jit(solution)/shard_map/pallas_call | solution.py:49
  27.1 4.2 %collective-permute-done.8.received_ref = bf16[32,4352]{1,0:T(8,128)(2,1)S(1)} collective-permute-done((bf16[32,4352]{1,0:T(8,128)(2,1)S(1)}, bf16[32,4352]{1,0:T(8,128)(2,1)S(1)}, u32[]{:S(2)}, u32[]{:S(2)}) %collective-permute-start.8) | collective-permute-done | bytes 278560 | tf_op jit(solution)/shard_map/ppermute | solution.py:36
  31.3 0.1 shard_map.110.mine_ref.refs_7_
  31.5 1.5 %collective-permute-done.9.other_ref.refs_8_ = bf16[32,4224]{1,0:T(8,128)(2,1)S(1)} collective-permute-done((bf16[32,4224]{1,0:T(8,128)(2,1)S(1)}, bf16[32,4224]{1,0:T(8,128)(2,1)S(1)}, u32[]{:S(2)}, u32[]{:S(2)}) %collective-permute-start.9) | collective-permute-done | bytes 270368 | tf_op jit(solution)/shard_map/ppermute | solution.py:36
  33.0 1.7 %shard_map.111 = bf16[128,512]{1,0:T(8,128)(2,1)} custom-call(bf16[32,4224]{1,0:T(8,128)(2,1)S(1)} %shard_map.110.mine_ref.refs_7_, bf16[32,4224]{1,0:T(8,128)(2,1)S(1)} %collective-permute-done.9.other_ref.refs_8_, bf16[512,1408]{1,0:T(8,128)(2,1)S(1)} %get-tuple-element.32.refs_1_.refs_4_.gate_ref, ...), custom_call_target="tpu_custom_call" | custom-call | flops 1 | bytes 1 | tf_op jit(solution)/shard_map/pallas_call | solution.py:49
  34.7 5.0 %all-to-all-start = ((bf16[8,16,512]{2,1,0:T(8,128)(2,1)}), bf16[8,16,512]{2,1,0:T(8,128)(2,1)S(1)}, u32[]{:S(2)}, u32[]{:S(2)}) async-start(bf16[8,16,512]{2,1,0:T(8,128)(2,1)} %bitcast.5), calls=%async_computation | async-start | bytes 262144 | tf_op jit(solution)/shard_map/all_to_all | solution.py:358
  39.6 4.0 %shard_map.113 = (f32[512,1408]{1,0:T(8,128)}, f32[512,1408]{1,0:T(8,128)}, f32[1408,512]{1,0:T(8,128)}) custom-call(bf16[32,1024]{1,0:T(8,128)(2,1)S(1)} %get-tuple-element.26.refs_0_, bf16[32,1024]{1,0:T(8,128)(2,1)S(1)} %collective-permute-done.refs_1_, bf16[32,1024]{1,0:T(8,128)(2,1)S(1)} %collective-permute-done.1.refs_2_, ...), custom_call_target="tpu_custom_call" | custom-call | flops 10000000 | bytes 10000000 | tf_op jit(solution)/shard_map/pallas_call | solution.py:361
  43.7 3.3 %all-to-all-done = bf16[8,16,512]{2,1,0:T(8,128)(2,1)S(1)} async-done(((bf16[8,16,512]{2,1,0:T(8,128)(2,1)}), bf16[8,16,512]{2,1,0:T(8,128)(2,1)S(1)}, u32[]{:S(2)}, u32[]{:S(2)}) %all-to-all-start) | async-done | bytes 131104 | tf_op jit(solution)/shard_map/all_to_all | solution.py:358
  47.0 0.9 %shard_map.112 = bf16[128,512]{1,0:T(8,128)(2,1)} custom-call(bf16[128,128]{1,0:T(8,128)(2,1)S(1)} %get-tuple-element.25.marker_hbm.chosen_ref, bf16[128,512]{1,0:T(8,128)(2,1)S(1)} %bitcast.10), custom_call_target="tpu_custom_call" | custom-call | flops 1 | bytes 1 | tf_op jit(solution)/shard_map/pallas_call | solution.py:49
  (15 shorter events, 0.5 us)
Async XLA Ops:
  1.9 8.0 %collective-permute-start = (bf16[32,1024]{1,0:T(8,128)(2,1)S(1)}, bf16[32,1024]{1,0:T(8,128)(2,1)S(1)}, u32[]{:S(2)}, u32[]{:S(2)}) collective-permute-start(bf16[32,1024]{1,0:T(8,128)(2,1)S(1)} %get-tuple-element.27), channel_id=1, source_target_pairs={{0,6},{1,7},{2,4},{3,5},{4,2},{5,3},{6,0},{7,1},{8,14},{9,15},{10,... | collective-permute-start | bytes 196616 | tf_op jit(solution)/shard_map/ppermute | solution.py:36
  7.0 5.6 %collective-permute-start.1 = (bf16[32,1024]{1,0:T(8,128)(2,1)S(1)}, bf16[32,1024]{1,0:T(8,128)(2,1)S(1)}, u32[]{:S(2)}, u32[]{:S(2)}) collective-permute-start(bf16[32,1024]{1,0:T(8,128)(2,1)S(1)} %get-tuple-element.28), channel_id=1, source_target_pairs={{0,4},{1,5},{2,6},{3,7},{4,0},{5,1},{6,2},{7,3},{8,12},{9,13},{10,... | collective-permute-start | bytes 196616 | tf_op jit(solution)/shard_map/ppermute | solution.py:36
  7.0 5.6 %collective-permute-start.2 = (bf16[32,1024]{1,0:T(8,128)(2,1)S(1)}, bf16[32,1024]{1,0:T(8,128)(2,1)S(1)}, u32[]{:S(2)}, u32[]{:S(2)}) collective-permute-start(bf16[32,1024]{1,0:T(8,128)(2,1)S(1)} %get-tuple-element.29), channel_id=1, source_target_pairs={{0,2},{1,3},{2,0},{3,1},{4,6},{5,7},{6,4},{7,5},{8,10},{9,11},{10,... | collective-permute-start | bytes 196616 | tf_op jit(solution)/shard_map/ppermute | solution.py:36
  13.7 1.7 %collective-permute-start.5 = (bf16[32,4224]{1,0:T(8,128)(2,1)S(1)}, bf16[32,4224]{1,0:T(8,128)(2,1)S(1)}, u32[]{:S(2)}, u32[]{:S(2)}) collective-permute-start(bf16[32,4224]{1,0:T(8,128)(2,1)S(1)} %get-tuple-element.38), channel_id=1, source_target_pairs={{0,8},{8,0},{16,24},{24,16},{1,9},{9,1},{17,25},{25,17},{2,10},{10... | collective-permute-start | bytes 811016 | tf_op jit(solution)/shard_map/ppermute | solution.py:36
  13.8 5.9 %collective-permute-start.3 = (bf16[64,1024]{1,0:T(8,128)(2,1)S(1)}, bf16[64,1024]{1,0:T(8,128)(2,1)S(1)}, u32[]{:S(2)}, u32[]{:S(2)}) collective-permute-start(bf16[64,1024]{1,0:T(8,128)(2,1)S(1)} %pad_maximum_fusion), channel_id=1, source_target_pairs={{0,1},{1,0},{2,3},{3,2},{4,5},{5,4},{6,7},{7,6},{8,9},{9,8},{10,11... | collective-permute-start | bytes 393224 | tf_op jit(solution)/shard_map/ppermute | solution.py:36
  15.5 8.8 %collective-permute-start.6 = (bf16[32,4352]{1,0:T(8,128)(2,1)S(1)}, bf16[32,4352]{1,0:T(8,128)(2,1)S(1)}, u32[]{:S(2)}, u32[]{:S(2)}) collective-permute-start(bf16[32,4352]{1,0:T(8,128)(2,1)S(1)} %get-tuple-element.40), channel_id=1, source_target_pairs={{0,16},{8,24},{16,0},{24,8},{1,17},{9,25},{17,1},{25,9},{2,18},{10... | collective-permute-start | bytes 835592 | tf_op jit(solution)/shard_map/ppermute | solution.py:36
  20.8 1.6 %collective-permute-start.4 = (bf16[32,4224]{1,0:T(8,128)(2,1)S(1)}, bf16[32,4224]{1,0:T(8,128)(2,1)S(1)}, u32[]{:S(2)}, u32[]{:S(2)}) collective-permute-start(bf16[32,4224]{1,0:T(8,128)(2,1)S(1)} %get-tuple-element.35), channel_id=1, source_target_pairs={{0,8},{8,0},{16,24},{24,16},{1,9},{9,1},{17,25},{25,17},{2,10},{10... | collective-permute-start | bytes 811016 | tf_op jit(solution)/shard_map/ppermute | solution.py:36
  22.5 8.8 %collective-permute-start.8 = (bf16[32,4352]{1,0:T(8,128)(2,1)S(1)}, bf16[32,4352]{1,0:T(8,128)(2,1)S(1)}, u32[]{:S(2)}, u32[]{:S(2)}) collective-permute-start(bf16[32,4352]{1,0:T(8,128)(2,1)S(1)} %get-tuple-element.42), channel_id=1, source_target_pairs={{0,16},{8,24},{16,0},{24,8},{1,17},{9,25},{17,1},{25,9},{2,18},{10... | collective-permute-start | bytes 835592 | tf_op jit(solution)/shard_map/ppermute | solution.py:36
  24.4 1.6 %collective-permute-start.7 = (bf16[32,4224]{1,0:T(8,128)(2,1)S(1)}, bf16[32,4224]{1,0:T(8,128)(2,1)S(1)}, u32[]{:S(2)}, u32[]{:S(2)}) collective-permute-start(bf16[32,4224]{1,0:T(8,128)(2,1)S(1)} %shard_map.108.mine_ref.refs_5_), channel_id=1, source_target_pairs={{0,8},{8,0},{16,24},{24,16},{1,9},{9,1},{17,25},{25,17},{2,10},{10... | collective-permute-start | bytes 811016 | tf_op jit(solution)/shard_map/ppermute | solution.py:36
  31.4 1.6 %collective-permute-start.9 = (bf16[32,4224]{1,0:T(8,128)(2,1)S(1)}, bf16[32,4224]{1,0:T(8,128)(2,1)S(1)}, u32[]{:S(2)}, u32[]{:S(2)}) collective-permute-start(bf16[32,4224]{1,0:T(8,128)(2,1)S(1)} %shard_map.110.mine_ref.refs_7_), channel_id=1, source_target_pairs={{0,8},{8,0},{16,24},{24,16},{1,9},{9,1},{17,25},{25,17},{2,10},{10... | collective-permute-start | bytes 811016 | tf_op jit(solution)/shard_map/ppermute | solution.py:36
  34.7 12.3 %all-to-all-start = ((bf16[8,16,512]{2,1,0:T(8,128)(2,1)}), bf16[8,16,512]{2,1,0:T(8,128)(2,1)S(1)}, u32[]{:S(2)}, u32[]{:S(2)}) async-start(bf16[8,16,512]{2,1,0:T(8,128)(2,1)} %bitcast.5), calls=%async_computation | async-start | bytes 262144 | tf_op jit(solution)/shard_map/all_to_all | solution.py:358

commit v4 on v3

--- a/solution.py
+++ b/solution.py
@@ -34,6 +34,10 @@
 def swap(value, bit, axis="dp"):
     size = lax.axis_size(axis)
     return lax.ppermute(value, axis, [(i, i ^ bit) for i in range(size)])
+
+
+FAR_PRODUCTS_COST = 10**9
+FAR_DELTAS_COST = 2 * 10**9
 
 
 def after(values, marker):
@@ -122,13 +126,14 @@
         copy.wait()
 
 
-def straight_rows(refs):
-    return jnp.concatenate([ref[:ref.shape[0] // 2] for ref in refs], axis=0)
+def near_rows(own_ref, from_pair_ref, *group_refs):
+    halves = [ref[:ref.shape[0] // 2] for ref in group_refs]
+    return jnp.concatenate([own_ref[...]] + halves + [from_pair_ref[...]], axis=0)
 
 
 def products_kernel(*refs):
     *row_refs, gate_ref, up_ref, down_ref, mine_ref, other_ref = refs
-    rows = straight_rows(row_refs) if len(row_refs) > 1 else row_refs[0][...]
+    rows = near_rows(*row_refs) if len(row_refs) > 1 else row_refs[0][...]
     half = rows.shape[0] // 2
     width = rows.shape[1] // 2
     hidden_units = gate_ref.shape[1]
@@ -146,11 +151,9 @@
 
 
 def sums_kernel(mine_ref, received_ref, sums_ref, packed_ref):
-    cols = mine_ref.shape[1]
-    sums = mine_ref[...] + received_ref[:, :cols].astype(jnp.float32)
+    sums = mine_ref[...] + received_ref[...].astype(jnp.float32)
     sums_ref[...] = sums
-    packed_ref[:, :cols] = sums.astype(jnp.bfloat16)
-    packed_ref[:, cols:] = jnp.zeros((sums.shape[0], packed_ref.shape[1] - cols), jnp.bfloat16)
+    packed_ref[...] = sums.astype(jnp.bfloat16)
 
 
 def deltas_kernel(sums_ref, received_ref, out_ref):
@@ -167,7 +170,7 @@
     )
 
 
-def slot_grad_kernel(groups, mine_ref, other_ref, gate_ref, up_ref, *refs):
+def slot_grad_kernel(order, mine_ref, other_ref, gate_ref, up_ref, *refs):
     *earlier_ref, out_ref = refs
     hidden_units = gate_ref.shape[1]
     rows = in_order(lax.axis_index("dp") % 2, mine_ref[...], other_ref[...])
@@ -179,11 +182,11 @@
         out_ref[...] = out
         return
     me = lax.axis_index("expert")
-    block = out_ref.shape[0] // (2 * len(groups))
-    for side, rows in enumerate((earlier_ref[0][...], out)):
-        for place, group in enumerate(groups):
-            start = pl.multiple_of((me ^ (2 * group + side)) * block, block)
-            out_ref[pl.ds(start, block)] = rows[place * block:(place + 1) * block]
+    block = out_ref.shape[0] // len(order)
+    rows = jnp.concatenate([earlier_ref[0][...], out], axis=0)
+    for place, k in enumerate(order):
+        start = pl.multiple_of((me ^ k) * block, block)
+        out_ref[pl.ds(start, block)] = rows[place * block:(place + 1) * block]
 
 
 def weight_grads_kernel(*refs):
@@ -198,12 +201,11 @@
     @pl.when(step == 0)
     def _():
         core = lax.axis_index("dp") % 2
-        half = deltas_ref.shape[0] // 2
-        rows_ref[:half] = straight_rows(row_refs[:-1])
-        rows_ref[half:] = row_refs[-1][...]
-        for place in range(2):
-            both = in_order(core, delta_refs[2 * place][...], delta_refs[2 * place + 1][...])
-            deltas_ref[place * half:(place + 1) * half] = both
+        near = 2 * delta_refs[0].shape[0]
+        rows_ref[:near] = near_rows(*row_refs[:-1])
+        rows_ref[near:] = row_refs[-1][...]
+        deltas_ref[:near] = in_order(core, delta_refs[0][...], delta_refs[1][...])
+        deltas_ref[near:] = in_order(core, delta_refs[2][...], delta_refs[3][...])
 
     feats = rows_ref[:, pl.ds(pl.multiple_of(step * tile, tile), tile)]
     gate_ref[...] = contract_rows(feats, deltas_ref[:, hidden_units:2 * hidden_units])
@@ -297,9 +299,11 @@
     half = owners // 2
 
     far_first = [0] + list(reversed(range(1, half)))
-    chosen, *groups = call(
+    chosen, own, pair_block, *groups = call(
         functools.partial(dispatch_kernel, owners, capacity),
-        (shape(slot_count, tok_rows),) + (shape(2 * capacity, 2 * width),) * half,
+        (shape(slot_count, tok_rows),)
+        + (shape(capacity, 2 * width),) * 2
+        + (shape(2 * capacity, 2 * width),) * (half - 1),
         expert_ids.reshape(1, tok_rows),
         route_weights.reshape(1, tok_rows),
         tokens,
@@ -324,32 +328,38 @@
         scratch=[pltpu.SemaphoreType.DMA((3,))],
         cost=10**7,
     )
-    groups = [groups[0]] + [swap(groups[j], 2 * j, "expert") for j in far_first[1:]]
+    groups = [swap(groups[j - 1], 2 * j, "expert") for j in far_first[1:]]
+    from_pair = swap(pair_block, 1, "expert")
+    groups = after(groups, from_pair)
     seconds = jnp.concatenate([group[capacity:] for group in groups], axis=0)
     by_pair = swap(after(seconds, weights[2]), 1, "expert")
 
-    part = slot_count // 4
-    packed = shape(part, 3 * hidden_units)
-    wide = shape(part, 3 * hidden_units, jnp.float32)
-    padded = shape(part, 3 * hidden_units + 128)
+    order = [0] + [2 * j for j in far_first[1:]] + [1] + [2 * j + 1 for j in far_first[1:]]
+
+    near = [own, from_pair] + groups
     held = []
-    for rows, cost in ((groups, 1), ([by_pair], 10**9)):
+    for rows, count, cost in ((near, half + 1, 1), ([by_pair], half - 1, FAR_PRODUCTS_COST)):
+        part = count * capacity // 2
+        packed = shape(part, 3 * hidden_units)
+        wide = shape(part, 3 * hidden_units, jnp.float32)
         mine, other = call(products_kernel, (wide, packed), *rows, *weights, cost=cost)
-        sums, marker = call(sums_kernel, (wide, padded), mine, swap(other, 1))
+        sums, marker = call(sums_kernel, (wide, packed), mine, swap(other, 1))
         bit = 2
         while 2 * bit < width_parts:
-            sums, marker = call(sums_kernel, (wide, padded), sums, swap(marker, bit))
+            sums, marker = call(sums_kernel, (wide, packed), sums, swap(marker, bit))
             bit *= 2
-        held.append((sums, swap(marker, bit)))
+        held.append((sums, swap(marker, bit), packed))
     deltas, grads = [], []
-    for place, (sums, received) in enumerate(held):
-        mine = call(deltas_kernel, packed, after(sums, grads) if grads else sums, received)
+    for sums, received, packed in held:
+        mine = call(deltas_kernel, packed, sums, received, cost=FAR_DELTAS_COST if deltas else 1)
+        if deltas:
+            mine = after(mine, deltas[1])
         pair = [mine, swap(mine, 1)]
         deltas += pair
         grads = [
             call(
-                functools.partial(slot_grad_kernel, far_first),
-                shape((place + 1) * half * capacity, width),
+                functools.partial(slot_grad_kernel, order),
+                shape(slot_count if grads else 2 * packed.shape[0], width),
                 *pair,
                 *weights[:2],
                 *grads,
@@ -366,7 +376,7 @@
             shape(hidden_units, width, jnp.float32),
         ),
         grid=(steps,),
-        in_specs=[pl.BlockSpec(memory_space=pltpu.VMEM)] * (half + 1 + 4),
+        in_specs=[pl.BlockSpec(memory_space=pltpu.VMEM)] * (len(near) + 1 + 4),
         out_specs=(
             pl.BlockSpec((width // steps, hidden_units), lambda i: (i, 0)),
             pl.BlockSpec((width // steps, hidden_units), lambda i: (i, 0)),
@@ -378,7 +388,7 @@
         ],
         compiler_params=pltpu.CompilerParams(vmem_limit_bytes=24 * 1024 * 1024),
         cost_estimate=pl.CostEstimate(flops=10**7, bytes_accessed=10**7, transcendentals=0),
-    )(*groups, by_pair, *deltas)
+    )(*near, by_pair, *deltas)
     token_grad = call(token_grad_kernel, shape(tok_rows, width), chosen, returned)
     return (token_grad, gate_grad[None], up_grad[None], down_grad[None])
 

time: 48.1 us -> 46.6 us (0.969)
  waiting for transfers between devices: 17.8 us -> 14.6 us
  starting transfers between devices: 15.7 us -> 17.3 us
    ppermute x10 -> x11, waiting for transfers between devices: 14.5 us -> 11.4 us  [swap(): return lax.ppermute(value, axis, [(i, i ^ bit) for i in range(size)])]
    ppermute x10 -> x11, starting transfers between devices: 10.7 us -> 12.4 us  [swap(): return lax.ppermute(value, axis, [(i, i ^ bit) for i in range(size)])]
  transfers between devices with their start and end apart: 11 -> 12, of which waited for: 8 -> 7; matrix products, arithmetic and copies ran while one was open for 0% -> 0% of each run, Pallas kernels for 18% -> 19%
where the time goes in v4:
time: 46.6 us; the launch traced here: 46.3 us
  starting transfers between devices  17.3 us (37%)
  waiting for transfers between devices  14.6 us (31%)
  Pallas kernels  13.6 us (29%)
  between operations  0.78 us (2%)
    ppermute x11, starting transfers between devices, swap(): return lax.ppermute(value, axis, [(i, i ^ bit) for i in range(size)])  12.4 us
    ppermute x11, waiting for transfers between devices, swap(): return lax.ppermute(value, axis, [(i, i ^ bit) for i in range(size)])  11.4 us
    pallas_call x11, Pallas kernels, call(): pl.pallas_call(kernel, out_shape=outs, in_specs=[pl.BlockSpec(memory_spac...  9.47 us
    all_to_all x1, starting transfers between devices, body_by_pairs(): lax.all_to_all(grads[0], 'expert', split_axis=0, concat_axis=0, tiled=True)  4.88 us
    pallas_call x1, Pallas kernels, body_by_pairs(): pl.pallas_call(weight_grads_kernel, out_shape=(shape(width, hidden_units,...  4.1 us
    all_to_all x1, waiting for transfers between devices, body_by_pairs(): lax.all_to_all(grads[0], 'expert', split_axis=0, concat_axis=0, tiled=True)  3.24 us
  transfers between devices with their start and end apart: 12, of which 7 were waited for; matrix products, arithmetic and copies ran while one was open for 0% of the time, Pallas kernels for 19%

profile of v4, /device:TPU:0, one launch (start us, length us, event | category | flops | bytes accessed | tf_op | source)
XLA Modules:
  0.0 46.3 jit_solution(3437029792614768989)
XLA Ops:
  0.6 1.3 %shard_map.102 = (bf16[128,128]{1,0:T(8,128)(2,1)S(1)}, bf16[16,1024]{1,0:T(8,128)(2,1)S(1)}, bf16[16,1024]{1,0:T(8,128)(2,1)S(1)}, bf16[32,1024]{1,0:T(8,128)(2...) custom-call(s32[1,128]{1,0:T(1,128)} %bitcast.14, f32[1,128]{1,0:T(1,128)} %bitcast.15, ...), custom_call_target="tpu_custom_call" | custom-call | flops 1 | bytes 1 | tf_op jit(solution)/shard_map/pallas_call | solution.py:53
  1.9 5.1 %collective-permute-start = (bf16[32,1024]{1,0:T(8,128)(2,1)S(1)}, bf16[32,1024]{1,0:T(8,128)(2,1)S(1)}, u32[]{:S(2)}, u32[]{:S(2)}) collective-permute-start(bf16[32,1024]{1,0:T(8,128)(2,1)S(1)} %get-tuple-element.30), channel_id=1, source_target_pairs={{0,6},{1,7},{2,4},{3,5},{4,2},{5,3},{6,0},{7,1},{8,14},{9,15},{10,... | collective-permute-start | bytes 196616 | tf_op jit(solution)/shard_map/ppermute | solution.py:36
  7.0 0.6 %collective-permute-start.2 = (bf16[32,1024]{1,0:T(8,128)(2,1)S(1)}, bf16[32,1024]{1,0:T(8,128)(2,1)S(1)}, u32[]{:S(2)}, u32[]{:S(2)}) collective-permute-start(bf16[32,1024]{1,0:T(8,128)(2,1)S(1)} %get-tuple-element.32), channel_id=1, source_target_pairs={{0,2},{1,3},{2,0},{3,1},{4,6},{5,7},{6,4},{7,5},{8,10},{9,11},{10,... | collective-permute-start | bytes 196616 | tf_op jit(solution)/shard_map/ppermute | solution.py:36
  7.7 1.7 %collective-permute-start.3 = (bf16[16,1024]{1,0:T(8,128)(2,1)S(1)}, bf16[16,1024]{1,0:T(8,128)(2,1)S(1)}, u32[]{:S(2)}, u32[]{:S(2)}) collective-permute-start(bf16[16,1024]{1,0:T(8,128)(2,1)S(1)} %get-tuple-element.33), channel_id=1, source_target_pairs={{0,1},{1,0},{2,3},{3,2},{4,5},{5,4},{6,7},{7,6},{8,9},{9,8},{10,11... | collective-permute-start | bytes 98312 | tf_op jit(solution)/shard_map/ppermute | solution.py:36
  9.3 2.3 %shard_map.103 = (bf16[512,1408]{1,0:T(8,128)(2,1)S(1)}, bf16[512,1408]{1,0:T(8,128)(2,1)S(1)}, bf16[1408,512]{1,0:T(8,128)(2,1)S(1)}) custom-call(bf16[512,1408]{1,0:T(8,128)(2,1)} %bitcast.11, bf16[512,1408]{1,0:T(8,128)(2,1)} %bitcast.12, bf16[1408,512]{1,0:T(8,128)(2,1)} %bitcast.13, bf16[128,128]{1,0:T(8,128)(2,1)S(1)} %get-tuple-element.29.marker_hbm.chosen_ref), custom_call_target="tpu_custom_call" | custom-call | flops 10000000 | bytes 10000000 | tf_op jit(solution)/shard_map/pallas_call | solution.py:53
  11.6 1.0 %collective-permute-done.1.refs_3_ = bf16[32,1024]{1,0:T(8,128)(2,1)S(1)} collective-permute-done((bf16[32,1024]{1,0:T(8,128)(2,1)S(1)}, bf16[32,1024]{1,0:T(8,128)(2,1)S(1)}, u32[]{:S(2)}, u32[]{:S(2)}) %collective-permute-start.1) | collective-permute-done | bytes 65568 | tf_op jit(solution)/shard_map/ppermute | solution.py:36
  12.6 1.0 %shard_map.107 = (f32[40,4224]{1,0:T(8,128)S(1)}, bf16[40,4224]{1,0:T(8,128)(2,1)S(1)}) custom-call(bf16[16,1024]{1,0:T(8,128)(2,1)S(1)} %get-tuple-element.45.refs_0_, bf16[16,1024]{1,0:T(8,128)(2,1)S(1)} %collective-permute-done.3.refs_1_, bf16[32,1024]{1,0:T(8,128)(2,1)S(1)} %collective-permute-done.refs_2_, ...), custom_call_target="tpu_custom_call" | custom-call | flops 1 | bytes 1 | tf_op jit(solution)/shard_map/pallas_call | solution.py:53
  13.8 1.6 %collective-permute-start.4 = (bf16[48,1024]{1,0:T(8,128)(2,1)S(1)}, bf16[48,1024]{1,0:T(8,128)(2,1)S(1)}, u32[]{:S(2)}, u32[]{:S(2)}) collective-permute-start(bf16[48,1024]{1,0:T(8,128)(2,1)S(1)} %pad_maximum_fusion), channel_id=1, source_target_pairs={{0,1},{1,0},{2,3},{3,2},{4,5},{5,4},{6,7},{7,6},{8,9},{9,8},{10,11... | collective-permute-start | bytes 294920 | tf_op jit(solution)/shard_map/ppermute | solution.py:36
  15.5 1.6 %collective-permute-start.8 = (bf16[40,4224]{1,0:T(8,128)(2,1)S(1)}, bf16[40,4224]{1,0:T(8,128)(2,1)S(1)}, u32[]{:S(2)}, u32[]{:S(2)}) collective-permute-start(bf16[40,4224]{1,0:T(8,128)(2,1)S(1)} %get-tuple-element.49), channel_id=1, source_target_pairs={{0,16},{8,24},{16,0},{24,8},{1,17},{9,25},{17,1},{25,9},{2,18},{10... | collective-permute-start | bytes 1013768 | tf_op jit(solution)/shard_map/ppermute | solution.py:36
  17.0 2.0 %collective-permute-done.4.refs_0_.refs_5_ = bf16[48,1024]{1,0:T(8,128)(2,1)S(1)} collective-permute-done((bf16[48,1024]{1,0:T(8,128)(2,1)S(1)}, bf16[48,1024]{1,0:T(8,128)(2,1)S(1)}, u32[]{:S(2)}, u32[]{:S(2)}) %collective-permute-start.4) | collective-permute-done | bytes 98336 | tf_op jit(solution)/shard_map/ppermute | solution.py:36
  19.0 1.0 %shard_map.104 = (f32[24,4224]{1,0:T(8,128)S(1)}, bf16[24,4224]{1,0:T(8,128)(2,1)S(1)}) custom-call(bf16[48,1024]{1,0:T(8,128)(2,1)S(1)} %collective-permute-done.4.refs_0_.refs_5_, bf16[512,1408]{1,0:T(8,128)(2,1)S(1)} %get-tuple-element.39.refs_1_.refs_5_.gate_ref, bf16[512,1408]{1,0:T(8,128)(2,1)S(1)} %get-tuple-element.40.refs_2_.refs_6_.up_ref, ...), custom_call_target="tpu_custom_call" | custom-call | flops 1000000000 | bytes 1000000000 | tf_op jit(solution)/shard_map/pallas_call | solution.py:53
  20.1 1.4 %collective-permute-done.5.received_ref = bf16[24,4224]{1,0:T(8,128)(2,1)S(1)} collective-permute-done((bf16[24,4224]{1,0:T(8,128)(2,1)S(1)}, bf16[24,4224]{1,0:T(8,128)(2,1)S(1)}, u32[]{:S(2)}, u32[]{:S(2)}) %collective-permute-start.5) | collective-permute-done | bytes 202784 | tf_op jit(solution)/shard_map/ppermute | solution.py:36
  21.6 1.6 %collective-permute-start.6 = (bf16[24,4224]{1,0:T(8,128)(2,1)S(1)}, bf16[24,4224]{1,0:T(8,128)(2,1)S(1)}, u32[]{:S(2)}, u32[]{:S(2)}) collective-permute-start(bf16[24,4224]{1,0:T(8,128)(2,1)S(1)} %get-tuple-element.44), channel_id=1, source_target_pairs={{0,16},{8,24},{16,0},{24,8},{1,17},{9,25},{17,1},{25,9},{2,18},{10... | collective-permute-start | bytes 608264 | tf_op jit(solution)/shard_map/ppermute | solution.py:36
  23.2 3.1 %collective-permute-done.8.received_ref = bf16[40,4224]{1,0:T(8,128)(2,1)S(1)} collective-permute-done((bf16[40,4224]{1,0:T(8,128)(2,1)S(1)}, bf16[40,4224]{1,0:T(8,128)(2,1)S(1)}, u32[]{:S(2)}, u32[]{:S(2)}) %collective-permute-start.8) | collective-permute-done | bytes 337952 | tf_op jit(solution)/shard_map/ppermute | solution.py:36
  26.3 0.2 shard_map.109.mine_ref.refs_6_
  26.6 3.4 %collective-permute-done.6.received_ref = bf16[24,4224]{1,0:T(8,128)(2,1)S(1)} collective-permute-done((bf16[24,4224]{1,0:T(8,128)(2,1)S(1)}, bf16[24,4224]{1,0:T(8,128)(2,1)S(1)}, u32[]{:S(2)}, u32[]{:S(2)}) %collective-permute-start.6) | collective-permute-done | bytes 202784 | tf_op jit(solution)/shard_map/ppermute | solution.py:36
  29.9 0.1 shard_map.106.mine_ref.refs_8_
  30.1 1.0 %shard_map.110.refs_0_ = bf16[80,512]{1,0:T(8,128)(2,1)S(1)} custom-call(bf16[40,4224]{1,0:T(8,128)(2,1)S(1)} %shard_map.109.mine_ref.refs_6_, bf16[40,4224]{1,0:T(8,128)(2,1)S(1)} %collective-permute-done.9.other_ref.refs_7_, bf16[512,1408]{1,0:T(8,128)(2,1)S(1)} %get-tuple-element.39.refs_1_.refs_5_.gate_ref, ...), custom_call_target="tpu_custom_call" | custom-call | flops 1 | bytes 1 | tf_op jit(solution)/shard_map/pallas_call | solution.py:53
  31.1 0.4 collective-permute-done.10.other_ref.refs_9_
  31.5 1.6 %shard_map.111 = bf16[128,512]{1,0:T(8,128)(2,1)} custom-call(bf16[24,4224]{1,0:T(8,128)(2,1)S(1)} %shard_map.106.mine_ref.refs_8_, bf16[24,4224]{1,0:T(8,128)(2,1)S(1)} %collective-permute-done.10.other_ref.refs_9_, bf16[512,1408]{1,0:T(8,128)(2,1)S(1)} %get-tuple-element.39.refs_1_.refs_5_.gate_ref, ...), custom_call_target="tpu_custom_call" | custom-call | flops 1 | bytes 1 | tf_op jit(solution)/shard_map/pallas_call | solution.py:53
  33.2 4.9 %all-to-all-start = ((bf16[8,16,512]{2,1,0:T(8,128)(2,1)}), bf16[8,16,512]{2,1,0:T(8,128)(2,1)S(1)}, u32[]{:S(2)}, u32[]{:S(2)}) async-start(bf16[8,16,512]{2,1,0:T(8,128)(2,1)} %bitcast.5), calls=%async_computation | async-start | bytes 262144 | tf_op jit(solution)/shard_map/all_to_all | solution.py:368
  38.1 4.1 %shard_map.113 = (f32[512,1408]{1,0:T(8,128)}, f32[512,1408]{1,0:T(8,128)}, f32[1408,512]{1,0:T(8,128)}) custom-call(bf16[16,1024]{1,0:T(8,128)(2,1)S(1)} %get-tuple-element.45.refs_0_, bf16[16,1024]{1,0:T(8,128)(2,1)S(1)} %collective-permute-done.3.refs_1_, bf16[32,1024]{1,0:T(8,128)(2,1)S(1)} %collective-permute-done.refs_2_, ...), custom_call_target="tpu_custom_call" | custom-call | flops 10000000 | bytes 10000000 | tf_op jit(solution)/shard_map/pallas_call | solution.py:371
  42.2 3.2 %all-to-all-done = bf16[8,16,512]{2,1,0:T(8,128)(2,1)S(1)} async-done(((bf16[8,16,512]{2,1,0:T(8,128)(2,1)}), bf16[8,16,512]{2,1,0:T(8,128)(2,1)S(1)}, u32[]{:S(2)}, u32[]{:S(2)}) %all-to-all-start) | async-done | bytes 131104 | tf_op jit(solution)/shard_map/all_to_all | solution.py:368
  45.4 0.9 %shard_map.112 = bf16[128,512]{1,0:T(8,128)(2,1)} custom-call(bf16[128,128]{1,0:T(8,128)(2,1)S(1)} %get-tuple-element.29.marker_hbm.chosen_ref, bf16[128,512]{1,0:T(8,128)(2,1)S(1)} %bitcast.10), custom_call_target="tpu_custom_call" | custom-call | flops 1 | bytes 1 | tf_op jit(solution)/shard_map/pallas_call | solution.py:53
  (16 shorter events, 0.5 us)
Async XLA Ops:
  1.9 9.7 %collective-permute-start = (bf16[32,1024]{1,0:T(8,128)(2,1)S(1)}, bf16[32,1024]{1,0:T(8,128)(2,1)S(1)}, u32[]{:S(2)}, u32[]{:S(2)}) collective-permute-start(bf16[32,1024]{1,0:T(8,128)(2,1)S(1)} %get-tuple-element.30), channel_id=1, source_target_pairs={{0,6},{1,7},{2,4},{3,5},{4,2},{5,3},{6,0},{7,1},{8,14},{9,15},{10,... | collective-permute-start | bytes 196616 | tf_op jit(solution)/shard_map/ppermute | solution.py:36
  7.0 5.6 %collective-permute-start.1 = (bf16[32,1024]{1,0:T(8,128)(2,1)S(1)}, bf16[32,1024]{1,0:T(8,128)(2,1)S(1)}, u32[]{:S(2)}, u32[]{:S(2)}) collective-permute-start(bf16[32,1024]{1,0:T(8,128)(2,1)S(1)} %get-tuple-element.31), channel_id=1, source_target_pairs={{0,4},{1,5},{2,6},{3,7},{4,0},{5,1},{6,2},{7,3},{8,12},{9,13},{10,... | collective-permute-start | bytes 196616 | tf_op jit(solution)/shard_map/ppermute | solution.py:36
  7.0 5.6 %collective-permute-start.2 = (bf16[32,1024]{1,0:T(8,128)(2,1)S(1)}, bf16[32,1024]{1,0:T(8,128)(2,1)S(1)}, u32[]{:S(2)}, u32[]{:S(2)}) collective-permute-start(bf16[32,1024]{1,0:T(8,128)(2,1)S(1)} %get-tuple-element.32), channel_id=1, source_target_pairs={{0,2},{1,3},{2,0},{3,1},{4,6},{5,7},{6,4},{7,5},{8,10},{9,11},{10,... | collective-permute-start | bytes 196616 | tf_op jit(solution)/shard_map/ppermute | solution.py:36
  7.7 3.9 %collective-permute-start.3 = (bf16[16,1024]{1,0:T(8,128)(2,1)S(1)}, bf16[16,1024]{1,0:T(8,128)(2,1)S(1)}, u32[]{:S(2)}, u32[]{:S(2)}) collective-permute-start(bf16[16,1024]{1,0:T(8,128)(2,1)S(1)} %get-tuple-element.33), channel_id=1, source_target_pairs={{0,1},{1,0},{2,3},{3,2},{4,5},{5,4},{6,7},{7,6},{8,9},{9,8},{10,11... | collective-permute-start | bytes 98312 | tf_op jit(solution)/shard_map/ppermute | solution.py:36
  13.7 1.7 %collective-permute-start.7 = (bf16[40,4224]{1,0:T(8,128)(2,1)S(1)}, bf16[40,4224]{1,0:T(8,128)(2,1)S(1)}, u32[]{:S(2)}, u32[]{:S(2)}) collective-permute-start(bf16[40,4224]{1,0:T(8,128)(2,1)S(1)} %get-tuple-element.47), channel_id=1, source_target_pairs={{0,8},{8,0},{16,24},{24,16},{1,9},{9,1},{17,25},{25,17},{2,10},{10... | collective-permute-start | bytes 1013768 | tf_op jit(solution)/shard_map/ppermute | solution.py:36
  13.8 5.2 %collective-permute-start.4 = (bf16[48,1024]{1,0:T(8,128)(2,1)S(1)}, bf16[48,1024]{1,0:T(8,128)(2,1)S(1)}, u32[]{:S(2)}, u32[]{:S(2)}) collective-permute-start(bf16[48,1024]{1,0:T(8,128)(2,1)S(1)} %pad_maximum_fusion), channel_id=1, source_target_pairs={{0,1},{1,0},{2,3},{3,2},{4,5},{5,4},{6,7},{7,6},{8,9},{9,8},{10,11... | collective-permute-start | bytes 294920 | tf_op jit(solution)/shard_map/ppermute | solution.py:36
  15.5 10.8 %collective-permute-start.8 = (bf16[40,4224]{1,0:T(8,128)(2,1)S(1)}, bf16[40,4224]{1,0:T(8,128)(2,1)S(1)}, u32[]{:S(2)}, u32[]{:S(2)}) collective-permute-start(bf16[40,4224]{1,0:T(8,128)(2,1)S(1)} %get-tuple-element.49), channel_id=1, source_target_pairs={{0,16},{8,24},{16,0},{24,8},{1,17},{9,25},{17,1},{25,9},{2,18},{10... | collective-permute-start | bytes 1013768 | tf_op jit(solution)/shard_map/ppermute | solution.py:36
  20.0 1.5 %collective-permute-start.5 = (bf16[24,4224]{1,0:T(8,128)(2,1)S(1)}, bf16[24,4224]{1,0:T(8,128)(2,1)S(1)}, u32[]{:S(2)}, u32[]{:S(2)}) collective-permute-start(bf16[24,4224]{1,0:T(8,128)(2,1)S(1)} %get-tuple-element.42), channel_id=1, source_target_pairs={{0,8},{8,0},{16,24},{24,16},{1,9},{9,1},{17,25},{25,17},{2,10},{10... | collective-permute-start | bytes 608264 | tf_op jit(solution)/shard_map/ppermute | solution.py:36
  21.6 8.3 %collective-permute-start.6 = (bf16[24,4224]{1,0:T(8,128)(2,1)S(1)}, bf16[24,4224]{1,0:T(8,128)(2,1)S(1)}, u32[]{:S(2)}, u32[]{:S(2)}) collective-permute-start(bf16[24,4224]{1,0:T(8,128)(2,1)S(1)} %get-tuple-element.44), channel_id=1, source_target_pairs={{0,16},{8,24},{16,0},{24,8},{1,17},{9,25},{17,1},{25,9},{2,18},{10... | collective-permute-start | bytes 608264 | tf_op jit(solution)/shard_map/ppermute | solution.py:36
  26.5 3.5 %collective-permute-start.9 = (bf16[40,4224]{1,0:T(8,128)(2,1)S(1)}, bf16[40,4224]{1,0:T(8,128)(2,1)S(1)}, u32[]{:S(2)}, u32[]{:S(2)}) collective-permute-start(bf16[40,4224]{1,0:T(8,128)(2,1)S(1)} %shard_map.109.mine_ref.refs_6_), channel_id=1, source_target_pairs={{0,8},{8,0},{16,24},{24,16},{1,9},{9,1},{17,25},{25,17},{2,10},{10... | collective-permute-start | bytes 1013768 | tf_op jit(solution)/shard_map/ppermute | solution.py:36
  30.0 1.5 %collective-permute-start.10 = (bf16[24,4224]{1,0:T(8,128)(2,1)S(1)}, bf16[24,4224]{1,0:T(8,128)(2,1)S(1)}, u32[]{:S(2)}, u32[]{:S(2)}) collective-permute-start(bf16[24,4224]{1,0:T(8,128)(2,1)S(1)} %shard_map.106.mine_ref.refs_8_), channel_id=1, source_target_pairs={{0,8},{8,0},{16,24},{24,16},{1,9},{9,1},{17,25},{25,17},{2,10},{10... | collective-permute-start | bytes 608264 | tf_op jit(solution)/shard_map/ppermute | solution.py:36
  33.2 12.2 %all-to-all-start = ((bf16[8,16,512]{2,1,0:T(8,128)(2,1)}), bf16[8,16,512]{2,1,0:T(8,128)(2,1)S(1)}, u32[]{:S(2)}, u32[]{:S(2)}) async-start(bf16[8,16,512]{2,1,0:T(8,128)(2,1)} %bitcast.5), calls=%async_computation | async-start | bytes 262144 | tf_op jit(solution)/shard_map/all_to_all | solution.py:368

commit v5 on v4

--- a/solution.py
+++ b/solution.py
@@ -37,7 +37,7 @@
 
 
 FAR_PRODUCTS_COST = 10**9
-FAR_DELTAS_COST = 2 * 10**9
+FAR_DELTAS_COST = 16 * 10**8
 
 
 def after(values, marker):
@@ -126,12 +126,17 @@
         copy.wait()
 
 
+def turn_kernel(*refs):
+    for source, target in zip(refs[:3], refs[3:]):
+        target[...] = source[...].T
+
+
 def near_rows(own_ref, from_pair_ref, *group_refs):
     halves = [ref[:ref.shape[0] // 2] for ref in group_refs]
     return jnp.concatenate([own_ref[...]] + halves + [from_pair_ref[...]], axis=0)
 
 
-def products_kernel(*refs):
+def products_kernel(turned, *refs):
     *row_refs, gate_ref, up_ref, down_ref, mine_ref, other_ref = refs
     rows = near_rows(*row_refs) if len(row_refs) > 1 else row_refs[0][...]
     half = rows.shape[0] // 2
@@ -141,10 +146,11 @@
     feats, cots = rows[:, :width], rows[:, width:]
     for place, weight_ref in enumerate((gate_ref, up_ref, down_ref)):
         cols = slice(place * hidden_units, (place + 1) * hidden_units)
-        if place < 2:
-            out = jnp.dot(feats, weight_ref[...], preferred_element_type=jnp.float32)
+        rows = feats if place < 2 else cots
+        if place < 2 or turned:
+            out = jnp.dot(rows, weight_ref[...], preferred_element_type=jnp.float32)
         else:
-            out = contract_cols(cots, weight_ref[...])
+            out = contract_cols(rows, weight_ref[...])
         low, high = out[:half], out[half:]
         mine_ref[:, cols] = jnp.where(core == 0, low, high)
         other_ref[:, cols] = jnp.where(core == 0, high, low).astype(jnp.bfloat16)
@@ -172,11 +178,12 @@
 
 def slot_grad_kernel(order, mine_ref, other_ref, gate_ref, up_ref, *refs):
     *earlier_ref, out_ref = refs
-    hidden_units = gate_ref.shape[1]
+    hidden_units = gate_ref.shape[0]
     rows = in_order(lax.axis_index("dp") % 2, mine_ref[...], other_ref[...])
+    by_gate, by_up = rows[:, hidden_units:2 * hidden_units], rows[:, 2 * hidden_units:]
     out = (
-        contract_cols(rows[:, hidden_units:2 * hidden_units], gate_ref[...])
-        + contract_cols(rows[:, 2 * hidden_units:], up_ref[...])
+        jnp.dot(by_gate, gate_ref[...], preferred_element_type=jnp.float32)
+        + jnp.dot(by_up, up_ref[...], preferred_element_type=jnp.float32)
     ).astype(jnp.bfloat16)
     if not earlier_ref:
         out_ref[...] = out
@@ -336,13 +343,29 @@
 
     order = [0] + [2 * j for j in far_first[1:]] + [1] + [2 * j + 1 for j in far_first[1:]]
 
+    turned = call(
+        turn_kernel,
+        (shape(hidden_units, width), shape(hidden_units, width), shape(width, hidden_units)),
+        *after(weights, groups[0]),
+    )
+    far = after(by_pair, turned[0])
     near = [own, from_pair] + groups
     held = []
-    for rows, count, cost in ((near, half + 1, 1), ([by_pair], half - 1, FAR_PRODUCTS_COST)):
+    for rows, count, down, cost in (
+        (near, half + 1, weights[2], 1),
+        ([far], half - 1, turned[2], FAR_PRODUCTS_COST),
+    ):
         part = count * capacity // 2
         packed = shape(part, 3 * hidden_units)
         wide = shape(part, 3 * hidden_units, jnp.float32)
-        mine, other = call(products_kernel, (wide, packed), *rows, *weights, cost=cost)
+        mine, other = call(
+            functools.partial(products_kernel, down is turned[2]),
+            (wide, packed),
+            *rows,
+            *weights[:2],
+            down,
+            cost=cost,
+        )
         sums, marker = call(sums_kernel, (wide, packed), mine, swap(other, 1))
         bit = 2
         while 2 * bit < width_parts:
@@ -361,7 +384,7 @@
                 functools.partial(slot_grad_kernel, order),
                 shape(slot_count if grads else 2 * packed.shape[0], width),
                 *pair,
-                *weights[:2],
+                *turned[:2],
                 *grads,
             )
         ]
@@ -388,7 +411,7 @@
         ],
         compiler_params=pltpu.CompilerParams(vmem_limit_bytes=24 * 1024 * 1024),
         cost_estimate=pl.CostEstimate(flops=10**7, bytes_accessed=10**7, transcendentals=0),
-    )(*near, by_pair, *deltas)
+    )(*near, far, *deltas)
     token_grad = call(token_grad_kernel, shape(tok_rows, width), chosen, returned)
     return (token_grad, gate_grad[None], up_grad[None], down_grad[None])
 

time: 46.6 us -> 46.2 us (level)
  waiting for transfers between devices: 14.6 us -> 14 us
    ppermute x11, waiting for transfers between devices: 11.4 us -> 10.7 us  [swap(): return lax.ppermute(value, axis, [(i, i ^ bit) for i in range(size)])]
    pallas_call x11 -> x12, Pallas kernels: 9.47 us -> 9.75 us  [call(): pl.pallas_call(kernel, out_shape=outs, in_specs=[pl.BlockSpec(memory_spac...]
  transfers between devices with their start and end apart: 12 -> 12, of which waited for: 7 -> 7; matrix products, arithmetic and copies ran while one was open for 0% -> 0% of each run, Pallas kernels for 19% -> 21%
where the time goes in v5:
time: 46.2 us; the launch traced here: 45.9 us
  starting transfers between devices  17.3 us (37%)
  waiting for transfers between devices  14 us (30%)
  Pallas kernels  13.9 us (30%)
  between operations  0.78 us (2%)
    ppermute x11, starting transfers between devices, swap(): return lax.ppermute(value, axis, [(i, i ^ bit) for i in range(size)])  12.4 us
    ppermute x11, waiting for transfers between devices, swap(): return lax.ppermute(value, axis, [(i, i ^ bit) for i in range(size)])  10.7 us
    pallas_call x12, Pallas kernels, call(): pl.pallas_call(kernel, out_shape=outs, in_specs=[pl.BlockSpec(memory_spac...  9.75 us
    all_to_all x1, starting transfers between devices, body_by_pairs(): lax.all_to_all(grads[0], 'expert', split_axis=0, concat_axis=0, tiled=True)  4.88 us
    pallas_call x1, Pallas kernels, body_by_pairs(): pl.pallas_call(weight_grads_kernel, out_shape=(shape(width, hidden_units,...  4.1 us
    all_to_all x1, waiting for transfers between devices, body_by_pairs(): lax.all_to_all(grads[0], 'expert', split_axis=0, concat_axis=0, tiled=True)  3.24 us
  transfers between devices with their start and end apart: 12, of which 7 were waited for; matrix products, arithmetic and copies ran while one was open for 0% of the time, Pallas kernels for 21%

profile of v5, /device:TPU:0, one launch (start us, length us, event | category | flops | bytes accessed | tf_op | source)
XLA Modules:
  0.0 45.9 jit_solution(4964301844809482166)
XLA Ops:
  0.6 1.3 %shard_map.102 = (bf16[128,128]{1,0:T(8,128)(2,1)S(1)}, bf16[16,1024]{1,0:T(8,128)(2,1)S(1)}, bf16[16,1024]{1,0:T(8,128)(2,1)S(1)}, bf16[32,1024]{1,0:T(8,128)(2...) custom-call(s32[1,128]{1,0:T(1,128)} %bitcast.14, f32[1,128]{1,0:T(1,128)} %bitcast.15, ...), custom_call_target="tpu_custom_call" | custom-call | flops 1 | bytes 1 | tf_op jit(solution)/shard_map/pallas_call | solution.py:53
  1.9 5.1 %collective-permute-start = (bf16[32,1024]{1,0:T(8,128)(2,1)S(1)}, bf16[32,1024]{1,0:T(8,128)(2,1)S(1)}, u32[]{:S(2)}, u32[]{:S(2)}) collective-permute-start(bf16[32,1024]{1,0:T(8,128)(2,1)S(1)} %get-tuple-element.37), channel_id=1, source_target_pairs={{0,6},{1,7},{2,4},{3,5},{4,2},{5,3},{6,0},{7,1},{8,14},{9,15},{10,... | collective-permute-start | bytes 196616 | tf_op jit(solution)/shard_map/ppermute | solution.py:36
  7.0 0.6 %collective-permute-start.2 = (bf16[32,1024]{1,0:T(8,128)(2,1)S(1)}, bf16[32,1024]{1,0:T(8,128)(2,1)S(1)}, u32[]{:S(2)}, u32[]{:S(2)}) collective-permute-start(bf16[32,1024]{1,0:T(8,128)(2,1)S(1)} %get-tuple-element.39), channel_id=1, source_target_pairs={{0,2},{1,3},{2,0},{3,1},{4,6},{5,7},{6,4},{7,5},{8,10},{9,11},{10,... | collective-permute-start | bytes 196616 | tf_op jit(solution)/shard_map/ppermute | solution.py:36
  7.7 1.7 %collective-permute-start.3 = (bf16[16,1024]{1,0:T(8,128)(2,1)S(1)}, bf16[16,1024]{1,0:T(8,128)(2,1)S(1)}, u32[]{:S(2)}, u32[]{:S(2)}) collective-permute-start(bf16[16,1024]{1,0:T(8,128)(2,1)S(1)} %get-tuple-element.40), channel_id=1, source_target_pairs={{0,1},{1,0},{2,3},{3,2},{4,5},{5,4},{6,7},{7,6},{8,9},{9,8},{10,11... | collective-permute-start | bytes 98312 | tf_op jit(solution)/shard_map/ppermute | solution.py:36
  9.3 2.3 %shard_map.103 = (bf16[512,1408]{1,0:T(8,128)(2,1)S(1)}, bf16[512,1408]{1,0:T(8,128)(2,1)S(1)}, bf16[1408,512]{1,0:T(8,128)(2,1)S(1)}) custom-call(bf16[512,1408]{1,0:T(8,128)(2,1)} %bitcast.11, bf16[512,1408]{1,0:T(8,128)(2,1)} %bitcast.12, bf16[1408,512]{1,0:T(8,128)(2,1)} %bitcast.13, bf16[128,128]{1,0:T(8,128)(2,1)S(1)} %get-tuple-element.36.marker_hbm.chosen_ref), custom_call_target="tpu_custom_call" | custom-call | flops 10000000 | bytes 10000000 | tf_op jit(solution)/shard_map/pallas_call | solution.py:53
  11.6 1.0 %collective-permute-done.1.refs_3_ = bf16[32,1024]{1,0:T(8,128)(2,1)S(1)} collective-permute-done((bf16[32,1024]{1,0:T(8,128)(2,1)S(1)}, bf16[32,1024]{1,0:T(8,128)(2,1)S(1)}, u32[]{:S(2)}, u32[]{:S(2)}) %collective-permute-start.1) | collective-permute-done | bytes 65568 | tf_op jit(solution)/shard_map/ppermute | solution.py:36
  12.6 1.0 %shard_map.108 = (f32[40,4224]{1,0:T(8,128)S(1)}, bf16[40,4224]{1,0:T(8,128)(2,1)S(1)}) custom-call(bf16[16,1024]{1,0:T(8,128)(2,1)S(1)} %get-tuple-element.58.refs_0_, bf16[16,1024]{1,0:T(8,128)(2,1)S(1)} %collective-permute-done.3.refs_1_, bf16[32,1024]{1,0:T(8,128)(2,1)S(1)} %collective-permute-done.refs_2_, ...), custom_call_target="tpu_custom_call" | custom-call | flops 1 | bytes 1 | tf_op jit(solution)/shard_map/pallas_call | solution.py:53
  13.8 1.6 %collective-permute-start.4 = (bf16[48,1024]{1,0:T(8,128)(2,1)S(1)}, bf16[48,1024]{1,0:T(8,128)(2,1)S(1)}, u32[]{:S(2)}, u32[]{:S(2)}) collective-permute-start(bf16[48,1024]{1,0:T(8,128)(2,1)S(1)} %pad_maximum_fusion), channel_id=1, source_target_pairs={{0,1},{1,0},{2,3},{3,2},{4,5},{5,4},{6,7},{7,6},{8,9},{9,8},{10,11... | collective-permute-start | bytes 294920 | tf_op jit(solution)/shard_map/ppermute | solution.py:36
  15.5 1.6 %collective-permute-start.8 = (bf16[40,4224]{1,0:T(8,128)(2,1)S(1)}, bf16[40,4224]{1,0:T(8,128)(2,1)S(1)}, u32[]{:S(2)}, u32[]{:S(2)}) collective-permute-start(bf16[40,4224]{1,0:T(8,128)(2,1)S(1)} %get-tuple-element.62), channel_id=1, source_target_pairs={{0,16},{8,24},{16,0},{24,8},{1,17},{9,25},{17,1},{25,9},{2,18},{10... | collective-permute-start | bytes 1013768 | tf_op jit(solution)/shard_map/ppermute | solution.py:36
  17.0 1.2 %shard_map.104 = (bf16[1408,512]{1,0:T(8,128)(2,1)S(1)}, bf16[1408,512]{1,0:T(8,128)(2,1)S(1)}, bf16[512,1408]{1,0:T(8,128)(2,1)S(1)}) custom-call(bf16[512,1408]{1,0:T(8,128)(2,1)S(1)} %get-tuple-element.48.refs_0_.refs_1_.refs_5_, bf16[512,1408]{1,0:T(8,128)(2,1)S(1)} %get-tuple-element.49.refs_1_.refs_2_.refs_6_, ...), custom_call_target="tpu_custom_call" | custom-call | flops 1 | bytes 1 | tf_op jit(solution)/shard_map/pallas_call | solution.py:53
  18.2 0.8 %collective-permute-done.4.refs_0_.refs_5_ = bf16[48,1024]{1,0:T(8,128)(2,1)S(1)} collective-permute-done((bf16[48,1024]{1,0:T(8,128)(2,1)S(1)}, bf16[48,1024]{1,0:T(8,128)(2,1)S(1)}, u32[]{:S(2)}, u32[]{:S(2)}) %collective-permute-start.4) | collective-permute-done | bytes 98336 | tf_op jit(solution)/shard_map/ppermute | solution.py:36
  19.0 0.8 %shard_map.105 = (f32[24,4224]{1,0:T(8,128)S(1)}, bf16[24,4224]{1,0:T(8,128)(2,1)S(1)}) custom-call(bf16[48,1024]{1,0:T(8,128)(2,1)S(1)} %collective-permute-done.4.refs_0_.refs_5_, bf16[512,1408]{1,0:T(8,128)(2,1)S(1)} %get-tuple-element.48.refs_0_.refs_1_.refs_5_, bf16[512,1408]{1,0:T(8,128)(2,1)S(1)} %get-tuple-element.49.refs_1_.refs_2_.refs_6_, ...), custom_call_target="tpu_custom_call" | custom-call | flops 1000000000 | bytes 1000000000 | tf_op jit(solution)/shard_map/pallas_call | solution.py:53
  19.9 1.4 %collective-permute-done.5.received_ref = bf16[24,4224]{1,0:T(8,128)(2,1)S(1)} collective-permute-done((bf16[24,4224]{1,0:T(8,128)(2,1)S(1)}, bf16[24,4224]{1,0:T(8,128)(2,1)S(1)}, u32[]{:S(2)}, u32[]{:S(2)}) %collective-permute-start.5) | collective-permute-done | bytes 202784 | tf_op jit(solution)/shard_map/ppermute | solution.py:36
  21.4 1.6 %collective-permute-start.6 = (bf16[24,4224]{1,0:T(8,128)(2,1)S(1)}, bf16[24,4224]{1,0:T(8,128)(2,1)S(1)}, u32[]{:S(2)}, u32[]{:S(2)}) collective-permute-start(bf16[24,4224]{1,0:T(8,128)(2,1)S(1)} %get-tuple-element.57), channel_id=1, source_target_pairs={{0,16},{8,24},{16,0},{24,8},{1,17},{9,25},{17,1},{25,9},{2,18},{10... | collective-permute-start | bytes 608264 | tf_op jit(solution)/shard_map/ppermute | solution.py:36
  23.0 3.3 %collective-permute-done.8.received_ref = bf16[40,4224]{1,0:T(8,128)(2,1)S(1)} collective-permute-done((bf16[40,4224]{1,0:T(8,128)(2,1)S(1)}, bf16[40,4224]{1,0:T(8,128)(2,1)S(1)}, u32[]{:S(2)}, u32[]{:S(2)}) %collective-permute-start.8) | collective-permute-done | bytes 337952 | tf_op jit(solution)/shard_map/ppermute | solution.py:36
  26.3 0.2 shard_map.110.mine_ref.refs_6_
  26.6 3.3 %collective-permute-done.6.received_ref = bf16[24,4224]{1,0:T(8,128)(2,1)S(1)} collective-permute-done((bf16[24,4224]{1,0:T(8,128)(2,1)S(1)}, bf16[24,4224]{1,0:T(8,128)(2,1)S(1)}, u32[]{:S(2)}, u32[]{:S(2)}) %collective-permute-start.6) | collective-permute-done | bytes 202784 | tf_op jit(solution)/shard_map/ppermute | solution.py:36
  30.1 0.6 %shard_map.111.refs_0_ = bf16[80,512]{1,0:T(8,128)(2,1)S(1)} custom-call(bf16[40,4224]{1,0:T(8,128)(2,1)S(1)} %shard_map.110.mine_ref.refs_6_, bf16[40,4224]{1,0:T(8,128)(2,1)S(1)} %collective-permute-done.9.other_ref.refs_7_, bf16[1408,512]{1,0:T(8,128)(2,1)S(1)} %get-tuple-element.51.gate_ref, bf16[1408,512]{1,0:T(8,128)(2,1)S(1)} %get-tuple-element.64.up_ref), custom_call_target="tpu_custom_call" | custom-call | flops 1 | bytes 1 | tf_op jit(solution)/shard_map/pallas_call | solution.py:53
  30.7 0.8 %collective-permute-done.10.other_ref.refs_9_ = bf16[24,4224]{1,0:T(8,128)(2,1)S(1)} collective-permute-done((bf16[24,4224]{1,0:T(8,128)(2,1)S(1)}, bf16[24,4224]{1,0:T(8,128)(2,1)S(1)}, u32[]{:S(2)}, u32[]{:S(2)}) %collective-permute-start.10) | collective-permute-done | bytes 202784 | tf_op jit(solution)/shard_map/ppermute | solution.py:36
  31.5 1.3 %shard_map.112 = bf16[128,512]{1,0:T(8,128)(2,1)} custom-call(bf16[24,4224]{1,0:T(8,128)(2,1)S(1)} %shard_map.107.mine_ref.refs_8_, bf16[24,4224]{1,0:T(8,128)(2,1)S(1)} %collective-permute-done.10.other_ref.refs_9_, bf16[1408,512]{1,0:T(8,128)(2,1)S(1)} %get-tuple-element.51.gate_ref, bf16[1408,512]{1,0:T(8,128)(2,1)S(1)} %get-tuple-element.64.up_ref, ...), custom_call_target="tpu_custom_call" | custom-call | flops 1 | bytes 1 | tf_op jit(solution)/shard_map/pallas_call | solution.py:53
  32.8 4.9 %all-to-all-start = ((bf16[8,16,512]{2,1,0:T(8,128)(2,1)}), bf16[8,16,512]{2,1,0:T(8,128)(2,1)S(1)}, u32[]{:S(2)}, u32[]{:S(2)}) async-start(bf16[8,16,512]{2,1,0:T(8,128)(2,1)} %bitcast.5), calls=%async_computation | async-start | bytes 262144 | tf_op jit(solution)/shard_map/all_to_all | solution.py:391
  37.7 4.1 %shard_map.114 = (f32[512,1408]{1,0:T(8,128)}, f32[512,1408]{1,0:T(8,128)}, f32[1408,512]{1,0:T(8,128)}) custom-call(bf16[16,1024]{1,0:T(8,128)(2,1)S(1)} %get-tuple-element.58.refs_0_, bf16[16,1024]{1,0:T(8,128)(2,1)S(1)} %collective-permute-done.3.refs_1_, bf16[32,1024]{1,0:T(8,128)(2,1)S(1)} %collective-permute-done.refs_2_, ...), custom_call_target="tpu_custom_call" | custom-call | flops 10000000 | bytes 10000000 | tf_op jit(solution)/shard_map/pallas_call | solution.py:394
  41.8 3.2 %all-to-all-done = bf16[8,16,512]{2,1,0:T(8,128)(2,1)S(1)} async-done(((bf16[8,16,512]{2,1,0:T(8,128)(2,1)}), bf16[8,16,512]{2,1,0:T(8,128)(2,1)S(1)}, u32[]{:S(2)}, u32[]{:S(2)}) %all-to-all-start) | async-done | bytes 131104 | tf_op jit(solution)/shard_map/all_to_all | solution.py:391
  45.0 0.9 %shard_map.113 = bf16[128,512]{1,0:T(8,128)(2,1)} custom-call(bf16[128,128]{1,0:T(8,128)(2,1)S(1)} %get-tuple-element.36.marker_hbm.chosen_ref, bf16[128,512]{1,0:T(8,128)(2,1)S(1)} %bitcast.10), custom_call_target="tpu_custom_call" | custom-call | flops 1 | bytes 1 | tf_op jit(solution)/shard_map/pallas_call | solution.py:53
  (17 shorter events, 0.6 us)
Async XLA Ops:
  1.9 9.7 %collective-permute-start = (bf16[32,1024]{1,0:T(8,128)(2,1)S(1)}, bf16[32,1024]{1,0:T(8,128)(2,1)S(1)}, u32[]{:S(2)}, u32[]{:S(2)}) collective-permute-start(bf16[32,1024]{1,0:T(8,128)(2,1)S(1)} %get-tuple-element.37), channel_id=1, source_target_pairs={{0,6},{1,7},{2,4},{3,5},{4,2},{5,3},{6,0},{7,1},{8,14},{9,15},{10,... | collective-permute-start | bytes 196616 | tf_op jit(solution)/shard_map/ppermute | solution.py:36
  7.0 5.6 %collective-permute-start.1 = (bf16[32,1024]{1,0:T(8,128)(2,1)S(1)}, bf16[32,1024]{1,0:T(8,128)(2,1)S(1)}, u32[]{:S(2)}, u32[]{:S(2)}) collective-permute-start(bf16[32,1024]{1,0:T(8,128)(2,1)S(1)} %get-tuple-element.38), channel_id=1, source_target_pairs={{0,4},{1,5},{2,6},{3,7},{4,0},{5,1},{6,2},{7,3},{8,12},{9,13},{10,... | collective-permute-start | bytes 196616 | tf_op jit(solution)/shard_map/ppermute | solution.py:36
  7.0 5.6 %collective-permute-start.2 = (bf16[32,1024]{1,0:T(8,128)(2,1)S(1)}, bf16[32,1024]{1,0:T(8,128)(2,1)S(1)}, u32[]{:S(2)}, u32[]{:S(2)}) collective-permute-start(bf16[32,1024]{1,0:T(8,128)(2,1)S(1)} %get-tuple-element.39), channel_id=1, source_target_pairs={{0,2},{1,3},{2,0},{3,1},{4,6},{5,7},{6,4},{7,5},{8,10},{9,11},{10,... | collective-permute-start | bytes 196616 | tf_op jit(solution)/shard_map/ppermute | solution.py:36
  7.7 3.9 %collective-permute-start.3 = (bf16[16,1024]{1,0:T(8,128)(2,1)S(1)}, bf16[16,1024]{1,0:T(8,128)(2,1)S(1)}, u32[]{:S(2)}, u32[]{:S(2)}) collective-permute-start(bf16[16,1024]{1,0:T(8,128)(2,1)S(1)} %get-tuple-element.40), channel_id=1, source_target_pairs={{0,1},{1,0},{2,3},{3,2},{4,5},{5,4},{6,7},{7,6},{8,9},{9,8},{10,11... | collective-permute-start | bytes 98312 | tf_op jit(solution)/shard_map/ppermute | solution.py:36
  13.7 1.7 %collective-permute-start.7 = (bf16[40,4224]{1,0:T(8,128)(2,1)S(1)}, bf16[40,4224]{1,0:T(8,128)(2,1)S(1)}, u32[]{:S(2)}, u32[]{:S(2)}) collective-permute-start(bf16[40,4224]{1,0:T(8,128)(2,1)S(1)} %get-tuple-element.60), channel_id=1, source_target_pairs={{0,8},{8,0},{16,24},{24,16},{1,9},{9,1},{17,25},{25,17},{2,10},{10... | collective-permute-start | bytes 1013768 | tf_op jit(solution)/shard_map/ppermute | solution.py:36
  13.8 5.2 %collective-permute-start.4 = (bf16[48,1024]{1,0:T(8,128)(2,1)S(1)}, bf16[48,1024]{1,0:T(8,128)(2,1)S(1)}, u32[]{:S(2)}, u32[]{:S(2)}) collective-permute-start(bf16[48,1024]{1,0:T(8,128)(2,1)S(1)} %pad_maximum_fusion), channel_id=1, source_target_pairs={{0,1},{1,0},{2,3},{3,2},{4,5},{5,4},{6,7},{7,6},{8,9},{9,8},{10,11... | collective-permute-start | bytes 294920 | tf_op jit(solution)/shard_map/ppermute | solution.py:36
  15.5 10.8 %collective-permute-start.8 = (bf16[40,4224]{1,0:T(8,128)(2,1)S(1)}, bf16[40,4224]{1,0:T(8,128)(2,1)S(1)}, u32[]{:S(2)}, u32[]{:S(2)}) collective-permute-start(bf16[40,4224]{1,0:T(8,128)(2,1)S(1)} %get-tuple-element.62), channel_id=1, source_target_pairs={{0,16},{8,24},{16,0},{24,8},{1,17},{9,25},{17,1},{25,9},{2,18},{10... | collective-permute-start | bytes 1013768 | tf_op jit(solution)/shard_map/ppermute | solution.py:36
  19.9 1.5 %collective-permute-start.5 = (bf16[24,4224]{1,0:T(8,128)(2,1)S(1)}, bf16[24,4224]{1,0:T(8,128)(2,1)S(1)}, u32[]{:S(2)}, u32[]{:S(2)}) collective-permute-start(bf16[24,4224]{1,0:T(8,128)(2,1)S(1)} %get-tuple-element.55), channel_id=1, source_target_pairs={{0,8},{8,0},{16,24},{24,16},{1,9},{9,1},{17,25},{25,17},{2,10},{10... | collective-permute-start | bytes 608264 | tf_op jit(solution)/shard_map/ppermute | solution.py:36
  21.4 8.5 %collective-permute-start.6 = (bf16[24,4224]{1,0:T(8,128)(2,1)S(1)}, bf16[24,4224]{1,0:T(8,128)(2,1)S(1)}, u32[]{:S(2)}, u32[]{:S(2)}) collective-permute-start(bf16[24,4224]{1,0:T(8,128)(2,1)S(1)} %get-tuple-element.57), channel_id=1, source_target_pairs={{0,16},{8,24},{16,0},{24,8},{1,17},{9,25},{17,1},{25,9},{2,18},{10... | collective-permute-start | bytes 608264 | tf_op jit(solution)/shard_map/ppermute | solution.py:36
  26.5 3.5 %collective-permute-start.9 = (bf16[40,4224]{1,0:T(8,128)(2,1)S(1)}, bf16[40,4224]{1,0:T(8,128)(2,1)S(1)}, u32[]{:S(2)}, u32[]{:S(2)}) collective-permute-start(bf16[40,4224]{1,0:T(8,128)(2,1)S(1)} %shard_map.110.mine_ref.refs_6_), channel_id=1, source_target_pairs={{0,8},{8,0},{16,24},{24,16},{1,9},{9,1},{17,25},{25,17},{2,10},{10... | collective-permute-start | bytes 1013768 | tf_op jit(solution)/shard_map/ppermute | solution.py:36
  30.0 1.5 %collective-permute-start.10 = (bf16[24,4224]{1,0:T(8,128)(2,1)S(1)}, bf16[24,4224]{1,0:T(8,128)(2,1)S(1)}, u32[]{:S(2)}, u32[]{:S(2)}) collective-permute-start(bf16[24,4224]{1,0:T(8,128)(2,1)S(1)} %shard_map.107.mine_ref.refs_8_), channel_id=1, source_target_pairs={{0,8},{8,0},{16,24},{24,16},{1,9},{9,1},{17,25},{25,17},{2,10},{10... | collective-permute-start | bytes 608264 | tf_op jit(solution)/shard_map/ppermute | solution.py:36
  32.8 12.2 %all-to-all-start = ((bf16[8,16,512]{2,1,0:T(8,128)(2,1)}), bf16[8,16,512]{2,1,0:T(8,128)(2,1)S(1)}, u32[]{:S(2)}, u32[]{:S(2)}) async-start(bf16[8,16,512]{2,1,0:T(8,128)(2,1)} %bitcast.5), calls=%async_computation | async-start | bytes 262144 | tf_op jit(solution)/shard_map/all_to_all | solution.py:391

commit v6 on v5

--- a/solution.py
+++ b/solution.py
@@ -97,9 +97,9 @@
     )
     rank = jnp.sum(named * counts, axis=0, keepdims=True).astype(jnp.int32)
     slots = lax.broadcasted_iota(jnp.int32, (slot_count, pairs), 0)
-    chosen_ref[...] = (slots == ids * capacity + rank).astype(jnp.float32).astype(jnp.bfloat16)
     chosen = (slots == (ids ^ me) * capacity + rank).astype(jnp.float32)
     select = chosen.astype(jnp.bfloat16)
+    chosen_ref[...] = select
     for copy in copies[1:]:
         copy.wait()
     scale = jnp.sum(chosen * weights_ref[...], axis=1, keepdims=True)
@@ -176,53 +176,91 @@
     )
 
 
-def slot_grad_kernel(order, mine_ref, other_ref, gate_ref, up_ref, *refs):
-    *earlier_ref, out_ref = refs
+def slot_grad_rows(mine_ref, other_ref, gate_ref, up_ref):
     hidden_units = gate_ref.shape[0]
     rows = in_order(lax.axis_index("dp") % 2, mine_ref[...], other_ref[...])
     by_gate, by_up = rows[:, hidden_units:2 * hidden_units], rows[:, 2 * hidden_units:]
-    out = (
+    return (
         jnp.dot(by_gate, gate_ref[...], preferred_element_type=jnp.float32)
         + jnp.dot(by_up, up_ref[...], preferred_element_type=jnp.float32)
     ).astype(jnp.bfloat16)
-    if not earlier_ref:
-        out_ref[...] = out
-        return
-    me = lax.axis_index("expert")
-    block = out_ref.shape[0] // len(order)
-    rows = jnp.concatenate([earlier_ref[0][...], out], axis=0)
-    for place, k in enumerate(order):
-        start = pl.multiple_of((me ^ k) * block, block)
-        out_ref[pl.ds(start, block)] = rows[place * block:(place + 1) * block]
-
-
-def weight_grads_kernel(*refs):
-    *in_refs, gate_ref, up_ref, down_ref, rows_ref, deltas_ref = refs
+
+
+def near_grad_kernel(mine_ref, other_ref, gate_ref, up_ref, *block_refs):
+    out = slot_grad_rows(mine_ref, other_ref, gate_ref, up_ref)
+    block = block_refs[0].shape[0]
+    for place, ref in enumerate(block_refs):
+        ref[...] = out[place * block:(place + 1) * block]
+
+
+def far_grad_kernel(mine_ref, other_ref, gate_ref, up_ref, pair_ref, out_ref):
+    block = pair_ref.shape[0]
+    out_ref[:block] = pair_ref[...]
+    out_ref[block:] = slot_grad_rows(mine_ref, other_ref, gate_ref, up_ref)
+
+
+def weight_grads_kernel(names, tiles, *refs):
+    outs = len(names)
+    *in_refs, rows_ref, deltas_ref, sems = refs
+    in_refs, out_refs, tile_refs = in_refs[:-2 * outs], in_refs[-2 * outs:-outs], in_refs[-outs:]
     row_refs, delta_refs = in_refs[:-4], in_refs[-4:]
-    step = pl.program_id(0)
-    tile = gate_ref.shape[0]
-    down_tile = down_ref.shape[0]
     width = rows_ref.shape[1] // 2
-    hidden_units = gate_ref.shape[1]
-
-    @pl.when(step == 0)
-    def _():
-        core = lax.axis_index("dp") % 2
-        near = 2 * delta_refs[0].shape[0]
-        rows_ref[:near] = near_rows(*row_refs[:-1])
-        rows_ref[near:] = row_refs[-1][...]
-        deltas_ref[:near] = in_order(core, delta_refs[0][...], delta_refs[1][...])
-        deltas_ref[near:] = in_order(core, delta_refs[2][...], delta_refs[3][...])
-
-    feats = rows_ref[:, pl.ds(pl.multiple_of(step * tile, tile), tile)]
-    gate_ref[...] = contract_rows(feats, deltas_ref[:, hidden_units:2 * hidden_units])
-    up_ref[...] = contract_rows(feats, deltas_ref[:, 2 * hidden_units:])
-    hidden = deltas_ref[:, pl.ds(pl.multiple_of(step * down_tile, down_tile), down_tile)]
-    down_ref[...] = contract_rows(hidden, rows_ref[:, width:])
-
-
-def token_grad_kernel(chosen_ref, returned_ref, out_ref):
-    out_ref[...] = contract_rows(chosen_ref[...], returned_ref[...]).astype(jnp.bfloat16)
+    hidden_units = deltas_ref.shape[1] // 3
+    core = lax.axis_index("dp") % 2
+    near = 2 * delta_refs[0].shape[0]
+    rows_ref[:near] = near_rows(*row_refs[:-1])
+    rows_ref[near:] = row_refs[-1][...]
+    deltas_ref[:near] = in_order(core, delta_refs[0][...], delta_refs[1][...])
+    deltas_ref[near:] = in_order(core, delta_refs[2][...], delta_refs[3][...])
+
+    copies = []
+    for name, tile, out_ref, tile_ref in zip(names, tiles, out_refs, tile_refs):
+        for at in range(0, out_ref.shape[0], tile):
+            rows = min(tile, out_ref.shape[0] - at)
+            if name == "down":
+                out = contract_rows(deltas_ref[:, at:at + rows], rows_ref[:, width:])
+            else:
+                start = hidden_units * (1 if name == "gate" else 2)
+                out = contract_rows(
+                    rows_ref[:, at:at + rows], deltas_ref[:, start:start + hidden_units]
+                )
+            tile_ref[at:at + rows] = out
+            span = pl.ds(at, rows)
+            copies.append(
+                pltpu.make_async_copy(tile_ref.at[span], out_ref.at[span], sems.at[len(copies)])
+            )
+            copies[-1].start()
+    for copy in copies:
+        copy.wait()
+
+
+def weight_grads(names, width, hidden_units, slot_count, inputs):
+    sizes = {"gate": (width, hidden_units), "up": (width, hidden_units), "down": (hidden_units, width)}
+    outs = [shape(*sizes[name], jnp.float32) for name in names]
+    tiles = [384 if name == "down" else 128 for name in names]
+    copies = sum(-(-out.shape[0] // tile) for out, tile in zip(outs, tiles))
+    return pl.pallas_call(
+        functools.partial(weight_grads_kernel, names, tiles),
+        out_shape=outs,
+        in_specs=[pl.BlockSpec(memory_space=pltpu.VMEM)] * len(inputs),
+        out_specs=[pl.BlockSpec(memory_space=pltpu.HBM)] * len(outs),
+        scratch_shapes=[pltpu.VMEM(out.shape, out.dtype) for out in outs]
+        + [
+            pltpu.VMEM((slot_count, 2 * width), jnp.bfloat16),
+            pltpu.VMEM((slot_count, 3 * hidden_units), jnp.bfloat16),
+            pltpu.SemaphoreType.DMA((copies,)),
+        ],
+        compiler_params=pltpu.CompilerParams(vmem_limit_bytes=24 * 1024 * 1024),
+        cost_estimate=pl.CostEstimate(flops=10**7, bytes_accessed=10**7, transcendentals=0),
+    )(*inputs)
+
+
+def token_grad_kernel(chosen_ref, own_ref, from_pair_ref, *refs):
+    *group_refs, out_ref = refs
+    block = own_ref.shape[0]
+    rows = [own_ref[...], from_pair_ref[:block]] + [ref[...] for ref in reversed(group_refs)]
+    returned = jnp.concatenate(rows, axis=0)
+    out_ref[...] = contract_rows(chosen_ref[...], returned).astype(jnp.bfloat16)
 
 
 def body_by_all_to_all(tokens, cotangent, expert_ids, route_weights, gate_weight, up_weight, down_weight):
@@ -340,8 +378,6 @@
     groups = after(groups, from_pair)
     seconds = jnp.concatenate([group[capacity:] for group in groups], axis=0)
     by_pair = swap(after(seconds, weights[2]), 1, "expert")
-
-    order = [0] + [2 * j for j in far_first[1:]] + [1] + [2 * j + 1 for j in far_first[1:]]
 
     turned = call(
         turn_kernel,
@@ -379,40 +415,31 @@
             mine = after(mine, deltas[1])
         pair = [mine, swap(mine, 1)]
         deltas += pair
-        grads = [
-            call(
-                functools.partial(slot_grad_kernel, order),
-                shape(slot_count if grads else 2 * packed.shape[0], width),
-                *pair,
-                *turned[:2],
-                *grads,
+        block = shape(capacity, width)
+        if grads:
+            to_pair = call(
+                far_grad_kernel, shape(half * capacity, width), *pair, *turned[:2], grads[-1]
             )
-        ]
-    returned = lax.all_to_all(grads[0], "expert", split_axis=0, concat_axis=0, tiled=True)
-    steps = 4 if width % 512 == 0 else 1
-    down_tile = -(-hidden_units // (128 * steps)) * 128
-    gate_grad, up_grad, down_grad = pl.pallas_call(
-        weight_grads_kernel,
-        out_shape=(
-            shape(width, hidden_units, jnp.float32),
-            shape(width, hidden_units, jnp.float32),
-            shape(hidden_units, width, jnp.float32),
-        ),
-        grid=(steps,),
-        in_specs=[pl.BlockSpec(memory_space=pltpu.VMEM)] * (len(near) + 1 + 4),
-        out_specs=(
-            pl.BlockSpec((width // steps, hidden_units), lambda i: (i, 0)),
-            pl.BlockSpec((width // steps, hidden_units), lambda i: (i, 0)),
-            pl.BlockSpec((down_tile, width), lambda i: (i, 0)),
-        ),
-        scratch_shapes=[
-            pltpu.VMEM((slot_count, 2 * width), jnp.bfloat16),
-            pltpu.VMEM((slot_count, 3 * hidden_units), jnp.bfloat16),
-        ],
-        compiler_params=pltpu.CompilerParams(vmem_limit_bytes=24 * 1024 * 1024),
-        cost_estimate=pl.CostEstimate(flops=10**7, bytes_accessed=10**7, transcendentals=0),
-    )(*near, far, *deltas)
-    token_grad = call(token_grad_kernel, shape(tok_rows, width), chosen, returned)
+        else:
+            grads = call(near_grad_kernel, (block,) * (half + 1), *pair, *turned[:2])
+
+    returned_pair = swap(to_pair, 1, "expert")
+    sizes = (width, hidden_units, slot_count, (*near, far, *deltas))
+    (gate_grad,) = weight_grads(("gate",), *sizes)
+    returned_pair = after(returned_pair, gate_grad)
+    returned = {}
+    for place, j in enumerate(far_first[1:], 1):
+        more = returned_pair[place * capacity:(place + 1) * capacity]
+        returned[j] = swap(jnp.concatenate([grads[place], more], axis=0), 2 * j, "expert")
+    up_grad, down_grad = weight_grads(("up", "down"), *sizes)
+    token_grad = call(
+        token_grad_kernel,
+        shape(tok_rows, width),
+        chosen,
+        grads[0],
+        returned_pair,
+        *[returned[j] for j in far_first[1:]],
+    )
     return (token_grad, gate_grad[None], up_grad[None], down_grad[None])
 
 

time: 46.2 us -> 45.1 us (0.976)
  waiting for transfers between devices: 14 us -> 11.9 us
  starting transfers between devices: 17.3 us -> 18.4 us
    ppermute x11 -> x15, starting transfers between devices: 12.4 us -> 18.4 us  [swap(): return lax.ppermute(value, axis, [(i, i ^ bit) for i in range(size)])]
    all_to_all x1 -> x0, starting transfers between devices: 4.88 us -> none  [body_by_pairs(): lax.all_to_all(grads[0], 'expert', split_axis=0, concat_axis=0, tiled=True)]
    all_to_all x1 -> x0, waiting for transfers between devices: 3.24 us -> none  [body_by_pairs(): lax.all_to_all(grads[0], 'expert', split_axis=0, concat_axis=0, tiled=True)]
    ppermute x11 -> x15, waiting for transfers between devices: 10.7 us -> 11.9 us  [swap(): return lax.ppermute(value, axis, [(i, i ^ bit) for i in range(size)])]
    pallas_call x12, Pallas kernels: 9.75 us -> 9.04 us  [call(): pl.pallas_call(kernel, out_shape=outs, in_specs=[pl.BlockSpec(memory_spac...]
    pallas_call x1 -> x2, Pallas kernels: 4.1 us -> 4.79 us  [weight_grads(): pl.pallas_call(functools.partial(weight_grads_kernel, names, tiles), out_...]
  transfers between devices with their start and end apart: 12 -> 15, of which waited for: 7 -> 8; matrix products, arithmetic and copies ran while one was open for 0% -> 0% of each run, Pallas kernels for 21% -> 22%
where the time goes in v6:
time: 45.1 us; the launch traced here: 45 us
  starting transfers between devices  18.4 us (41%)
  Pallas kernels  13.8 us (31%)
  waiting for transfers between devices  11.9 us (26%)
  between operations  0.83 us (2%)
    ppermute x15, starting transfers between devices, swap(): return lax.ppermute(value, axis, [(i, i ^ bit) for i in range(size)])  18.4 us
    ppermute x15, waiting for transfers between devices, swap(): return lax.ppermute(value, axis, [(i, i ^ bit) for i in range(size)])  11.9 us
    pallas_call x12, Pallas kernels, call(): pl.pallas_call(kernel, out_shape=outs, in_specs=[pl.BlockSpec(memory_spac...  9.04 us
    pallas_call x2, Pallas kernels, weight_grads(): pl.pallas_call(functools.partial(weight_grads_kernel, names, tiles), out_...  4.79 us
  transfers between devices with their start and end apart: 15, of which 8 were waited for; matrix products, arithmetic and copies ran while one was open for 0% of the time, Pallas kernels for 22%

profile of v6, /device:TPU:0, one launch (start us, length us, event | category | flops | bytes accessed | tf_op | source)
XLA Modules:
  0.0 45.0 jit_solution(13778412708762982849)
XLA Ops:
  0.6 1.3 %shard_map.102 = (bf16[128,128]{1,0:T(8,128)(2,1)S(1)}, bf16[16,1024]{1,0:T(8,128)(2,1)S(1)}, bf16[16,1024]{1,0:T(8,128)(2,1)S(1)}, bf16[32,1024]{1,0:T(8,128)(2...) custom-call(s32[1,128]{1,0:T(1,128)} %bitcast.12, f32[1,128]{1,0:T(1,128)} %bitcast.13, ...), custom_call_target="tpu_custom_call" | custom-call | flops 1 | bytes 1 | tf_op jit(solution)/shard_map/pallas_call | solution.py:53
  1.9 5.1 %collective-permute-start.1 = (bf16[32,1024]{1,0:T(8,128)(2,1)S(1)}, bf16[32,1024]{1,0:T(8,128)(2,1)S(1)}, u32[]{:S(2)}, u32[]{:S(2)}) collective-permute-start(bf16[32,1024]{1,0:T(8,128)(2,1)S(1)} %get-tuple-element.44), channel_id=1, source_target_pairs={{0,6},{1,7},{2,4},{3,5},{4,2},{5,3},{6,0},{7,1},{8,14},{9,15},{10,... | collective-permute-start | bytes 196616 | tf_op jit(solution)/shard_map/ppermute | solution.py:36
  7.0 0.6 %collective-permute-start.3 = (bf16[32,1024]{1,0:T(8,128)(2,1)S(1)}, bf16[32,1024]{1,0:T(8,128)(2,1)S(1)}, u32[]{:S(2)}, u32[]{:S(2)}) collective-permute-start(bf16[32,1024]{1,0:T(8,128)(2,1)S(1)} %get-tuple-element.46), channel_id=1, source_target_pairs={{0,2},{1,3},{2,0},{3,1},{4,6},{5,7},{6,4},{7,5},{8,10},{9,11},{10,... | collective-permute-start | bytes 196616 | tf_op jit(solution)/shard_map/ppermute | solution.py:36
  7.7 1.7 %collective-permute-start = (bf16[16,1024]{1,0:T(8,128)(2,1)S(1)}, bf16[16,1024]{1,0:T(8,128)(2,1)S(1)}, u32[]{:S(2)}, u32[]{:S(2)}) collective-permute-start(bf16[16,1024]{1,0:T(8,128)(2,1)S(1)} %get-tuple-element.43), channel_id=1, source_target_pairs={{0,1},{1,0},{2,3},{3,2},{4,5},{5,4},{6,7},{7,6},{8,9},{9,8},{10,11... | collective-permute-start | bytes 98312 | tf_op jit(solution)/shard_map/ppermute | solution.py:36
  9.3 2.3 %shard_map.103 = (bf16[512,1408]{1,0:T(8,128)(2,1)S(1)}, bf16[512,1408]{1,0:T(8,128)(2,1)S(1)}, bf16[1408,512]{1,0:T(8,128)(2,1)S(1)}) custom-call(bf16[512,1408]{1,0:T(8,128)(2,1)} %bitcast.9, bf16[512,1408]{1,0:T(8,128)(2,1)} %bitcast.10, bf16[1408,512]{1,0:T(8,128)(2,1)} %bitcast.11, bf16[128,128]{1,0:T(8,128)(2,1)S(1)} %get-tuple-element.41.marker_hbm.chosen_ref), custom_call_target="tpu_custom_call" | custom-call | flops 10000000 | bytes 10000000 | tf_op jit(solution)/shard_map/pallas_call | solution.py:53
  11.6 1.0 %collective-permute-done.2.refs_3_ = bf16[32,1024]{1,0:T(8,128)(2,1)S(1)} collective-permute-done((bf16[32,1024]{1,0:T(8,128)(2,1)S(1)}, bf16[32,1024]{1,0:T(8,128)(2,1)S(1)}, u32[]{:S(2)}, u32[]{:S(2)}) %collective-permute-start.2) | collective-permute-done | bytes 65568 | tf_op jit(solution)/shard_map/ppermute | solution.py:36
  12.6 1.0 %shard_map.104 = (f32[40,4224]{1,0:T(8,128)S(1)}, bf16[40,4224]{1,0:T(8,128)(2,1)S(1)}) custom-call(bf16[16,1024]{1,0:T(8,128)(2,1)S(1)} %get-tuple-element.42.refs_0_, bf16[16,1024]{1,0:T(8,128)(2,1)S(1)} %collective-permute-done.refs_1_, bf16[32,1024]{1,0:T(8,128)(2,1)S(1)} %collective-permute-done.1.refs_2_, ...), custom_call_target="tpu_custom_call" | custom-call | flops 1 | bytes 1 | tf_op jit(solution)/shard_map/pallas_call | solution.py:53
  13.8 1.6 %collective-permute-start.7 = (bf16[48,1024]{1,0:T(8,128)(2,1)S(1)}, bf16[48,1024]{1,0:T(8,128)(2,1)S(1)}, u32[]{:S(2)}, u32[]{:S(2)}) collective-permute-start(bf16[48,1024]{1,0:T(8,128)(2,1)S(1)} %pad_maximum_fusion), channel_id=1, source_target_pairs={{0,1},{1,0},{2,3},{3,2},{4,5},{5,4},{6,7},{7,6},{8,9},{9,8},{10,11... | collective-permute-start | bytes 294920 | tf_op jit(solution)/shard_map/ppermute | solution.py:36
  15.5 1.6 %collective-permute-start.5 = (bf16[40,4224]{1,0:T(8,128)(2,1)S(1)}, bf16[40,4224]{1,0:T(8,128)(2,1)S(1)}, u32[]{:S(2)}, u32[]{:S(2)}) collective-permute-start(bf16[40,4224]{1,0:T(8,128)(2,1)S(1)} %get-tuple-element.56), channel_id=1, source_target_pairs={{0,16},{8,24},{16,0},{24,8},{1,17},{9,25},{17,1},{25,9},{2,18},{10... | collective-permute-start | bytes 1013768 | tf_op jit(solution)/shard_map/ppermute | solution.py:36
  17.0 1.2 %shard_map.107 = (bf16[1408,512]{1,0:T(8,128)(2,1)S(1)}, bf16[1408,512]{1,0:T(8,128)(2,1)S(1)}, bf16[512,1408]{1,0:T(8,128)(2,1)S(1)}) custom-call(bf16[512,1408]{1,0:T(8,128)(2,1)S(1)} %get-tuple-element.57.refs_5_.refs_0_.refs_1_, bf16[512,1408]{1,0:T(8,128)(2,1)S(1)} %get-tuple-element.58.refs_6_.refs_1_.refs_2_, ...), custom_call_target="tpu_custom_call" | custom-call | flops 1 | bytes 1 | tf_op jit(solution)/shard_map/pallas_call | solution.py:53
  18.2 0.8 %collective-permute-done.7.refs_0_.refs_5_ = bf16[48,1024]{1,0:T(8,128)(2,1)S(1)} collective-permute-done((bf16[48,1024]{1,0:T(8,128)(2,1)S(1)}, bf16[48,1024]{1,0:T(8,128)(2,1)S(1)}, u32[]{:S(2)}, u32[]{:S(2)}) %collective-permute-start.7) | collective-permute-done | bytes 98336 | tf_op jit(solution)/shard_map/ppermute | solution.py:36
  19.0 0.8 %shard_map.109 = (f32[24,4224]{1,0:T(8,128)S(1)}, bf16[24,4224]{1,0:T(8,128)(2,1)S(1)}) custom-call(bf16[48,1024]{1,0:T(8,128)(2,1)S(1)} %collective-permute-done.7.refs_0_.refs_5_, bf16[512,1408]{1,0:T(8,128)(2,1)S(1)} %get-tuple-element.57.refs_5_.refs_0_.refs_1_, bf16[512,1408]{1,0:T(8,128)(2,1)S(1)} %get-tuple-element.58.refs_6_.refs_1_.refs_2_, ...), custom_call_target="tpu_custom_call" | custom-call | flops 1000000000 | bytes 1000000000 | tf_op jit(solution)/shard_map/pallas_call | solution.py:53
  19.9 1.4 %collective-permute-done.8.received_ref = bf16[24,4224]{1,0:T(8,128)(2,1)S(1)} collective-permute-done((bf16[24,4224]{1,0:T(8,128)(2,1)S(1)}, bf16[24,4224]{1,0:T(8,128)(2,1)S(1)}, u32[]{:S(2)}, u32[]{:S(2)}) %collective-permute-start.8) | collective-permute-done | bytes 202784 | tf_op jit(solution)/shard_map/ppermute | solution.py:36
  21.4 1.6 %collective-permute-start.9 = (bf16[24,4224]{1,0:T(8,128)(2,1)S(1)}, bf16[24,4224]{1,0:T(8,128)(2,1)S(1)}, u32[]{:S(2)}, u32[]{:S(2)}) collective-permute-start(bf16[24,4224]{1,0:T(8,128)(2,1)S(1)} %get-tuple-element.69), channel_id=1, source_target_pairs={{0,16},{8,24},{16,0},{24,8},{1,17},{9,25},{17,1},{25,9},{2,18},{10... | collective-permute-start | bytes 608264 | tf_op jit(solution)/shard_map/ppermute | solution.py:36
  23.0 3.3 %collective-permute-done.5.received_ref = bf16[40,4224]{1,0:T(8,128)(2,1)S(1)} collective-permute-done((bf16[40,4224]{1,0:T(8,128)(2,1)S(1)}, bf16[40,4224]{1,0:T(8,128)(2,1)S(1)}, u32[]{:S(2)}, u32[]{:S(2)}) %collective-permute-start.5) | collective-permute-done | bytes 337952 | tf_op jit(solution)/shard_map/ppermute | solution.py:36
  26.6 3.3 %collective-permute-done.9.received_ref = bf16[24,4224]{1,0:T(8,128)(2,1)S(1)} collective-permute-done((bf16[24,4224]{1,0:T(8,128)(2,1)S(1)}, bf16[24,4224]{1,0:T(8,128)(2,1)S(1)}, u32[]{:S(2)}, u32[]{:S(2)}) %collective-permute-start.9) | collective-permute-done | bytes 202784 | tf_op jit(solution)/shard_map/ppermute | solution.py:36
  30.7 0.8 %collective-permute-done.10.other_ref.refs_9_ = bf16[24,4224]{1,0:T(8,128)(2,1)S(1)} collective-permute-done((bf16[24,4224]{1,0:T(8,128)(2,1)S(1)}, bf16[24,4224]{1,0:T(8,128)(2,1)S(1)}, u32[]{:S(2)}, u32[]{:S(2)}) %collective-permute-start.10) | collective-permute-done | bytes 202784 | tf_op jit(solution)/shard_map/ppermute | solution.py:36
  32.2 1.5 %collective-permute-start.11 = (bf16[64,512]{1,0:T(8,128)(2,1)S(1)}, bf16[64,512]{1,0:T(8,128)(2,1)S(1)}, u32[]{:S(2)}, u32[]{:S(2)}) collective-permute-start(bf16[64,512]{1,0:T(8,128)(2,1)S(1)} %shard_map.112), channel_id=1, source_target_pairs={{0,1},{1,0},{2,3},{3,2},{4,5},{5,4},{6,7},{7,6},{8,9},{9,8},{10,11... | collective-permute-start | bytes 196616 | tf_op jit(solution)/shard_map/ppermute | solution.py:36
  33.7 1.9 %shard_map.113 = f32[512,1408]{1,0:T(8,128)} custom-call(bf16[16,1024]{1,0:T(8,128)(2,1)S(1)} %get-tuple-element.42.refs_0_, bf16[16,1024]{1,0:T(8,128)(2,1)S(1)} %collective-permute-done.refs_1_, bf16[32,1024]{1,0:T(8,128)(2,1)S(1)} %collective-permute-done.1.refs_2_, bf16[32,1024]{1,0:T(8,128)(2,1)S(1)} %collective-permute-done.2.refs_3_, ...), custom_call_target="tpu_custom_call" | custom-call | flops 10000000 | bytes 10000000 | tf_op jit(solution)/shard_map/pallas_call | solution.py:242
  35.6 0.9 %collective-permute-done.11.from_pair_ref = bf16[64,512]{1,0:T(8,128)(2,1)S(1)} collective-permute-done((bf16[64,512]{1,0:T(8,128)(2,1)S(1)}, bf16[64,512]{1,0:T(8,128)(2,1)S(1)}, u32[]{:S(2)}, u32[]{:S(2)}) %collective-permute-start.11) | collective-permute-done | bytes 65568 | tf_op jit(solution)/shard_map/ppermute | solution.py:36
  36.5 2.8 %collective-permute-start.12 = (bf16[32,512]{1,0:T(8,128)(2,1)S(1)}, bf16[32,512]{1,0:T(8,128)(2,1)S(1)}, u32[]{:S(2)}, u32[]{:S(2)}) collective-permute-start(bf16[32,512]{1,0:T(8,128)(2,1)S(1)} %pad_maximum_fusion.1), channel_id=1, source_target_pairs={{0,6},{1,7},{2,4},{3,5},{4,2},{5,3},{6,0},{7,1},{8,14},{9,15},{10,... | collective-permute-start | bytes 98312 | tf_op jit(solution)/shard_map/ppermute | solution.py:36
  39.3 1.7 %collective-permute-start.14 = (bf16[32,512]{1,0:T(8,128)(2,1)S(1)}, bf16[32,512]{1,0:T(8,128)(2,1)S(1)}, u32[]{:S(2)}, u32[]{:S(2)}) collective-permute-start(bf16[32,512]{1,0:T(8,128)(2,1)S(1)} %pad_maximum_fusion.3), channel_id=1, source_target_pairs={{0,2},{1,3},{2,0},{3,1},{4,6},{5,7},{6,4},{7,5},{8,10},{9,11},{10,... | collective-permute-start | bytes 98312 | tf_op jit(solution)/shard_map/ppermute | solution.py:36
  41.0 2.9 %shard_map.115 = (f32[512,1408]{1,0:T(8,128)}, f32[1408,512]{1,0:T(8,128)}) custom-call(bf16[16,1024]{1,0:T(8,128)(2,1)S(1)} %get-tuple-element.42.refs_0_, bf16[16,1024]{1,0:T(8,128)(2,1)S(1)} %collective-permute-done.refs_1_, bf16[32,1024]{1,0:T(8,128)(2,1)S(1)} %collective-permute-done.1.refs_2_, bf16[32,1024]{1,0:T(8,128)(2,1)S(1)} %collective-permute-done.2.refs_3_, ...), custom_call_target="tpu_custom_call" | custom-call | flops 10000000 | bytes 10000000 | tf_op jit(solution)/shard_map/pallas_call | solution.py:242
  44.1 0.9 %shard_map.114 = bf16[128,512]{1,0:T(8,128)(2,1)} custom-call(bf16[128,128]{1,0:T(8,128)(2,1)S(1)} %get-tuple-element.41.marker_hbm.chosen_ref, bf16[16,512]{1,0:T(8,128)(2,1)S(1)} %get-tuple-element.62.own_ref, bf16[64,512]{1,0:T(8,128)(2,1)S(1)} %collective-permute-done.11.from_pair_ref, bf16[32,512]{1,0:T(8,128)(2,1)S(1)} %collective-permute-done.12.refs_0_, ...), custom_call_target="tpu_custom_call" | custom-call | flops 1 | bytes 1 | tf_op jit(solution)/shard_map/pallas_call | solution.py:53
  (28 shorter events, 2.2 us)
Async XLA Ops:
  1.9 9.7 %collective-permute-start.1 = (bf16[32,1024]{1,0:T(8,128)(2,1)S(1)}, bf16[32,1024]{1,0:T(8,128)(2,1)S(1)}, u32[]{:S(2)}, u32[]{:S(2)}) collective-permute-start(bf16[32,1024]{1,0:T(8,128)(2,1)S(1)} %get-tuple-element.44), channel_id=1, source_target_pairs={{0,6},{1,7},{2,4},{3,5},{4,2},{5,3},{6,0},{7,1},{8,14},{9,15},{10,... | collective-permute-start | bytes 196616 | tf_op jit(solution)/shard_map/ppermute | solution.py:36
  7.0 5.6 %collective-permute-start.2 = (bf16[32,1024]{1,0:T(8,128)(2,1)S(1)}, bf16[32,1024]{1,0:T(8,128)(2,1)S(1)}, u32[]{:S(2)}, u32[]{:S(2)}) collective-permute-start(bf16[32,1024]{1,0:T(8,128)(2,1)S(1)} %get-tuple-element.45), channel_id=1, source_target_pairs={{0,4},{1,5},{2,6},{3,7},{4,0},{5,1},{6,2},{7,3},{8,12},{9,13},{10,... | collective-permute-start | bytes 196616 | tf_op jit(solution)/shard_map/ppermute | solution.py:36
  7.0 5.6 %collective-permute-start.3 = (bf16[32,1024]{1,0:T(8,128)(2,1)S(1)}, bf16[32,1024]{1,0:T(8,128)(2,1)S(1)}, u32[]{:S(2)}, u32[]{:S(2)}) collective-permute-start(bf16[32,1024]{1,0:T(8,128)(2,1)S(1)} %get-tuple-element.46), channel_id=1, source_target_pairs={{0,2},{1,3},{2,0},{3,1},{4,6},{5,7},{6,4},{7,5},{8,10},{9,11},{10,... | collective-permute-start | bytes 196616 | tf_op jit(solution)/shard_map/ppermute | solution.py:36
  7.7 3.9 %collective-permute-start = (bf16[16,1024]{1,0:T(8,128)(2,1)S(1)}, bf16[16,1024]{1,0:T(8,128)(2,1)S(1)}, u32[]{:S(2)}, u32[]{:S(2)}) collective-permute-start(bf16[16,1024]{1,0:T(8,128)(2,1)S(1)} %get-tuple-element.43), channel_id=1, source_target_pairs={{0,1},{1,0},{2,3},{3,2},{4,5},{5,4},{6,7},{7,6},{8,9},{9,8},{10,11... | collective-permute-start | bytes 98312 | tf_op jit(solution)/shard_map/ppermute | solution.py:36
  13.6 1.7 %collective-permute-start.4 = (bf16[40,4224]{1,0:T(8,128)(2,1)S(1)}, bf16[40,4224]{1,0:T(8,128)(2,1)S(1)}, u32[]{:S(2)}, u32[]{:S(2)}) collective-permute-start(bf16[40,4224]{1,0:T(8,128)(2,1)S(1)} %get-tuple-element.54), channel_id=1, source_target_pairs={{0,8},{8,0},{16,24},{24,16},{1,9},{9,1},{17,25},{25,17},{2,10},{10... | collective-permute-start | bytes 1013768 | tf_op jit(solution)/shard_map/ppermute | solution.py:36
  13.8 5.2 %collective-permute-start.7 = (bf16[48,1024]{1,0:T(8,128)(2,1)S(1)}, bf16[48,1024]{1,0:T(8,128)(2,1)S(1)}, u32[]{:S(2)}, u32[]{:S(2)}) collective-permute-start(bf16[48,1024]{1,0:T(8,128)(2,1)S(1)} %pad_maximum_fusion), channel_id=1, source_target_pairs={{0,1},{1,0},{2,3},{3,2},{4,5},{5,4},{6,7},{7,6},{8,9},{9,8},{10,11... | collective-permute-start | bytes 294920 | tf_op jit(solution)/shard_map/ppermute | solution.py:36
  15.5 10.8 %collective-permute-start.5 = (bf16[40,4224]{1,0:T(8,128)(2,1)S(1)}, bf16[40,4224]{1,0:T(8,128)(2,1)S(1)}, u32[]{:S(2)}, u32[]{:S(2)}) collective-permute-start(bf16[40,4224]{1,0:T(8,128)(2,1)S(1)} %get-tuple-element.56), channel_id=1, source_target_pairs={{0,16},{8,24},{16,0},{24,8},{1,17},{9,25},{17,1},{25,9},{2,18},{10... | collective-permute-start | bytes 1013768 | tf_op jit(solution)/shard_map/ppermute | solution.py:36
  19.8 1.5 %collective-permute-start.8 = (bf16[24,4224]{1,0:T(8,128)(2,1)S(1)}, bf16[24,4224]{1,0:T(8,128)(2,1)S(1)}, u32[]{:S(2)}, u32[]{:S(2)}) collective-permute-start(bf16[24,4224]{1,0:T(8,128)(2,1)S(1)} %get-tuple-element.67), channel_id=1, source_target_pairs={{0,8},{8,0},{16,24},{24,16},{1,9},{9,1},{17,25},{25,17},{2,10},{10... | collective-permute-start | bytes 608264 | tf_op jit(solution)/shard_map/ppermute | solution.py:36
  21.4 8.5 %collective-permute-start.9 = (bf16[24,4224]{1,0:T(8,128)(2,1)S(1)}, bf16[24,4224]{1,0:T(8,128)(2,1)S(1)}, u32[]{:S(2)}, u32[]{:S(2)}) collective-permute-start(bf16[24,4224]{1,0:T(8,128)(2,1)S(1)} %get-tuple-element.69), channel_id=1, source_target_pairs={{0,16},{8,24},{16,0},{24,8},{1,17},{9,25},{17,1},{25,9},{2,18},{10... | collective-permute-start | bytes 608264 | tf_op jit(solution)/shard_map/ppermute | solution.py:36
  26.5 3.5 %collective-permute-start.6 = (bf16[40,4224]{1,0:T(8,128)(2,1)S(1)}, bf16[40,4224]{1,0:T(8,128)(2,1)S(1)}, u32[]{:S(2)}, u32[]{:S(2)}) collective-permute-start(bf16[40,4224]{1,0:T(8,128)(2,1)S(1)} %shard_map.106.mine_ref.refs_6_), channel_id=1, source_target_pairs={{0,8},{8,0},{16,24},{24,16},{1,9},{9,1},{17,25},{25,17},{2,10},{10... | collective-permute-start | bytes 1013768 | tf_op jit(solution)/shard_map/ppermute | solution.py:36
  30.0 1.5 %collective-permute-start.10 = (bf16[24,4224]{1,0:T(8,128)(2,1)S(1)}, bf16[24,4224]{1,0:T(8,128)(2,1)S(1)}, u32[]{:S(2)}, u32[]{:S(2)}) collective-permute-start(bf16[24,4224]{1,0:T(8,128)(2,1)S(1)} %shard_map.111.mine_ref.refs_8_), channel_id=1, source_target_pairs={{0,8},{8,0},{16,24},{24,16},{1,9},{9,1},{17,25},{25,17},{2,10},{10... | collective-permute-start | bytes 608264 | tf_op jit(solution)/shard_map/ppermute | solution.py:36
  32.2 4.3 %collective-permute-start.11 = (bf16[64,512]{1,0:T(8,128)(2,1)S(1)}, bf16[64,512]{1,0:T(8,128)(2,1)S(1)}, u32[]{:S(2)}, u32[]{:S(2)}) collective-permute-start(bf16[64,512]{1,0:T(8,128)(2,1)S(1)} %shard_map.112), channel_id=1, source_target_pairs={{0,1},{1,0},{2,3},{3,2},{4,5},{5,4},{6,7},{7,6},{8,9},{9,8},{10,11... | collective-permute-start | bytes 196616 | tf_op jit(solution)/shard_map/ppermute | solution.py:36
  36.5 7.3 %collective-permute-start.12 = (bf16[32,512]{1,0:T(8,128)(2,1)S(1)}, bf16[32,512]{1,0:T(8,128)(2,1)S(1)}, u32[]{:S(2)}, u32[]{:S(2)}) collective-permute-start(bf16[32,512]{1,0:T(8,128)(2,1)S(1)} %pad_maximum_fusion.1), channel_id=1, source_target_pairs={{0,6},{1,7},{2,4},{3,5},{4,2},{5,3},{6,0},{7,1},{8,14},{9,15},{10,... | collective-permute-start | bytes 98312 | tf_op jit(solution)/shard_map/ppermute | solution.py:36
  39.3 4.8 %collective-permute-start.13 = (bf16[32,512]{1,0:T(8,128)(2,1)S(1)}, bf16[32,512]{1,0:T(8,128)(2,1)S(1)}, u32[]{:S(2)}, u32[]{:S(2)}) collective-permute-start(bf16[32,512]{1,0:T(8,128)(2,1)S(1)} %pad_maximum_fusion.2), channel_id=1, source_target_pairs={{0,4},{1,5},{2,6},{3,7},{4,0},{5,1},{6,2},{7,3},{8,12},{9,13},{10,... | collective-permute-start | bytes 98312 | tf_op jit(solution)/shard_map/ppermute | solution.py:36
  39.3 4.8 %collective-permute-start.14 = (bf16[32,512]{1,0:T(8,128)(2,1)S(1)}, bf16[32,512]{1,0:T(8,128)(2,1)S(1)}, u32[]{:S(2)}, u32[]{:S(2)}) collective-permute-start(bf16[32,512]{1,0:T(8,128)(2,1)S(1)} %pad_maximum_fusion.3), channel_id=1, source_target_pairs={{0,2},{1,3},{2,0},{3,1},{4,6},{5,7},{6,4},{7,5},{8,10},{9,11},{10,... | collective-permute-start | bytes 98312 | tf_op jit(solution)/shard_map/ppermute | solution.py:36

commit v7 on v6

--- a/solution.py
+++ b/solution.py
@@ -36,8 +36,9 @@
     return lax.ppermute(value, axis, [(i, i ^ bit) for i in range(size)])
 
 
-FAR_PRODUCTS_COST = 10**9
-FAR_DELTAS_COST = 16 * 10**8
+FAR_PRODUCTS_COST = 3 * 10**8
+FAR_DELTAS_COST = 8 * 10**8
+OWN_DELTAS_COST = 3 * 10**9
 
 
 def after(values, marker):
@@ -131,14 +132,21 @@
         target[...] = source[...].T
 
 
-def near_rows(own_ref, from_pair_ref, *group_refs):
+def near_rows(from_pair_ref, *group_refs):
     halves = [ref[:ref.shape[0] // 2] for ref in group_refs]
-    return jnp.concatenate([own_ref[...]] + halves + [from_pair_ref[...]], axis=0)
+    return jnp.concatenate(halves + [from_pair_ref[...]], axis=0)
+
+
+def with_own_rows(own, rows):
+    part, half = own.shape[0] // 2, rows.shape[0] // 2
+    return jnp.concatenate([own[:part], rows[:half], own[part:], rows[half:]], axis=0)
 
 
 def products_kernel(turned, *refs):
     *row_refs, gate_ref, up_ref, down_ref, mine_ref, other_ref = refs
-    rows = near_rows(*row_refs) if len(row_refs) > 1 else row_refs[0][...]
+    rows = row_refs[-1][...]
+    if len(row_refs) > 1:
+        rows = with_own_rows(rows, near_rows(*row_refs[:-1]))
     half = rows.shape[0] // 2
     width = rows.shape[1] // 2
     hidden_units = gate_ref.shape[1]
@@ -156,10 +164,14 @@
         other_ref[:, cols] = jnp.where(core == 0, high, low).astype(jnp.bfloat16)
 
 
-def sums_kernel(mine_ref, received_ref, sums_ref, packed_ref):
+def sums_kernel(mine_ref, received_ref, *refs):
     sums = mine_ref[...] + received_ref[...].astype(jnp.float32)
-    sums_ref[...] = sums
-    packed_ref[...] = sums.astype(jnp.bfloat16)
+    at = 0
+    for sums_ref, packed_ref in zip(refs[::2], refs[1::2]):
+        part = sums[at:at + sums_ref.shape[0]]
+        sums_ref[...] = part
+        packed_ref[...] = part.astype(jnp.bfloat16)
+        at += part.shape[0]
 
 
 def deltas_kernel(sums_ref, received_ref, out_ref):
@@ -186,7 +198,7 @@
     ).astype(jnp.bfloat16)
 
 
-def near_grad_kernel(mine_ref, other_ref, gate_ref, up_ref, *block_refs):
+def slot_grad_kernel(mine_ref, other_ref, gate_ref, up_ref, *block_refs):
     out = slot_grad_rows(mine_ref, other_ref, gate_ref, up_ref)
     block = block_refs[0].shape[0]
     for place, ref in enumerate(block_refs):
@@ -203,15 +215,17 @@
     outs = len(names)
     *in_refs, rows_ref, deltas_ref, sems = refs
     in_refs, out_refs, tile_refs = in_refs[:-2 * outs], in_refs[-2 * outs:-outs], in_refs[-outs:]
-    row_refs, delta_refs = in_refs[:-4], in_refs[-4:]
+    row_refs, delta_refs = in_refs[:-6], in_refs[-6:]
     width = rows_ref.shape[1] // 2
     hidden_units = deltas_ref.shape[1] // 3
     core = lax.axis_index("dp") % 2
-    near = 2 * delta_refs[0].shape[0]
-    rows_ref[:near] = near_rows(*row_refs[:-1])
-    rows_ref[near:] = row_refs[-1][...]
-    deltas_ref[:near] = in_order(core, delta_refs[0][...], delta_refs[1][...])
-    deltas_ref[near:] = in_order(core, delta_refs[2][...], delta_refs[3][...])
+    at = 0
+    for place, rows in enumerate((near_rows(*row_refs[:-2]), row_refs[-2][...], row_refs[-1][...])):
+        span = slice(at, at + rows.shape[0])
+        rows_ref[span] = rows
+        mine, other = delta_refs[2 * place:2 * place + 2]
+        deltas_ref[span] = in_order(core, mine[...], other[...])
+        at = span.stop
 
     copies = []
     for name, tile, out_ref, tile_ref in zip(names, tiles, out_refs, tile_refs):
@@ -385,58 +399,76 @@
         *after(weights, groups[0]),
     )
     far = after(by_pair, turned[0])
-    near = [own, from_pair] + groups
-    held = []
-    for rows, count, down, cost in (
-        (near, half + 1, weights[2], 1),
-        ([far], half - 1, turned[2], FAR_PRODUCTS_COST),
-    ):
-        part = count * capacity // 2
-        packed = shape(part, 3 * hidden_units)
-        wide = shape(part, 3 * hidden_units, jnp.float32)
+    near = [from_pair] + groups
+
+    def pieces(*parts):
+        shapes = []
+        for part in parts:
+            shapes += [shape(part, 3 * hidden_units, jnp.float32), shape(part, 3 * hidden_units)]
+        return shapes
+
+    def sums_over_cores(rows, down, cost, *parts):
         mine, other = call(
             functools.partial(products_kernel, down is turned[2]),
-            (wide, packed),
+            pieces(sum(parts)),
             *rows,
             *weights[:2],
             down,
             cost=cost,
         )
-        sums, marker = call(sums_kernel, (wide, packed), mine, swap(other, 1))
+        out = call(sums_kernel, pieces(*parts), mine, swap(other, 1))
+        return list(zip(out[::2], out[1::2]))
+
+    def exchanged(sums, marker):
         bit = 2
         while 2 * bit < width_parts:
-            sums, marker = call(sums_kernel, (wide, packed), sums, swap(marker, bit))
+            sums, marker = call(sums_kernel, pieces(sums.shape[0]), sums, swap(marker, bit))
             bit *= 2
-        held.append((sums, swap(marker, bit), packed))
-    deltas, grads = [], []
-    for sums, received, packed in held:
-        mine = call(deltas_kernel, packed, sums, received, cost=FAR_DELTAS_COST if deltas else 1)
-        if deltas:
-            mine = after(mine, deltas[1])
-        pair = [mine, swap(mine, 1)]
-        deltas += pair
-        block = shape(capacity, width)
-        if grads:
-            to_pair = call(
-                far_grad_kernel, shape(half * capacity, width), *pair, *turned[:2], grads[-1]
-            )
-        else:
-            grads = call(near_grad_kernel, (block,) * (half + 1), *pair, *turned[:2])
+        return sums, swap(marker, bit)
+
+    def deltas_of(sums, received, cost):
+        return call(deltas_kernel, shape(*sums.shape), sums, received, cost=cost)
+
+    own_half = capacity // 2
+    own_sums, near_sums = sums_over_cores(
+        near + [own], weights[2], 1, own_half, half * capacity // 2
+    )
+    (far_sums,) = sums_over_cores([far], turned[2], FAR_PRODUCTS_COST, (half - 1) * capacity // 2)
+    near_sums, far_sums = exchanged(*near_sums), exchanged(*far_sums)
+    own_sums = exchanged(*own_sums)
+
+    near_mine = deltas_of(*near_sums, 1)
+    near_deltas = near_mine, swap(near_mine, 1)
+    far_mine = after(deltas_of(*far_sums, FAR_DELTAS_COST), near_deltas[1])
+    far_deltas = far_mine, swap(far_mine, 1)
+    own_mine = deltas_of(*own_sums, OWN_DELTAS_COST)
+    own_deltas = own_mine, swap(own_mine, 1)
+    block = shape(capacity, width)
+    grads = call(slot_grad_kernel, (block,) * half, *near_deltas, *turned[:2])
+    (own_grad,) = call(slot_grad_kernel, (block,), *own_deltas, *turned[:2])
+    to_pair = call(
+        far_grad_kernel,
+        shape(half * capacity, width),
+        *after(far_deltas, own_mine),
+        *turned[:2],
+        grads[-1],
+    )
+    deltas = near_deltas + own_deltas + far_deltas
 
     returned_pair = swap(to_pair, 1, "expert")
-    sizes = (width, hidden_units, slot_count, (*near, far, *deltas))
+    sizes = (width, hidden_units, slot_count, (*near, own, far, *deltas))
     (gate_grad,) = weight_grads(("gate",), *sizes)
-    returned_pair = after(returned_pair, gate_grad)
+    returned_pair = after(returned_pair, (gate_grad, own_grad))
     returned = {}
     for place, j in enumerate(far_first[1:], 1):
         more = returned_pair[place * capacity:(place + 1) * capacity]
-        returned[j] = swap(jnp.concatenate([grads[place], more], axis=0), 2 * j, "expert")
+        returned[j] = swap(jnp.concatenate([grads[place - 1], more], axis=0), 2 * j, "expert")
     up_grad, down_grad = weight_grads(("up", "down"), *sizes)
     token_grad = call(
         token_grad_kernel,
         shape(tok_rows, width),
         chosen,
-        grads[0],
+        own_grad,
         returned_pair,
         *[returned[j] for j in far_first[1:]],
     )

time: 45.1 us -> 44.6 us (0.989)
  waiting for transfers between devices: 11.9 us -> 9.18 us
  starting transfers between devices: 18.4 us -> 20.1 us
  Pallas kernels: 13.8 us -> 14.3 us
    ppermute x15 -> x17, waiting for transfers between devices: 11.9 us -> 9.18 us  [swap(): return lax.ppermute(value, axis, [(i, i ^ bit) for i in range(size)])]
    ppermute x15 -> x17, starting transfers between devices: 18.4 us -> 20.1 us  [swap(): return lax.ppermute(value, axis, [(i, i ^ bit) for i in range(size)])]
    pallas_call x12 -> x14, Pallas kernels: 9.04 us -> 9.54 us  [call(): pl.pallas_call(kernel, out_shape=outs, in_specs=[pl.BlockSpec(memory_spac...]
  transfers between devices with their start and end apart: 15 -> 17, of which waited for: 8 -> 9; matrix products, arithmetic and copies ran while one was open for 0% -> 0% of each run, Pallas kernels for 22% -> 25%
where the time goes in v7:
time: 44.6 us; the launch traced here: 44.5 us
  starting transfers between devices  20.1 us (45%)
  Pallas kernels  14.3 us (32%)
  waiting for transfers between devices  9.18 us (21%)
  between operations  0.84 us (2%)
    ppermute x17, starting transfers between devices, swap(): return lax.ppermute(value, axis, [(i, i ^ bit) for i in range(size)])  20.1 us
    pallas_call x14, Pallas kernels, call(): pl.pallas_call(kernel, out_shape=outs, in_specs=[pl.BlockSpec(memory_spac...  9.54 us
    ppermute x17, waiting for transfers between devices, swap(): return lax.ppermute(value, axis, [(i, i ^ bit) for i in range(size)])  9.18 us
    pallas_call x2, Pallas kernels, weight_grads(): pl.pallas_call(functools.partial(weight_grads_kernel, names, tiles), out_...  4.8 us
  transfers between devices with their start and end apart: 17, of which 9 were waited for; matrix products, arithmetic and copies ran while one was open for 0% of the time, Pallas kernels for 25%

profile of v7, /device:TPU:0, one launch (start us, length us, event | category | flops | bytes accessed | tf_op | source)
XLA Modules:
  0.0 44.5 jit_solution(1019633561518495138)
XLA Ops:
  0.6 1.3 %shard_map.102 = (bf16[128,128]{1,0:T(8,128)(2,1)S(1)}, bf16[16,1024]{1,0:T(8,128)(2,1)S(1)}, bf16[16,1024]{1,0:T(8,128)(2,1)S(1)}, bf16[32,1024]{1,0:T(8,128)(2...) custom-call(s32[1,128]{1,0:T(1,128)} %bitcast.12, f32[1,128]{1,0:T(1,128)} %bitcast.13, ...), custom_call_target="tpu_custom_call" | custom-call | flops 1 | bytes 1 | tf_op jit(solution)/shard_map/pallas_call | solution.py:54
  1.9 5.1 %collective-permute-start.1 = (bf16[32,1024]{1,0:T(8,128)(2,1)S(1)}, bf16[32,1024]{1,0:T(8,128)(2,1)S(1)}, u32[]{:S(2)}, u32[]{:S(2)}) collective-permute-start(bf16[32,1024]{1,0:T(8,128)(2,1)S(1)} %get-tuple-element.46), channel_id=1, source_target_pairs={{0,6},{1,7},{2,4},{3,5},{4,2},{5,3},{6,0},{7,1},{8,14},{9,15},{10,... | collective-permute-start | bytes 196616 | tf_op jit(solution)/shard_map/ppermute | solution.py:36
  7.0 0.6 %collective-permute-start.3 = (bf16[32,1024]{1,0:T(8,128)(2,1)S(1)}, bf16[32,1024]{1,0:T(8,128)(2,1)S(1)}, u32[]{:S(2)}, u32[]{:S(2)}) collective-permute-start(bf16[32,1024]{1,0:T(8,128)(2,1)S(1)} %get-tuple-element.48), channel_id=1, source_target_pairs={{0,2},{1,3},{2,0},{3,1},{4,6},{5,7},{6,4},{7,5},{8,10},{9,11},{10,... | collective-permute-start | bytes 196616 | tf_op jit(solution)/shard_map/ppermute | solution.py:36
  7.7 1.7 %collective-permute-start = (bf16[16,1024]{1,0:T(8,128)(2,1)S(1)}, bf16[16,1024]{1,0:T(8,128)(2,1)S(1)}, u32[]{:S(2)}, u32[]{:S(2)}) collective-permute-start(bf16[16,1024]{1,0:T(8,128)(2,1)S(1)} %get-tuple-element.45), channel_id=1, source_target_pairs={{0,1},{1,0},{2,3},{3,2},{4,5},{5,4},{6,7},{7,6},{8,9},{9,8},{10,11... | collective-permute-start | bytes 98312 | tf_op jit(solution)/shard_map/ppermute | solution.py:36
  9.3 2.3 %shard_map.103 = (bf16[512,1408]{1,0:T(8,128)(2,1)S(1)}, bf16[512,1408]{1,0:T(8,128)(2,1)S(1)}, bf16[1408,512]{1,0:T(8,128)(2,1)S(1)}) custom-call(bf16[512,1408]{1,0:T(8,128)(2,1)} %bitcast.9, bf16[512,1408]{1,0:T(8,128)(2,1)} %bitcast.10, bf16[1408,512]{1,0:T(8,128)(2,1)} %bitcast.11, bf16[128,128]{1,0:T(8,128)(2,1)S(1)} %get-tuple-element.44.marker_hbm.chosen_ref), custom_call_target="tpu_custom_call" | custom-call | flops 10000000 | bytes 10000000 | tf_op jit(solution)/shard_map/pallas_call | solution.py:54
  11.6 1.0 %collective-permute-done.2.refs_2_ = bf16[32,1024]{1,0:T(8,128)(2,1)S(1)} collective-permute-done((bf16[32,1024]{1,0:T(8,128)(2,1)S(1)}, bf16[32,1024]{1,0:T(8,128)(2,1)S(1)}, u32[]{:S(2)}, u32[]{:S(2)}) %collective-permute-start.2) | collective-permute-done | bytes 65568 | tf_op jit(solution)/shard_map/ppermute | solution.py:36
  12.6 1.0 %shard_map.104 = (f32[40,4224]{1,0:T(8,128)S(1)}, bf16[40,4224]{1,0:T(8,128)(2,1)S(1)}) custom-call(bf16[16,1024]{1,0:T(8,128)(2,1)S(1)} %collective-permute-done.refs_0_, bf16[32,1024]{1,0:T(8,128)(2,1)S(1)} %collective-permute-done.1.refs_1_, bf16[32,1024]{1,0:T(8,128)(2,1)S(1)} %collective-permute-done.2.refs_2_, ...), custom_call_target="tpu_custom_call" | custom-call | flops 1 | bytes 1 | tf_op jit(solution)/shard_map/pallas_call | solution.py:54
  13.8 1.6 %collective-permute-start.7 = (bf16[48,1024]{1,0:T(8,128)(2,1)S(1)}, bf16[48,1024]{1,0:T(8,128)(2,1)S(1)}, u32[]{:S(2)}, u32[]{:S(2)}) collective-permute-start(bf16[48,1024]{1,0:T(8,128)(2,1)S(1)} %pad_maximum_fusion), channel_id=1, source_target_pairs={{0,1},{1,0},{2,3},{3,2},{4,5},{5,4},{6,7},{7,6},{8,9},{9,8},{10,11... | collective-permute-start | bytes 294920 | tf_op jit(solution)/shard_map/ppermute | solution.py:36
  15.5 1.6 %collective-permute-start.10 = (bf16[32,4224]{1,0:T(8,128)(2,1)S(1)}, bf16[32,4224]{1,0:T(8,128)(2,1)S(1)}, u32[]{:S(2)}, u32[]{:S(2)}) collective-permute-start(bf16[32,4224]{1,0:T(8,128)(2,1)S(1)} %get-tuple-element.73), channel_id=1, source_target_pairs={{0,16},{8,24},{16,0},{24,8},{1,17},{9,25},{17,1},{25,9},{2,18},{10... | collective-permute-start | bytes 811016 | tf_op jit(solution)/shard_map/ppermute | solution.py:36
  17.0 1.2 %shard_map.107 = (bf16[1408,512]{1,0:T(8,128)(2,1)S(1)}, bf16[1408,512]{1,0:T(8,128)(2,1)S(1)}, bf16[512,1408]{1,0:T(8,128)(2,1)S(1)}) custom-call(bf16[512,1408]{1,0:T(8,128)(2,1)S(1)} %get-tuple-element.60.refs_5_.refs_0_.refs_1_, bf16[512,1408]{1,0:T(8,128)(2,1)S(1)} %get-tuple-element.61.refs_6_.refs_1_.refs_2_, ...), custom_call_target="tpu_custom_call" | custom-call | flops 1 | bytes 1 | tf_op jit(solution)/shard_map/pallas_call | solution.py:54
  18.2 0.8 %collective-permute-done.7.refs_0_.refs_5_ = bf16[48,1024]{1,0:T(8,128)(2,1)S(1)} collective-permute-done((bf16[48,1024]{1,0:T(8,128)(2,1)S(1)}, bf16[48,1024]{1,0:T(8,128)(2,1)S(1)}, u32[]{:S(2)}, u32[]{:S(2)}) %collective-permute-start.7) | collective-permute-done | bytes 98336 | tf_op jit(solution)/shard_map/ppermute | solution.py:36
  19.0 0.8 %shard_map.109 = (f32[24,4224]{1,0:T(8,128)S(1)}, bf16[24,4224]{1,0:T(8,128)(2,1)S(1)}) custom-call(bf16[48,1024]{1,0:T(8,128)(2,1)S(1)} %collective-permute-done.7.refs_0_.refs_5_, bf16[512,1408]{1,0:T(8,128)(2,1)S(1)} %get-tuple-element.60.refs_5_.refs_0_.refs_1_, bf16[512,1408]{1,0:T(8,128)(2,1)S(1)} %get-tuple-element.61.refs_6_.refs_1_.refs_2_, ...), custom_call_target="tpu_custom_call" | custom-call | flops 300000000 | bytes 300000000 | tf_op jit(solution)/shard_map/pallas_call | solution.py:54
  19.9 1.4 %collective-permute-done.8.received_ref = bf16[24,4224]{1,0:T(8,128)(2,1)S(1)} collective-permute-done((bf16[24,4224]{1,0:T(8,128)(2,1)S(1)}, bf16[24,4224]{1,0:T(8,128)(2,1)S(1)}, u32[]{:S(2)}, u32[]{:S(2)}) %collective-permute-start.8) | collective-permute-done | bytes 202784 | tf_op jit(solution)/shard_map/ppermute | solution.py:36
  21.4 1.6 %collective-permute-start.9 = (bf16[24,4224]{1,0:T(8,128)(2,1)S(1)}, bf16[24,4224]{1,0:T(8,128)(2,1)S(1)}, u32[]{:S(2)}, u32[]{:S(2)}) collective-permute-start(bf16[24,4224]{1,0:T(8,128)(2,1)S(1)} %get-tuple-element.71), channel_id=1, source_target_pairs={{0,16},{8,24},{16,0},{24,8},{1,17},{9,25},{17,1},{25,9},{2,18},{10... | collective-permute-start | bytes 608264 | tf_op jit(solution)/shard_map/ppermute | solution.py:36
  23.0 1.1 %collective-permute-done.10.received_ref = bf16[32,4224]{1,0:T(8,128)(2,1)S(1)} collective-permute-done((bf16[32,4224]{1,0:T(8,128)(2,1)S(1)}, bf16[32,4224]{1,0:T(8,128)(2,1)S(1)}, u32[]{:S(2)}, u32[]{:S(2)}) %collective-permute-start.10) | collective-permute-done | bytes 270368 | tf_op jit(solution)/shard_map/ppermute | solution.py:36
  24.3 1.6 %collective-permute-start.5 = (bf16[8,4224]{1,0:T(8,128)(2,1)S(1)}, bf16[8,4224]{1,0:T(8,128)(2,1)S(1)}, u32[]{:S(2)}, u32[]{:S(2)}) collective-permute-start(bf16[8,4224]{1,0:T(8,128)(2,1)S(1)} %get-tuple-element.59), channel_id=1, source_target_pairs={{0,16},{8,24},{16,0},{24,8},{1,17},{9,25},{17,1},{25,9},{2,18},{10... | collective-permute-start | bytes 202760 | tf_op jit(solution)/shard_map/ppermute | solution.py:36
  25.9 3.4 %collective-permute-done.9.received_ref = bf16[24,4224]{1,0:T(8,128)(2,1)S(1)} collective-permute-done((bf16[24,4224]{1,0:T(8,128)(2,1)S(1)}, bf16[24,4224]{1,0:T(8,128)(2,1)S(1)}, u32[]{:S(2)}, u32[]{:S(2)}) %collective-permute-start.9) | collective-permute-done | bytes 202784 | tf_op jit(solution)/shard_map/ppermute | solution.py:36
  30.2 0.6 %shard_map.113 = (bf16[16,512]{1,0:T(8,128)(2,1)S(1)}, bf16[16,512]{1,0:T(8,128)(2,1)S(1)}, bf16[16,512]{1,0:T(8,128)(2,1)S(1)}, bf16[16,512]{1,0:T(8,128)(2,1)S(1)}) custom-call(bf16[32,4224]{1,0:T(8,128)(2,1)S(1)} %shard_map.112.mine_ref.refs_6_, bf16[32,4224]{1,0:T(8,128)(2,1)S(1)} %collective-permute-done.11.other_ref.refs_7_, ...), custom_call_target="tpu_custom_call" | custom-call | flops 1 | bytes 1 | tf_op jit(solution)/shard_map/pallas_call | solution.py:54
  31.6 1.6 %collective-permute-start.13 = (bf16[64,512]{1,0:T(8,128)(2,1)S(1)}, bf16[64,512]{1,0:T(8,128)(2,1)S(1)}, u32[]{:S(2)}, u32[]{:S(2)}) collective-permute-start(bf16[64,512]{1,0:T(8,128)(2,1)S(1)} %shard_map.114), channel_id=1, source_target_pairs={{0,1},{1,0},{2,3},{3,2},{4,5},{5,4},{6,7},{7,6},{8,9},{9,8},{10,11... | collective-permute-start | bytes 196616 | tf_op jit(solution)/shard_map/ppermute | solution.py:36
  33.6 1.9 %shard_map.115 = f32[512,1408]{1,0:T(8,128)} custom-call(bf16[16,1024]{1,0:T(8,128)(2,1)S(1)} %collective-permute-done.refs_0_, bf16[32,1024]{1,0:T(8,128)(2,1)S(1)} %collective-permute-done.1.refs_1_, bf16[32,1024]{1,0:T(8,128)(2,1)S(1)} %collective-permute-done.2.refs_2_, bf16[32,1024]{1,0:T(8,128)(2,1)S(1)} %collective-permute-done.3.refs_3_, ...), custom_call_target="tpu_custom_call" | custom-call | flops 10000000 | bytes 10000000 | tf_op jit(solution)/shard_map/pallas_call | solution.py:256
  36.0 2.8 %collective-permute-start.14 = (bf16[32,512]{1,0:T(8,128)(2,1)S(1)}, bf16[32,512]{1,0:T(8,128)(2,1)S(1)}, u32[]{:S(2)}, u32[]{:S(2)}) collective-permute-start(bf16[32,512]{1,0:T(8,128)(2,1)S(1)} %pad_maximum_fusion.1), channel_id=1, source_target_pairs={{0,6},{1,7},{2,4},{3,5},{4,2},{5,3},{6,0},{7,1},{8,14},{9,15},{10,... | collective-permute-start | bytes 98312 | tf_op jit(solution)/shard_map/ppermute | solution.py:36
  38.8 1.7 %collective-permute-start.16 = (bf16[32,512]{1,0:T(8,128)(2,1)S(1)}, bf16[32,512]{1,0:T(8,128)(2,1)S(1)}, u32[]{:S(2)}, u32[]{:S(2)}) collective-permute-start(bf16[32,512]{1,0:T(8,128)(2,1)S(1)} %pad_maximum_fusion.3), channel_id=1, source_target_pairs={{0,2},{1,3},{2,0},{3,1},{4,6},{5,7},{6,4},{7,5},{8,10},{9,11},{10,... | collective-permute-start | bytes 98312 | tf_op jit(solution)/shard_map/ppermute | solution.py:36
  40.4 2.9 %shard_map.117 = (f32[512,1408]{1,0:T(8,128)}, f32[1408,512]{1,0:T(8,128)}) custom-call(bf16[16,1024]{1,0:T(8,128)(2,1)S(1)} %collective-permute-done.refs_0_, bf16[32,1024]{1,0:T(8,128)(2,1)S(1)} %collective-permute-done.1.refs_1_, bf16[32,1024]{1,0:T(8,128)(2,1)S(1)} %collective-permute-done.2.refs_2_, ...), custom_call_target="tpu_custom_call" | custom-call | flops 10000000 | bytes 10000000 | tf_op jit(solution)/shard_map/pallas_call | solution.py:256
  43.6 0.9 %shard_map.116 = bf16[128,512]{1,0:T(8,128)(2,1)} custom-call(bf16[128,128]{1,0:T(8,128)(2,1)S(1)} %get-tuple-element.44.marker_hbm.chosen_ref, bf16[16,512]{1,0:T(8,128)(2,1)S(1)} %shard_map.108.own_ref, bf16[64,512]{1,0:T(8,128)(2,1)S(1)} %collective-permute-done.13.from_pair_ref, bf16[32,512]{1,0:T(8,128)(2,1)S(1)} %collective-permute-done.14.refs_0_, ...), custom_call_target="tpu_custom_call" | custom-call | flops 1 | bytes 1 | tf_op jit(solution)/shard_map/pallas_call | solution.py:54
  (34 shorter events, 3.3 us)
Async XLA Ops:
  1.9 9.7 %collective-permute-start.1 = (bf16[32,1024]{1,0:T(8,128)(2,1)S(1)}, bf16[32,1024]{1,0:T(8,128)(2,1)S(1)}, u32[]{:S(2)}, u32[]{:S(2)}) collective-permute-start(bf16[32,1024]{1,0:T(8,128)(2,1)S(1)} %get-tuple-element.46), channel_id=1, source_target_pairs={{0,6},{1,7},{2,4},{3,5},{4,2},{5,3},{6,0},{7,1},{8,14},{9,15},{10,... | collective-permute-start | bytes 196616 | tf_op jit(solution)/shard_map/ppermute | solution.py:36
  7.0 5.6 %collective-permute-start.2 = (bf16[32,1024]{1,0:T(8,128)(2,1)S(1)}, bf16[32,1024]{1,0:T(8,128)(2,1)S(1)}, u32[]{:S(2)}, u32[]{:S(2)}) collective-permute-start(bf16[32,1024]{1,0:T(8,128)(2,1)S(1)} %get-tuple-element.47), channel_id=1, source_target_pairs={{0,4},{1,5},{2,6},{3,7},{4,0},{5,1},{6,2},{7,3},{8,12},{9,13},{10,... | collective-permute-start | bytes 196616 | tf_op jit(solution)/shard_map/ppermute | solution.py:36
  7.0 5.6 %collective-permute-start.3 = (bf16[32,1024]{1,0:T(8,128)(2,1)S(1)}, bf16[32,1024]{1,0:T(8,128)(2,1)S(1)}, u32[]{:S(2)}, u32[]{:S(2)}) collective-permute-start(bf16[32,1024]{1,0:T(8,128)(2,1)S(1)} %get-tuple-element.48), channel_id=1, source_target_pairs={{0,2},{1,3},{2,0},{3,1},{4,6},{5,7},{6,4},{7,5},{8,10},{9,11},{10,... | collective-permute-start | bytes 196616 | tf_op jit(solution)/shard_map/ppermute | solution.py:36
  7.7 3.9 %collective-permute-start = (bf16[16,1024]{1,0:T(8,128)(2,1)S(1)}, bf16[16,1024]{1,0:T(8,128)(2,1)S(1)}, u32[]{:S(2)}, u32[]{:S(2)}) collective-permute-start(bf16[16,1024]{1,0:T(8,128)(2,1)S(1)} %get-tuple-element.45), channel_id=1, source_target_pairs={{0,1},{1,0},{2,3},{3,2},{4,5},{5,4},{6,7},{7,6},{8,9},{9,8},{10,11... | collective-permute-start | bytes 98312 | tf_op jit(solution)/shard_map/ppermute | solution.py:36
  13.7 1.7 %collective-permute-start.4 = (bf16[40,4224]{1,0:T(8,128)(2,1)S(1)}, bf16[40,4224]{1,0:T(8,128)(2,1)S(1)}, u32[]{:S(2)}, u32[]{:S(2)}) collective-permute-start(bf16[40,4224]{1,0:T(8,128)(2,1)S(1)} %get-tuple-element.57), channel_id=1, source_target_pairs={{0,8},{8,0},{16,24},{24,16},{1,9},{9,1},{17,25},{25,17},{2,10},{10... | collective-permute-start | bytes 1013768 | tf_op jit(solution)/shard_map/ppermute | solution.py:36
  13.8 5.2 %collective-permute-start.7 = (bf16[48,1024]{1,0:T(8,128)(2,1)S(1)}, bf16[48,1024]{1,0:T(8,128)(2,1)S(1)}, u32[]{:S(2)}, u32[]{:S(2)}) collective-permute-start(bf16[48,1024]{1,0:T(8,128)(2,1)S(1)} %pad_maximum_fusion), channel_id=1, source_target_pairs={{0,1},{1,0},{2,3},{3,2},{4,5},{5,4},{6,7},{7,6},{8,9},{9,8},{10,11... | collective-permute-start | bytes 294920 | tf_op jit(solution)/shard_map/ppermute | solution.py:36
  15.5 8.6 %collective-permute-start.10 = (bf16[32,4224]{1,0:T(8,128)(2,1)S(1)}, bf16[32,4224]{1,0:T(8,128)(2,1)S(1)}, u32[]{:S(2)}, u32[]{:S(2)}) collective-permute-start(bf16[32,4224]{1,0:T(8,128)(2,1)S(1)} %get-tuple-element.73), channel_id=1, source_target_pairs={{0,16},{8,24},{16,0},{24,8},{1,17},{9,25},{17,1},{25,9},{2,18},{10... | collective-permute-start | bytes 811016 | tf_op jit(solution)/shard_map/ppermute | solution.py:36
  19.9 1.5 %collective-permute-start.8 = (bf16[24,4224]{1,0:T(8,128)(2,1)S(1)}, bf16[24,4224]{1,0:T(8,128)(2,1)S(1)}, u32[]{:S(2)}, u32[]{:S(2)}) collective-permute-start(bf16[24,4224]{1,0:T(8,128)(2,1)S(1)} %get-tuple-element.69), channel_id=1, source_target_pairs={{0,8},{8,0},{16,24},{24,16},{1,9},{9,1},{17,25},{25,17},{2,10},{10... | collective-permute-start | bytes 608264 | tf_op jit(solution)/shard_map/ppermute | solution.py:36
  21.4 7.9 %collective-permute-start.9 = (bf16[24,4224]{1,0:T(8,128)(2,1)S(1)}, bf16[24,4224]{1,0:T(8,128)(2,1)S(1)}, u32[]{:S(2)}, u32[]{:S(2)}) collective-permute-start(bf16[24,4224]{1,0:T(8,128)(2,1)S(1)} %get-tuple-element.71), channel_id=1, source_target_pairs={{0,16},{8,24},{16,0},{24,8},{1,17},{9,25},{17,1},{25,9},{2,18},{10... | collective-permute-start | bytes 608264 | tf_op jit(solution)/shard_map/ppermute | solution.py:36
  24.3 5.2 %collective-permute-start.11 = (bf16[32,4224]{1,0:T(8,128)(2,1)S(1)}, bf16[32,4224]{1,0:T(8,128)(2,1)S(1)}, u32[]{:S(2)}, u32[]{:S(2)}) collective-permute-start(bf16[32,4224]{1,0:T(8,128)(2,1)S(1)} %shard_map.112.mine_ref.refs_6_), channel_id=1, source_target_pairs={{0,8},{8,0},{16,24},{24,16},{1,9},{9,1},{17,25},{25,17},{2,10},{10... | collective-permute-start | bytes 811016 | tf_op jit(solution)/shard_map/ppermute | solution.py:36
  24.3 5.7 %collective-permute-start.5 = (bf16[8,4224]{1,0:T(8,128)(2,1)S(1)}, bf16[8,4224]{1,0:T(8,128)(2,1)S(1)}, u32[]{:S(2)}, u32[]{:S(2)}) collective-permute-start(bf16[8,4224]{1,0:T(8,128)(2,1)S(1)} %get-tuple-element.59), channel_id=1, source_target_pairs={{0,16},{8,24},{16,0},{24,8},{1,17},{9,25},{17,1},{25,9},{2,18},{10... | collective-permute-start | bytes 202760 | tf_op jit(solution)/shard_map/ppermute | solution.py:36
  29.4 1.5 %collective-permute-start.12 = (bf16[24,4224]{1,0:T(8,128)(2,1)S(1)}, bf16[24,4224]{1,0:T(8,128)(2,1)S(1)}, u32[]{:S(2)}, u32[]{:S(2)}) collective-permute-start(bf16[24,4224]{1,0:T(8,128)(2,1)S(1)} %shard_map.111.mine_ref.refs_10_), channel_id=1, source_target_pairs={{0,8},{8,0},{16,24},{24,16},{1,9},{9,1},{17,25},{25,17},{2,10},{10... | collective-permute-start | bytes 608264 | tf_op jit(solution)/shard_map/ppermute | solution.py:36
  30.1 3.1 %collective-permute-start.6 = (bf16[8,4224]{1,0:T(8,128)(2,1)S(1)}, bf16[8,4224]{1,0:T(8,128)(2,1)S(1)}, u32[]{:S(2)}, u32[]{:S(2)}) collective-permute-start(bf16[8,4224]{1,0:T(8,128)(2,1)S(1)} %shard_map.106.mine_ref.refs_8_), channel_id=1, source_target_pairs={{0,8},{8,0},{16,24},{24,16},{1,9},{9,1},{17,25},{25,17},{2,10},{10... | collective-permute-start | bytes 202760 | tf_op jit(solution)/shard_map/ppermute | solution.py:36
  31.6 4.4 %collective-permute-start.13 = (bf16[64,512]{1,0:T(8,128)(2,1)S(1)}, bf16[64,512]{1,0:T(8,128)(2,1)S(1)}, u32[]{:S(2)}, u32[]{:S(2)}) collective-permute-start(bf16[64,512]{1,0:T(8,128)(2,1)S(1)} %shard_map.114), channel_id=1, source_target_pairs={{0,1},{1,0},{2,3},{3,2},{4,5},{5,4},{6,7},{7,6},{8,9},{9,8},{10,11... | collective-permute-start | bytes 196616 | tf_op jit(solution)/shard_map/ppermute | solution.py:36
  36.0 7.3 %collective-permute-start.14 = (bf16[32,512]{1,0:T(8,128)(2,1)S(1)}, bf16[32,512]{1,0:T(8,128)(2,1)S(1)}, u32[]{:S(2)}, u32[]{:S(2)}) collective-permute-start(bf16[32,512]{1,0:T(8,128)(2,1)S(1)} %pad_maximum_fusion.1), channel_id=1, source_target_pairs={{0,6},{1,7},{2,4},{3,5},{4,2},{5,3},{6,0},{7,1},{8,14},{9,15},{10,... | collective-permute-start | bytes 98312 | tf_op jit(solution)/shard_map/ppermute | solution.py:36
  38.8 4.8 %collective-permute-start.15 = (bf16[32,512]{1,0:T(8,128)(2,1)S(1)}, bf16[32,512]{1,0:T(8,128)(2,1)S(1)}, u32[]{:S(2)}, u32[]{:S(2)}) collective-permute-start(bf16[32,512]{1,0:T(8,128)(2,1)S(1)} %pad_maximum_fusion.2), channel_id=1, source_target_pairs={{0,4},{1,5},{2,6},{3,7},{4,0},{5,1},{6,2},{7,3},{8,12},{9,13},{10,... | collective-permute-start | bytes 98312 | tf_op jit(solution)/shard_map/ppermute | solution.py:36
  38.8 4.8 %collective-permute-start.16 = (bf16[32,512]{1,0:T(8,128)(2,1)S(1)}, bf16[32,512]{1,0:T(8,128)(2,1)S(1)}, u32[]{:S(2)}, u32[]{:S(2)}) collective-permute-start(bf16[32,512]{1,0:T(8,128)(2,1)S(1)} %pad_maximum_fusion.3), channel_id=1, source_target_pairs={{0,2},{1,3},{2,0},{3,1},{4,6},{5,7},{6,4},{7,5},{8,10},{9,11},{10,... | collective-permute-start | bytes 98312 | tf_op jit(solution)/shard_map/ppermute | solution.py:36

commit v8 on v7

--- a/solution.py
+++ b/solution.py
@@ -114,27 +114,29 @@
         at += out_ref.shape[0]
 
 
-def load_kernel(gate_hbm, up_hbm, down_hbm, marker_hbm, gate_ref, up_ref, down_ref, sems):
+def load_kernel(down_hbm, gate_hbm, up_hbm, marker_hbm, turned_ref, gate_ref, up_ref, down_ref, sems):
     copies = [
         pltpu.make_async_copy(source, target, sems.at[place])
         for place, (source, target) in enumerate(
-            ((gate_hbm, gate_ref), (up_hbm, up_ref), (down_hbm, down_ref))
+            ((down_hbm, down_ref), (gate_hbm, gate_ref), (up_hbm, up_ref))
         )
     ]
     for copy in copies:
         copy.start()
-    for copy in copies:
+    copies[0].wait()
+    turned_ref[...] = down_ref[...].T
+    for copy in copies[1:]:
         copy.wait()
 
 
 def turn_kernel(*refs):
-    for source, target in zip(refs[:3], refs[3:]):
+    for source, target in zip(refs[:2], refs[2:]):
         target[...] = source[...].T
 
 
-def near_rows(from_pair_ref, *group_refs):
-    halves = [ref[:ref.shape[0] // 2] for ref in group_refs]
-    return jnp.concatenate(halves + [from_pair_ref[...]], axis=0)
+def near_rows(from_pair_ref, *group_refs, cols=slice(None)):
+    halves = [ref[:ref.shape[0] // 2, cols] for ref in group_refs]
+    return jnp.concatenate(halves + [from_pair_ref[:, cols]], axis=0)
 
 
 def with_own_rows(own, rows):
@@ -142,7 +144,7 @@
     return jnp.concatenate([own[:part], rows[:half], own[part:], rows[half:]], axis=0)
 
 
-def products_kernel(turned, *refs):
+def products_kernel(*refs):
     *row_refs, gate_ref, up_ref, down_ref, mine_ref, other_ref = refs
     rows = row_refs[-1][...]
     if len(row_refs) > 1:
@@ -155,10 +157,7 @@
     for place, weight_ref in enumerate((gate_ref, up_ref, down_ref)):
         cols = slice(place * hidden_units, (place + 1) * hidden_units)
         rows = feats if place < 2 else cots
-        if place < 2 or turned:
-            out = jnp.dot(rows, weight_ref[...], preferred_element_type=jnp.float32)
-        else:
-            out = contract_cols(rows, weight_ref[...])
+        out = jnp.dot(rows, weight_ref[...], preferred_element_type=jnp.float32)
         low, high = out[:half], out[half:]
         mine_ref[:, cols] = jnp.where(core == 0, low, high)
         other_ref[:, cols] = jnp.where(core == 0, high, low).astype(jnp.bfloat16)
@@ -219,25 +218,34 @@
     width = rows_ref.shape[1] // 2
     hidden_units = deltas_ref.shape[1] // 3
     core = lax.axis_index("dp") % 2
-    at = 0
-    for place, rows in enumerate((near_rows(*row_refs[:-2]), row_refs[-2][...], row_refs[-1][...])):
-        span = slice(at, at + rows.shape[0])
-        rows_ref[span] = rows
-        mine, other = delta_refs[2 * place:2 * place + 2]
-        deltas_ref[span] = in_order(core, mine[...], other[...])
-        at = span.stop
+
+    def gather_rows(cols):
+        *near_refs, own_ref, far_ref = row_refs
+        near = near_rows(*near_refs, cols=cols)
+        rows_ref[:, cols] = jnp.concatenate([near, own_ref[:, cols], far_ref[:, cols]], axis=0)
+
+    def gather_deltas(cols):
+        at = 0
+        for mine, other in zip(delta_refs[::2], delta_refs[1::2]):
+            both = in_order(core, mine[:, cols], other[:, cols])
+            deltas_ref[at:at + both.shape[0], cols] = both
+            at += both.shape[0]
 
     copies = []
     for name, tile, out_ref, tile_ref in zip(names, tiles, out_refs, tile_refs):
+        place = ("down", "gate", "up").index(name)
+        of_name = slice(place * hidden_units, (place + 1) * hidden_units)
+        gather_deltas(of_name)
+        if name == "down":
+            gather_rows(slice(width, 2 * width))
+        elif name == names[0]:
+            gather_rows(slice(0, width))
         for at in range(0, out_ref.shape[0], tile):
             rows = min(tile, out_ref.shape[0] - at)
             if name == "down":
                 out = contract_rows(deltas_ref[:, at:at + rows], rows_ref[:, width:])
             else:
-                start = hidden_units * (1 if name == "gate" else 2)
-                out = contract_rows(
-                    rows_ref[:, at:at + rows], deltas_ref[:, start:start + hidden_units]
-                )
+                out = contract_rows(rows_ref[:, at:at + rows], deltas_ref[:, of_name])
             tile_ref[at:at + rows] = out
             span = pl.ds(at, rows)
             copies.append(
@@ -376,28 +384,27 @@
             pltpu.SemaphoreType.DMA((4,)),
         ],
     )
-    weights = call(
+    down, gate, up = call(
         load_kernel,
-        (shape(width, hidden_units), shape(width, hidden_units), shape(hidden_units, width)),
+        (shape(width, hidden_units),) * 3,
+        down_weight[0],
         gate_weight[0],
         up_weight[0],
-        down_weight[0],
         chosen,
         far=range(3),
-        scratch=[pltpu.SemaphoreType.DMA((3,))],
+        scratch=[
+            pltpu.VMEM((hidden_units, width), jnp.bfloat16),
+            pltpu.SemaphoreType.DMA((3,)),
+        ],
         cost=10**7,
     )
     groups = [swap(groups[j - 1], 2 * j, "expert") for j in far_first[1:]]
     from_pair = swap(pair_block, 1, "expert")
     groups = after(groups, from_pair)
     seconds = jnp.concatenate([group[capacity:] for group in groups], axis=0)
-    by_pair = swap(after(seconds, weights[2]), 1, "expert")
-
-    turned = call(
-        turn_kernel,
-        (shape(hidden_units, width), shape(hidden_units, width), shape(width, hidden_units)),
-        *after(weights, groups[0]),
-    )
+    by_pair = swap(after(seconds, up), 1, "expert")
+
+    turned = call(turn_kernel, (shape(hidden_units, width),) * 2, *after((gate, up), groups[0]))
     far = after(by_pair, turned[0])
     near = [from_pair] + groups
 
@@ -407,14 +414,9 @@
             shapes += [shape(part, 3 * hidden_units, jnp.float32), shape(part, 3 * hidden_units)]
         return shapes
 
-    def sums_over_cores(rows, down, cost, *parts):
+    def sums_over_cores(rows, cost, *parts):
         mine, other = call(
-            functools.partial(products_kernel, down is turned[2]),
-            pieces(sum(parts)),
-            *rows,
-            *weights[:2],
-            down,
-            cost=cost,
+            products_kernel, pieces(sum(parts)), *rows, gate, up, down, cost=cost
         )
         out = call(sums_kernel, pieces(*parts), mine, swap(other, 1))
         return list(zip(out[::2], out[1::2]))
@@ -431,9 +433,9 @@
 
     own_half = capacity // 2
     own_sums, near_sums = sums_over_cores(
-        near + [own], weights[2], 1, own_half, half * capacity // 2
-    )
-    (far_sums,) = sums_over_cores([far], turned[2], FAR_PRODUCTS_COST, (half - 1) * capacity // 2)
+        near + [own], 1, own_half, half * capacity // 2
+    )
+    (far_sums,) = sums_over_cores([far], FAR_PRODUCTS_COST, (half - 1) * capacity // 2)
     near_sums, far_sums = exchanged(*near_sums), exchanged(*far_sums)
     own_sums = exchanged(*own_sums)
 
@@ -444,13 +446,13 @@
     own_mine = deltas_of(*own_sums, OWN_DELTAS_COST)
     own_deltas = own_mine, swap(own_mine, 1)
     block = shape(capacity, width)
-    grads = call(slot_grad_kernel, (block,) * half, *near_deltas, *turned[:2])
-    (own_grad,) = call(slot_grad_kernel, (block,), *own_deltas, *turned[:2])
+    grads = call(slot_grad_kernel, (block,) * half, *near_deltas, *turned)
+    (own_grad,) = call(slot_grad_kernel, (block,), *own_deltas, *turned)
     to_pair = call(
         far_grad_kernel,
         shape(half * capacity, width),
         *after(far_deltas, own_mine),
-        *turned[:2],
+        *turned,
         grads[-1],
     )
     deltas = near_deltas + own_deltas + far_deltas

time: 44.6 us -> 44.4 us (level)
  Pallas kernels: 14.3 us -> 13.7 us
    pallas_call x14, Pallas kernels: 9.54 us -> 8.93 us  [call(): pl.pallas_call(kernel, out_shape=outs, in_specs=[pl.BlockSpec(memory_spac...]
  transfers between devices with their start and end apart: 17 -> 17, of which waited for: 9 -> 9; matrix products, arithmetic and copies ran while one was open for 0% -> 0% of each run, Pallas kernels for 25% -> 24%
where the time goes in v8:
time: 44.4 us; the launch traced here: 44.2 us
  starting transfers between devices  20.1 us (45%)
  Pallas kernels  13.7 us (31%)
  waiting for transfers between devices  9.57 us (22%)
  between operations  0.85 us (2%)
    ppermute x17, starting transfers between devices, swap(): return lax.ppermute(value, axis, [(i, i ^ bit) for i in range(size)])  20.1 us
    ppermute x17, waiting for transfers between devices, swap(): return lax.ppermute(value, axis, [(i, i ^ bit) for i in range(size)])  9.57 us
    pallas_call x14, Pallas kernels, call(): pl.pallas_call(kernel, out_shape=outs, in_specs=[pl.BlockSpec(memory_spac...  8.93 us
    pallas_call x2, Pallas kernels, weight_grads(): pl.pallas_call(functools.partial(weight_grads_kernel, names, tiles), out_...  4.79 us
  transfers between devices with their start and end apart: 17, of which 9 were waited for; matrix products, arithmetic and copies ran while one was open for 0% of the time, Pallas kernels for 24%

profile of v8, /device:TPU:0, one launch (start us, length us, event | category | flops | bytes accessed | tf_op | source)
XLA Modules:
  0.0 44.2 jit_solution(6230346418689086349)
XLA Ops:
  0.6 1.3 %shard_map.102 = (bf16[128,128]{1,0:T(8,128)(2,1)S(1)}, bf16[16,1024]{1,0:T(8,128)(2,1)S(1)}, bf16[16,1024]{1,0:T(8,128)(2,1)S(1)}, bf16[32,1024]{1,0:T(8,128)(2...) custom-call(s32[1,128]{1,0:T(1,128)} %bitcast.12, f32[1,128]{1,0:T(1,128)} %bitcast.13, ...), custom_call_target="tpu_custom_call" | custom-call | flops 1 | bytes 1 | tf_op jit(solution)/shard_map/pallas_call | solution.py:54
  1.9 5.1 %collective-permute-start.1 = (bf16[32,1024]{1,0:T(8,128)(2,1)S(1)}, bf16[32,1024]{1,0:T(8,128)(2,1)S(1)}, u32[]{:S(2)}, u32[]{:S(2)}) collective-permute-start(bf16[32,1024]{1,0:T(8,128)(2,1)S(1)} %get-tuple-element.44), channel_id=1, source_target_pairs={{0,6},{1,7},{2,4},{3,5},{4,2},{5,3},{6,0},{7,1},{8,14},{9,15},{10,... | collective-permute-start | bytes 196616 | tf_op jit(solution)/shard_map/ppermute | solution.py:36
  7.0 0.6 %collective-permute-start.3 = (bf16[32,1024]{1,0:T(8,128)(2,1)S(1)}, bf16[32,1024]{1,0:T(8,128)(2,1)S(1)}, u32[]{:S(2)}, u32[]{:S(2)}) collective-permute-start(bf16[32,1024]{1,0:T(8,128)(2,1)S(1)} %get-tuple-element.46), channel_id=1, source_target_pairs={{0,2},{1,3},{2,0},{3,1},{4,6},{5,7},{6,4},{7,5},{8,10},{9,11},{10,... | collective-permute-start | bytes 196616 | tf_op jit(solution)/shard_map/ppermute | solution.py:36
  7.7 1.7 %collective-permute-start = (bf16[16,1024]{1,0:T(8,128)(2,1)S(1)}, bf16[16,1024]{1,0:T(8,128)(2,1)S(1)}, u32[]{:S(2)}, u32[]{:S(2)}) collective-permute-start(bf16[16,1024]{1,0:T(8,128)(2,1)S(1)} %get-tuple-element.43), channel_id=1, source_target_pairs={{0,1},{1,0},{2,3},{3,2},{4,5},{5,4},{6,7},{7,6},{8,9},{9,8},{10,11... | collective-permute-start | bytes 98312 | tf_op jit(solution)/shard_map/ppermute | solution.py:36
  9.3 2.3 %shard_map.103 = (bf16[512,1408]{1,0:T(8,128)(2,1)S(1)}, bf16[512,1408]{1,0:T(8,128)(2,1)S(1)}, bf16[512,1408]{1,0:T(8,128)(2,1)S(1)}) custom-call(bf16[1408,512]{1,0:T(8,128)(2,1)} %bitcast.9, bf16[512,1408]{1,0:T(8,128)(2,1)} %bitcast.10, bf16[512,1408]{1,0:T(8,128)(2,1)} %bitcast.11, bf16[128,128]{1,0:T(8,128)(2,1)S(1)} %get-tuple-element.42.marker_hbm.chosen_ref), custom_call_target="tpu_custom_call" | custom-call | flops 10000000 | bytes 10000000 | tf_op jit(solution)/shard_map/pallas_call | solution.py:54
  11.6 1.0 %collective-permute-done.2.refs_2_ = bf16[32,1024]{1,0:T(8,128)(2,1)S(1)} collective-permute-done((bf16[32,1024]{1,0:T(8,128)(2,1)S(1)}, bf16[32,1024]{1,0:T(8,128)(2,1)S(1)}, u32[]{:S(2)}, u32[]{:S(2)}) %collective-permute-start.2) | collective-permute-done | bytes 65568 | tf_op jit(solution)/shard_map/ppermute | solution.py:36
  12.6 0.8 %shard_map.104 = (f32[40,4224]{1,0:T(8,128)S(1)}, bf16[40,4224]{1,0:T(8,128)(2,1)S(1)}) custom-call(bf16[16,1024]{1,0:T(8,128)(2,1)S(1)} %collective-permute-done.refs_0_, bf16[32,1024]{1,0:T(8,128)(2,1)S(1)} %collective-permute-done.1.refs_1_, bf16[32,1024]{1,0:T(8,128)(2,1)S(1)} %collective-permute-done.2.refs_2_, ...), custom_call_target="tpu_custom_call" | custom-call | flops 1 | bytes 1 | tf_op jit(solution)/shard_map/pallas_call | solution.py:54
  13.6 1.6 %collective-permute-start.7 = (bf16[48,1024]{1,0:T(8,128)(2,1)S(1)}, bf16[48,1024]{1,0:T(8,128)(2,1)S(1)}, u32[]{:S(2)}, u32[]{:S(2)}) collective-permute-start(bf16[48,1024]{1,0:T(8,128)(2,1)S(1)} %pad_maximum_fusion), channel_id=1, source_target_pairs={{0,1},{1,0},{2,3},{3,2},{4,5},{5,4},{6,7},{7,6},{8,9},{9,8},{10,11... | collective-permute-start | bytes 294920 | tf_op jit(solution)/shard_map/ppermute | solution.py:36
  15.3 1.6 %collective-permute-start.10 = (bf16[32,4224]{1,0:T(8,128)(2,1)S(1)}, bf16[32,4224]{1,0:T(8,128)(2,1)S(1)}, u32[]{:S(2)}, u32[]{:S(2)}) collective-permute-start(bf16[32,4224]{1,0:T(8,128)(2,1)S(1)} %get-tuple-element.69), channel_id=1, source_target_pairs={{0,16},{8,24},{16,0},{24,8},{1,17},{9,25},{17,1},{25,9},{2,18},{10... | collective-permute-start | bytes 811016 | tf_op jit(solution)/shard_map/ppermute | solution.py:36
  16.8 0.8 %shard_map.107 = (bf16[1408,512]{1,0:T(8,128)(2,1)S(1)}, bf16[1408,512]{1,0:T(8,128)(2,1)S(1)}) custom-call(bf16[512,1408]{1,0:T(8,128)(2,1)S(1)} %get-tuple-element.58.refs_5_.refs_0_.refs_1_, bf16[512,1408]{1,0:T(8,128)(2,1)S(1)} %get-tuple-element.59.refs_6_.refs_1_.refs_2_), custom_call_target="tpu_custom_call" | custom-call | flops 1 | bytes 1 | tf_op jit(solution)/shard_map/pallas_call | solution.py:54
  17.6 1.2 %collective-permute-done.7.refs_0_.refs_5_ = bf16[48,1024]{1,0:T(8,128)(2,1)S(1)} collective-permute-done((bf16[48,1024]{1,0:T(8,128)(2,1)S(1)}, bf16[48,1024]{1,0:T(8,128)(2,1)S(1)}, u32[]{:S(2)}, u32[]{:S(2)}) %collective-permute-start.7) | collective-permute-done | bytes 98336 | tf_op jit(solution)/shard_map/ppermute | solution.py:36
  18.8 0.8 %shard_map.109 = (f32[24,4224]{1,0:T(8,128)S(1)}, bf16[24,4224]{1,0:T(8,128)(2,1)S(1)}) custom-call(bf16[48,1024]{1,0:T(8,128)(2,1)S(1)} %collective-permute-done.7.refs_0_.refs_5_, bf16[512,1408]{1,0:T(8,128)(2,1)S(1)} %get-tuple-element.58.refs_5_.refs_0_.refs_1_, bf16[512,1408]{1,0:T(8,128)(2,1)S(1)} %get-tuple-element.59.refs_6_.refs_1_.refs_2_, ...), custom_call_target="tpu_custom_call" | custom-call | flops 300000000 | bytes 300000000 | tf_op jit(solution)/shard_map/pallas_call | solution.py:54
  19.7 1.4 %collective-permute-done.8.received_ref = bf16[24,4224]{1,0:T(8,128)(2,1)S(1)} collective-permute-done((bf16[24,4224]{1,0:T(8,128)(2,1)S(1)}, bf16[24,4224]{1,0:T(8,128)(2,1)S(1)}, u32[]{:S(2)}, u32[]{:S(2)}) %collective-permute-start.8) | collective-permute-done | bytes 202784 | tf_op jit(solution)/shard_map/ppermute | solution.py:36
  21.2 1.6 %collective-permute-start.9 = (bf16[24,4224]{1,0:T(8,128)(2,1)S(1)}, bf16[24,4224]{1,0:T(8,128)(2,1)S(1)}, u32[]{:S(2)}, u32[]{:S(2)}) collective-permute-start(bf16[24,4224]{1,0:T(8,128)(2,1)S(1)} %get-tuple-element.67), channel_id=1, source_target_pairs={{0,16},{8,24},{16,0},{24,8},{1,17},{9,25},{17,1},{25,9},{2,18},{10... | collective-permute-start | bytes 608264 | tf_op jit(solution)/shard_map/ppermute | solution.py:36
  22.8 1.1 %collective-permute-done.10.received_ref = bf16[32,4224]{1,0:T(8,128)(2,1)S(1)} collective-permute-done((bf16[32,4224]{1,0:T(8,128)(2,1)S(1)}, bf16[32,4224]{1,0:T(8,128)(2,1)S(1)}, u32[]{:S(2)}, u32[]{:S(2)}) %collective-permute-start.10) | collective-permute-done | bytes 270368 | tf_op jit(solution)/shard_map/ppermute | solution.py:36
  24.1 1.6 %collective-permute-start.5 = (bf16[8,4224]{1,0:T(8,128)(2,1)S(1)}, bf16[8,4224]{1,0:T(8,128)(2,1)S(1)}, u32[]{:S(2)}, u32[]{:S(2)}) collective-permute-start(bf16[8,4224]{1,0:T(8,128)(2,1)S(1)} %get-tuple-element.57), channel_id=1, source_target_pairs={{0,16},{8,24},{16,0},{24,8},{1,17},{9,25},{17,1},{25,9},{2,18},{10... | collective-permute-start | bytes 202760 | tf_op jit(solution)/shard_map/ppermute | solution.py:36
  25.7 3.4 %collective-permute-done.9.received_ref = bf16[24,4224]{1,0:T(8,128)(2,1)S(1)} collective-permute-done((bf16[24,4224]{1,0:T(8,128)(2,1)S(1)}, bf16[24,4224]{1,0:T(8,128)(2,1)S(1)}, u32[]{:S(2)}, u32[]{:S(2)}) %collective-permute-start.9) | collective-permute-done | bytes 202784 | tf_op jit(solution)/shard_map/ppermute | solution.py:36
  30.0 0.6 %shard_map.113 = (bf16[16,512]{1,0:T(8,128)(2,1)S(1)}, bf16[16,512]{1,0:T(8,128)(2,1)S(1)}, bf16[16,512]{1,0:T(8,128)(2,1)S(1)}, bf16[16,512]{1,0:T(8,128)(2,1)S(1)}) custom-call(bf16[32,4224]{1,0:T(8,128)(2,1)S(1)} %shard_map.112.mine_ref.refs_6_, bf16[32,4224]{1,0:T(8,128)(2,1)S(1)} %collective-permute-done.11.other_ref.refs_7_, ...), custom_call_target="tpu_custom_call" | custom-call | flops 1 | bytes 1 | tf_op jit(solution)/shard_map/pallas_call | solution.py:54
  31.3 1.6 %collective-permute-start.13 = (bf16[64,512]{1,0:T(8,128)(2,1)S(1)}, bf16[64,512]{1,0:T(8,128)(2,1)S(1)}, u32[]{:S(2)}, u32[]{:S(2)}) collective-permute-start(bf16[64,512]{1,0:T(8,128)(2,1)S(1)} %shard_map.114), channel_id=1, source_target_pairs={{0,1},{1,0},{2,3},{3,2},{4,5},{5,4},{6,7},{7,6},{8,9},{9,8},{10,11... | collective-permute-start | bytes 196616 | tf_op jit(solution)/shard_map/ppermute | solution.py:36
  33.4 1.9 %shard_map.115 = f32[512,1408]{1,0:T(8,128)} custom-call(bf16[16,1024]{1,0:T(8,128)(2,1)S(1)} %collective-permute-done.refs_0_, bf16[32,1024]{1,0:T(8,128)(2,1)S(1)} %collective-permute-done.1.refs_1_, bf16[32,1024]{1,0:T(8,128)(2,1)S(1)} %collective-permute-done.2.refs_2_, bf16[32,1024]{1,0:T(8,128)(2,1)S(1)} %collective-permute-done.3.refs_3_, ...), custom_call_target="tpu_custom_call" | custom-call | flops 10000000 | bytes 10000000 | tf_op jit(solution)/shard_map/pallas_call | solution.py:264
  35.8 2.8 %collective-permute-start.14 = (bf16[32,512]{1,0:T(8,128)(2,1)S(1)}, bf16[32,512]{1,0:T(8,128)(2,1)S(1)}, u32[]{:S(2)}, u32[]{:S(2)}) collective-permute-start(bf16[32,512]{1,0:T(8,128)(2,1)S(1)} %pad_maximum_fusion.1), channel_id=1, source_target_pairs={{0,6},{1,7},{2,4},{3,5},{4,2},{5,3},{6,0},{7,1},{8,14},{9,15},{10,... | collective-permute-start | bytes 98312 | tf_op jit(solution)/shard_map/ppermute | solution.py:36
  38.6 1.7 %collective-permute-start.16 = (bf16[32,512]{1,0:T(8,128)(2,1)S(1)}, bf16[32,512]{1,0:T(8,128)(2,1)S(1)}, u32[]{:S(2)}, u32[]{:S(2)}) collective-permute-start(bf16[32,512]{1,0:T(8,128)(2,1)S(1)} %pad_maximum_fusion.3), channel_id=1, source_target_pairs={{0,2},{1,3},{2,0},{3,1},{4,6},{5,7},{6,4},{7,5},{8,10},{9,11},{10,... | collective-permute-start | bytes 98312 | tf_op jit(solution)/shard_map/ppermute | solution.py:36
  40.2 2.9 %shard_map.117 = (f32[512,1408]{1,0:T(8,128)}, f32[1408,512]{1,0:T(8,128)}) custom-call(bf16[16,1024]{1,0:T(8,128)(2,1)S(1)} %collective-permute-done.refs_0_, bf16[32,1024]{1,0:T(8,128)(2,1)S(1)} %collective-permute-done.1.refs_1_, bf16[32,1024]{1,0:T(8,128)(2,1)S(1)} %collective-permute-done.2.refs_2_, ...), custom_call_target="tpu_custom_call" | custom-call | flops 10000000 | bytes 10000000 | tf_op jit(solution)/shard_map/pallas_call | solution.py:264
  43.4 0.9 %shard_map.116 = bf16[128,512]{1,0:T(8,128)(2,1)} custom-call(bf16[128,128]{1,0:T(8,128)(2,1)S(1)} %get-tuple-element.42.marker_hbm.chosen_ref, bf16[16,512]{1,0:T(8,128)(2,1)S(1)} %shard_map.108.own_ref, bf16[64,512]{1,0:T(8,128)(2,1)S(1)} %collective-permute-done.13.from_pair_ref, bf16[32,512]{1,0:T(8,128)(2,1)S(1)} %collective-permute-done.14.refs_0_, ...), custom_call_target="tpu_custom_call" | custom-call | flops 1 | bytes 1 | tf_op jit(solution)/shard_map/pallas_call | solution.py:54
  (34 shorter events, 3.3 us)
Async XLA Ops:
  1.9 9.7 %collective-permute-start.1 = (bf16[32,1024]{1,0:T(8,128)(2,1)S(1)}, bf16[32,1024]{1,0:T(8,128)(2,1)S(1)}, u32[]{:S(2)}, u32[]{:S(2)}) collective-permute-start(bf16[32,1024]{1,0:T(8,128)(2,1)S(1)} %get-tuple-element.44), channel_id=1, source_target_pairs={{0,6},{1,7},{2,4},{3,5},{4,2},{5,3},{6,0},{7,1},{8,14},{9,15},{10,... | collective-permute-start | bytes 196616 | tf_op jit(solution)/shard_map/ppermute | solution.py:36
  7.0 5.6 %collective-permute-start.2 = (bf16[32,1024]{1,0:T(8,128)(2,1)S(1)}, bf16[32,1024]{1,0:T(8,128)(2,1)S(1)}, u32[]{:S(2)}, u32[]{:S(2)}) collective-permute-start(bf16[32,1024]{1,0:T(8,128)(2,1)S(1)} %get-tuple-element.45), channel_id=1, source_target_pairs={{0,4},{1,5},{2,6},{3,7},{4,0},{5,1},{6,2},{7,3},{8,12},{9,13},{10,... | collective-permute-start | bytes 196616 | tf_op jit(solution)/shard_map/ppermute | solution.py:36
  7.0 5.6 %collective-permute-start.3 = (bf16[32,1024]{1,0:T(8,128)(2,1)S(1)}, bf16[32,1024]{1,0:T(8,128)(2,1)S(1)}, u32[]{:S(2)}, u32[]{:S(2)}) collective-permute-start(bf16[32,1024]{1,0:T(8,128)(2,1)S(1)} %get-tuple-element.46), channel_id=1, source_target_pairs={{0,2},{1,3},{2,0},{3,1},{4,6},{5,7},{6,4},{7,5},{8,10},{9,11},{10,... | collective-permute-start | bytes 196616 | tf_op jit(solution)/shard_map/ppermute | solution.py:36
  7.7 3.9 %collective-permute-start = (bf16[16,1024]{1,0:T(8,128)(2,1)S(1)}, bf16[16,1024]{1,0:T(8,128)(2,1)S(1)}, u32[]{:S(2)}, u32[]{:S(2)}) collective-permute-start(bf16[16,1024]{1,0:T(8,128)(2,1)S(1)} %get-tuple-element.43), channel_id=1, source_target_pairs={{0,1},{1,0},{2,3},{3,2},{4,5},{5,4},{6,7},{7,6},{8,9},{9,8},{10,11... | collective-permute-start | bytes 98312 | tf_op jit(solution)/shard_map/ppermute | solution.py:36
  13.5 1.7 %collective-permute-start.4 = (bf16[40,4224]{1,0:T(8,128)(2,1)S(1)}, bf16[40,4224]{1,0:T(8,128)(2,1)S(1)}, u32[]{:S(2)}, u32[]{:S(2)}) collective-permute-start(bf16[40,4224]{1,0:T(8,128)(2,1)S(1)} %get-tuple-element.55), channel_id=1, source_target_pairs={{0,8},{8,0},{16,24},{24,16},{1,9},{9,1},{17,25},{25,17},{2,10},{10... | collective-permute-start | bytes 1013768 | tf_op jit(solution)/shard_map/ppermute | solution.py:36
  13.6 5.2 %collective-permute-start.7 = (bf16[48,1024]{1,0:T(8,128)(2,1)S(1)}, bf16[48,1024]{1,0:T(8,128)(2,1)S(1)}, u32[]{:S(2)}, u32[]{:S(2)}) collective-permute-start(bf16[48,1024]{1,0:T(8,128)(2,1)S(1)} %pad_maximum_fusion), channel_id=1, source_target_pairs={{0,1},{1,0},{2,3},{3,2},{4,5},{5,4},{6,7},{7,6},{8,9},{9,8},{10,11... | collective-permute-start | bytes 294920 | tf_op jit(solution)/shard_map/ppermute | solution.py:36
  15.3 8.6 %collective-permute-start.10 = (bf16[32,4224]{1,0:T(8,128)(2,1)S(1)}, bf16[32,4224]{1,0:T(8,128)(2,1)S(1)}, u32[]{:S(2)}, u32[]{:S(2)}) collective-permute-start(bf16[32,4224]{1,0:T(8,128)(2,1)S(1)} %get-tuple-element.69), channel_id=1, source_target_pairs={{0,16},{8,24},{16,0},{24,8},{1,17},{9,25},{17,1},{25,9},{2,18},{10... | collective-permute-start | bytes 811016 | tf_op jit(solution)/shard_map/ppermute | solution.py:36
  19.7 1.5 %collective-permute-start.8 = (bf16[24,4224]{1,0:T(8,128)(2,1)S(1)}, bf16[24,4224]{1,0:T(8,128)(2,1)S(1)}, u32[]{:S(2)}, u32[]{:S(2)}) collective-permute-start(bf16[24,4224]{1,0:T(8,128)(2,1)S(1)} %get-tuple-element.65), channel_id=1, source_target_pairs={{0,8},{8,0},{16,24},{24,16},{1,9},{9,1},{17,25},{25,17},{2,10},{10... | collective-permute-start | bytes 608264 | tf_op jit(solution)/shard_map/ppermute | solution.py:36
  21.2 7.9 %collective-permute-start.9 = (bf16[24,4224]{1,0:T(8,128)(2,1)S(1)}, bf16[24,4224]{1,0:T(8,128)(2,1)S(1)}, u32[]{:S(2)}, u32[]{:S(2)}) collective-permute-start(bf16[24,4224]{1,0:T(8,128)(2,1)S(1)} %get-tuple-element.67), channel_id=1, source_target_pairs={{0,16},{8,24},{16,0},{24,8},{1,17},{9,25},{17,1},{25,9},{2,18},{10... | collective-permute-start | bytes 608264 | tf_op jit(solution)/shard_map/ppermute | solution.py:36
  24.1 5.2 %collective-permute-start.11 = (bf16[32,4224]{1,0:T(8,128)(2,1)S(1)}, bf16[32,4224]{1,0:T(8,128)(2,1)S(1)}, u32[]{:S(2)}, u32[]{:S(2)}) collective-permute-start(bf16[32,4224]{1,0:T(8,128)(2,1)S(1)} %shard_map.112.mine_ref.refs_6_), channel_id=1, source_target_pairs={{0,8},{8,0},{16,24},{24,16},{1,9},{9,1},{17,25},{25,17},{2,10},{10... | collective-permute-start | bytes 811016 | tf_op jit(solution)/shard_map/ppermute | solution.py:36
  24.1 5.7 %collective-permute-start.5 = (bf16[8,4224]{1,0:T(8,128)(2,1)S(1)}, bf16[8,4224]{1,0:T(8,128)(2,1)S(1)}, u32[]{:S(2)}, u32[]{:S(2)}) collective-permute-start(bf16[8,4224]{1,0:T(8,128)(2,1)S(1)} %get-tuple-element.57), channel_id=1, source_target_pairs={{0,16},{8,24},{16,0},{24,8},{1,17},{9,25},{17,1},{25,9},{2,18},{10... | collective-permute-start | bytes 202760 | tf_op jit(solution)/shard_map/ppermute | solution.py:36
  29.2 1.5 %collective-permute-start.12 = (bf16[24,4224]{1,0:T(8,128)(2,1)S(1)}, bf16[24,4224]{1,0:T(8,128)(2,1)S(1)}, u32[]{:S(2)}, u32[]{:S(2)}) collective-permute-start(bf16[24,4224]{1,0:T(8,128)(2,1)S(1)} %shard_map.111.mine_ref.refs_10_), channel_id=1, source_target_pairs={{0,8},{8,0},{16,24},{24,16},{1,9},{9,1},{17,25},{25,17},{2,10},{10... | collective-permute-start | bytes 608264 | tf_op jit(solution)/shard_map/ppermute | solution.py:36
  29.9 3.1 %collective-permute-start.6 = (bf16[8,4224]{1,0:T(8,128)(2,1)S(1)}, bf16[8,4224]{1,0:T(8,128)(2,1)S(1)}, u32[]{:S(2)}, u32[]{:S(2)}) collective-permute-start(bf16[8,4224]{1,0:T(8,128)(2,1)S(1)} %shard_map.106.mine_ref.refs_8_), channel_id=1, source_target_pairs={{0,8},{8,0},{16,24},{24,16},{1,9},{9,1},{17,25},{25,17},{2,10},{10... | collective-permute-start | bytes 202760 | tf_op jit(solution)/shard_map/ppermute | solution.py:36
  31.3 4.4 %collective-permute-start.13 = (bf16[64,512]{1,0:T(8,128)(2,1)S(1)}, bf16[64,512]{1,0:T(8,128)(2,1)S(1)}, u32[]{:S(2)}, u32[]{:S(2)}) collective-permute-start(bf16[64,512]{1,0:T(8,128)(2,1)S(1)} %shard_map.114), channel_id=1, source_target_pairs={{0,1},{1,0},{2,3},{3,2},{4,5},{5,4},{6,7},{7,6},{8,9},{9,8},{10,11... | collective-permute-start | bytes 196616 | tf_op jit(solution)/shard_map/ppermute | solution.py:36
  35.8 7.3 %collective-permute-start.14 = (bf16[32,512]{1,0:T(8,128)(2,1)S(1)}, bf16[32,512]{1,0:T(8,128)(2,1)S(1)}, u32[]{:S(2)}, u32[]{:S(2)}) collective-permute-start(bf16[32,512]{1,0:T(8,128)(2,1)S(1)} %pad_maximum_fusion.1), channel_id=1, source_target_pairs={{0,6},{1,7},{2,4},{3,5},{4,2},{5,3},{6,0},{7,1},{8,14},{9,15},{10,... | collective-permute-start | bytes 98312 | tf_op jit(solution)/shard_map/ppermute | solution.py:36
  38.5 4.8 %collective-permute-start.15 = (bf16[32,512]{1,0:T(8,128)(2,1)S(1)}, bf16[32,512]{1,0:T(8,128)(2,1)S(1)}, u32[]{:S(2)}, u32[]{:S(2)}) collective-permute-start(bf16[32,512]{1,0:T(8,128)(2,1)S(1)} %pad_maximum_fusion.2), channel_id=1, source_target_pairs={{0,4},{1,5},{2,6},{3,7},{4,0},{5,1},{6,2},{7,3},{8,12},{9,13},{10,... | collective-permute-start | bytes 98312 | tf_op jit(solution)/shard_map/ppermute | solution.py:36
  38.6 4.8 %collective-permute-start.16 = (bf16[32,512]{1,0:T(8,128)(2,1)S(1)}, bf16[32,512]{1,0:T(8,128)(2,1)S(1)}, u32[]{:S(2)}, u32[]{:S(2)}) collective-permute-start(bf16[32,512]{1,0:T(8,128)(2,1)S(1)} %pad_maximum_fusion.3), channel_id=1, source_target_pairs={{0,2},{1,3},{2,0},{3,1},{4,6},{5,7},{6,4},{7,5},{8,10},{9,11},{10,... | collective-permute-start | bytes 98312 | tf_op jit(solution)/shard_map/ppermute | solution.py:36

commit v9 on v8

--- a/solution.py
+++ b/solution.py
@@ -38,7 +38,7 @@
 
 FAR_PRODUCTS_COST = 3 * 10**8
 FAR_DELTAS_COST = 8 * 10**8
-OWN_DELTAS_COST = 3 * 10**9
+OWN_DELTAS_COST = 18 * 10**8
 
 
 def after(values, marker):
@@ -404,8 +404,6 @@
     seconds = jnp.concatenate([group[capacity:] for group in groups], axis=0)
     by_pair = swap(after(seconds, up), 1, "expert")
 
-    turned = call(turn_kernel, (shape(hidden_units, width),) * 2, *after((gate, up), groups[0]))
-    far = after(by_pair, turned[0])
     near = [from_pair] + groups
 
     def pieces(*parts):
@@ -435,18 +433,19 @@
     own_sums, near_sums = sums_over_cores(
         near + [own], 1, own_half, half * capacity // 2
     )
-    (far_sums,) = sums_over_cores([far], FAR_PRODUCTS_COST, (half - 1) * capacity // 2)
+    (far_sums,) = sums_over_cores([by_pair], FAR_PRODUCTS_COST, (half - 1) * capacity // 2)
     near_sums, far_sums = exchanged(*near_sums), exchanged(*far_sums)
-    own_sums = exchanged(*own_sums)
 
     near_mine = deltas_of(*near_sums, 1)
+    turned = call(turn_kernel, (shape(hidden_units, width),) * 2, *after((gate, up), near_mine))
+    own_sums = exchanged(own_sums[0], after(own_sums[1], turned[0]))
     near_deltas = near_mine, swap(near_mine, 1)
     far_mine = after(deltas_of(*far_sums, FAR_DELTAS_COST), near_deltas[1])
     far_deltas = far_mine, swap(far_mine, 1)
-    own_mine = deltas_of(*own_sums, OWN_DELTAS_COST)
-    own_deltas = own_mine, swap(own_mine, 1)
     block = shape(capacity, width)
     grads = call(slot_grad_kernel, (block,) * half, *near_deltas, *turned)
+    own_mine = deltas_of(after(own_sums[0], grads[0]), own_sums[1], OWN_DELTAS_COST)
+    own_deltas = own_mine, swap(own_mine, 1)
     (own_grad,) = call(slot_grad_kernel, (block,), *own_deltas, *turned)
     to_pair = call(
         far_grad_kernel,
@@ -458,7 +457,7 @@
     deltas = near_deltas + own_deltas + far_deltas
 
     returned_pair = swap(to_pair, 1, "expert")
-    sizes = (width, hidden_units, slot_count, (*near, own, far, *deltas))
+    sizes = (width, hidden_units, slot_count, (*near, own, by_pair, *deltas))
     (gate_grad,) = weight_grads(("gate",), *sizes)
     returned_pair = after(returned_pair, (gate_grad, own_grad))
     returned = {}

time: 44.4 us -> 43.8 us (0.986)
  waiting for transfers between devices: 9.57 us -> 8.84 us
    ppermute x17, waiting for transfers between devices: 9.57 us -> 8.84 us  [swap(): return lax.ppermute(value, axis, [(i, i ^ bit) for i in range(size)])]
  transfers between devices with their start and end apart: 17 -> 17, of which waited for: 9 -> 9; matrix products, arithmetic and copies ran while one was open for 0% -> 0% of each run, Pallas kernels for 24% -> 25%
where the time goes in v9:
time: 43.8 us; the launch traced here: 43.6 us
  starting transfers between devices  20.2 us (46%)
  Pallas kernels  13.7 us (31%)
  waiting for transfers between devices  8.84 us (20%)
  between operations  0.84 us (2%)
    ppermute x17, starting transfers between devices, swap(): return lax.ppermute(value, axis, [(i, i ^ bit) for i in range(size)])  20.2 us
    pallas_call x14, Pallas kernels, call(): pl.pallas_call(kernel, out_shape=outs, in_specs=[pl.BlockSpec(memory_spac...  8.93 us
    ppermute x17, waiting for transfers between devices, swap(): return lax.ppermute(value, axis, [(i, i ^ bit) for i in range(size)])  8.84 us
    pallas_call x2, Pallas kernels, weight_grads(): pl.pallas_call(functools.partial(weight_grads_kernel, names, tiles), out_...  4.78 us
  transfers between devices with their start and end apart: 17, of which 9 were waited for; matrix products, arithmetic and copies ran while one was open for 0% of the time, Pallas kernels for 25%

profile of v9, /device:TPU:0, one launch (start us, length us, event | category | flops | bytes accessed | tf_op | source)
XLA Modules:
  0.0 43.6 jit_solution(8275180754794862682)
XLA Ops:
  0.6 1.3 %shard_map.102 = (bf16[128,128]{1,0:T(8,128)(2,1)S(1)}, bf16[16,1024]{1,0:T(8,128)(2,1)S(1)}, bf16[16,1024]{1,0:T(8,128)(2,1)S(1)}, bf16[32,1024]{1,0:T(8,128)(2...) custom-call(s32[1,128]{1,0:T(1,128)} %bitcast.12, f32[1,128]{1,0:T(1,128)} %bitcast.13, ...), custom_call_target="tpu_custom_call" | custom-call | flops 1 | bytes 1 | tf_op jit(solution)/shard_map/pallas_call | solution.py:54
  1.9 5.1 %collective-permute-start.1 = (bf16[32,1024]{1,0:T(8,128)(2,1)S(1)}, bf16[32,1024]{1,0:T(8,128)(2,1)S(1)}, u32[]{:S(2)}, u32[]{:S(2)}) collective-permute-start(bf16[32,1024]{1,0:T(8,128)(2,1)S(1)} %get-tuple-element.45), channel_id=1, source_target_pairs={{0,6},{1,7},{2,4},{3,5},{4,2},{5,3},{6,0},{7,1},{8,14},{9,15},{10,... | collective-permute-start | bytes 196616 | tf_op jit(solution)/shard_map/ppermute | solution.py:36
  7.0 0.6 %collective-permute-start.3 = (bf16[32,1024]{1,0:T(8,128)(2,1)S(1)}, bf16[32,1024]{1,0:T(8,128)(2,1)S(1)}, u32[]{:S(2)}, u32[]{:S(2)}) collective-permute-start(bf16[32,1024]{1,0:T(8,128)(2,1)S(1)} %get-tuple-element.47), channel_id=1, source_target_pairs={{0,2},{1,3},{2,0},{3,1},{4,6},{5,7},{6,4},{7,5},{8,10},{9,11},{10,... | collective-permute-start | bytes 196616 | tf_op jit(solution)/shard_map/ppermute | solution.py:36
  7.7 1.7 %collective-permute-start = (bf16[16,1024]{1,0:T(8,128)(2,1)S(1)}, bf16[16,1024]{1,0:T(8,128)(2,1)S(1)}, u32[]{:S(2)}, u32[]{:S(2)}) collective-permute-start(bf16[16,1024]{1,0:T(8,128)(2,1)S(1)} %get-tuple-element.44), channel_id=1, source_target_pairs={{0,1},{1,0},{2,3},{3,2},{4,5},{5,4},{6,7},{7,6},{8,9},{9,8},{10,11... | collective-permute-start | bytes 98312 | tf_op jit(solution)/shard_map/ppermute | solution.py:36
  9.3 2.3 %shard_map.103 = (bf16[512,1408]{1,0:T(8,128)(2,1)S(1)}, bf16[512,1408]{1,0:T(8,128)(2,1)S(1)}, bf16[512,1408]{1,0:T(8,128)(2,1)S(1)}) custom-call(bf16[1408,512]{1,0:T(8,128)(2,1)} %bitcast.9, bf16[512,1408]{1,0:T(8,128)(2,1)} %bitcast.10, bf16[512,1408]{1,0:T(8,128)(2,1)} %bitcast.11, bf16[128,128]{1,0:T(8,128)(2,1)S(1)} %get-tuple-element.43.marker_hbm.chosen_ref), custom_call_target="tpu_custom_call" | custom-call | flops 10000000 | bytes 10000000 | tf_op jit(solution)/shard_map/pallas_call | solution.py:54
  11.6 1.0 %collective-permute-done.2.refs_2_ = bf16[32,1024]{1,0:T(8,128)(2,1)S(1)} collective-permute-done((bf16[32,1024]{1,0:T(8,128)(2,1)S(1)}, bf16[32,1024]{1,0:T(8,128)(2,1)S(1)}, u32[]{:S(2)}, u32[]{:S(2)}) %collective-permute-start.2) | collective-permute-done | bytes 65568 | tf_op jit(solution)/shard_map/ppermute | solution.py:36
  12.6 0.8 %shard_map.104 = (f32[40,4224]{1,0:T(8,128)S(1)}, bf16[40,4224]{1,0:T(8,128)(2,1)S(1)}) custom-call(bf16[16,1024]{1,0:T(8,128)(2,1)S(1)} %collective-permute-done.refs_0_, bf16[32,1024]{1,0:T(8,128)(2,1)S(1)} %collective-permute-done.1.refs_1_, bf16[32,1024]{1,0:T(8,128)(2,1)S(1)} %collective-permute-done.2.refs_2_, ...), custom_call_target="tpu_custom_call" | custom-call | flops 1 | bytes 1 | tf_op jit(solution)/shard_map/pallas_call | solution.py:54
  13.6 1.6 %collective-permute-start.9 = (bf16[48,1024]{1,0:T(8,128)(2,1)S(1)}, bf16[48,1024]{1,0:T(8,128)(2,1)S(1)}, u32[]{:S(2)}, u32[]{:S(2)}) collective-permute-start(bf16[48,1024]{1,0:T(8,128)(2,1)S(1)} %pad_maximum_fusion), channel_id=1, source_target_pairs={{0,1},{1,0},{2,3},{3,2},{4,5},{5,4},{6,7},{7,6},{8,9},{9,8},{10,11... | collective-permute-start | bytes 294920 | tf_op jit(solution)/shard_map/ppermute | solution.py:36
  15.3 1.6 %collective-permute-start.5 = (bf16[32,4224]{1,0:T(8,128)(2,1)S(1)}, bf16[32,4224]{1,0:T(8,128)(2,1)S(1)}, u32[]{:S(2)}, u32[]{:S(2)}) collective-permute-start(bf16[32,4224]{1,0:T(8,128)(2,1)S(1)} %get-tuple-element.59), channel_id=1, source_target_pairs={{0,16},{8,24},{16,0},{24,8},{1,17},{9,25},{17,1},{25,9},{2,18},{10... | collective-permute-start | bytes 811016 | tf_op jit(solution)/shard_map/ppermute | solution.py:36
  16.8 2.0 %collective-permute-done.9.refs_0_.refs_5_ = bf16[48,1024]{1,0:T(8,128)(2,1)S(1)} collective-permute-done((bf16[48,1024]{1,0:T(8,128)(2,1)S(1)}, bf16[48,1024]{1,0:T(8,128)(2,1)S(1)}, u32[]{:S(2)}, u32[]{:S(2)}) %collective-permute-start.9) | collective-permute-done | bytes 98336 | tf_op jit(solution)/shard_map/ppermute | solution.py:36
  18.8 0.8 %shard_map.111 = (f32[24,4224]{1,0:T(8,128)S(1)}, bf16[24,4224]{1,0:T(8,128)(2,1)S(1)}) custom-call(bf16[48,1024]{1,0:T(8,128)(2,1)S(1)} %collective-permute-done.9.refs_0_.refs_5_, bf16[512,1408]{1,0:T(8,128)(2,1)S(1)} %get-tuple-element.60.refs_5_.refs_0_.refs_1_, bf16[512,1408]{1,0:T(8,128)(2,1)S(1)} %get-tuple-element.61.refs_6_.refs_1_.refs_2_, ...), custom_call_target="tpu_custom_call" | custom-call | flops 300000000 | bytes 300000000 | tf_op jit(solution)/shard_map/pallas_call | solution.py:54
  19.7 1.4 %collective-permute-done.10.received_ref = bf16[24,4224]{1,0:T(8,128)(2,1)S(1)} collective-permute-done((bf16[24,4224]{1,0:T(8,128)(2,1)S(1)}, bf16[24,4224]{1,0:T(8,128)(2,1)S(1)}, u32[]{:S(2)}, u32[]{:S(2)}) %collective-permute-start.10) | collective-permute-done | bytes 202784 | tf_op jit(solution)/shard_map/ppermute | solution.py:36
  21.2 1.6 %collective-permute-start.11 = (bf16[24,4224]{1,0:T(8,128)(2,1)S(1)}, bf16[24,4224]{1,0:T(8,128)(2,1)S(1)}, u32[]{:S(2)}, u32[]{:S(2)}) collective-permute-start(bf16[24,4224]{1,0:T(8,128)(2,1)S(1)} %get-tuple-element.72), channel_id=1, source_target_pairs={{0,16},{8,24},{16,0},{24,8},{1,17},{9,25},{17,1},{25,9},{2,18},{10... | collective-permute-start | bytes 608264 | tf_op jit(solution)/shard_map/ppermute | solution.py:36
  22.8 1.1 %collective-permute-done.5.received_ref = bf16[32,4224]{1,0:T(8,128)(2,1)S(1)} collective-permute-done((bf16[32,4224]{1,0:T(8,128)(2,1)S(1)}, bf16[32,4224]{1,0:T(8,128)(2,1)S(1)}, u32[]{:S(2)}, u32[]{:S(2)}) %collective-permute-start.5) | collective-permute-done | bytes 270368 | tf_op jit(solution)/shard_map/ppermute | solution.py:36
  24.1 0.8 %shard_map.107 = (bf16[1408,512]{1,0:T(8,128)(2,1)S(1)}, bf16[1408,512]{1,0:T(8,128)(2,1)S(1)}) custom-call(bf16[512,1408]{1,0:T(8,128)(2,1)S(1)} %get-tuple-element.60.refs_5_.refs_0_.refs_1_, bf16[512,1408]{1,0:T(8,128)(2,1)S(1)} %get-tuple-element.61.refs_6_.refs_1_.refs_2_), custom_call_target="tpu_custom_call" | custom-call | flops 1 | bytes 1 | tf_op jit(solution)/shard_map/pallas_call | solution.py:54
  24.9 1.6 %collective-permute-start.7 = (bf16[8,4224]{1,0:T(8,128)(2,1)S(1)}, bf16[8,4224]{1,0:T(8,128)(2,1)S(1)}, u32[]{:S(2)}, u32[]{:S(2)}) collective-permute-start(bf16[8,4224]{1,0:T(8,128)(2,1)S(1)} %get-tuple-element.67), channel_id=1, source_target_pairs={{0,16},{8,24},{16,0},{24,8},{1,17},{9,25},{17,1},{25,9},{2,18},{10... | collective-permute-start | bytes 202760 | tf_op jit(solution)/shard_map/ppermute | solution.py:36
  26.5 2.1 %collective-permute-done.11.received_ref = bf16[24,4224]{1,0:T(8,128)(2,1)S(1)} collective-permute-done((bf16[24,4224]{1,0:T(8,128)(2,1)S(1)}, bf16[24,4224]{1,0:T(8,128)(2,1)S(1)}, u32[]{:S(2)}, u32[]{:S(2)}) %collective-permute-start.11) | collective-permute-done | bytes 202784 | tf_op jit(solution)/shard_map/ppermute | solution.py:36
  28.8 0.6 %shard_map.108 = (bf16[16,512]{1,0:T(8,128)(2,1)S(1)}, bf16[16,512]{1,0:T(8,128)(2,1)S(1)}, bf16[16,512]{1,0:T(8,128)(2,1)S(1)}, bf16[16,512]{1,0:T(8,128)(2,1)S(1)}) custom-call(bf16[32,4224]{1,0:T(8,128)(2,1)S(1)} %shard_map.106.mine_ref.refs_6_, bf16[32,4224]{1,0:T(8,128)(2,1)S(1)} %collective-permute-done.6.other_ref.refs_7_, ...), custom_call_target="tpu_custom_call" | custom-call | flops 1 | bytes 1 | tf_op jit(solution)/shard_map/pallas_call | solution.py:54
  30.8 1.6 %collective-permute-start.13 = (bf16[64,512]{1,0:T(8,128)(2,1)S(1)}, bf16[64,512]{1,0:T(8,128)(2,1)S(1)}, u32[]{:S(2)}, u32[]{:S(2)}) collective-permute-start(bf16[64,512]{1,0:T(8,128)(2,1)S(1)} %shard_map.114), channel_id=1, source_target_pairs={{0,1},{1,0},{2,3},{3,2},{4,5},{5,4},{6,7},{7,6},{8,9},{9,8},{10,11... | collective-permute-start | bytes 196616 | tf_op jit(solution)/shard_map/ppermute | solution.py:36
  33.0 1.9 %shard_map.115 = f32[512,1408]{1,0:T(8,128)} custom-call(bf16[16,1024]{1,0:T(8,128)(2,1)S(1)} %collective-permute-done.refs_0_, bf16[32,1024]{1,0:T(8,128)(2,1)S(1)} %collective-permute-done.1.refs_1_, bf16[32,1024]{1,0:T(8,128)(2,1)S(1)} %collective-permute-done.2.refs_2_, bf16[32,1024]{1,0:T(8,128)(2,1)S(1)} %collective-permute-done.3.refs_3_, ...), custom_call_target="tpu_custom_call" | custom-call | flops 10000000 | bytes 10000000 | tf_op jit(solution)/shard_map/pallas_call | solution.py:264
  35.2 2.8 %collective-permute-start.14 = (bf16[32,512]{1,0:T(8,128)(2,1)S(1)}, bf16[32,512]{1,0:T(8,128)(2,1)S(1)}, u32[]{:S(2)}, u32[]{:S(2)}) collective-permute-start(bf16[32,512]{1,0:T(8,128)(2,1)S(1)} %pad_maximum_fusion.1), channel_id=1, source_target_pairs={{0,6},{1,7},{2,4},{3,5},{4,2},{5,3},{6,0},{7,1},{8,14},{9,15},{10,... | collective-permute-start | bytes 98312 | tf_op jit(solution)/shard_map/ppermute | solution.py:36
  38.0 1.7 %collective-permute-start.16 = (bf16[32,512]{1,0:T(8,128)(2,1)S(1)}, bf16[32,512]{1,0:T(8,128)(2,1)S(1)}, u32[]{:S(2)}, u32[]{:S(2)}) collective-permute-start(bf16[32,512]{1,0:T(8,128)(2,1)S(1)} %pad_maximum_fusion.3), channel_id=1, source_target_pairs={{0,2},{1,3},{2,0},{3,1},{4,6},{5,7},{6,4},{7,5},{8,10},{9,11},{10,... | collective-permute-start | bytes 98312 | tf_op jit(solution)/shard_map/ppermute | solution.py:36
  39.6 2.9 %shard_map.117 = (f32[512,1408]{1,0:T(8,128)}, f32[1408,512]{1,0:T(8,128)}) custom-call(bf16[16,1024]{1,0:T(8,128)(2,1)S(1)} %collective-permute-done.refs_0_, bf16[32,1024]{1,0:T(8,128)(2,1)S(1)} %collective-permute-done.1.refs_1_, bf16[32,1024]{1,0:T(8,128)(2,1)S(1)} %collective-permute-done.2.refs_2_, ...), custom_call_target="tpu_custom_call" | custom-call | flops 10000000 | bytes 10000000 | tf_op jit(solution)/shard_map/pallas_call | solution.py:264
  42.8 0.9 %shard_map.116 = bf16[128,512]{1,0:T(8,128)(2,1)} custom-call(bf16[128,128]{1,0:T(8,128)(2,1)S(1)} %get-tuple-element.43.marker_hbm.chosen_ref, bf16[16,512]{1,0:T(8,128)(2,1)S(1)} %shard_map.110.own_ref, bf16[64,512]{1,0:T(8,128)(2,1)S(1)} %collective-permute-done.13.from_pair_ref, bf16[32,512]{1,0:T(8,128)(2,1)S(1)} %collective-permute-done.14.refs_0_, ...), custom_call_target="tpu_custom_call" | custom-call | flops 1 | bytes 1 | tf_op jit(solution)/shard_map/pallas_call | solution.py:54
  (34 shorter events, 3.1 us)
Async XLA Ops:
  1.9 9.7 %collective-permute-start.1 = (bf16[32,1024]{1,0:T(8,128)(2,1)S(1)}, bf16[32,1024]{1,0:T(8,128)(2,1)S(1)}, u32[]{:S(2)}, u32[]{:S(2)}) collective-permute-start(bf16[32,1024]{1,0:T(8,128)(2,1)S(1)} %get-tuple-element.45), channel_id=1, source_target_pairs={{0,6},{1,7},{2,4},{3,5},{4,2},{5,3},{6,0},{7,1},{8,14},{9,15},{10,... | collective-permute-start | bytes 196616 | tf_op jit(solution)/shard_map/ppermute | solution.py:36
  7.0 5.6 %collective-permute-start.2 = (bf16[32,1024]{1,0:T(8,128)(2,1)S(1)}, bf16[32,1024]{1,0:T(8,128)(2,1)S(1)}, u32[]{:S(2)}, u32[]{:S(2)}) collective-permute-start(bf16[32,1024]{1,0:T(8,128)(2,1)S(1)} %get-tuple-element.46), channel_id=1, source_target_pairs={{0,4},{1,5},{2,6},{3,7},{4,0},{5,1},{6,2},{7,3},{8,12},{9,13},{10,... | collective-permute-start | bytes 196616 | tf_op jit(solution)/shard_map/ppermute | solution.py:36
  7.0 5.6 %collective-permute-start.3 = (bf16[32,1024]{1,0:T(8,128)(2,1)S(1)}, bf16[32,1024]{1,0:T(8,128)(2,1)S(1)}, u32[]{:S(2)}, u32[]{:S(2)}) collective-permute-start(bf16[32,1024]{1,0:T(8,128)(2,1)S(1)} %get-tuple-element.47), channel_id=1, source_target_pairs={{0,2},{1,3},{2,0},{3,1},{4,6},{5,7},{6,4},{7,5},{8,10},{9,11},{10,... | collective-permute-start | bytes 196616 | tf_op jit(solution)/shard_map/ppermute | solution.py:36
  7.7 3.9 %collective-permute-start = (bf16[16,1024]{1,0:T(8,128)(2,1)S(1)}, bf16[16,1024]{1,0:T(8,128)(2,1)S(1)}, u32[]{:S(2)}, u32[]{:S(2)}) collective-permute-start(bf16[16,1024]{1,0:T(8,128)(2,1)S(1)} %get-tuple-element.44), channel_id=1, source_target_pairs={{0,1},{1,0},{2,3},{3,2},{4,5},{5,4},{6,7},{7,6},{8,9},{9,8},{10,11... | collective-permute-start | bytes 98312 | tf_op jit(solution)/shard_map/ppermute | solution.py:36
  13.5 1.7 %collective-permute-start.4 = (bf16[40,4224]{1,0:T(8,128)(2,1)S(1)}, bf16[40,4224]{1,0:T(8,128)(2,1)S(1)}, u32[]{:S(2)}, u32[]{:S(2)}) collective-permute-start(bf16[40,4224]{1,0:T(8,128)(2,1)S(1)} %get-tuple-element.56), channel_id=1, source_target_pairs={{0,8},{8,0},{16,24},{24,16},{1,9},{9,1},{17,25},{25,17},{2,10},{10... | collective-permute-start | bytes 1013768 | tf_op jit(solution)/shard_map/ppermute | solution.py:36
  13.6 5.2 %collective-permute-start.9 = (bf16[48,1024]{1,0:T(8,128)(2,1)S(1)}, bf16[48,1024]{1,0:T(8,128)(2,1)S(1)}, u32[]{:S(2)}, u32[]{:S(2)}) collective-permute-start(bf16[48,1024]{1,0:T(8,128)(2,1)S(1)} %pad_maximum_fusion), channel_id=1, source_target_pairs={{0,1},{1,0},{2,3},{3,2},{4,5},{5,4},{6,7},{7,6},{8,9},{9,8},{10,11... | collective-permute-start | bytes 294920 | tf_op jit(solution)/shard_map/ppermute | solution.py:36
  15.3 8.6 %collective-permute-start.5 = (bf16[32,4224]{1,0:T(8,128)(2,1)S(1)}, bf16[32,4224]{1,0:T(8,128)(2,1)S(1)}, u32[]{:S(2)}, u32[]{:S(2)}) collective-permute-start(bf16[32,4224]{1,0:T(8,128)(2,1)S(1)} %get-tuple-element.59), channel_id=1, source_target_pairs={{0,16},{8,24},{16,0},{24,8},{1,17},{9,25},{17,1},{25,9},{2,18},{10... | collective-permute-start | bytes 811016 | tf_op jit(solution)/shard_map/ppermute | solution.py:36
  19.7 1.5 %collective-permute-start.10 = (bf16[24,4224]{1,0:T(8,128)(2,1)S(1)}, bf16[24,4224]{1,0:T(8,128)(2,1)S(1)}, u32[]{:S(2)}, u32[]{:S(2)}) collective-permute-start(bf16[24,4224]{1,0:T(8,128)(2,1)S(1)} %get-tuple-element.70), channel_id=1, source_target_pairs={{0,8},{8,0},{16,24},{24,16},{1,9},{9,1},{17,25},{25,17},{2,10},{10... | collective-permute-start | bytes 608264 | tf_op jit(solution)/shard_map/ppermute | solution.py:36
  21.2 7.4 %collective-permute-start.11 = (bf16[24,4224]{1,0:T(8,128)(2,1)S(1)}, bf16[24,4224]{1,0:T(8,128)(2,1)S(1)}, u32[]{:S(2)}, u32[]{:S(2)}) collective-permute-start(bf16[24,4224]{1,0:T(8,128)(2,1)S(1)} %get-tuple-element.72), channel_id=1, source_target_pairs={{0,16},{8,24},{16,0},{24,8},{1,17},{9,25},{17,1},{25,9},{2,18},{10... | collective-permute-start | bytes 608264 | tf_op jit(solution)/shard_map/ppermute | solution.py:36
  24.1 4.6 %collective-permute-start.6 = (bf16[32,4224]{1,0:T(8,128)(2,1)S(1)}, bf16[32,4224]{1,0:T(8,128)(2,1)S(1)}, u32[]{:S(2)}, u32[]{:S(2)}) collective-permute-start(bf16[32,4224]{1,0:T(8,128)(2,1)S(1)} %shard_map.106.mine_ref.refs_6_), channel_id=1, source_target_pairs={{0,8},{8,0},{16,24},{24,16},{1,9},{9,1},{17,25},{25,17},{2,10},{10... | collective-permute-start | bytes 811016 | tf_op jit(solution)/shard_map/ppermute | solution.py:36
  24.9 4.9 %collective-permute-start.7 = (bf16[8,4224]{1,0:T(8,128)(2,1)S(1)}, bf16[8,4224]{1,0:T(8,128)(2,1)S(1)}, u32[]{:S(2)}, u32[]{:S(2)}) collective-permute-start(bf16[8,4224]{1,0:T(8,128)(2,1)S(1)} %get-tuple-element.67), channel_id=1, source_target_pairs={{0,16},{8,24},{16,0},{24,8},{1,17},{9,25},{17,1},{25,9},{2,18},{10... | collective-permute-start | bytes 202760 | tf_op jit(solution)/shard_map/ppermute | solution.py:36
  28.7 1.5 %collective-permute-start.12 = (bf16[24,4224]{1,0:T(8,128)(2,1)S(1)}, bf16[24,4224]{1,0:T(8,128)(2,1)S(1)}, u32[]{:S(2)}, u32[]{:S(2)}) collective-permute-start(bf16[24,4224]{1,0:T(8,128)(2,1)S(1)} %shard_map.113.mine_ref.refs_10_), channel_id=1, source_target_pairs={{0,8},{8,0},{16,24},{24,16},{1,9},{9,1},{17,25},{25,17},{2,10},{10... | collective-permute-start | bytes 608264 | tf_op jit(solution)/shard_map/ppermute | solution.py:36
  29.9 2.6 %collective-permute-start.8 = (bf16[8,4224]{1,0:T(8,128)(2,1)S(1)}, bf16[8,4224]{1,0:T(8,128)(2,1)S(1)}, u32[]{:S(2)}, u32[]{:S(2)}) collective-permute-start(bf16[8,4224]{1,0:T(8,128)(2,1)S(1)} %shard_map.109.mine_ref.refs_8_), channel_id=1, source_target_pairs={{0,8},{8,0},{16,24},{24,16},{1,9},{9,1},{17,25},{25,17},{2,10},{10... | collective-permute-start | bytes 202760 | tf_op jit(solution)/shard_map/ppermute | solution.py:36
  30.8 4.3 %collective-permute-start.13 = (bf16[64,512]{1,0:T(8,128)(2,1)S(1)}, bf16[64,512]{1,0:T(8,128)(2,1)S(1)}, u32[]{:S(2)}, u32[]{:S(2)}) collective-permute-start(bf16[64,512]{1,0:T(8,128)(2,1)S(1)} %shard_map.114), channel_id=1, source_target_pairs={{0,1},{1,0},{2,3},{3,2},{4,5},{5,4},{6,7},{7,6},{8,9},{9,8},{10,11... | collective-permute-start | bytes 196616 | tf_op jit(solution)/shard_map/ppermute | solution.py:36
  35.2 7.3 %collective-permute-start.14 = (bf16[32,512]{1,0:T(8,128)(2,1)S(1)}, bf16[32,512]{1,0:T(8,128)(2,1)S(1)}, u32[]{:S(2)}, u32[]{:S(2)}) collective-permute-start(bf16[32,512]{1,0:T(8,128)(2,1)S(1)} %pad_maximum_fusion.1), channel_id=1, source_target_pairs={{0,6},{1,7},{2,4},{3,5},{4,2},{5,3},{6,0},{7,1},{8,14},{9,15},{10,... | collective-permute-start | bytes 98312 | tf_op jit(solution)/shard_map/ppermute | solution.py:36
  38.0 4.8 %collective-permute-start.15 = (bf16[32,512]{1,0:T(8,128)(2,1)S(1)}, bf16[32,512]{1,0:T(8,128)(2,1)S(1)}, u32[]{:S(2)}, u32[]{:S(2)}) collective-permute-start(bf16[32,512]{1,0:T(8,128)(2,1)S(1)} %pad_maximum_fusion.2), channel_id=1, source_target_pairs={{0,4},{1,5},{2,6},{3,7},{4,0},{5,1},{6,2},{7,3},{8,12},{9,13},{10,... | collective-permute-start | bytes 98312 | tf_op jit(solution)/shard_map/ppermute | solution.py:36
  38.0 4.8 %collective-permute-start.16 = (bf16[32,512]{1,0:T(8,128)(2,1)S(1)}, bf16[32,512]{1,0:T(8,128)(2,1)S(1)}, u32[]{:S(2)}, u32[]{:S(2)}) collective-permute-start(bf16[32,512]{1,0:T(8,128)(2,1)S(1)} %pad_maximum_fusion.3), channel_id=1, source_target_pairs={{0,2},{1,3},{2,0},{3,1},{4,6},{5,7},{6,4},{7,5},{8,10},{9,11},{10,... | collective-permute-start | bytes 98312 | tf_op jit(solution)/shard_map/ppermute | solution.py:36

commit v10 on v9

--- a/solution.py
+++ b/solution.py
@@ -38,7 +38,7 @@
 
 FAR_PRODUCTS_COST = 3 * 10**8
 FAR_DELTAS_COST = 8 * 10**8
-OWN_DELTAS_COST = 18 * 10**8
+OWN_DELTAS_COST = 11 * 10**8
 
 
 def after(values, marker):
@@ -80,24 +80,21 @@
     ]
     for copy in copies:
         copy.start()
-    copies[0].wait()
     pairs = ids_ref.shape[1]
     width = tokens_ref.shape[1]
     slot_count = owners * capacity
     me = lax.axis_index("expert")
-    ids = ids_ref[...]
-    named = ids == lax.broadcasted_iota(jnp.int32, (owners, pairs), 0)
     before = lax.broadcasted_iota(jnp.int32, (pairs, pairs), 0) < lax.broadcasted_iota(
         jnp.int32, (pairs, pairs), 1
     )
-    named = named.astype(jnp.float32)
-    counts = jnp.dot(
-        named.astype(jnp.bfloat16),
-        before.astype(jnp.float32).astype(jnp.bfloat16),
-        preferred_element_type=jnp.float32,
-    )
+    before = before.astype(jnp.float32).astype(jnp.bfloat16)
+    experts = lax.broadcasted_iota(jnp.int32, (owners, pairs), 0)
+    slots = lax.broadcasted_iota(jnp.int32, (slot_count, pairs), 0)
+    copies[0].wait()
+    ids = ids_ref[...]
+    named = (ids == experts).astype(jnp.float32)
+    counts = jnp.dot(named.astype(jnp.bfloat16), before, preferred_element_type=jnp.float32)
     rank = jnp.sum(named * counts, axis=0, keepdims=True).astype(jnp.int32)
-    slots = lax.broadcasted_iota(jnp.int32, (slot_count, pairs), 0)
     chosen = (slots == (ids ^ me) * capacity + rank).astype(jnp.float32)
     select = chosen.astype(jnp.bfloat16)
     chosen_ref[...] = select
@@ -130,7 +127,8 @@
 
 
 def turn_kernel(*refs):
-    for source, target in zip(refs[:2], refs[2:]):
+    half = len(refs) // 2
+    for source, target in zip(refs[:half], refs[half:]):
         target[...] = source[...].T
 
 
@@ -173,12 +171,18 @@
         at += part.shape[0]
 
 
-def deltas_kernel(sums_ref, received_ref, out_ref):
+def deltas_kernel(sums_ref, received_ref, *out_refs):
     hidden_units = sums_ref.shape[1] // 3
     cols = [slice(i * hidden_units, (i + 1) * hidden_units) for i in range(3)]
     parts = [sums_ref[:, c] + received_ref[:, c].astype(jnp.float32) for c in cols]
-    for c, part in zip(cols, local_deltas(*parts)):
-        out_ref[:, c] = part
+    hidden, gate_delta, up_delta = local_deltas(*parts)
+    if len(out_refs) == 1:
+        values = [hidden, gate_delta, up_delta]
+    else:
+        out_refs[0][...] = hidden
+        values = [gate_delta, up_delta]
+    for c, value in zip(cols, values):
+        out_refs[-1][:, c] = value
 
 
 def in_order(core, mine, other):
@@ -190,7 +194,7 @@
 def slot_grad_rows(mine_ref, other_ref, gate_ref, up_ref):
     hidden_units = gate_ref.shape[0]
     rows = in_order(lax.axis_index("dp") % 2, mine_ref[...], other_ref[...])
-    by_gate, by_up = rows[:, hidden_units:2 * hidden_units], rows[:, 2 * hidden_units:]
+    by_gate, by_up = rows[:, -2 * hidden_units:-hidden_units], rows[:, -hidden_units:]
     return (
         jnp.dot(by_gate, gate_ref[...], preferred_element_type=jnp.float32)
         + jnp.dot(by_up, up_ref[...], preferred_element_type=jnp.float32)
@@ -214,7 +218,7 @@
     outs = len(names)
     *in_refs, rows_ref, deltas_ref, sems = refs
     in_refs, out_refs, tile_refs = in_refs[:-2 * outs], in_refs[-2 * outs:-outs], in_refs[-outs:]
-    row_refs, delta_refs = in_refs[:-6], in_refs[-6:]
+    row_refs, delta_refs = in_refs[:-8], in_refs[-8:]
     width = rows_ref.shape[1] // 2
     hidden_units = deltas_ref.shape[1] // 3
     core = lax.axis_index("dp") % 2
@@ -226,8 +230,12 @@
 
     def gather_deltas(cols):
         at = 0
-        for mine, other in zip(delta_refs[::2], delta_refs[1::2]):
-            both = in_order(core, mine[:, cols], other[:, cols])
+        for place in range(3):
+            mine, other, of = *delta_refs[2 * place:2 * place + 2], cols
+            if place == 2 and cols.start:
+                mine, other = delta_refs[6:]
+                of = slice(cols.start - hidden_units, cols.stop - hidden_units)
+            both = in_order(core, mine[:, of], other[:, of])
             deltas_ref[at:at + both.shape[0], cols] = both
             at += both.shape[0]
 
@@ -282,7 +290,8 @@
     block = own_ref.shape[0]
     rows = [own_ref[...], from_pair_ref[:block]] + [ref[...] for ref in reversed(group_refs)]
     returned = jnp.concatenate(rows, axis=0)
-    out_ref[...] = contract_rows(chosen_ref[...], returned).astype(jnp.bfloat16)
+    out = jnp.dot(chosen_ref[...], returned, preferred_element_type=jnp.float32)
+    out_ref[...] = out.astype(jnp.bfloat16)
 
 
 def body_by_all_to_all(tokens, cotangent, expert_ids, route_weights, gate_weight, up_weight, down_weight):
@@ -437,11 +446,25 @@
     near_sums, far_sums = exchanged(*near_sums), exchanged(*far_sums)
 
     near_mine = deltas_of(*near_sums, 1)
-    turned = call(turn_kernel, (shape(hidden_units, width),) * 2, *after((gate, up), near_mine))
+    *turned, chosen = call(
+        turn_kernel,
+        (shape(hidden_units, width),) * 2 + (shape(tok_rows, slot_count),),
+        *after((gate, up, chosen), near_mine),
+    )
     own_sums = exchanged(own_sums[0], after(own_sums[1], turned[0]))
     near_deltas = near_mine, swap(near_mine, 1)
-    far_mine = after(deltas_of(*far_sums, FAR_DELTAS_COST), near_deltas[1])
+    part = far_sums[0].shape[0]
+    far_hidden, far_mine = after(
+        call(
+            deltas_kernel,
+            (shape(part, hidden_units), shape(part, 2 * hidden_units)),
+            *far_sums,
+            cost=FAR_DELTAS_COST,
+        ),
+        near_deltas[1],
+    )
     far_deltas = far_mine, swap(far_mine, 1)
+    hidden_pair = far_hidden, swap(far_hidden, 1)
     block = shape(capacity, width)
     grads = call(slot_grad_kernel, (block,) * half, *near_deltas, *turned)
     own_mine = deltas_of(after(own_sums[0], grads[0]), own_sums[1], OWN_DELTAS_COST)
@@ -454,17 +477,19 @@
         *turned,
         grads[-1],
     )
-    deltas = near_deltas + own_deltas + far_deltas
+    without_hidden = near_deltas + own_deltas + far_deltas + far_deltas
+    deltas = near_deltas + own_deltas + hidden_pair + far_deltas
 
     returned_pair = swap(to_pair, 1, "expert")
-    sizes = (width, hidden_units, slot_count, (*near, own, by_pair, *deltas))
-    (gate_grad,) = weight_grads(("gate",), *sizes)
+    rows = (*near, own, by_pair)
+    sizes = (width, hidden_units, slot_count)
+    (gate_grad,) = weight_grads(("gate",), *sizes, (*rows, *without_hidden))
     returned_pair = after(returned_pair, (gate_grad, own_grad))
     returned = {}
     for place, j in enumerate(far_first[1:], 1):
         more = returned_pair[place * capacity:(place + 1) * capacity]
         returned[j] = swap(jnp.concatenate([grads[place - 1], more], axis=0), 2 * j, "expert")
-    up_grad, down_grad = weight_grads(("up", "down"), *sizes)
+    up_grad, down_grad = weight_grads(("up", "down"), *sizes, (*rows, *deltas))
     token_grad = call(
         token_grad_kernel,
         shape(tok_rows, width),

time: 43.8 us -> 43.7 us (level)
    ppermute x17 -> x18, waiting for transfers between devices: 8.84 us -> 8.77 us  [swap(): return lax.ppermute(value, axis, [(i, i ^ bit) for i in range(size)])]
    ppermute x17 -> x18, starting transfers between devices: 20.2 us -> 20.2 us  [swap(): return lax.ppermute(value, axis, [(i, i ^ bit) for i in range(size)])]
  transfers between devices with their start and end apart: 17 -> 18, of which waited for: 9 -> 9; matrix products, arithmetic and copies ran while one was open for 0% -> 0% of each run, Pallas kernels for 25% -> 25%
where the time goes in v10:
time: 43.7 us; the launch traced here: 43.6 us
  starting transfers between devices  20.2 us (46%)
  Pallas kernels  13.7 us (31%)
  waiting for transfers between devices  8.77 us (20%)
  between operations  0.84 us (2%)
    ppermute x18, starting transfers between devices, swap(): return lax.ppermute(value, axis, [(i, i ^ bit) for i in range(size)])  20.2 us
    pallas_call x14, Pallas kernels, call(): pl.pallas_call(kernel, out_shape=outs, in_specs=[pl.BlockSpec(memory_spac...  8.9 us
    ppermute x18, waiting for transfers between devices, swap(): return lax.ppermute(value, axis, [(i, i ^ bit) for i in range(size)])  8.77 us
    pallas_call x2, Pallas kernels, weight_grads(): pl.pallas_call(functools.partial(weight_grads_kernel, names, tiles), out_...  4.79 us
  transfers between devices with their start and end apart: 18, of which 9 were waited for; matrix products, arithmetic and copies ran while one was open for 0% of the time, Pallas kernels for 25%

profile of v10, /device:TPU:0, one launch (start us, length us, event | category | flops | bytes accessed | tf_op | source)
XLA Modules:
  0.0 43.6 jit_solution(3172754664149999272)
XLA Ops:
  0.6 1.3 %shard_map.102 = (bf16[128,128]{1,0:T(8,128)(2,1)S(1)}, bf16[16,1024]{1,0:T(8,128)(2,1)S(1)}, bf16[16,1024]{1,0:T(8,128)(2,1)S(1)}, bf16[32,1024]{1,0:T(8,128)(2...) custom-call(s32[1,128]{1,0:T(1,128)} %bitcast.12, f32[1,128]{1,0:T(1,128)} %bitcast.13, ...), custom_call_target="tpu_custom_call" | custom-call | flops 1 | bytes 1 | tf_op jit(solution)/shard_map/pallas_call | solution.py:54
  1.9 5.1 %collective-permute-start.1 = (bf16[32,1024]{1,0:T(8,128)(2,1)S(1)}, bf16[32,1024]{1,0:T(8,128)(2,1)S(1)}, u32[]{:S(2)}, u32[]{:S(2)}) collective-permute-start(bf16[32,1024]{1,0:T(8,128)(2,1)S(1)} %get-tuple-element.52), channel_id=1, source_target_pairs={{0,6},{1,7},{2,4},{3,5},{4,2},{5,3},{6,0},{7,1},{8,14},{9,15},{10,... | collective-permute-start | bytes 196616 | tf_op jit(solution)/shard_map/ppermute | solution.py:36
  7.0 0.6 %collective-permute-start.3 = (bf16[32,1024]{1,0:T(8,128)(2,1)S(1)}, bf16[32,1024]{1,0:T(8,128)(2,1)S(1)}, u32[]{:S(2)}, u32[]{:S(2)}) collective-permute-start(bf16[32,1024]{1,0:T(8,128)(2,1)S(1)} %get-tuple-element.54), channel_id=1, source_target_pairs={{0,2},{1,3},{2,0},{3,1},{4,6},{5,7},{6,4},{7,5},{8,10},{9,11},{10,... | collective-permute-start | bytes 196616 | tf_op jit(solution)/shard_map/ppermute | solution.py:36
  7.7 1.7 %collective-permute-start = (bf16[16,1024]{1,0:T(8,128)(2,1)S(1)}, bf16[16,1024]{1,0:T(8,128)(2,1)S(1)}, u32[]{:S(2)}, u32[]{:S(2)}) collective-permute-start(bf16[16,1024]{1,0:T(8,128)(2,1)S(1)} %get-tuple-element.51), channel_id=1, source_target_pairs={{0,1},{1,0},{2,3},{3,2},{4,5},{5,4},{6,7},{7,6},{8,9},{9,8},{10,11... | collective-permute-start | bytes 98312 | tf_op jit(solution)/shard_map/ppermute | solution.py:36
  9.3 2.3 %shard_map.103 = (bf16[512,1408]{1,0:T(8,128)(2,1)S(1)}, bf16[512,1408]{1,0:T(8,128)(2,1)S(1)}, bf16[512,1408]{1,0:T(8,128)(2,1)S(1)}) custom-call(bf16[1408,512]{1,0:T(8,128)(2,1)} %bitcast.9, bf16[512,1408]{1,0:T(8,128)(2,1)} %bitcast.10, bf16[512,1408]{1,0:T(8,128)(2,1)} %bitcast.11, bf16[128,128]{1,0:T(8,128)(2,1)S(1)} %get-tuple-element.66.marker_hbm.refs_2_), custom_call_target="tpu_custom_call" | custom-call | flops 10000000 | bytes 10000000 | tf_op jit(solution)/shard_map/pallas_call | solution.py:54
  11.6 1.0 %collective-permute-done.2.refs_2_ = bf16[32,1024]{1,0:T(8,128)(2,1)S(1)} collective-permute-done((bf16[32,1024]{1,0:T(8,128)(2,1)S(1)}, bf16[32,1024]{1,0:T(8,128)(2,1)S(1)}, u32[]{:S(2)}, u32[]{:S(2)}) %collective-permute-start.2) | collective-permute-done | bytes 65568 | tf_op jit(solution)/shard_map/ppermute | solution.py:36
  12.6 0.8 %shard_map.104 = (f32[40,4224]{1,0:T(8,128)S(1)}, bf16[40,4224]{1,0:T(8,128)(2,1)S(1)}) custom-call(bf16[16,1024]{1,0:T(8,128)(2,1)S(1)} %collective-permute-done.refs_0_, bf16[32,1024]{1,0:T(8,128)(2,1)S(1)} %collective-permute-done.1.refs_1_, bf16[32,1024]{1,0:T(8,128)(2,1)S(1)} %collective-permute-done.2.refs_2_, ...), custom_call_target="tpu_custom_call" | custom-call | flops 1 | bytes 1 | tf_op jit(solution)/shard_map/pallas_call | solution.py:54
  13.6 1.6 %collective-permute-start.9 = (bf16[48,1024]{1,0:T(8,128)(2,1)S(1)}, bf16[48,1024]{1,0:T(8,128)(2,1)S(1)}, u32[]{:S(2)}, u32[]{:S(2)}) collective-permute-start(bf16[48,1024]{1,0:T(8,128)(2,1)S(1)} %pad_maximum_fusion), channel_id=1, source_target_pairs={{0,1},{1,0},{2,3},{3,2},{4,5},{5,4},{6,7},{7,6},{8,9},{9,8},{10,11... | collective-permute-start | bytes 294920 | tf_op jit(solution)/shard_map/ppermute | solution.py:36
  15.3 1.6 %collective-permute-start.5 = (bf16[32,4224]{1,0:T(8,128)(2,1)S(1)}, bf16[32,4224]{1,0:T(8,128)(2,1)S(1)}, u32[]{:S(2)}, u32[]{:S(2)}) collective-permute-start(bf16[32,4224]{1,0:T(8,128)(2,1)S(1)} %get-tuple-element.63), channel_id=1, source_target_pairs={{0,16},{8,24},{16,0},{24,8},{1,17},{9,25},{17,1},{25,9},{2,18},{10... | collective-permute-start | bytes 811016 | tf_op jit(solution)/shard_map/ppermute | solution.py:36
  16.8 2.0 %collective-permute-done.9.refs_0_.refs_5_ = bf16[48,1024]{1,0:T(8,128)(2,1)S(1)} collective-permute-done((bf16[48,1024]{1,0:T(8,128)(2,1)S(1)}, bf16[48,1024]{1,0:T(8,128)(2,1)S(1)}, u32[]{:S(2)}, u32[]{:S(2)}) %collective-permute-start.9) | collective-permute-done | bytes 98336 | tf_op jit(solution)/shard_map/ppermute | solution.py:36
  18.8 0.8 %shard_map.111 = (f32[24,4224]{1,0:T(8,128)S(1)}, bf16[24,4224]{1,0:T(8,128)(2,1)S(1)}) custom-call(bf16[48,1024]{1,0:T(8,128)(2,1)S(1)} %collective-permute-done.9.refs_0_.refs_5_, bf16[512,1408]{1,0:T(8,128)(2,1)S(1)} %get-tuple-element.64.refs_5_.refs_0_.refs_1_, bf16[512,1408]{1,0:T(8,128)(2,1)S(1)} %get-tuple-element.65.refs_6_.refs_1_.refs_2_, ...), custom_call_target="tpu_custom_call" | custom-call | flops 300000000 | bytes 300000000 | tf_op jit(solution)/shard_map/pallas_call | solution.py:54
  19.7 1.4 %collective-permute-done.10.received_ref = bf16[24,4224]{1,0:T(8,128)(2,1)S(1)} collective-permute-done((bf16[24,4224]{1,0:T(8,128)(2,1)S(1)}, bf16[24,4224]{1,0:T(8,128)(2,1)S(1)}, u32[]{:S(2)}, u32[]{:S(2)}) %collective-permute-start.10) | collective-permute-done | bytes 202784 | tf_op jit(solution)/shard_map/ppermute | solution.py:36
  21.2 1.6 %collective-permute-start.11 = (bf16[24,4224]{1,0:T(8,128)(2,1)S(1)}, bf16[24,4224]{1,0:T(8,128)(2,1)S(1)}, u32[]{:S(2)}, u32[]{:S(2)}) collective-permute-start(bf16[24,4224]{1,0:T(8,128)(2,1)S(1)} %get-tuple-element.79), channel_id=1, source_target_pairs={{0,16},{8,24},{16,0},{24,8},{1,17},{9,25},{17,1},{25,9},{2,18},{10... | collective-permute-start | bytes 608264 | tf_op jit(solution)/shard_map/ppermute | solution.py:36
  22.8 1.1 %collective-permute-done.5.received_ref = bf16[32,4224]{1,0:T(8,128)(2,1)S(1)} collective-permute-done((bf16[32,4224]{1,0:T(8,128)(2,1)S(1)}, bf16[32,4224]{1,0:T(8,128)(2,1)S(1)}, u32[]{:S(2)}, u32[]{:S(2)}) %collective-permute-start.5) | collective-permute-done | bytes 270368 | tf_op jit(solution)/shard_map/ppermute | solution.py:36
  24.1 0.8 %shard_map.107 = (bf16[1408,512]{1,0:T(8,128)(2,1)S(1)}, bf16[1408,512]{1,0:T(8,128)(2,1)S(1)}, bf16[128,128]{1,0:T(8,128)(2,1)S(1)}) custom-call(bf16[512,1408]{1,0:T(8,128)(2,1)S(1)} %get-tuple-element.64.refs_5_.refs_0_.refs_1_, bf16[512,1408]{1,0:T(8,128)(2,1)S(1)} %get-tuple-element.65.refs_6_.refs_1_.refs_2_, ...), custom_call_target="tpu_custom_call" | custom-call | flops 1 | bytes 1 | tf_op jit(solution)/shard_map/pallas_call | solution.py:54
  25.0 1.6 %collective-permute-start.7 = (bf16[8,4224]{1,0:T(8,128)(2,1)S(1)}, bf16[8,4224]{1,0:T(8,128)(2,1)S(1)}, u32[]{:S(2)}, u32[]{:S(2)}) collective-permute-start(bf16[8,4224]{1,0:T(8,128)(2,1)S(1)} %get-tuple-element.74), channel_id=1, source_target_pairs={{0,16},{8,24},{16,0},{24,8},{1,17},{9,25},{17,1},{25,9},{2,18},{10... | collective-permute-start | bytes 202760 | tf_op jit(solution)/shard_map/ppermute | solution.py:36
  26.5 2.1 %collective-permute-done.11.received_ref = bf16[24,4224]{1,0:T(8,128)(2,1)S(1)} collective-permute-done((bf16[24,4224]{1,0:T(8,128)(2,1)S(1)}, bf16[24,4224]{1,0:T(8,128)(2,1)S(1)}, u32[]{:S(2)}, u32[]{:S(2)}) %collective-permute-start.11) | collective-permute-done | bytes 202784 | tf_op jit(solution)/shard_map/ppermute | solution.py:36
  28.8 0.6 %shard_map.108 = (bf16[16,512]{1,0:T(8,128)(2,1)S(1)}, bf16[16,512]{1,0:T(8,128)(2,1)S(1)}, bf16[16,512]{1,0:T(8,128)(2,1)S(1)}, bf16[16,512]{1,0:T(8,128)(2,1)S(1)}) custom-call(bf16[32,4224]{1,0:T(8,128)(2,1)S(1)} %shard_map.106.mine_ref.refs_6_, bf16[32,4224]{1,0:T(8,128)(2,1)S(1)} %collective-permute-done.6.other_ref.refs_7_, ...), custom_call_target="tpu_custom_call" | custom-call | flops 1 | bytes 1 | tf_op jit(solution)/shard_map/pallas_call | solution.py:54
  30.7 1.7 %collective-permute-start.13 = (bf16[64,512]{1,0:T(8,128)(2,1)S(1)}, bf16[64,512]{1,0:T(8,128)(2,1)S(1)}, u32[]{:S(2)}, u32[]{:S(2)}) collective-permute-start(bf16[64,512]{1,0:T(8,128)(2,1)S(1)} %shard_map.114), channel_id=1, source_target_pairs={{0,1},{1,0},{2,3},{3,2},{4,5},{5,4},{6,7},{7,6},{8,9},{9,8},{10,11... | collective-permute-start | bytes 196616 | tf_op jit(solution)/shard_map/ppermute | solution.py:36
  32.9 1.9 %shard_map.115 = f32[512,1408]{1,0:T(8,128)} custom-call(bf16[16,1024]{1,0:T(8,128)(2,1)S(1)} %collective-permute-done.refs_0_, bf16[32,1024]{1,0:T(8,128)(2,1)S(1)} %collective-permute-done.1.refs_1_, bf16[32,1024]{1,0:T(8,128)(2,1)S(1)} %collective-permute-done.2.refs_2_, bf16[32,1024]{1,0:T(8,128)(2,1)S(1)} %collective-permute-done.3.refs_3_, ...), custom_call_target="tpu_custom_call" | custom-call | flops 10000000 | bytes 10000000 | tf_op jit(solution)/shard_map/pallas_call | solution.py:272
  35.1 2.8 %collective-permute-start.14 = (bf16[32,512]{1,0:T(8,128)(2,1)S(1)}, bf16[32,512]{1,0:T(8,128)(2,1)S(1)}, u32[]{:S(2)}, u32[]{:S(2)}) collective-permute-start(bf16[32,512]{1,0:T(8,128)(2,1)S(1)} %pad_maximum_fusion.1), channel_id=1, source_target_pairs={{0,6},{1,7},{2,4},{3,5},{4,2},{5,3},{6,0},{7,1},{8,14},{9,15},{10,... | collective-permute-start | bytes 98312 | tf_op jit(solution)/shard_map/ppermute | solution.py:36
  37.9 1.7 %collective-permute-start.16 = (bf16[32,512]{1,0:T(8,128)(2,1)S(1)}, bf16[32,512]{1,0:T(8,128)(2,1)S(1)}, u32[]{:S(2)}, u32[]{:S(2)}) collective-permute-start(bf16[32,512]{1,0:T(8,128)(2,1)S(1)} %pad_maximum_fusion.3), channel_id=1, source_target_pairs={{0,2},{1,3},{2,0},{3,1},{4,6},{5,7},{6,4},{7,5},{8,10},{9,11},{10,... | collective-permute-start | bytes 98312 | tf_op jit(solution)/shard_map/ppermute | solution.py:36
  39.6 2.9 %shard_map.117 = (f32[512,1408]{1,0:T(8,128)}, f32[1408,512]{1,0:T(8,128)}) custom-call(bf16[16,1024]{1,0:T(8,128)(2,1)S(1)} %collective-permute-done.refs_0_, bf16[32,1024]{1,0:T(8,128)(2,1)S(1)} %collective-permute-done.1.refs_1_, bf16[32,1024]{1,0:T(8,128)(2,1)S(1)} %collective-permute-done.2.refs_2_, ...), custom_call_target="tpu_custom_call" | custom-call | flops 10000000 | bytes 10000000 | tf_op jit(solution)/shard_map/pallas_call | solution.py:272
  42.7 0.8 %shard_map.116 = bf16[128,512]{1,0:T(8,128)(2,1)} custom-call(bf16[128,128]{1,0:T(8,128)(2,1)S(1)} %get-tuple-element.67.chosen_ref, bf16[16,512]{1,0:T(8,128)(2,1)S(1)} %shard_map.110.own_ref, bf16[64,512]{1,0:T(8,128)(2,1)S(1)} %collective-permute-done.13.from_pair_ref, bf16[32,512]{1,0:T(8,128)(2,1)S(1)} %collective-permute-done.14.refs_0_, ...), custom_call_target="tpu_custom_call" | custom-call | flops 1 | bytes 1 | tf_op jit(solution)/shard_map/pallas_call | solution.py:54
  (36 shorter events, 3.1 us)
Async XLA Ops:
  1.9 9.7 %collective-permute-start.1 = (bf16[32,1024]{1,0:T(8,128)(2,1)S(1)}, bf16[32,1024]{1,0:T(8,128)(2,1)S(1)}, u32[]{:S(2)}, u32[]{:S(2)}) collective-permute-start(bf16[32,1024]{1,0:T(8,128)(2,1)S(1)} %get-tuple-element.52), channel_id=1, source_target_pairs={{0,6},{1,7},{2,4},{3,5},{4,2},{5,3},{6,0},{7,1},{8,14},{9,15},{10,... | collective-permute-start | bytes 196616 | tf_op jit(solution)/shard_map/ppermute | solution.py:36
  7.0 5.6 %collective-permute-start.2 = (bf16[32,1024]{1,0:T(8,128)(2,1)S(1)}, bf16[32,1024]{1,0:T(8,128)(2,1)S(1)}, u32[]{:S(2)}, u32[]{:S(2)}) collective-permute-start(bf16[32,1024]{1,0:T(8,128)(2,1)S(1)} %get-tuple-element.53), channel_id=1, source_target_pairs={{0,4},{1,5},{2,6},{3,7},{4,0},{5,1},{6,2},{7,3},{8,12},{9,13},{10,... | collective-permute-start | bytes 196616 | tf_op jit(solution)/shard_map/ppermute | solution.py:36
  7.0 5.6 %collective-permute-start.3 = (bf16[32,1024]{1,0:T(8,128)(2,1)S(1)}, bf16[32,1024]{1,0:T(8,128)(2,1)S(1)}, u32[]{:S(2)}, u32[]{:S(2)}) collective-permute-start(bf16[32,1024]{1,0:T(8,128)(2,1)S(1)} %get-tuple-element.54), channel_id=1, source_target_pairs={{0,2},{1,3},{2,0},{3,1},{4,6},{5,7},{6,4},{7,5},{8,10},{9,11},{10,... | collective-permute-start | bytes 196616 | tf_op jit(solution)/shard_map/ppermute | solution.py:36
  7.7 3.9 %collective-permute-start = (bf16[16,1024]{1,0:T(8,128)(2,1)S(1)}, bf16[16,1024]{1,0:T(8,128)(2,1)S(1)}, u32[]{:S(2)}, u32[]{:S(2)}) collective-permute-start(bf16[16,1024]{1,0:T(8,128)(2,1)S(1)} %get-tuple-element.51), channel_id=1, source_target_pairs={{0,1},{1,0},{2,3},{3,2},{4,5},{5,4},{6,7},{7,6},{8,9},{9,8},{10,11... | collective-permute-start | bytes 98312 | tf_op jit(solution)/shard_map/ppermute | solution.py:36
  13.5 1.7 %collective-permute-start.4 = (bf16[40,4224]{1,0:T(8,128)(2,1)S(1)}, bf16[40,4224]{1,0:T(8,128)(2,1)S(1)}, u32[]{:S(2)}, u32[]{:S(2)}) collective-permute-start(bf16[40,4224]{1,0:T(8,128)(2,1)S(1)} %get-tuple-element.61), channel_id=1, source_target_pairs={{0,8},{8,0},{16,24},{24,16},{1,9},{9,1},{17,25},{25,17},{2,10},{10... | collective-permute-start | bytes 1013768 | tf_op jit(solution)/shard_map/ppermute | solution.py:36
  13.6 5.2 %collective-permute-start.9 = (bf16[48,1024]{1,0:T(8,128)(2,1)S(1)}, bf16[48,1024]{1,0:T(8,128)(2,1)S(1)}, u32[]{:S(2)}, u32[]{:S(2)}) collective-permute-start(bf16[48,1024]{1,0:T(8,128)(2,1)S(1)} %pad_maximum_fusion), channel_id=1, source_target_pairs={{0,1},{1,0},{2,3},{3,2},{4,5},{5,4},{6,7},{7,6},{8,9},{9,8},{10,11... | collective-permute-start | bytes 294920 | tf_op jit(solution)/shard_map/ppermute | solution.py:36
  15.3 8.6 %collective-permute-start.5 = (bf16[32,4224]{1,0:T(8,128)(2,1)S(1)}, bf16[32,4224]{1,0:T(8,128)(2,1)S(1)}, u32[]{:S(2)}, u32[]{:S(2)}) collective-permute-start(bf16[32,4224]{1,0:T(8,128)(2,1)S(1)} %get-tuple-element.63), channel_id=1, source_target_pairs={{0,16},{8,24},{16,0},{24,8},{1,17},{9,25},{17,1},{25,9},{2,18},{10... | collective-permute-start | bytes 811016 | tf_op jit(solution)/shard_map/ppermute | solution.py:36
  19.7 1.5 %collective-permute-start.10 = (bf16[24,4224]{1,0:T(8,128)(2,1)S(1)}, bf16[24,4224]{1,0:T(8,128)(2,1)S(1)}, u32[]{:S(2)}, u32[]{:S(2)}) collective-permute-start(bf16[24,4224]{1,0:T(8,128)(2,1)S(1)} %get-tuple-element.77), channel_id=1, source_target_pairs={{0,8},{8,0},{16,24},{24,16},{1,9},{9,1},{17,25},{25,17},{2,10},{10... | collective-permute-start | bytes 608264 | tf_op jit(solution)/shard_map/ppermute | solution.py:36
  21.2 7.3 %collective-permute-start.11 = (bf16[24,4224]{1,0:T(8,128)(2,1)S(1)}, bf16[24,4224]{1,0:T(8,128)(2,1)S(1)}, u32[]{:S(2)}, u32[]{:S(2)}) collective-permute-start(bf16[24,4224]{1,0:T(8,128)(2,1)S(1)} %get-tuple-element.79), channel_id=1, source_target_pairs={{0,16},{8,24},{16,0},{24,8},{1,17},{9,25},{17,1},{25,9},{2,18},{10... | collective-permute-start | bytes 608264 | tf_op jit(solution)/shard_map/ppermute | solution.py:36
  24.1 4.6 %collective-permute-start.6 = (bf16[32,4224]{1,0:T(8,128)(2,1)S(1)}, bf16[32,4224]{1,0:T(8,128)(2,1)S(1)}, u32[]{:S(2)}, u32[]{:S(2)}) collective-permute-start(bf16[32,4224]{1,0:T(8,128)(2,1)S(1)} %shard_map.106.mine_ref.refs_6_), channel_id=1, source_target_pairs={{0,8},{8,0},{16,24},{24,16},{1,9},{9,1},{17,25},{25,17},{2,10},{10... | collective-permute-start | bytes 811016 | tf_op jit(solution)/shard_map/ppermute | solution.py:36
  25.0 4.9 %collective-permute-start.7 = (bf16[8,4224]{1,0:T(8,128)(2,1)S(1)}, bf16[8,4224]{1,0:T(8,128)(2,1)S(1)}, u32[]{:S(2)}, u32[]{:S(2)}) collective-permute-start(bf16[8,4224]{1,0:T(8,128)(2,1)S(1)} %get-tuple-element.74), channel_id=1, source_target_pairs={{0,16},{8,24},{16,0},{24,8},{1,17},{9,25},{17,1},{25,9},{2,18},{10... | collective-permute-start | bytes 202760 | tf_op jit(solution)/shard_map/ppermute | solution.py:36
  28.7 1.4 %collective-permute-start.12 = (bf16[24,2816]{1,0:T(8,128)(2,1)S(1)}, bf16[24,2816]{1,0:T(8,128)(2,1)S(1)}, u32[]{:S(2)}, u32[]{:S(2)}) collective-permute-start(bf16[24,2816]{1,0:T(8,128)(2,1)S(1)} %get-tuple-element.83.mine_ref.refs_10_.refs_12_), channel_id=1, source_target_pairs={{0,8},{8,0},{16,24},{24,16},{1,9},{9,1},{17,25},{25,17},{2,10},{10... | collective-permute-start | bytes 405512 | tf_op jit(solution)/shard_map/ppermute | solution.py:36
  29.9 2.5 %collective-permute-start.8 = (bf16[8,4224]{1,0:T(8,128)(2,1)S(1)}, bf16[8,4224]{1,0:T(8,128)(2,1)S(1)}, u32[]{:S(2)}, u32[]{:S(2)}) collective-permute-start(bf16[8,4224]{1,0:T(8,128)(2,1)S(1)} %shard_map.109.mine_ref.refs_8_), channel_id=1, source_target_pairs={{0,8},{8,0},{16,24},{24,16},{1,9},{9,1},{17,25},{25,17},{2,10},{10... | collective-permute-start | bytes 202760 | tf_op jit(solution)/shard_map/ppermute | solution.py:36
  30.7 4.4 %collective-permute-start.13 = (bf16[64,512]{1,0:T(8,128)(2,1)S(1)}, bf16[64,512]{1,0:T(8,128)(2,1)S(1)}, u32[]{:S(2)}, u32[]{:S(2)}) collective-permute-start(bf16[64,512]{1,0:T(8,128)(2,1)S(1)} %shard_map.114), channel_id=1, source_target_pairs={{0,1},{1,0},{2,3},{3,2},{4,5},{5,4},{6,7},{7,6},{8,9},{9,8},{10,11... | collective-permute-start | bytes 196616 | tf_op jit(solution)/shard_map/ppermute | solution.py:36
  32.4 7.2 %collective-permute-start.17 = (bf16[24,1408]{1,0:T(8,128)(2,1)S(1)}, bf16[24,1408]{1,0:T(8,128)(2,1)S(1)}, u32[]{:S(2)}, u32[]{:S(2)}) collective-permute-start(bf16[24,1408]{1,0:T(8,128)(2,1)S(1)} %get-tuple-element.89.refs_10_), channel_id=1, source_target_pairs={{0,8},{8,0},{16,24},{24,16},{1,9},{9,1},{17,25},{25,17},{2,10},{10... | collective-permute-start | bytes 202760 | tf_op jit(solution)/shard_map/ppermute | solution.py:36
  35.1 7.3 %collective-permute-start.14 = (bf16[32,512]{1,0:T(8,128)(2,1)S(1)}, bf16[32,512]{1,0:T(8,128)(2,1)S(1)}, u32[]{:S(2)}, u32[]{:S(2)}) collective-permute-start(bf16[32,512]{1,0:T(8,128)(2,1)S(1)} %pad_maximum_fusion.1), channel_id=1, source_target_pairs={{0,6},{1,7},{2,4},{3,5},{4,2},{5,3},{6,0},{7,1},{8,14},{9,15},{10,... | collective-permute-start | bytes 98312 | tf_op jit(solution)/shard_map/ppermute | solution.py:36
  37.9 4.8 %collective-permute-start.15 = (bf16[32,512]{1,0:T(8,128)(2,1)S(1)}, bf16[32,512]{1,0:T(8,128)(2,1)S(1)}, u32[]{:S(2)}, u32[]{:S(2)}) collective-permute-start(bf16[32,512]{1,0:T(8,128)(2,1)S(1)} %pad_maximum_fusion.2), channel_id=1, source_target_pairs={{0,4},{1,5},{2,6},{3,7},{4,0},{5,1},{6,2},{7,3},{8,12},{9,13},{10,... | collective-permute-start | bytes 98312 | tf_op jit(solution)/shard_map/ppermute | solution.py:36
  37.9 4.8 %collective-permute-start.16 = (bf16[32,512]{1,0:T(8,128)(2,1)S(1)}, bf16[32,512]{1,0:T(8,128)(2,1)S(1)}, u32[]{:S(2)}, u32[]{:S(2)}) collective-permute-start(bf16[32,512]{1,0:T(8,128)(2,1)S(1)} %pad_maximum_fusion.3), channel_id=1, source_target_pairs={{0,2},{1,3},{2,0},{3,1},{4,6},{5,7},{6,4},{7,5},{8,10},{9,11},{10,... | collective-permute-start | bytes 98312 | tf_op jit(solution)/shard_map/ppermute | solution.py:36

commit v11 on v10

--- a/solution.py
+++ b/solution.py
@@ -214,75 +214,84 @@
     out_ref[block:] = slot_grad_rows(mine_ref, other_ref, gate_ref, up_ref)
 
 
-def weight_grads_kernel(names, tiles, *refs):
-    outs = len(names)
-    *in_refs, rows_ref, deltas_ref, sems = refs
-    in_refs, out_refs, tile_refs = in_refs[:-2 * outs], in_refs[-2 * outs:-outs], in_refs[-outs:]
-    row_refs, delta_refs = in_refs[:-8], in_refs[-8:]
+def gather_deltas(target_ref, delta_refs, cols):
+    core = lax.axis_index("dp") % 2
+    at = 0
+    for mine, other, of in zip(delta_refs[::2], delta_refs[1::2], cols):
+        both = in_order(core, mine[:, of], other[:, of])
+        target_ref[at:at + both.shape[0]] = both
+        at += both.shape[0]
+
+
+def send_tiles(left, right, tile, tile_ref, out_ref, sems, copies, start=0, stop=None):
+    stop = stop or out_ref.shape[0]
+    for at in range(start, stop, tile):
+        rows = min(tile, stop - at)
+        tile_ref[at:at + rows] = contract_rows(left[:, at:at + rows], right)
+        span = pl.ds(at, rows)
+        copies.append(
+            pltpu.make_async_copy(tile_ref.at[span], out_ref.at[span], sems.at[len(copies)])
+        )
+        copies[-1].start()
+
+
+def gate_grad_kernel(*refs):
+    *in_refs, gate_ref, up_grad_ref, rows_ref, up_ref, tile_ref, up_tile_ref, deltas_ref, sems = refs
+    row_refs, delta_refs = in_refs[:-6], in_refs[-6:]
+    *near_refs, own_ref, far_ref = row_refs
     width = rows_ref.shape[1] // 2
-    hidden_units = deltas_ref.shape[1] // 3
-    core = lax.axis_index("dp") % 2
+    hidden_units = up_ref.shape[1]
 
     def gather_rows(cols):
-        *near_refs, own_ref, far_ref = row_refs
         near = near_rows(*near_refs, cols=cols)
         rows_ref[:, cols] = jnp.concatenate([near, own_ref[:, cols], far_ref[:, cols]], axis=0)
 
-    def gather_deltas(cols):
-        at = 0
-        for place in range(3):
-            mine, other, of = *delta_refs[2 * place:2 * place + 2], cols
-            if place == 2 and cols.start:
-                mine, other = delta_refs[6:]
-                of = slice(cols.start - hidden_units, cols.stop - hidden_units)
-            both = in_order(core, mine[:, of], other[:, of])
-            deltas_ref[at:at + both.shape[0], cols] = both
-            at += both.shape[0]
-
+    def columns(place):
+        whole = slice(place * hidden_units, (place + 1) * hidden_units)
+        return whole, whole, slice(whole.start - hidden_units, whole.stop - hidden_units)
+
+    gather_deltas(deltas_ref, delta_refs, columns(1))
+    gather_rows(slice(0, width))
     copies = []
-    for name, tile, out_ref, tile_ref in zip(names, tiles, out_refs, tile_refs):
-        place = ("down", "gate", "up").index(name)
-        of_name = slice(place * hidden_units, (place + 1) * hidden_units)
-        gather_deltas(of_name)
-        if name == "down":
-            gather_rows(slice(width, 2 * width))
-        elif name == names[0]:
-            gather_rows(slice(0, width))
-        for at in range(0, out_ref.shape[0], tile):
-            rows = min(tile, out_ref.shape[0] - at)
-            if name == "down":
-                out = contract_rows(deltas_ref[:, at:at + rows], rows_ref[:, width:])
-            else:
-                out = contract_rows(rows_ref[:, at:at + rows], deltas_ref[:, of_name])
-            tile_ref[at:at + rows] = out
-            span = pl.ds(at, rows)
-            copies.append(
-                pltpu.make_async_copy(tile_ref.at[span], out_ref.at[span], sems.at[len(copies)])
-            )
-            copies[-1].start()
+    send_tiles(rows_ref[:, :width], deltas_ref[...], 128, tile_ref, gate_ref, sems, copies)
+    gather_deltas(up_ref, delta_refs, columns(2))
+    send_tiles(
+        rows_ref[:, :width], up_ref[...], 128, up_tile_ref, up_grad_ref, sems, copies, stop=128
+    )
+    gather_rows(slice(width, 2 * width))
     for copy in copies:
         copy.wait()
 
 
-def weight_grads(names, width, hidden_units, slot_count, inputs):
-    sizes = {"gate": (width, hidden_units), "up": (width, hidden_units), "down": (hidden_units, width)}
-    outs = [shape(*sizes[name], jnp.float32) for name in names]
-    tiles = [384 if name == "down" else 128 for name in names]
-    copies = sum(-(-out.shape[0] // tile) for out, tile in zip(outs, tiles))
+def up_down_grad_kernel(started_ref, rows_ref, deltas_ref, *refs):
+    *hidden_refs, up_ref, down_ref, up_tile_ref, down_tile_ref, hidden_ref, sems = refs
+    width = rows_ref.shape[1] // 2
+    hidden_units = hidden_ref.shape[1]
+    copies = []
+    send_tiles(
+        rows_ref[:, :width], deltas_ref[...], 128, up_tile_ref, up_ref, sems, copies, start=128
+    )
+    gather_deltas(hidden_ref, hidden_refs, (slice(0, hidden_units),) * 3)
+    send_tiles(hidden_ref[...], rows_ref[:, width:], 384, down_tile_ref, down_ref, sems, copies)
+    for copy in copies:
+        copy.wait()
+
+
+def grads_call(kernel, grads, extra, delta_shape, *args, started=False):
+    spaces = [pltpu.HBM] * len(grads) + [pltpu.VMEM] * len(extra)
+    copies = sum(-(-grad.shape[0] // 128) for grad in grads)
+    in_spaces = [pltpu.HBM if started and place == 0 else pltpu.VMEM for place in range(len(args))]
     return pl.pallas_call(
-        functools.partial(weight_grads_kernel, names, tiles),
-        out_shape=outs,
-        in_specs=[pl.BlockSpec(memory_space=pltpu.VMEM)] * len(inputs),
-        out_specs=[pl.BlockSpec(memory_space=pltpu.HBM)] * len(outs),
-        scratch_shapes=[pltpu.VMEM(out.shape, out.dtype) for out in outs]
-        + [
-            pltpu.VMEM((slot_count, 2 * width), jnp.bfloat16),
-            pltpu.VMEM((slot_count, 3 * hidden_units), jnp.bfloat16),
-            pltpu.SemaphoreType.DMA((copies,)),
-        ],
+        kernel,
+        out_shape=(*grads, *extra),
+        input_output_aliases={0: 0} if started else {},
+        in_specs=[pl.BlockSpec(memory_space=space) for space in in_spaces],
+        out_specs=tuple(pl.BlockSpec(memory_space=space) for space in spaces),
+        scratch_shapes=[pltpu.VMEM(grad.shape, grad.dtype) for grad in grads]
+        + [pltpu.VMEM(delta_shape.shape, delta_shape.dtype), pltpu.SemaphoreType.DMA((copies,))],
         compiler_params=pltpu.CompilerParams(vmem_limit_bytes=24 * 1024 * 1024),
         cost_estimate=pl.CostEstimate(flops=10**7, bytes_accessed=10**7, transcendentals=0),
-    )(*inputs)
+    )(*args)
 
 
 def token_grad_kernel(chosen_ref, own_ref, from_pair_ref, *refs):
@@ -477,19 +486,39 @@
         *turned,
         grads[-1],
     )
-    without_hidden = near_deltas + own_deltas + far_deltas + far_deltas
-    deltas = near_deltas + own_deltas + hidden_pair + far_deltas
-
     returned_pair = swap(to_pair, 1, "expert")
-    rows = (*near, own, by_pair)
-    sizes = (width, hidden_units, slot_count)
-    (gate_grad,) = weight_grads(("gate",), *sizes, (*rows, *without_hidden))
+    wide = shape(width, hidden_units, jnp.float32)
+    one_delta = shape(slot_count, hidden_units)
+    gate_grad, up_started, all_rows, up_deltas = grads_call(
+        gate_grad_kernel,
+        (wide, wide),
+        (shape(slot_count, 2 * width), one_delta),
+        one_delta,
+        *near,
+        own,
+        by_pair,
+        *near_deltas,
+        *own_deltas,
+        *far_deltas,
+    )
     returned_pair = after(returned_pair, (gate_grad, own_grad))
     returned = {}
     for place, j in enumerate(far_first[1:], 1):
         more = returned_pair[place * capacity:(place + 1) * capacity]
         returned[j] = swap(jnp.concatenate([grads[place - 1], more], axis=0), 2 * j, "expert")
-    up_grad, down_grad = weight_grads(("up", "down"), *sizes, (*rows, *deltas))
+    up_grad, down_grad = grads_call(
+        up_down_grad_kernel,
+        (wide, shape(hidden_units, width, jnp.float32)),
+        (),
+        one_delta,
+        up_started,
+        all_rows,
+        up_deltas,
+        *near_deltas,
+        *own_deltas,
+        *hidden_pair,
+        started=True,
+    )
     token_grad = call(
         token_grad_kernel,
         shape(tok_rows, width),

time: 43.7 us -> 43.7 us (level)
  transfers between devices with their start and end apart: 18 -> 18, of which waited for: 9 -> 8; matrix products, arithmetic and copies ran while one was open for 0% -> 0% of each run, Pallas kernels for 25% -> 25%
where the time goes in v11:
time: 43.7 us; the launch traced here: 43.6 us
  starting transfers between devices  20.2 us (46%)
  Pallas kernels  13.8 us (32%)
  waiting for transfers between devices  8.67 us (20%)
  between operations  0.85 us (2%)
    ppermute x18, starting transfers between devices, swap(): return lax.ppermute(value, axis, [(i, i ^ bit) for i in range(size)])  20.2 us
    pallas_call x14, Pallas kernels, call(): pl.pallas_call(kernel, out_shape=outs, in_specs=[pl.BlockSpec(memory_spac...  8.9 us
    ppermute x18, waiting for transfers between devices, swap(): return lax.ppermute(value, axis, [(i, i ^ bit) for i in range(size)])  8.67 us
    pallas_call x2, Pallas kernels, grads_call(): pl.pallas_call(kernel, out_shape=(*grads, *extra), input_output_aliases={...  4.9 us
  transfers between devices with their start and end apart: 18, of which 8 were waited for; matrix products, arithmetic and copies ran while one was open for 0% of the time, Pallas kernels for 25%

profile of v11, /device:TPU:0, one launch (start us, length us, event | category | flops | bytes accessed | tf_op | source)
XLA Modules:
  0.0 43.6 jit_solution(12406209281133398286)
XLA Ops:
  0.6 1.3 %shard_map.102 = (bf16[128,128]{1,0:T(8,128)(2,1)S(1)}, bf16[16,1024]{1,0:T(8,128)(2,1)S(1)}, bf16[16,1024]{1,0:T(8,128)(2,1)S(1)}, bf16[32,1024]{1,0:T(8,128)(2...) custom-call(s32[1,128]{1,0:T(1,128)} %bitcast.12, f32[1,128]{1,0:T(1,128)} %bitcast.13, ...), custom_call_target="tpu_custom_call" | custom-call | flops 1 | bytes 1 | tf_op jit(solution)/shard_map/pallas_call | solution.py:54
  1.9 5.1 %collective-permute-start.1 = (bf16[32,1024]{1,0:T(8,128)(2,1)S(1)}, bf16[32,1024]{1,0:T(8,128)(2,1)S(1)}, u32[]{:S(2)}, u32[]{:S(2)}) collective-permute-start(bf16[32,1024]{1,0:T(8,128)(2,1)S(1)} %get-tuple-element.56), channel_id=1, source_target_pairs={{0,6},{1,7},{2,4},{3,5},{4,2},{5,3},{6,0},{7,1},{8,14},{9,15},{10,... | collective-permute-start | bytes 196616 | tf_op jit(solution)/shard_map/ppermute | solution.py:36
  7.0 0.6 %collective-permute-start.3 = (bf16[32,1024]{1,0:T(8,128)(2,1)S(1)}, bf16[32,1024]{1,0:T(8,128)(2,1)S(1)}, u32[]{:S(2)}, u32[]{:S(2)}) collective-permute-start(bf16[32,1024]{1,0:T(8,128)(2,1)S(1)} %get-tuple-element.58), channel_id=1, source_target_pairs={{0,2},{1,3},{2,0},{3,1},{4,6},{5,7},{6,4},{7,5},{8,10},{9,11},{10,... | collective-permute-start | bytes 196616 | tf_op jit(solution)/shard_map/ppermute | solution.py:36
  7.7 1.7 %collective-permute-start = (bf16[16,1024]{1,0:T(8,128)(2,1)S(1)}, bf16[16,1024]{1,0:T(8,128)(2,1)S(1)}, u32[]{:S(2)}, u32[]{:S(2)}) collective-permute-start(bf16[16,1024]{1,0:T(8,128)(2,1)S(1)} %get-tuple-element.55), channel_id=1, source_target_pairs={{0,1},{1,0},{2,3},{3,2},{4,5},{5,4},{6,7},{7,6},{8,9},{9,8},{10,11... | collective-permute-start | bytes 98312 | tf_op jit(solution)/shard_map/ppermute | solution.py:36
  9.3 2.3 %shard_map.103 = (bf16[512,1408]{1,0:T(8,128)(2,1)S(1)}, bf16[512,1408]{1,0:T(8,128)(2,1)S(1)}, bf16[512,1408]{1,0:T(8,128)(2,1)S(1)}) custom-call(bf16[1408,512]{1,0:T(8,128)(2,1)} %bitcast.9, bf16[512,1408]{1,0:T(8,128)(2,1)} %bitcast.10, bf16[512,1408]{1,0:T(8,128)(2,1)} %bitcast.11, bf16[128,128]{1,0:T(8,128)(2,1)S(1)} %get-tuple-element.70.marker_hbm.refs_2_), custom_call_target="tpu_custom_call" | custom-call | flops 10000000 | bytes 10000000 | tf_op jit(solution)/shard_map/pallas_call | solution.py:54
  11.6 1.0 %collective-permute-done.2.refs_2_ = bf16[32,1024]{1,0:T(8,128)(2,1)S(1)} collective-permute-done((bf16[32,1024]{1,0:T(8,128)(2,1)S(1)}, bf16[32,1024]{1,0:T(8,128)(2,1)S(1)}, u32[]{:S(2)}, u32[]{:S(2)}) %collective-permute-start.2) | collective-permute-done | bytes 65568 | tf_op jit(solution)/shard_map/ppermute | solution.py:36
  12.6 0.8 %shard_map.104 = (f32[40,4224]{1,0:T(8,128)S(1)}, bf16[40,4224]{1,0:T(8,128)(2,1)S(1)}) custom-call(bf16[16,1024]{1,0:T(8,128)(2,1)S(1)} %collective-permute-done.refs_0_, bf16[32,1024]{1,0:T(8,128)(2,1)S(1)} %collective-permute-done.1.refs_1_, bf16[32,1024]{1,0:T(8,128)(2,1)S(1)} %collective-permute-done.2.refs_2_, ...), custom_call_target="tpu_custom_call" | custom-call | flops 1 | bytes 1 | tf_op jit(solution)/shard_map/pallas_call | solution.py:54
  13.6 1.6 %collective-permute-start.9 = (bf16[48,1024]{1,0:T(8,128)(2,1)S(1)}, bf16[48,1024]{1,0:T(8,128)(2,1)S(1)}, u32[]{:S(2)}, u32[]{:S(2)}) collective-permute-start(bf16[48,1024]{1,0:T(8,128)(2,1)S(1)} %pad_maximum_fusion), channel_id=1, source_target_pairs={{0,1},{1,0},{2,3},{3,2},{4,5},{5,4},{6,7},{7,6},{8,9},{9,8},{10,11... | collective-permute-start | bytes 294920 | tf_op jit(solution)/shard_map/ppermute | solution.py:36
  15.3 1.6 %collective-permute-start.5 = (bf16[32,4224]{1,0:T(8,128)(2,1)S(1)}, bf16[32,4224]{1,0:T(8,128)(2,1)S(1)}, u32[]{:S(2)}, u32[]{:S(2)}) collective-permute-start(bf16[32,4224]{1,0:T(8,128)(2,1)S(1)} %get-tuple-element.67), channel_id=1, source_target_pairs={{0,16},{8,24},{16,0},{24,8},{1,17},{9,25},{17,1},{25,9},{2,18},{10... | collective-permute-start | bytes 811016 | tf_op jit(solution)/shard_map/ppermute | solution.py:36
  16.8 2.0 %collective-permute-done.9.refs_0_.refs_5_ = bf16[48,1024]{1,0:T(8,128)(2,1)S(1)} collective-permute-done((bf16[48,1024]{1,0:T(8,128)(2,1)S(1)}, bf16[48,1024]{1,0:T(8,128)(2,1)S(1)}, u32[]{:S(2)}, u32[]{:S(2)}) %collective-permute-start.9) | collective-permute-done | bytes 98336 | tf_op jit(solution)/shard_map/ppermute | solution.py:36
  18.8 0.8 %shard_map.111 = (f32[24,4224]{1,0:T(8,128)S(1)}, bf16[24,4224]{1,0:T(8,128)(2,1)S(1)}) custom-call(bf16[48,1024]{1,0:T(8,128)(2,1)S(1)} %collective-permute-done.9.refs_0_.refs_5_, bf16[512,1408]{1,0:T(8,128)(2,1)S(1)} %get-tuple-element.68.refs_5_.refs_0_.refs_1_, bf16[512,1408]{1,0:T(8,128)(2,1)S(1)} %get-tuple-element.69.refs_6_.refs_1_.refs_2_, ...), custom_call_target="tpu_custom_call" | custom-call | flops 300000000 | bytes 300000000 | tf_op jit(solution)/shard_map/pallas_call | solution.py:54
  19.7 1.4 %collective-permute-done.10.received_ref = bf16[24,4224]{1,0:T(8,128)(2,1)S(1)} collective-permute-done((bf16[24,4224]{1,0:T(8,128)(2,1)S(1)}, bf16[24,4224]{1,0:T(8,128)(2,1)S(1)}, u32[]{:S(2)}, u32[]{:S(2)}) %collective-permute-start.10) | collective-permute-done | bytes 202784 | tf_op jit(solution)/shard_map/ppermute | solution.py:36
  21.2 1.6 %collective-permute-start.11 = (bf16[24,4224]{1,0:T(8,128)(2,1)S(1)}, bf16[24,4224]{1,0:T(8,128)(2,1)S(1)}, u32[]{:S(2)}, u32[]{:S(2)}) collective-permute-start(bf16[24,4224]{1,0:T(8,128)(2,1)S(1)} %get-tuple-element.83), channel_id=1, source_target_pairs={{0,16},{8,24},{16,0},{24,8},{1,17},{9,25},{17,1},{25,9},{2,18},{10... | collective-permute-start | bytes 608264 | tf_op jit(solution)/shard_map/ppermute | solution.py:36
  22.8 1.1 %collective-permute-done.5.received_ref = bf16[32,4224]{1,0:T(8,128)(2,1)S(1)} collective-permute-done((bf16[32,4224]{1,0:T(8,128)(2,1)S(1)}, bf16[32,4224]{1,0:T(8,128)(2,1)S(1)}, u32[]{:S(2)}, u32[]{:S(2)}) %collective-permute-start.5) | collective-permute-done | bytes 270368 | tf_op jit(solution)/shard_map/ppermute | solution.py:36
  24.1 0.8 %shard_map.107 = (bf16[1408,512]{1,0:T(8,128)(2,1)S(1)}, bf16[1408,512]{1,0:T(8,128)(2,1)S(1)}, bf16[128,128]{1,0:T(8,128)(2,1)S(1)}) custom-call(bf16[512,1408]{1,0:T(8,128)(2,1)S(1)} %get-tuple-element.68.refs_5_.refs_0_.refs_1_, bf16[512,1408]{1,0:T(8,128)(2,1)S(1)} %get-tuple-element.69.refs_6_.refs_1_.refs_2_, ...), custom_call_target="tpu_custom_call" | custom-call | flops 1 | bytes 1 | tf_op jit(solution)/shard_map/pallas_call | solution.py:54
  25.0 1.6 %collective-permute-start.7 = (bf16[8,4224]{1,0:T(8,128)(2,1)S(1)}, bf16[8,4224]{1,0:T(8,128)(2,1)S(1)}, u32[]{:S(2)}, u32[]{:S(2)}) collective-permute-start(bf16[8,4224]{1,0:T(8,128)(2,1)S(1)} %get-tuple-element.78), channel_id=1, source_target_pairs={{0,16},{8,24},{16,0},{24,8},{1,17},{9,25},{17,1},{25,9},{2,18},{10... | collective-permute-start | bytes 202760 | tf_op jit(solution)/shard_map/ppermute | solution.py:36
  26.5 2.1 %collective-permute-done.11.received_ref = bf16[24,4224]{1,0:T(8,128)(2,1)S(1)} collective-permute-done((bf16[24,4224]{1,0:T(8,128)(2,1)S(1)}, bf16[24,4224]{1,0:T(8,128)(2,1)S(1)}, u32[]{:S(2)}, u32[]{:S(2)}) %collective-permute-start.11) | collective-permute-done | bytes 202784 | tf_op jit(solution)/shard_map/ppermute | solution.py:36
  28.8 0.6 %shard_map.108 = (bf16[16,512]{1,0:T(8,128)(2,1)S(1)}, bf16[16,512]{1,0:T(8,128)(2,1)S(1)}, bf16[16,512]{1,0:T(8,128)(2,1)S(1)}, bf16[16,512]{1,0:T(8,128)(2,1)S(1)}) custom-call(bf16[32,4224]{1,0:T(8,128)(2,1)S(1)} %shard_map.106.mine_ref.refs_6_.refs_0_, bf16[32,4224]{1,0:T(8,128)(2,1)S(1)} %collective-permute-done.6.other_ref.refs_7_.refs_1_, ...), custom_call_target="tpu_custom_call" | custom-call | flops 1 | bytes 1 | tf_op jit(solution)/shard_map/pallas_call | solution.py:54
  30.7 1.7 %collective-permute-start.13 = (bf16[64,512]{1,0:T(8,128)(2,1)S(1)}, bf16[64,512]{1,0:T(8,128)(2,1)S(1)}, u32[]{:S(2)}, u32[]{:S(2)}) collective-permute-start(bf16[64,512]{1,0:T(8,128)(2,1)S(1)} %shard_map.114), channel_id=1, source_target_pairs={{0,1},{1,0},{2,3},{3,2},{4,5},{5,4},{6,7},{7,6},{8,9},{9,8},{10,11... | collective-permute-start | bytes 196616 | tf_op jit(solution)/shard_map/ppermute | solution.py:36
  32.9 2.2 %shard_map.115 = (f32[512,1408]{1,0:T(8,128)}, f32[512,1408]{1,0:T(8,128)}, bf16[128,1024]{1,0:T(8,128)(2,1)S(1)}, bf16[128,1408]{1,0:T(8,128)(2,1)S(1)}) custom-call(bf16[16,1024]{1,0:T(8,128)(2,1)S(1)} %collective-permute-done.refs_0_, bf16[32,1024]{1,0:T(8,128)(2,1)S(1)} %collective-permute-done.1.refs_1_, ...), custom_call_target="tpu_custom_call" | custom-call | flops 10000000 | bytes 10000000 | tf_op jit(solution)/shard_map/pallas_call | solution.py:284
  35.1 2.8 %collective-permute-start.14 = (bf16[32,512]{1,0:T(8,128)(2,1)S(1)}, bf16[32,512]{1,0:T(8,128)(2,1)S(1)}, u32[]{:S(2)}, u32[]{:S(2)}) collective-permute-start(bf16[32,512]{1,0:T(8,128)(2,1)S(1)} %pad_maximum_fusion.1), channel_id=1, source_target_pairs={{0,6},{1,7},{2,4},{3,5},{4,2},{5,3},{6,0},{7,1},{8,14},{9,15},{10,... | collective-permute-start | bytes 98312 | tf_op jit(solution)/shard_map/ppermute | solution.py:36
  37.9 1.7 %collective-permute-start.16 = (bf16[32,512]{1,0:T(8,128)(2,1)S(1)}, bf16[32,512]{1,0:T(8,128)(2,1)S(1)}, u32[]{:S(2)}, u32[]{:S(2)}) collective-permute-start(bf16[32,512]{1,0:T(8,128)(2,1)S(1)} %pad_maximum_fusion.3), channel_id=1, source_target_pairs={{0,2},{1,3},{2,0},{3,1},{4,6},{5,7},{6,4},{7,5},{8,10},{9,11},{10,... | collective-permute-start | bytes 98312 | tf_op jit(solution)/shard_map/ppermute | solution.py:36
  39.6 2.7 %shard_map.117 = (f32[512,1408]{1,0:T(8,128)}, f32[1408,512]{1,0:T(8,128)}) custom-call(f32[512,1408]{1,0:T(8,128)} %get-tuple-element.94.started_ref, bf16[128,1024]{1,0:T(8,128)(2,1)S(1)} %get-tuple-element.95.rows_ref, bf16[128,1408]{1,0:T(8,128)(2,1)S(1)} %get-tuple-element.96.deltas_ref, ...), custom_call_target="tpu_custom_call", output_to_operand_aliasing={{0}: (0, {})} | custom-call | flops 10000000 | bytes 10000000 | tf_op jit(solution)/shard_map/pallas_call | solution.py:284
  42.7 0.8 %shard_map.116 = bf16[128,512]{1,0:T(8,128)(2,1)} custom-call(bf16[128,128]{1,0:T(8,128)(2,1)S(1)} %get-tuple-element.71.chosen_ref, bf16[16,512]{1,0:T(8,128)(2,1)S(1)} %shard_map.110.own_ref, bf16[64,512]{1,0:T(8,128)(2,1)S(1)} %collective-permute-done.13.from_pair_ref, bf16[32,512]{1,0:T(8,128)(2,1)S(1)} %collective-permute-done.14.refs_0_, ...), custom_call_target="tpu_custom_call" | custom-call | flops 1 | bytes 1 | tf_op jit(solution)/shard_map/pallas_call | solution.py:54
  (36 shorter events, 3.0 us)
Async XLA Ops:
  1.9 9.7 %collective-permute-start.1 = (bf16[32,1024]{1,0:T(8,128)(2,1)S(1)}, bf16[32,1024]{1,0:T(8,128)(2,1)S(1)}, u32[]{:S(2)}, u32[]{:S(2)}) collective-permute-start(bf16[32,1024]{1,0:T(8,128)(2,1)S(1)} %get-tuple-element.56), channel_id=1, source_target_pairs={{0,6},{1,7},{2,4},{3,5},{4,2},{5,3},{6,0},{7,1},{8,14},{9,15},{10,... | collective-permute-start | bytes 196616 | tf_op jit(solution)/shard_map/ppermute | solution.py:36
  7.0 5.6 %collective-permute-start.2 = (bf16[32,1024]{1,0:T(8,128)(2,1)S(1)}, bf16[32,1024]{1,0:T(8,128)(2,1)S(1)}, u32[]{:S(2)}, u32[]{:S(2)}) collective-permute-start(bf16[32,1024]{1,0:T(8,128)(2,1)S(1)} %get-tuple-element.57), channel_id=1, source_target_pairs={{0,4},{1,5},{2,6},{3,7},{4,0},{5,1},{6,2},{7,3},{8,12},{9,13},{10,... | collective-permute-start | bytes 196616 | tf_op jit(solution)/shard_map/ppermute | solution.py:36
  7.0 5.6 %collective-permute-start.3 = (bf16[32,1024]{1,0:T(8,128)(2,1)S(1)}, bf16[32,1024]{1,0:T(8,128)(2,1)S(1)}, u32[]{:S(2)}, u32[]{:S(2)}) collective-permute-start(bf16[32,1024]{1,0:T(8,128)(2,1)S(1)} %get-tuple-element.58), channel_id=1, source_target_pairs={{0,2},{1,3},{2,0},{3,1},{4,6},{5,7},{6,4},{7,5},{8,10},{9,11},{10,... | collective-permute-start | bytes 196616 | tf_op jit(solution)/shard_map/ppermute | solution.py:36
  7.7 3.9 %collective-permute-start = (bf16[16,1024]{1,0:T(8,128)(2,1)S(1)}, bf16[16,1024]{1,0:T(8,128)(2,1)S(1)}, u32[]{:S(2)}, u32[]{:S(2)}) collective-permute-start(bf16[16,1024]{1,0:T(8,128)(2,1)S(1)} %get-tuple-element.55), channel_id=1, source_target_pairs={{0,1},{1,0},{2,3},{3,2},{4,5},{5,4},{6,7},{7,6},{8,9},{9,8},{10,11... | collective-permute-start | bytes 98312 | tf_op jit(solution)/shard_map/ppermute | solution.py:36
  13.5 1.7 %collective-permute-start.4 = (bf16[40,4224]{1,0:T(8,128)(2,1)S(1)}, bf16[40,4224]{1,0:T(8,128)(2,1)S(1)}, u32[]{:S(2)}, u32[]{:S(2)}) collective-permute-start(bf16[40,4224]{1,0:T(8,128)(2,1)S(1)} %get-tuple-element.65), channel_id=1, source_target_pairs={{0,8},{8,0},{16,24},{24,16},{1,9},{9,1},{17,25},{25,17},{2,10},{10... | collective-permute-start | bytes 1013768 | tf_op jit(solution)/shard_map/ppermute | solution.py:36
  13.6 5.2 %collective-permute-start.9 = (bf16[48,1024]{1,0:T(8,128)(2,1)S(1)}, bf16[48,1024]{1,0:T(8,128)(2,1)S(1)}, u32[]{:S(2)}, u32[]{:S(2)}) collective-permute-start(bf16[48,1024]{1,0:T(8,128)(2,1)S(1)} %pad_maximum_fusion), channel_id=1, source_target_pairs={{0,1},{1,0},{2,3},{3,2},{4,5},{5,4},{6,7},{7,6},{8,9},{9,8},{10,11... | collective-permute-start | bytes 294920 | tf_op jit(solution)/shard_map/ppermute | solution.py:36
  15.3 8.6 %collective-permute-start.5 = (bf16[32,4224]{1,0:T(8,128)(2,1)S(1)}, bf16[32,4224]{1,0:T(8,128)(2,1)S(1)}, u32[]{:S(2)}, u32[]{:S(2)}) collective-permute-start(bf16[32,4224]{1,0:T(8,128)(2,1)S(1)} %get-tuple-element.67), channel_id=1, source_target_pairs={{0,16},{8,24},{16,0},{24,8},{1,17},{9,25},{17,1},{25,9},{2,18},{10... | collective-permute-start | bytes 811016 | tf_op jit(solution)/shard_map/ppermute | solution.py:36
  19.7 1.5 %collective-permute-start.10 = (bf16[24,4224]{1,0:T(8,128)(2,1)S(1)}, bf16[24,4224]{1,0:T(8,128)(2,1)S(1)}, u32[]{:S(2)}, u32[]{:S(2)}) collective-permute-start(bf16[24,4224]{1,0:T(8,128)(2,1)S(1)} %get-tuple-element.81), channel_id=1, source_target_pairs={{0,8},{8,0},{16,24},{24,16},{1,9},{9,1},{17,25},{25,17},{2,10},{10... | collective-permute-start | bytes 608264 | tf_op jit(solution)/shard_map/ppermute | solution.py:36
  21.2 7.3 %collective-permute-start.11 = (bf16[24,4224]{1,0:T(8,128)(2,1)S(1)}, bf16[24,4224]{1,0:T(8,128)(2,1)S(1)}, u32[]{:S(2)}, u32[]{:S(2)}) collective-permute-start(bf16[24,4224]{1,0:T(8,128)(2,1)S(1)} %get-tuple-element.83), channel_id=1, source_target_pairs={{0,16},{8,24},{16,0},{24,8},{1,17},{9,25},{17,1},{25,9},{2,18},{10... | collective-permute-start | bytes 608264 | tf_op jit(solution)/shard_map/ppermute | solution.py:36
  24.1 4.6 %collective-permute-start.6 = (bf16[32,4224]{1,0:T(8,128)(2,1)S(1)}, bf16[32,4224]{1,0:T(8,128)(2,1)S(1)}, u32[]{:S(2)}, u32[]{:S(2)}) collective-permute-start(bf16[32,4224]{1,0:T(8,128)(2,1)S(1)} %shard_map.106.mine_ref.refs_6_.refs_0_), channel_id=1, source_target_pairs={{0,8},{8,0},{16,24},{24,16},{1,9},{9,1},{17,25},{25,17},{2,10},{10... | collective-permute-start | bytes 811016 | tf_op jit(solution)/shard_map/ppermute | solution.py:36
  25.0 4.9 %collective-permute-start.7 = (bf16[8,4224]{1,0:T(8,128)(2,1)S(1)}, bf16[8,4224]{1,0:T(8,128)(2,1)S(1)}, u32[]{:S(2)}, u32[]{:S(2)}) collective-permute-start(bf16[8,4224]{1,0:T(8,128)(2,1)S(1)} %get-tuple-element.78), channel_id=1, source_target_pairs={{0,16},{8,24},{16,0},{24,8},{1,17},{9,25},{17,1},{25,9},{2,18},{10... | collective-permute-start | bytes 202760 | tf_op jit(solution)/shard_map/ppermute | solution.py:36
  28.7 1.4 %collective-permute-start.12 = (bf16[24,2816]{1,0:T(8,128)(2,1)S(1)}, bf16[24,2816]{1,0:T(8,128)(2,1)S(1)}, u32[]{:S(2)}, u32[]{:S(2)}) collective-permute-start(bf16[24,2816]{1,0:T(8,128)(2,1)S(1)} %get-tuple-element.87.mine_ref.refs_10_), channel_id=1, source_target_pairs={{0,8},{8,0},{16,24},{24,16},{1,9},{9,1},{17,25},{25,17},{2,10},{10... | collective-permute-start | bytes 405512 | tf_op jit(solution)/shard_map/ppermute | solution.py:36
  29.9 2.5 %collective-permute-start.8 = (bf16[8,4224]{1,0:T(8,128)(2,1)S(1)}, bf16[8,4224]{1,0:T(8,128)(2,1)S(1)}, u32[]{:S(2)}, u32[]{:S(2)}) collective-permute-start(bf16[8,4224]{1,0:T(8,128)(2,1)S(1)} %shard_map.109.mine_ref.refs_8_.refs_2_), channel_id=1, source_target_pairs={{0,8},{8,0},{16,24},{24,16},{1,9},{9,1},{17,25},{25,17},{2,10},{10... | collective-permute-start | bytes 202760 | tf_op jit(solution)/shard_map/ppermute | solution.py:36
  30.7 4.4 %collective-permute-start.13 = (bf16[64,512]{1,0:T(8,128)(2,1)S(1)}, bf16[64,512]{1,0:T(8,128)(2,1)S(1)}, u32[]{:S(2)}, u32[]{:S(2)}) collective-permute-start(bf16[64,512]{1,0:T(8,128)(2,1)S(1)} %shard_map.114), channel_id=1, source_target_pairs={{0,1},{1,0},{2,3},{3,2},{4,5},{5,4},{6,7},{7,6},{8,9},{9,8},{10,11... | collective-permute-start | bytes 196616 | tf_op jit(solution)/shard_map/ppermute | solution.py:36
  32.4 7.2 %collective-permute-start.17 = (bf16[24,1408]{1,0:T(8,128)(2,1)S(1)}, bf16[24,1408]{1,0:T(8,128)(2,1)S(1)}, u32[]{:S(2)}, u32[]{:S(2)}) collective-permute-start(bf16[24,1408]{1,0:T(8,128)(2,1)S(1)} %get-tuple-element.97.refs_4_), channel_id=1, source_target_pairs={{0,8},{8,0},{16,24},{24,16},{1,9},{9,1},{17,25},{25,17},{2,10},{10... | collective-permute-start | bytes 202760 | tf_op jit(solution)/shard_map/ppermute | solution.py:36
  35.1 7.2 %collective-permute-start.14 = (bf16[32,512]{1,0:T(8,128)(2,1)S(1)}, bf16[32,512]{1,0:T(8,128)(2,1)S(1)}, u32[]{:S(2)}, u32[]{:S(2)}) collective-permute-start(bf16[32,512]{1,0:T(8,128)(2,1)S(1)} %pad_maximum_fusion.1), channel_id=1, source_target_pairs={{0,6},{1,7},{2,4},{3,5},{4,2},{5,3},{6,0},{7,1},{8,14},{9,15},{10,... | collective-permute-start | bytes 98312 | tf_op jit(solution)/shard_map/ppermute | solution.py:36
  37.9 4.8 %collective-permute-start.15 = (bf16[32,512]{1,0:T(8,128)(2,1)S(1)}, bf16[32,512]{1,0:T(8,128)(2,1)S(1)}, u32[]{:S(2)}, u32[]{:S(2)}) collective-permute-start(bf16[32,512]{1,0:T(8,128)(2,1)S(1)} %pad_maximum_fusion.2), channel_id=1, source_target_pairs={{0,4},{1,5},{2,6},{3,7},{4,0},{5,1},{6,2},{7,3},{8,12},{9,13},{10,... | collective-permute-start | bytes 98312 | tf_op jit(solution)/shard_map/ppermute | solution.py:36
  37.9 4.8 %collective-permute-start.16 = (bf16[32,512]{1,0:T(8,128)(2,1)S(1)}, bf16[32,512]{1,0:T(8,128)(2,1)S(1)}, u32[]{:S(2)}, u32[]{:S(2)}) collective-permute-start(bf16[32,512]{1,0:T(8,128)(2,1)S(1)} %pad_maximum_fusion.3), channel_id=1, source_target_pairs={{0,2},{1,3},{2,0},{3,1},{4,6},{5,7},{6,4},{7,5},{8,10},{9,11},{10,... | collective-permute-start | bytes 98312 | tf_op jit(solution)/shard_map/ppermute | solution.py:36

commit v12 on v11

--- a/solution.py
+++ b/solution.py
@@ -256,7 +256,7 @@
     send_tiles(rows_ref[:, :width], deltas_ref[...], 128, tile_ref, gate_ref, sems, copies)
     gather_deltas(up_ref, delta_refs, columns(2))
     send_tiles(
-        rows_ref[:, :width], up_ref[...], 128, up_tile_ref, up_grad_ref, sems, copies, stop=128
+        rows_ref[:, :width], up_ref[...], 128, up_tile_ref, up_grad_ref, sems, copies, stop=256
     )
     gather_rows(slice(width, 2 * width))
     for copy in copies:
@@ -269,7 +269,7 @@
     hidden_units = hidden_ref.shape[1]
     copies = []
     send_tiles(
-        rows_ref[:, :width], deltas_ref[...], 128, up_tile_ref, up_ref, sems, copies, start=128
+        rows_ref[:, :width], deltas_ref[...], 128, up_tile_ref, up_ref, sems, copies, start=256
     )
     gather_deltas(hidden_ref, hidden_refs, (slice(0, hidden_units),) * 3)
     send_tiles(hidden_ref[...], rows_ref[:, width:], 384, down_tile_ref, down_ref, sems, copies)
@@ -501,7 +501,7 @@
         *own_deltas,
         *far_deltas,
     )
-    returned_pair = after(returned_pair, (gate_grad, own_grad))
+    returned_pair = after(returned_pair, gate_grad)
     returned = {}
     for place, j in enumerate(far_first[1:], 1):
         more = returned_pair[place * capacity:(place + 1) * capacity]

time: 43.7 us -> 43.7 us (level)
  transfers between devices with their start and end apart: 18 -> 18, of which waited for: 8 -> 9; matrix products, arithmetic and copies ran while one was open for 0% -> 0% of each run, Pallas kernels for 25% -> 25%
where the time goes in v12:
time: 43.7 us; the launch traced here: 43.6 us
  starting transfers between devices  20.2 us (46%)
  Pallas kernels  13.8 us (32%)
  waiting for transfers between devices  8.67 us (20%)
  between operations  0.84 us (2%)
    ppermute x18, starting transfers between devices, swap(): return lax.ppermute(value, axis, [(i, i ^ bit) for i in range(size)])  20.2 us
    pallas_call x14, Pallas kernels, call(): pl.pallas_call(kernel, out_shape=outs, in_specs=[pl.BlockSpec(memory_spac...  8.9 us
    ppermute x18, waiting for transfers between devices, swap(): return lax.ppermute(value, axis, [(i, i ^ bit) for i in range(size)])  8.67 us
    pallas_call x2, Pallas kernels, grads_call(): pl.pallas_call(kernel, out_shape=(*grads, *extra), input_output_aliases={...  4.89 us
  transfers between devices with their start and end apart: 18, of which 9 were waited for; matrix products, arithmetic and copies ran while one was open for 0% of the time, Pallas kernels for 25%

profile of v12, /device:TPU:0, one launch (start us, length us, event | category | flops | bytes accessed | tf_op | source)
XLA Modules:
  0.0 43.6 jit_solution(3991029574072000051)
XLA Ops:
  0.6 1.3 %shard_map.102 = (bf16[128,128]{1,0:T(8,128)(2,1)S(1)}, bf16[16,1024]{1,0:T(8,128)(2,1)S(1)}, bf16[16,1024]{1,0:T(8,128)(2,1)S(1)}, bf16[32,1024]{1,0:T(8,128)(2...) custom-call(s32[1,128]{1,0:T(1,128)} %bitcast.12, f32[1,128]{1,0:T(1,128)} %bitcast.13, ...), custom_call_target="tpu_custom_call" | custom-call | flops 1 | bytes 1 | tf_op jit(solution)/shard_map/pallas_call | solution.py:54
  1.9 5.1 %collective-permute-start.1 = (bf16[32,1024]{1,0:T(8,128)(2,1)S(1)}, bf16[32,1024]{1,0:T(8,128)(2,1)S(1)}, u32[]{:S(2)}, u32[]{:S(2)}) collective-permute-start(bf16[32,1024]{1,0:T(8,128)(2,1)S(1)} %get-tuple-element.56), channel_id=1, source_target_pairs={{0,6},{1,7},{2,4},{3,5},{4,2},{5,3},{6,0},{7,1},{8,14},{9,15},{10,... | collective-permute-start | bytes 196616 | tf_op jit(solution)/shard_map/ppermute | solution.py:36
  7.0 0.6 %collective-permute-start.3 = (bf16[32,1024]{1,0:T(8,128)(2,1)S(1)}, bf16[32,1024]{1,0:T(8,128)(2,1)S(1)}, u32[]{:S(2)}, u32[]{:S(2)}) collective-permute-start(bf16[32,1024]{1,0:T(8,128)(2,1)S(1)} %get-tuple-element.58), channel_id=1, source_target_pairs={{0,2},{1,3},{2,0},{3,1},{4,6},{5,7},{6,4},{7,5},{8,10},{9,11},{10,... | collective-permute-start | bytes 196616 | tf_op jit(solution)/shard_map/ppermute | solution.py:36
  7.7 1.7 %collective-permute-start = (bf16[16,1024]{1,0:T(8,128)(2,1)S(1)}, bf16[16,1024]{1,0:T(8,128)(2,1)S(1)}, u32[]{:S(2)}, u32[]{:S(2)}) collective-permute-start(bf16[16,1024]{1,0:T(8,128)(2,1)S(1)} %get-tuple-element.55), channel_id=1, source_target_pairs={{0,1},{1,0},{2,3},{3,2},{4,5},{5,4},{6,7},{7,6},{8,9},{9,8},{10,11... | collective-permute-start | bytes 98312 | tf_op jit(solution)/shard_map/ppermute | solution.py:36
  9.3 2.3 %shard_map.103 = (bf16[512,1408]{1,0:T(8,128)(2,1)S(1)}, bf16[512,1408]{1,0:T(8,128)(2,1)S(1)}, bf16[512,1408]{1,0:T(8,128)(2,1)S(1)}) custom-call(bf16[1408,512]{1,0:T(8,128)(2,1)} %bitcast.9, bf16[512,1408]{1,0:T(8,128)(2,1)} %bitcast.10, bf16[512,1408]{1,0:T(8,128)(2,1)} %bitcast.11, bf16[128,128]{1,0:T(8,128)(2,1)S(1)} %get-tuple-element.70.marker_hbm.refs_2_), custom_call_target="tpu_custom_call" | custom-call | flops 10000000 | bytes 10000000 | tf_op jit(solution)/shard_map/pallas_call | solution.py:54
  11.6 1.0 %collective-permute-done.2.refs_2_ = bf16[32,1024]{1,0:T(8,128)(2,1)S(1)} collective-permute-done((bf16[32,1024]{1,0:T(8,128)(2,1)S(1)}, bf16[32,1024]{1,0:T(8,128)(2,1)S(1)}, u32[]{:S(2)}, u32[]{:S(2)}) %collective-permute-start.2) | collective-permute-done | bytes 65568 | tf_op jit(solution)/shard_map/ppermute | solution.py:36
  12.6 0.8 %shard_map.104 = (f32[40,4224]{1,0:T(8,128)S(1)}, bf16[40,4224]{1,0:T(8,128)(2,1)S(1)}) custom-call(bf16[16,1024]{1,0:T(8,128)(2,1)S(1)} %collective-permute-done.refs_0_, bf16[32,1024]{1,0:T(8,128)(2,1)S(1)} %collective-permute-done.1.refs_1_, bf16[32,1024]{1,0:T(8,128)(2,1)S(1)} %collective-permute-done.2.refs_2_, ...), custom_call_target="tpu_custom_call" | custom-call | flops 1 | bytes 1 | tf_op jit(solution)/shard_map/pallas_call | solution.py:54
  13.6 1.6 %collective-permute-start.9 = (bf16[48,1024]{1,0:T(8,128)(2,1)S(1)}, bf16[48,1024]{1,0:T(8,128)(2,1)S(1)}, u32[]{:S(2)}, u32[]{:S(2)}) collective-permute-start(bf16[48,1024]{1,0:T(8,128)(2,1)S(1)} %pad_maximum_fusion), channel_id=1, source_target_pairs={{0,1},{1,0},{2,3},{3,2},{4,5},{5,4},{6,7},{7,6},{8,9},{9,8},{10,11... | collective-permute-start | bytes 294920 | tf_op jit(solution)/shard_map/ppermute | solution.py:36
  15.3 1.6 %collective-permute-start.5 = (bf16[32,4224]{1,0:T(8,128)(2,1)S(1)}, bf16[32,4224]{1,0:T(8,128)(2,1)S(1)}, u32[]{:S(2)}, u32[]{:S(2)}) collective-permute-start(bf16[32,4224]{1,0:T(8,128)(2,1)S(1)} %get-tuple-element.67), channel_id=1, source_target_pairs={{0,16},{8,24},{16,0},{24,8},{1,17},{9,25},{17,1},{25,9},{2,18},{10... | collective-permute-start | bytes 811016 | tf_op jit(solution)/shard_map/ppermute | solution.py:36
  16.8 2.0 %collective-permute-done.9.refs_0_.refs_5_ = bf16[48,1024]{1,0:T(8,128)(2,1)S(1)} collective-permute-done((bf16[48,1024]{1,0:T(8,128)(2,1)S(1)}, bf16[48,1024]{1,0:T(8,128)(2,1)S(1)}, u32[]{:S(2)}, u32[]{:S(2)}) %collective-permute-start.9) | collective-permute-done | bytes 98336 | tf_op jit(solution)/shard_map/ppermute | solution.py:36
  18.8 0.8 %shard_map.111 = (f32[24,4224]{1,0:T(8,128)S(1)}, bf16[24,4224]{1,0:T(8,128)(2,1)S(1)}) custom-call(bf16[48,1024]{1,0:T(8,128)(2,1)S(1)} %collective-permute-done.9.refs_0_.refs_5_, bf16[512,1408]{1,0:T(8,128)(2,1)S(1)} %get-tuple-element.68.refs_5_.refs_0_.refs_1_, bf16[512,1408]{1,0:T(8,128)(2,1)S(1)} %get-tuple-element.69.refs_6_.refs_1_.refs_2_, ...), custom_call_target="tpu_custom_call" | custom-call | flops 300000000 | bytes 300000000 | tf_op jit(solution)/shard_map/pallas_call | solution.py:54
  19.7 1.4 %collective-permute-done.10.received_ref = bf16[24,4224]{1,0:T(8,128)(2,1)S(1)} collective-permute-done((bf16[24,4224]{1,0:T(8,128)(2,1)S(1)}, bf16[24,4224]{1,0:T(8,128)(2,1)S(1)}, u32[]{:S(2)}, u32[]{:S(2)}) %collective-permute-start.10) | collective-permute-done | bytes 202784 | tf_op jit(solution)/shard_map/ppermute | solution.py:36
  21.2 1.6 %collective-permute-start.11 = (bf16[24,4224]{1,0:T(8,128)(2,1)S(1)}, bf16[24,4224]{1,0:T(8,128)(2,1)S(1)}, u32[]{:S(2)}, u32[]{:S(2)}) collective-permute-start(bf16[24,4224]{1,0:T(8,128)(2,1)S(1)} %get-tuple-element.83), channel_id=1, source_target_pairs={{0,16},{8,24},{16,0},{24,8},{1,17},{9,25},{17,1},{25,9},{2,18},{10... | collective-permute-start | bytes 608264 | tf_op jit(solution)/shard_map/ppermute | solution.py:36
  22.8 1.1 %collective-permute-done.5.received_ref = bf16[32,4224]{1,0:T(8,128)(2,1)S(1)} collective-permute-done((bf16[32,4224]{1,0:T(8,128)(2,1)S(1)}, bf16[32,4224]{1,0:T(8,128)(2,1)S(1)}, u32[]{:S(2)}, u32[]{:S(2)}) %collective-permute-start.5) | collective-permute-done | bytes 270368 | tf_op jit(solution)/shard_map/ppermute | solution.py:36
  24.1 0.8 %shard_map.107 = (bf16[1408,512]{1,0:T(8,128)(2,1)S(1)}, bf16[1408,512]{1,0:T(8,128)(2,1)S(1)}, bf16[128,128]{1,0:T(8,128)(2,1)S(1)}) custom-call(bf16[512,1408]{1,0:T(8,128)(2,1)S(1)} %get-tuple-element.68.refs_5_.refs_0_.refs_1_, bf16[512,1408]{1,0:T(8,128)(2,1)S(1)} %get-tuple-element.69.refs_6_.refs_1_.refs_2_, ...), custom_call_target="tpu_custom_call" | custom-call | flops 1 | bytes 1 | tf_op jit(solution)/shard_map/pallas_call | solution.py:54
  25.0 1.6 %collective-permute-start.7 = (bf16[8,4224]{1,0:T(8,128)(2,1)S(1)}, bf16[8,4224]{1,0:T(8,128)(2,1)S(1)}, u32[]{:S(2)}, u32[]{:S(2)}) collective-permute-start(bf16[8,4224]{1,0:T(8,128)(2,1)S(1)} %get-tuple-element.78), channel_id=1, source_target_pairs={{0,16},{8,24},{16,0},{24,8},{1,17},{9,25},{17,1},{25,9},{2,18},{10... | collective-permute-start | bytes 202760 | tf_op jit(solution)/shard_map/ppermute | solution.py:36
  26.5 2.1 %collective-permute-done.11.received_ref = bf16[24,4224]{1,0:T(8,128)(2,1)S(1)} collective-permute-done((bf16[24,4224]{1,0:T(8,128)(2,1)S(1)}, bf16[24,4224]{1,0:T(8,128)(2,1)S(1)}, u32[]{:S(2)}, u32[]{:S(2)}) %collective-permute-start.11) | collective-permute-done | bytes 202784 | tf_op jit(solution)/shard_map/ppermute | solution.py:36
  28.8 0.6 %shard_map.108 = (bf16[16,512]{1,0:T(8,128)(2,1)S(1)}, bf16[16,512]{1,0:T(8,128)(2,1)S(1)}, bf16[16,512]{1,0:T(8,128)(2,1)S(1)}, bf16[16,512]{1,0:T(8,128)(2,1)S(1)}) custom-call(bf16[32,4224]{1,0:T(8,128)(2,1)S(1)} %shard_map.106.mine_ref.refs_6_.refs_0_, bf16[32,4224]{1,0:T(8,128)(2,1)S(1)} %collective-permute-done.6.other_ref.refs_7_.refs_1_, ...), custom_call_target="tpu_custom_call" | custom-call | flops 1 | bytes 1 | tf_op jit(solution)/shard_map/pallas_call | solution.py:54
  30.7 1.7 %collective-permute-start.13 = (bf16[64,512]{1,0:T(8,128)(2,1)S(1)}, bf16[64,512]{1,0:T(8,128)(2,1)S(1)}, u32[]{:S(2)}, u32[]{:S(2)}) collective-permute-start(bf16[64,512]{1,0:T(8,128)(2,1)S(1)} %shard_map.114), channel_id=1, source_target_pairs={{0,1},{1,0},{2,3},{3,2},{4,5},{5,4},{6,7},{7,6},{8,9},{9,8},{10,11... | collective-permute-start | bytes 196616 | tf_op jit(solution)/shard_map/ppermute | solution.py:36
  32.4 2.4 %shard_map.115 = (f32[512,1408]{1,0:T(8,128)}, f32[512,1408]{1,0:T(8,128)}, bf16[128,1024]{1,0:T(8,128)(2,1)S(1)}, bf16[128,1408]{1,0:T(8,128)(2,1)S(1)}) custom-call(bf16[16,1024]{1,0:T(8,128)(2,1)S(1)} %collective-permute-done.refs_0_, bf16[32,1024]{1,0:T(8,128)(2,1)S(1)} %collective-permute-done.1.refs_1_, ...), custom_call_target="tpu_custom_call" | custom-call | flops 10000000 | bytes 10000000 | tf_op jit(solution)/shard_map/pallas_call | solution.py:284
  35.1 2.8 %collective-permute-start.14 = (bf16[32,512]{1,0:T(8,128)(2,1)S(1)}, bf16[32,512]{1,0:T(8,128)(2,1)S(1)}, u32[]{:S(2)}, u32[]{:S(2)}) collective-permute-start(bf16[32,512]{1,0:T(8,128)(2,1)S(1)} %pad_maximum_fusion.1), channel_id=1, source_target_pairs={{0,6},{1,7},{2,4},{3,5},{4,2},{5,3},{6,0},{7,1},{8,14},{9,15},{10,... | collective-permute-start | bytes 98312 | tf_op jit(solution)/shard_map/ppermute | solution.py:36
  37.9 1.7 %collective-permute-start.16 = (bf16[32,512]{1,0:T(8,128)(2,1)S(1)}, bf16[32,512]{1,0:T(8,128)(2,1)S(1)}, u32[]{:S(2)}, u32[]{:S(2)}) collective-permute-start(bf16[32,512]{1,0:T(8,128)(2,1)S(1)} %pad_maximum_fusion.3), channel_id=1, source_target_pairs={{0,2},{1,3},{2,0},{3,1},{4,6},{5,7},{6,4},{7,5},{8,10},{9,11},{10,... | collective-permute-start | bytes 98312 | tf_op jit(solution)/shard_map/ppermute | solution.py:36
  40.1 2.5 %shard_map.117 = (f32[512,1408]{1,0:T(8,128)}, f32[1408,512]{1,0:T(8,128)}) custom-call(f32[512,1408]{1,0:T(8,128)} %get-tuple-element.94.started_ref, bf16[128,1024]{1,0:T(8,128)(2,1)S(1)} %get-tuple-element.95.rows_ref, bf16[128,1408]{1,0:T(8,128)(2,1)S(1)} %get-tuple-element.96.deltas_ref, ...), custom_call_target="tpu_custom_call", output_to_operand_aliasing={{0}: (0, {})} | custom-call | flops 10000000 | bytes 10000000 | tf_op jit(solution)/shard_map/pallas_call | solution.py:284
  42.7 0.8 %shard_map.116 = bf16[128,512]{1,0:T(8,128)(2,1)} custom-call(bf16[128,128]{1,0:T(8,128)(2,1)S(1)} %get-tuple-element.71.chosen_ref, bf16[16,512]{1,0:T(8,128)(2,1)S(1)} %shard_map.110.own_ref, bf16[64,512]{1,0:T(8,128)(2,1)S(1)} %collective-permute-done.13.from_pair_ref, bf16[32,512]{1,0:T(8,128)(2,1)S(1)} %collective-permute-done.14.refs_0_, ...), custom_call_target="tpu_custom_call" | custom-call | flops 1 | bytes 1 | tf_op jit(solution)/shard_map/pallas_call | solution.py:54
  (36 shorter events, 3.0 us)
Async XLA Ops:
  1.9 9.7 %collective-permute-start.1 = (bf16[32,1024]{1,0:T(8,128)(2,1)S(1)}, bf16[32,1024]{1,0:T(8,128)(2,1)S(1)}, u32[]{:S(2)}, u32[]{:S(2)}) collective-permute-start(bf16[32,1024]{1,0:T(8,128)(2,1)S(1)} %get-tuple-element.56), channel_id=1, source_target_pairs={{0,6},{1,7},{2,4},{3,5},{4,2},{5,3},{6,0},{7,1},{8,14},{9,15},{10,... | collective-permute-start | bytes 196616 | tf_op jit(solution)/shard_map/ppermute | solution.py:36
  7.0 5.6 %collective-permute-start.2 = (bf16[32,1024]{1,0:T(8,128)(2,1)S(1)}, bf16[32,1024]{1,0:T(8,128)(2,1)S(1)}, u32[]{:S(2)}, u32[]{:S(2)}) collective-permute-start(bf16[32,1024]{1,0:T(8,128)(2,1)S(1)} %get-tuple-element.57), channel_id=1, source_target_pairs={{0,4},{1,5},{2,6},{3,7},{4,0},{5,1},{6,2},{7,3},{8,12},{9,13},{10,... | collective-permute-start | bytes 196616 | tf_op jit(solution)/shard_map/ppermute | solution.py:36
  7.0 5.6 %collective-permute-start.3 = (bf16[32,1024]{1,0:T(8,128)(2,1)S(1)}, bf16[32,1024]{1,0:T(8,128)(2,1)S(1)}, u32[]{:S(2)}, u32[]{:S(2)}) collective-permute-start(bf16[32,1024]{1,0:T(8,128)(2,1)S(1)} %get-tuple-element.58), channel_id=1, source_target_pairs={{0,2},{1,3},{2,0},{3,1},{4,6},{5,7},{6,4},{7,5},{8,10},{9,11},{10,... | collective-permute-start | bytes 196616 | tf_op jit(solution)/shard_map/ppermute | solution.py:36
  7.7 3.9 %collective-permute-start = (bf16[16,1024]{1,0:T(8,128)(2,1)S(1)}, bf16[16,1024]{1,0:T(8,128)(2,1)S(1)}, u32[]{:S(2)}, u32[]{:S(2)}) collective-permute-start(bf16[16,1024]{1,0:T(8,128)(2,1)S(1)} %get-tuple-element.55), channel_id=1, source_target_pairs={{0,1},{1,0},{2,3},{3,2},{4,5},{5,4},{6,7},{7,6},{8,9},{9,8},{10,11... | collective-permute-start | bytes 98312 | tf_op jit(solution)/shard_map/ppermute | solution.py:36
  13.5 1.7 %collective-permute-start.4 = (bf16[40,4224]{1,0:T(8,128)(2,1)S(1)}, bf16[40,4224]{1,0:T(8,128)(2,1)S(1)}, u32[]{:S(2)}, u32[]{:S(2)}) collective-permute-start(bf16[40,4224]{1,0:T(8,128)(2,1)S(1)} %get-tuple-element.65), channel_id=1, source_target_pairs={{0,8},{8,0},{16,24},{24,16},{1,9},{9,1},{17,25},{25,17},{2,10},{10... | collective-permute-start | bytes 1013768 | tf_op jit(solution)/shard_map/ppermute | solution.py:36
  13.6 5.2 %collective-permute-start.9 = (bf16[48,1024]{1,0:T(8,128)(2,1)S(1)}, bf16[48,1024]{1,0:T(8,128)(2,1)S(1)}, u32[]{:S(2)}, u32[]{:S(2)}) collective-permute-start(bf16[48,1024]{1,0:T(8,128)(2,1)S(1)} %pad_maximum_fusion), channel_id=1, source_target_pairs={{0,1},{1,0},{2,3},{3,2},{4,5},{5,4},{6,7},{7,6},{8,9},{9,8},{10,11... | collective-permute-start | bytes 294920 | tf_op jit(solution)/shard_map/ppermute | solution.py:36
  15.3 8.6 %collective-permute-start.5 = (bf16[32,4224]{1,0:T(8,128)(2,1)S(1)}, bf16[32,4224]{1,0:T(8,128)(2,1)S(1)}, u32[]{:S(2)}, u32[]{:S(2)}) collective-permute-start(bf16[32,4224]{1,0:T(8,128)(2,1)S(1)} %get-tuple-element.67), channel_id=1, source_target_pairs={{0,16},{8,24},{16,0},{24,8},{1,17},{9,25},{17,1},{25,9},{2,18},{10... | collective-permute-start | bytes 811016 | tf_op jit(solution)/shard_map/ppermute | solution.py:36
  19.7 1.5 %collective-permute-start.10 = (bf16[24,4224]{1,0:T(8,128)(2,1)S(1)}, bf16[24,4224]{1,0:T(8,128)(2,1)S(1)}, u32[]{:S(2)}, u32[]{:S(2)}) collective-permute-start(bf16[24,4224]{1,0:T(8,128)(2,1)S(1)} %get-tuple-element.81), channel_id=1, source_target_pairs={{0,8},{8,0},{16,24},{24,16},{1,9},{9,1},{17,25},{25,17},{2,10},{10... | collective-permute-start | bytes 608264 | tf_op jit(solution)/shard_map/ppermute | solution.py:36
  21.2 7.3 %collective-permute-start.11 = (bf16[24,4224]{1,0:T(8,128)(2,1)S(1)}, bf16[24,4224]{1,0:T(8,128)(2,1)S(1)}, u32[]{:S(2)}, u32[]{:S(2)}) collective-permute-start(bf16[24,4224]{1,0:T(8,128)(2,1)S(1)} %get-tuple-element.83), channel_id=1, source_target_pairs={{0,16},{8,24},{16,0},{24,8},{1,17},{9,25},{17,1},{25,9},{2,18},{10... | collective-permute-start | bytes 608264 | tf_op jit(solution)/shard_map/ppermute | solution.py:36
  24.1 4.6 %collective-permute-start.6 = (bf16[32,4224]{1,0:T(8,128)(2,1)S(1)}, bf16[32,4224]{1,0:T(8,128)(2,1)S(1)}, u32[]{:S(2)}, u32[]{:S(2)}) collective-permute-start(bf16[32,4224]{1,0:T(8,128)(2,1)S(1)} %shard_map.106.mine_ref.refs_6_.refs_0_), channel_id=1, source_target_pairs={{0,8},{8,0},{16,24},{24,16},{1,9},{9,1},{17,25},{25,17},{2,10},{10... | collective-permute-start | bytes 811016 | tf_op jit(solution)/shard_map/ppermute | solution.py:36
  25.0 4.9 %collective-permute-start.7 = (bf16[8,4224]{1,0:T(8,128)(2,1)S(1)}, bf16[8,4224]{1,0:T(8,128)(2,1)S(1)}, u32[]{:S(2)}, u32[]{:S(2)}) collective-permute-start(bf16[8,4224]{1,0:T(8,128)(2,1)S(1)} %get-tuple-element.78), channel_id=1, source_target_pairs={{0,16},{8,24},{16,0},{24,8},{1,17},{9,25},{17,1},{25,9},{2,18},{10... | collective-permute-start | bytes 202760 | tf_op jit(solution)/shard_map/ppermute | solution.py:36
  28.7 1.4 %collective-permute-start.12 = (bf16[24,2816]{1,0:T(8,128)(2,1)S(1)}, bf16[24,2816]{1,0:T(8,128)(2,1)S(1)}, u32[]{:S(2)}, u32[]{:S(2)}) collective-permute-start(bf16[24,2816]{1,0:T(8,128)(2,1)S(1)} %get-tuple-element.87.mine_ref.refs_10_), channel_id=1, source_target_pairs={{0,8},{8,0},{16,24},{24,16},{1,9},{9,1},{17,25},{25,17},{2,10},{10... | collective-permute-start | bytes 405512 | tf_op jit(solution)/shard_map/ppermute | solution.py:36
  29.9 2.5 %collective-permute-start.8 = (bf16[8,4224]{1,0:T(8,128)(2,1)S(1)}, bf16[8,4224]{1,0:T(8,128)(2,1)S(1)}, u32[]{:S(2)}, u32[]{:S(2)}) collective-permute-start(bf16[8,4224]{1,0:T(8,128)(2,1)S(1)} %shard_map.109.mine_ref.refs_8_.refs_2_), channel_id=1, source_target_pairs={{0,8},{8,0},{16,24},{24,16},{1,9},{9,1},{17,25},{25,17},{2,10},{10... | collective-permute-start | bytes 202760 | tf_op jit(solution)/shard_map/ppermute | solution.py:36
  30.7 4.4 %collective-permute-start.13 = (bf16[64,512]{1,0:T(8,128)(2,1)S(1)}, bf16[64,512]{1,0:T(8,128)(2,1)S(1)}, u32[]{:S(2)}, u32[]{:S(2)}) collective-permute-start(bf16[64,512]{1,0:T(8,128)(2,1)S(1)} %shard_map.114), channel_id=1, source_target_pairs={{0,1},{1,0},{2,3},{3,2},{4,5},{5,4},{6,7},{7,6},{8,9},{9,8},{10,11... | collective-permute-start | bytes 196616 | tf_op jit(solution)/shard_map/ppermute | solution.py:36
  32.4 7.7 %collective-permute-start.17 = (bf16[24,1408]{1,0:T(8,128)(2,1)S(1)}, bf16[24,1408]{1,0:T(8,128)(2,1)S(1)}, u32[]{:S(2)}, u32[]{:S(2)}) collective-permute-start(bf16[24,1408]{1,0:T(8,128)(2,1)S(1)} %get-tuple-element.97.refs_4_), channel_id=1, source_target_pairs={{0,8},{8,0},{16,24},{24,16},{1,9},{9,1},{17,25},{25,17},{2,10},{10... | collective-permute-start | bytes 202760 | tf_op jit(solution)/shard_map/ppermute | solution.py:36
  35.1 7.4 %collective-permute-start.14 = (bf16[32,512]{1,0:T(8,128)(2,1)S(1)}, bf16[32,512]{1,0:T(8,128)(2,1)S(1)}, u32[]{:S(2)}, u32[]{:S(2)}) collective-permute-start(bf16[32,512]{1,0:T(8,128)(2,1)S(1)} %pad_maximum_fusion.1), channel_id=1, source_target_pairs={{0,6},{1,7},{2,4},{3,5},{4,2},{5,3},{6,0},{7,1},{8,14},{9,15},{10,... | collective-permute-start | bytes 98312 | tf_op jit(solution)/shard_map/ppermute | solution.py:36
  37.9 4.8 %collective-permute-start.15 = (bf16[32,512]{1,0:T(8,128)(2,1)S(1)}, bf16[32,512]{1,0:T(8,128)(2,1)S(1)}, u32[]{:S(2)}, u32[]{:S(2)}) collective-permute-start(bf16[32,512]{1,0:T(8,128)(2,1)S(1)} %pad_maximum_fusion.2), channel_id=1, source_target_pairs={{0,4},{1,5},{2,6},{3,7},{4,0},{5,1},{6,2},{7,3},{8,12},{9,13},{10,... | collective-permute-start | bytes 98312 | tf_op jit(solution)/shard_map/ppermute | solution.py:36
  37.9 4.8 %collective-permute-start.16 = (bf16[32,512]{1,0:T(8,128)(2,1)S(1)}, bf16[32,512]{1,0:T(8,128)(2,1)S(1)}, u32[]{:S(2)}, u32[]{:S(2)}) collective-permute-start(bf16[32,512]{1,0:T(8,128)(2,1)S(1)} %pad_maximum_fusion.3), channel_id=1, source_target_pairs={{0,2},{1,3},{2,0},{3,1},{4,6},{5,7},{6,4},{7,5},{8,10},{9,11},{10,... | collective-permute-start | bytes 98312 | tf_op jit(solution)/shard_map/ppermute | solution.py:36

commit v13 on v11

--- a/solution.py
+++ b/solution.py
@@ -272,7 +272,7 @@
         rows_ref[:, :width], deltas_ref[...], 128, up_tile_ref, up_ref, sems, copies, start=128
     )
     gather_deltas(hidden_ref, hidden_refs, (slice(0, hidden_units),) * 3)
-    send_tiles(hidden_ref[...], rows_ref[:, width:], 384, down_tile_ref, down_ref, sems, copies)
+    send_tiles(hidden_ref[...], rows_ref[:, width:], 256, down_tile_ref, down_ref, sems, copies)
     for copy in copies:
         copy.wait()
 

time: 43.7 us -> 43.7 us (level)
  no operation moved by 1% of the time
where the time goes in v13:
time: 43.7 us; the launch traced here: 43.6 us
  starting transfers between devices  20.2 us (46%)
  Pallas kernels  13.8 us (32%)
  waiting for transfers between devices  8.69 us (20%)
  between operations  0.85 us (2%)
    ppermute x18, starting transfers between devices, swap(): return lax.ppermute(value, axis, [(i, i ^ bit) for i in range(size)])  20.2 us
    pallas_call x14, Pallas kernels, call(): pl.pallas_call(kernel, out_shape=outs, in_specs=[pl.BlockSpec(memory_spac...  8.9 us
    ppermute x18, waiting for transfers between devices, swap(): return lax.ppermute(value, axis, [(i, i ^ bit) for i in range(size)])  8.69 us
    pallas_call x2, Pallas kernels, grads_call(): pl.pallas_call(kernel, out_shape=(*grads, *extra), input_output_aliases={...  4.88 us
  transfers between devices with their start and end apart: 18, of which 8 were waited for; matrix products, arithmetic and copies ran while one was open for 0% of the time, Pallas kernels for 25%

profile of v13, /device:TPU:0, one launch (start us, length us, event | category | flops | bytes accessed | tf_op | source)
XLA Modules:
  0.0 43.6 jit_solution(10151594116059435122)
XLA Ops:
  0.6 1.3 %shard_map.102 = (bf16[128,128]{1,0:T(8,128)(2,1)S(1)}, bf16[16,1024]{1,0:T(8,128)(2,1)S(1)}, bf16[16,1024]{1,0:T(8,128)(2,1)S(1)}, bf16[32,1024]{1,0:T(8,128)(2...) custom-call(s32[1,128]{1,0:T(1,128)} %bitcast.12, f32[1,128]{1,0:T(1,128)} %bitcast.13, ...), custom_call_target="tpu_custom_call" | custom-call | flops 1 | bytes 1 | tf_op jit(solution)/shard_map/pallas_call | solution.py:54
  1.9 5.1 %collective-permute-start.1 = (bf16[32,1024]{1,0:T(8,128)(2,1)S(1)}, bf16[32,1024]{1,0:T(8,128)(2,1)S(1)}, u32[]{:S(2)}, u32[]{:S(2)}) collective-permute-start(bf16[32,1024]{1,0:T(8,128)(2,1)S(1)} %get-tuple-element.56), channel_id=1, source_target_pairs={{0,6},{1,7},{2,4},{3,5},{4,2},{5,3},{6,0},{7,1},{8,14},{9,15},{10,... | collective-permute-start | bytes 196616 | tf_op jit(solution)/shard_map/ppermute | solution.py:36
  7.0 0.6 %collective-permute-start.3 = (bf16[32,1024]{1,0:T(8,128)(2,1)S(1)}, bf16[32,1024]{1,0:T(8,128)(2,1)S(1)}, u32[]{:S(2)}, u32[]{:S(2)}) collective-permute-start(bf16[32,1024]{1,0:T(8,128)(2,1)S(1)} %get-tuple-element.58), channel_id=1, source_target_pairs={{0,2},{1,3},{2,0},{3,1},{4,6},{5,7},{6,4},{7,5},{8,10},{9,11},{10,... | collective-permute-start | bytes 196616 | tf_op jit(solution)/shard_map/ppermute | solution.py:36
  7.7 1.7 %collective-permute-start = (bf16[16,1024]{1,0:T(8,128)(2,1)S(1)}, bf16[16,1024]{1,0:T(8,128)(2,1)S(1)}, u32[]{:S(2)}, u32[]{:S(2)}) collective-permute-start(bf16[16,1024]{1,0:T(8,128)(2,1)S(1)} %get-tuple-element.55), channel_id=1, source_target_pairs={{0,1},{1,0},{2,3},{3,2},{4,5},{5,4},{6,7},{7,6},{8,9},{9,8},{10,11... | collective-permute-start | bytes 98312 | tf_op jit(solution)/shard_map/ppermute | solution.py:36
  9.3 2.3 %shard_map.103 = (bf16[512,1408]{1,0:T(8,128)(2,1)S(1)}, bf16[512,1408]{1,0:T(8,128)(2,1)S(1)}, bf16[512,1408]{1,0:T(8,128)(2,1)S(1)}) custom-call(bf16[1408,512]{1,0:T(8,128)(2,1)} %bitcast.9, bf16[512,1408]{1,0:T(8,128)(2,1)} %bitcast.10, bf16[512,1408]{1,0:T(8,128)(2,1)} %bitcast.11, bf16[128,128]{1,0:T(8,128)(2,1)S(1)} %get-tuple-element.70.marker_hbm.refs_2_), custom_call_target="tpu_custom_call" | custom-call | flops 10000000 | bytes 10000000 | tf_op jit(solution)/shard_map/pallas_call | solution.py:54
  11.6 1.0 %collective-permute-done.2.refs_2_ = bf16[32,1024]{1,0:T(8,128)(2,1)S(1)} collective-permute-done((bf16[32,1024]{1,0:T(8,128)(2,1)S(1)}, bf16[32,1024]{1,0:T(8,128)(2,1)S(1)}, u32[]{:S(2)}, u32[]{:S(2)}) %collective-permute-start.2) | collective-permute-done | bytes 65568 | tf_op jit(solution)/shard_map/ppermute | solution.py:36
  12.6 0.8 %shard_map.104 = (f32[40,4224]{1,0:T(8,128)S(1)}, bf16[40,4224]{1,0:T(8,128)(2,1)S(1)}) custom-call(bf16[16,1024]{1,0:T(8,128)(2,1)S(1)} %collective-permute-done.refs_0_, bf16[32,1024]{1,0:T(8,128)(2,1)S(1)} %collective-permute-done.1.refs_1_, bf16[32,1024]{1,0:T(8,128)(2,1)S(1)} %collective-permute-done.2.refs_2_, ...), custom_call_target="tpu_custom_call" | custom-call | flops 1 | bytes 1 | tf_op jit(solution)/shard_map/pallas_call | solution.py:54
  13.6 1.6 %collective-permute-start.9 = (bf16[48,1024]{1,0:T(8,128)(2,1)S(1)}, bf16[48,1024]{1,0:T(8,128)(2,1)S(1)}, u32[]{:S(2)}, u32[]{:S(2)}) collective-permute-start(bf16[48,1024]{1,0:T(8,128)(2,1)S(1)} %pad_maximum_fusion), channel_id=1, source_target_pairs={{0,1},{1,0},{2,3},{3,2},{4,5},{5,4},{6,7},{7,6},{8,9},{9,8},{10,11... | collective-permute-start | bytes 294920 | tf_op jit(solution)/shard_map/ppermute | solution.py:36
  15.3 1.6 %collective-permute-start.5 = (bf16[32,4224]{1,0:T(8,128)(2,1)S(1)}, bf16[32,4224]{1,0:T(8,128)(2,1)S(1)}, u32[]{:S(2)}, u32[]{:S(2)}) collective-permute-start(bf16[32,4224]{1,0:T(8,128)(2,1)S(1)} %get-tuple-element.67), channel_id=1, source_target_pairs={{0,16},{8,24},{16,0},{24,8},{1,17},{9,25},{17,1},{25,9},{2,18},{10... | collective-permute-start | bytes 811016 | tf_op jit(solution)/shard_map/ppermute | solution.py:36
  16.8 2.0 %collective-permute-done.9.refs_0_.refs_5_ = bf16[48,1024]{1,0:T(8,128)(2,1)S(1)} collective-permute-done((bf16[48,1024]{1,0:T(8,128)(2,1)S(1)}, bf16[48,1024]{1,0:T(8,128)(2,1)S(1)}, u32[]{:S(2)}, u32[]{:S(2)}) %collective-permute-start.9) | collective-permute-done | bytes 98336 | tf_op jit(solution)/shard_map/ppermute | solution.py:36
  18.8 0.8 %shard_map.111 = (f32[24,4224]{1,0:T(8,128)S(1)}, bf16[24,4224]{1,0:T(8,128)(2,1)S(1)}) custom-call(bf16[48,1024]{1,0:T(8,128)(2,1)S(1)} %collective-permute-done.9.refs_0_.refs_5_, bf16[512,1408]{1,0:T(8,128)(2,1)S(1)} %get-tuple-element.68.refs_5_.refs_0_.refs_1_, bf16[512,1408]{1,0:T(8,128)(2,1)S(1)} %get-tuple-element.69.refs_6_.refs_1_.refs_2_, ...), custom_call_target="tpu_custom_call" | custom-call | flops 300000000 | bytes 300000000 | tf_op jit(solution)/shard_map/pallas_call | solution.py:54
  19.7 1.4 %collective-permute-done.10.received_ref = bf16[24,4224]{1,0:T(8,128)(2,1)S(1)} collective-permute-done((bf16[24,4224]{1,0:T(8,128)(2,1)S(1)}, bf16[24,4224]{1,0:T(8,128)(2,1)S(1)}, u32[]{:S(2)}, u32[]{:S(2)}) %collective-permute-start.10) | collective-permute-done | bytes 202784 | tf_op jit(solution)/shard_map/ppermute | solution.py:36
  21.2 1.6 %collective-permute-start.11 = (bf16[24,4224]{1,0:T(8,128)(2,1)S(1)}, bf16[24,4224]{1,0:T(8,128)(2,1)S(1)}, u32[]{:S(2)}, u32[]{:S(2)}) collective-permute-start(bf16[24,4224]{1,0:T(8,128)(2,1)S(1)} %get-tuple-element.83), channel_id=1, source_target_pairs={{0,16},{8,24},{16,0},{24,8},{1,17},{9,25},{17,1},{25,9},{2,18},{10... | collective-permute-start | bytes 608264 | tf_op jit(solution)/shard_map/ppermute | solution.py:36
  22.8 1.1 %collective-permute-done.5.received_ref = bf16[32,4224]{1,0:T(8,128)(2,1)S(1)} collective-permute-done((bf16[32,4224]{1,0:T(8,128)(2,1)S(1)}, bf16[32,4224]{1,0:T(8,128)(2,1)S(1)}, u32[]{:S(2)}, u32[]{:S(2)}) %collective-permute-start.5) | collective-permute-done | bytes 270368 | tf_op jit(solution)/shard_map/ppermute | solution.py:36
  24.1 0.8 %shard_map.107 = (bf16[1408,512]{1,0:T(8,128)(2,1)S(1)}, bf16[1408,512]{1,0:T(8,128)(2,1)S(1)}, bf16[128,128]{1,0:T(8,128)(2,1)S(1)}) custom-call(bf16[512,1408]{1,0:T(8,128)(2,1)S(1)} %get-tuple-element.68.refs_5_.refs_0_.refs_1_, bf16[512,1408]{1,0:T(8,128)(2,1)S(1)} %get-tuple-element.69.refs_6_.refs_1_.refs_2_, ...), custom_call_target="tpu_custom_call" | custom-call | flops 1 | bytes 1 | tf_op jit(solution)/shard_map/pallas_call | solution.py:54
  25.0 1.6 %collective-permute-start.7 = (bf16[8,4224]{1,0:T(8,128)(2,1)S(1)}, bf16[8,4224]{1,0:T(8,128)(2,1)S(1)}, u32[]{:S(2)}, u32[]{:S(2)}) collective-permute-start(bf16[8,4224]{1,0:T(8,128)(2,1)S(1)} %get-tuple-element.78), channel_id=1, source_target_pairs={{0,16},{8,24},{16,0},{24,8},{1,17},{9,25},{17,1},{25,9},{2,18},{10... | collective-permute-start | bytes 202760 | tf_op jit(solution)/shard_map/ppermute | solution.py:36
  26.5 2.1 %collective-permute-done.11.received_ref = bf16[24,4224]{1,0:T(8,128)(2,1)S(1)} collective-permute-done((bf16[24,4224]{1,0:T(8,128)(2,1)S(1)}, bf16[24,4224]{1,0:T(8,128)(2,1)S(1)}, u32[]{:S(2)}, u32[]{:S(2)}) %collective-permute-start.11) | collective-permute-done | bytes 202784 | tf_op jit(solution)/shard_map/ppermute | solution.py:36
  28.8 0.6 %shard_map.108 = (bf16[16,512]{1,0:T(8,128)(2,1)S(1)}, bf16[16,512]{1,0:T(8,128)(2,1)S(1)}, bf16[16,512]{1,0:T(8,128)(2,1)S(1)}, bf16[16,512]{1,0:T(8,128)(2,1)S(1)}) custom-call(bf16[32,4224]{1,0:T(8,128)(2,1)S(1)} %shard_map.106.mine_ref.refs_6_.refs_0_, bf16[32,4224]{1,0:T(8,128)(2,1)S(1)} %collective-permute-done.6.other_ref.refs_7_.refs_1_, ...), custom_call_target="tpu_custom_call" | custom-call | flops 1 | bytes 1 | tf_op jit(solution)/shard_map/pallas_call | solution.py:54
  30.7 1.7 %collective-permute-start.13 = (bf16[64,512]{1,0:T(8,128)(2,1)S(1)}, bf16[64,512]{1,0:T(8,128)(2,1)S(1)}, u32[]{:S(2)}, u32[]{:S(2)}) collective-permute-start(bf16[64,512]{1,0:T(8,128)(2,1)S(1)} %shard_map.114), channel_id=1, source_target_pairs={{0,1},{1,0},{2,3},{3,2},{4,5},{5,4},{6,7},{7,6},{8,9},{9,8},{10,11... | collective-permute-start | bytes 196616 | tf_op jit(solution)/shard_map/ppermute | solution.py:36
  32.9 2.2 %shard_map.115 = (f32[512,1408]{1,0:T(8,128)}, f32[512,1408]{1,0:T(8,128)}, bf16[128,1024]{1,0:T(8,128)(2,1)S(1)}, bf16[128,1408]{1,0:T(8,128)(2,1)S(1)}) custom-call(bf16[16,1024]{1,0:T(8,128)(2,1)S(1)} %collective-permute-done.refs_0_, bf16[32,1024]{1,0:T(8,128)(2,1)S(1)} %collective-permute-done.1.refs_1_, ...), custom_call_target="tpu_custom_call" | custom-call | flops 10000000 | bytes 10000000 | tf_op jit(solution)/shard_map/pallas_call | solution.py:284
  35.1 2.8 %collective-permute-start.14 = (bf16[32,512]{1,0:T(8,128)(2,1)S(1)}, bf16[32,512]{1,0:T(8,128)(2,1)S(1)}, u32[]{:S(2)}, u32[]{:S(2)}) collective-permute-start(bf16[32,512]{1,0:T(8,128)(2,1)S(1)} %pad_maximum_fusion.1), channel_id=1, source_target_pairs={{0,6},{1,7},{2,4},{3,5},{4,2},{5,3},{6,0},{7,1},{8,14},{9,15},{10,... | collective-permute-start | bytes 98312 | tf_op jit(solution)/shard_map/ppermute | solution.py:36
  37.9 1.7 %collective-permute-start.16 = (bf16[32,512]{1,0:T(8,128)(2,1)S(1)}, bf16[32,512]{1,0:T(8,128)(2,1)S(1)}, u32[]{:S(2)}, u32[]{:S(2)}) collective-permute-start(bf16[32,512]{1,0:T(8,128)(2,1)S(1)} %pad_maximum_fusion.3), channel_id=1, source_target_pairs={{0,2},{1,3},{2,0},{3,1},{4,6},{5,7},{6,4},{7,5},{8,10},{9,11},{10,... | collective-permute-start | bytes 98312 | tf_op jit(solution)/shard_map/ppermute | solution.py:36
  39.6 2.7 %shard_map.117 = (f32[512,1408]{1,0:T(8,128)}, f32[1408,512]{1,0:T(8,128)}) custom-call(f32[512,1408]{1,0:T(8,128)} %get-tuple-element.94.started_ref, bf16[128,1024]{1,0:T(8,128)(2,1)S(1)} %get-tuple-element.95.rows_ref, bf16[128,1408]{1,0:T(8,128)(2,1)S(1)} %get-tuple-element.96.deltas_ref, ...), custom_call_target="tpu_custom_call", output_to_operand_aliasing={{0}: (0, {})} | custom-call | flops 10000000 | bytes 10000000 | tf_op jit(solution)/shard_map/pallas_call | solution.py:284
  42.7 0.8 %shard_map.116 = bf16[128,512]{1,0:T(8,128)(2,1)} custom-call(bf16[128,128]{1,0:T(8,128)(2,1)S(1)} %get-tuple-element.71.chosen_ref, bf16[16,512]{1,0:T(8,128)(2,1)S(1)} %shard_map.110.own_ref, bf16[64,512]{1,0:T(8,128)(2,1)S(1)} %collective-permute-done.13.from_pair_ref, bf16[32,512]{1,0:T(8,128)(2,1)S(1)} %collective-permute-done.14.refs_0_, ...), custom_call_target="tpu_custom_call" | custom-call | flops 1 | bytes 1 | tf_op jit(solution)/shard_map/pallas_call | solution.py:54
  (36 shorter events, 3.0 us)
Async XLA Ops:
  1.9 9.7 %collective-permute-start.1 = (bf16[32,1024]{1,0:T(8,128)(2,1)S(1)}, bf16[32,1024]{1,0:T(8,128)(2,1)S(1)}, u32[]{:S(2)}, u32[]{:S(2)}) collective-permute-start(bf16[32,1024]{1,0:T(8,128)(2,1)S(1)} %get-tuple-element.56), channel_id=1, source_target_pairs={{0,6},{1,7},{2,4},{3,5},{4,2},{5,3},{6,0},{7,1},{8,14},{9,15},{10,... | collective-permute-start | bytes 196616 | tf_op jit(solution)/shard_map/ppermute | solution.py:36
  7.0 5.6 %collective-permute-start.2 = (bf16[32,1024]{1,0:T(8,128)(2,1)S(1)}, bf16[32,1024]{1,0:T(8,128)(2,1)S(1)}, u32[]{:S(2)}, u32[]{:S(2)}) collective-permute-start(bf16[32,1024]{1,0:T(8,128)(2,1)S(1)} %get-tuple-element.57), channel_id=1, source_target_pairs={{0,4},{1,5},{2,6},{3,7},{4,0},{5,1},{6,2},{7,3},{8,12},{9,13},{10,... | collective-permute-start | bytes 196616 | tf_op jit(solution)/shard_map/ppermute | solution.py:36
  7.0 5.6 %collective-permute-start.3 = (bf16[32,1024]{1,0:T(8,128)(2,1)S(1)}, bf16[32,1024]{1,0:T(8,128)(2,1)S(1)}, u32[]{:S(2)}, u32[]{:S(2)}) collective-permute-start(bf16[32,1024]{1,0:T(8,128)(2,1)S(1)} %get-tuple-element.58), channel_id=1, source_target_pairs={{0,2},{1,3},{2,0},{3,1},{4,6},{5,7},{6,4},{7,5},{8,10},{9,11},{10,... | collective-permute-start | bytes 196616 | tf_op jit(solution)/shard_map/ppermute | solution.py:36
  7.7 3.9 %collective-permute-start = (bf16[16,1024]{1,0:T(8,128)(2,1)S(1)}, bf16[16,1024]{1,0:T(8,128)(2,1)S(1)}, u32[]{:S(2)}, u32[]{:S(2)}) collective-permute-start(bf16[16,1024]{1,0:T(8,128)(2,1)S(1)} %get-tuple-element.55), channel_id=1, source_target_pairs={{0,1},{1,0},{2,3},{3,2},{4,5},{5,4},{6,7},{7,6},{8,9},{9,8},{10,11... | collective-permute-start | bytes 98312 | tf_op jit(solution)/shard_map/ppermute | solution.py:36
  13.5 1.7 %collective-permute-start.4 = (bf16[40,4224]{1,0:T(8,128)(2,1)S(1)}, bf16[40,4224]{1,0:T(8,128)(2,1)S(1)}, u32[]{:S(2)}, u32[]{:S(2)}) collective-permute-start(bf16[40,4224]{1,0:T(8,128)(2,1)S(1)} %get-tuple-element.65), channel_id=1, source_target_pairs={{0,8},{8,0},{16,24},{24,16},{1,9},{9,1},{17,25},{25,17},{2,10},{10... | collective-permute-start | bytes 1013768 | tf_op jit(solution)/shard_map/ppermute | solution.py:36
  13.6 5.2 %collective-permute-start.9 = (bf16[48,1024]{1,0:T(8,128)(2,1)S(1)}, bf16[48,1024]{1,0:T(8,128)(2,1)S(1)}, u32[]{:S(2)}, u32[]{:S(2)}) collective-permute-start(bf16[48,1024]{1,0:T(8,128)(2,1)S(1)} %pad_maximum_fusion), channel_id=1, source_target_pairs={{0,1},{1,0},{2,3},{3,2},{4,5},{5,4},{6,7},{7,6},{8,9},{9,8},{10,11... | collective-permute-start | bytes 294920 | tf_op jit(solution)/shard_map/ppermute | solution.py:36
  15.3 8.6 %collective-permute-start.5 = (bf16[32,4224]{1,0:T(8,128)(2,1)S(1)}, bf16[32,4224]{1,0:T(8,128)(2,1)S(1)}, u32[]{:S(2)}, u32[]{:S(2)}) collective-permute-start(bf16[32,4224]{1,0:T(8,128)(2,1)S(1)} %get-tuple-element.67), channel_id=1, source_target_pairs={{0,16},{8,24},{16,0},{24,8},{1,17},{9,25},{17,1},{25,9},{2,18},{10... | collective-permute-start | bytes 811016 | tf_op jit(solution)/shard_map/ppermute | solution.py:36
  19.7 1.5 %collective-permute-start.10 = (bf16[24,4224]{1,0:T(8,128)(2,1)S(1)}, bf16[24,4224]{1,0:T(8,128)(2,1)S(1)}, u32[]{:S(2)}, u32[]{:S(2)}) collective-permute-start(bf16[24,4224]{1,0:T(8,128)(2,1)S(1)} %get-tuple-element.81), channel_id=1, source_target_pairs={{0,8},{8,0},{16,24},{24,16},{1,9},{9,1},{17,25},{25,17},{2,10},{10... | collective-permute-start | bytes 608264 | tf_op jit(solution)/shard_map/ppermute | solution.py:36
  21.2 7.3 %collective-permute-start.11 = (bf16[24,4224]{1,0:T(8,128)(2,1)S(1)}, bf16[24,4224]{1,0:T(8,128)(2,1)S(1)}, u32[]{:S(2)}, u32[]{:S(2)}) collective-permute-start(bf16[24,4224]{1,0:T(8,128)(2,1)S(1)} %get-tuple-element.83), channel_id=1, source_target_pairs={{0,16},{8,24},{16,0},{24,8},{1,17},{9,25},{17,1},{25,9},{2,18},{10... | collective-permute-start | bytes 608264 | tf_op jit(solution)/shard_map/ppermute | solution.py:36
  24.1 4.6 %collective-permute-start.6 = (bf16[32,4224]{1,0:T(8,128)(2,1)S(1)}, bf16[32,4224]{1,0:T(8,128)(2,1)S(1)}, u32[]{:S(2)}, u32[]{:S(2)}) collective-permute-start(bf16[32,4224]{1,0:T(8,128)(2,1)S(1)} %shard_map.106.mine_ref.refs_6_.refs_0_), channel_id=1, source_target_pairs={{0,8},{8,0},{16,24},{24,16},{1,9},{9,1},{17,25},{25,17},{2,10},{10... | collective-permute-start | bytes 811016 | tf_op jit(solution)/shard_map/ppermute | solution.py:36
  25.0 4.9 %collective-permute-start.7 = (bf16[8,4224]{1,0:T(8,128)(2,1)S(1)}, bf16[8,4224]{1,0:T(8,128)(2,1)S(1)}, u32[]{:S(2)}, u32[]{:S(2)}) collective-permute-start(bf16[8,4224]{1,0:T(8,128)(2,1)S(1)} %get-tuple-element.78), channel_id=1, source_target_pairs={{0,16},{8,24},{16,0},{24,8},{1,17},{9,25},{17,1},{25,9},{2,18},{10... | collective-permute-start | bytes 202760 | tf_op jit(solution)/shard_map/ppermute | solution.py:36
  28.7 1.4 %collective-permute-start.12 = (bf16[24,2816]{1,0:T(8,128)(2,1)S(1)}, bf16[24,2816]{1,0:T(8,128)(2,1)S(1)}, u32[]{:S(2)}, u32[]{:S(2)}) collective-permute-start(bf16[24,2816]{1,0:T(8,128)(2,1)S(1)} %get-tuple-element.87.mine_ref.refs_10_), channel_id=1, source_target_pairs={{0,8},{8,0},{16,24},{24,16},{1,9},{9,1},{17,25},{25,17},{2,10},{10... | collective-permute-start | bytes 405512 | tf_op jit(solution)/shard_map/ppermute | solution.py:36
  29.9 2.5 %collective-permute-start.8 = (bf16[8,4224]{1,0:T(8,128)(2,1)S(1)}, bf16[8,4224]{1,0:T(8,128)(2,1)S(1)}, u32[]{:S(2)}, u32[]{:S(2)}) collective-permute-start(bf16[8,4224]{1,0:T(8,128)(2,1)S(1)} %shard_map.109.mine_ref.refs_8_.refs_2_), channel_id=1, source_target_pairs={{0,8},{8,0},{16,24},{24,16},{1,9},{9,1},{17,25},{25,17},{2,10},{10... | collective-permute-start | bytes 202760 | tf_op jit(solution)/shard_map/ppermute | solution.py:36
  30.7 4.4 %collective-permute-start.13 = (bf16[64,512]{1,0:T(8,128)(2,1)S(1)}, bf16[64,512]{1,0:T(8,128)(2,1)S(1)}, u32[]{:S(2)}, u32[]{:S(2)}) collective-permute-start(bf16[64,512]{1,0:T(8,128)(2,1)S(1)} %shard_map.114), channel_id=1, source_target_pairs={{0,1},{1,0},{2,3},{3,2},{4,5},{5,4},{6,7},{7,6},{8,9},{9,8},{10,11... | collective-permute-start | bytes 196616 | tf_op jit(solution)/shard_map/ppermute | solution.py:36
  32.4 7.2 %collective-permute-start.17 = (bf16[24,1408]{1,0:T(8,128)(2,1)S(1)}, bf16[24,1408]{1,0:T(8,128)(2,1)S(1)}, u32[]{:S(2)}, u32[]{:S(2)}) collective-permute-start(bf16[24,1408]{1,0:T(8,128)(2,1)S(1)} %get-tuple-element.97.refs_4_), channel_id=1, source_target_pairs={{0,8},{8,0},{16,24},{24,16},{1,9},{9,1},{17,25},{25,17},{2,10},{10... | collective-permute-start | bytes 202760 | tf_op jit(solution)/shard_map/ppermute | solution.py:36
  35.1 7.2 %collective-permute-start.14 = (bf16[32,512]{1,0:T(8,128)(2,1)S(1)}, bf16[32,512]{1,0:T(8,128)(2,1)S(1)}, u32[]{:S(2)}, u32[]{:S(2)}) collective-permute-start(bf16[32,512]{1,0:T(8,128)(2,1)S(1)} %pad_maximum_fusion.1), channel_id=1, source_target_pairs={{0,6},{1,7},{2,4},{3,5},{4,2},{5,3},{6,0},{7,1},{8,14},{9,15},{10,... | collective-permute-start | bytes 98312 | tf_op jit(solution)/shard_map/ppermute | solution.py:36
  37.9 4.8 %collective-permute-start.15 = (bf16[32,512]{1,0:T(8,128)(2,1)S(1)}, bf16[32,512]{1,0:T(8,128)(2,1)S(1)}, u32[]{:S(2)}, u32[]{:S(2)}) collective-permute-start(bf16[32,512]{1,0:T(8,128)(2,1)S(1)} %pad_maximum_fusion.2), channel_id=1, source_target_pairs={{0,4},{1,5},{2,6},{3,7},{4,0},{5,1},{6,2},{7,3},{8,12},{9,13},{10,... | collective-permute-start | bytes 98312 | tf_op jit(solution)/shard_map/ppermute | solution.py:36
  37.9 4.8 %collective-permute-start.16 = (bf16[32,512]{1,0:T(8,128)(2,1)S(1)}, bf16[32,512]{1,0:T(8,128)(2,1)S(1)}, u32[]{:S(2)}, u32[]{:S(2)}) collective-permute-start(bf16[32,512]{1,0:T(8,128)(2,1)S(1)} %pad_maximum_fusion.3), channel_id=1, source_target_pairs={{0,2},{1,3},{2,0},{3,1},{4,6},{5,7},{6,4},{7,5},{8,10},{9,11},{10,... | collective-permute-start | bytes 98312 | tf_op jit(solution)/shard_map/ppermute | solution.py:36
